TPU v7x, 32 devices: a whole 2x2x4 slice. The times are simulated.
32 devices in a mesh: blk: 2 (over x), wide: 16 (over z, y, core).
Axes of the slice: x: 2, y: 2, z: 4, core: 2. Of those that a mesh axis runs over, the one named last changes fastest.
Arguments:
- layer_input: bfloat16 [16, 256, 2048], P('wide', 'blk'), may hold values from -6 to 6
- lengths: int32 [16], P('wide'), may hold values from 129 to 256, as said below
- w_query: bfloat16 [2048, 2048], P(('blk', 'wide')), may hold values from -0.125 to 0.125
- w_key: bfloat16 [2048, 2048], P(('blk', 'wide')), may hold values from -0.125 to 0.125
- w_value: bfloat16 [2048, 2048], P(('blk', 'wide')), may hold values from -0.125 to 0.125
- w_output: bfloat16 [2048, 2048], P(('blk', 'wide')), may hold values from -0.125 to 0.125
- query_gain: bfloat16 [2048], P(('blk', 'wide')), may hold values from 0.099609375 to 1.8984375
- key_gain: bfloat16 [2048], P(('blk', 'wide')), may hold values from 0.099609375 to 1.8984375
- attn_gain: bfloat16 [2048], P(('blk', 'wide')), may hold values from 0.099609375 to 1.8984375
- mlp_gain: bfloat16 [2048], P(('blk', 'wide')), may hold values from 0.099609375 to 1.8984375
- w_gate: bfloat16 [2048, 8192], P('blk', 'wide'), may hold values from -0.125 to 0.125
- w_up: bfloat16 [2048, 8192], P('blk', 'wide'), may hold values from -0.125 to 0.125
- w_down: bfloat16 [2048, 8192], P('blk', 'wide'), may hold values from -0.0625 to 0.0625
- grad_output: bfloat16 [16, 256, 2048], P('wide', 'blk'), may hold values from -6 to 6
Outputs:
- output: bfloat16 [16, 256, 2048], P('wide', 'blk')
- input_grad: bfloat16 [16, 256, 2048], P('wide', 'blk')
- grad_w_query: float32 [2048, 2048], P(('blk', 'wide'))
- grad_w_key: float32 [2048, 2048], P(('blk', 'wide'))
- grad_w_value: float32 [2048, 2048], P(('blk', 'wide'))
- grad_w_output: float32 [2048, 2048], P(('blk', 'wide'))
- grad_query_gain: float32 [2048], P(('blk', 'wide'))
- grad_key_gain: float32 [2048], P(('blk', 'wide'))
- grad_attn_gain: float32 [2048], P(('blk', 'wide'))
- grad_mlp_gain: float32 [2048], P(('blk', 'wide'))
- grad_w_gate: float32 [2048, 8192], P('blk', 'wide')
- grad_w_up: float32 [2048, 8192], P('blk', 'wide')
- grad_w_down: float32 [2048, 8192], P('blk', 'wide')
Inputs may be any that keep to these rules, and one draw needn't show every extreme that they name: `lengths`: every sequence has at least 129 valid tokens, and one has exactly 256.
All inputs are finite; a program needn't handle non-finite values.
Results may differ from a plain program's by a relative error of at most 0.017.
Values may be sent and summed in bfloat16 or wider, within the bound.
No kernel may reach another device: no remote copies, remote signals or barrier semaphores. Data moves between devices by JAX's collectives and lax.ppermute only.
A program may use at most 384 MiB of HBM per device.

v0:
```python
from functools import partial
import math

import jax
import jax.numpy as jnp
from jax import lax
from jax.sharding import PartitionSpec as P

HEAD_DIM = 128


EPSILON = 1e-06
NEGATIVE = -1e30


def passed_along(value, axis, steps):
    count = lax.axis_size(axis)
    leading, last = (max(0, -steps), min(count, count - steps))
    return lax.ppermute(value, axis, [(source, source + steps) for source in range(leading, last)])


def rms_scale(values, gain):
    return values * lax.rsqrt(jnp.mean(values * values, axis=-1, keepdims=True) + EPSILON) * gain


def rotate(values, positions):
    count = values.shape[0]
    half = HEAD_DIM // 2
    frequency = jnp.exp(
        jnp.arange(half, dtype=jnp.float32) * (-2.0 * math.log(500000.0) / HEAD_DIM)
    )
    angles = positions.astype(jnp.float32)[:, None] * frequency[None, :]
    cosine = jnp.cos(angles)[:, None, :]
    sine = jnp.sin(angles)[:, None, :]
    heads_view = values.reshape(count, -1, HEAD_DIM)
    first = heads_view[..., :half]
    second = heads_view[..., half:]
    turned = jnp.concatenate(
        [first * cosine - second * sine, second * cosine + first * sine], axis=-1
    )
    return turned.reshape(count, -1)


def prepare(positions, query, key_proj, query_gain, key_gain):
    return (
        rotate(rms_scale(query, query_gain), positions),
        rotate(rms_scale(key_proj, key_gain), positions),
    )


def swiglu(gate, up_proj):
    return jax.nn.silu(gate) * up_proj


def rounded(values):
    return lax.optimization_barrier(values.astype(jnp.bfloat16)).astype(jnp.float32)


def contract(left, right, left_dim, right_dim):
    return lax.dot_general(
        left, right, (((left_dim,), (right_dim,)), ((), ())), preferred_element_type=jnp.float32
    )


def masked_scores(query_heads, key_heads, valid):
    logits = jnp.einsum(
        "qhd,khd->hqk", query_heads, key_heads, preferred_element_type=jnp.float32
    ) * HEAD_DIM ** (-0.5)
    return jnp.where(valid[None], logits, NEGATIVE)


def body(
    layer_input,
    lengths,
    w_query,
    w_key,
    w_value,
    w_output,
    query_gain,
    key_gain,
    attn_gain,
    mlp_gain,
    w_gate,
    w_up,
    w_down,
    grad_output,
):
    inputs = layer_input[0]
    tok_rows = inputs.shape[0]
    model_width = inputs.shape[1]
    length = lengths[0]
    blk_pos = lax.axis_index("blk")
    full_query, full_key, full_value, full_out, gain_query, gain_key, gain_attn, gain_mlp = (
        lax.all_gather(w_query, ("blk", "wide"), axis=0, tiled=True),
        lax.all_gather(w_key, ("blk", "wide"), axis=0, tiled=True),
        lax.all_gather(w_value, ("blk", "wide"), axis=0, tiled=True),
        lax.all_gather(w_output, ("blk", "wide"), axis=0, tiled=True),
        lax.all_gather(query_gain, ("blk", "wide"), axis=0, tiled=True),
        lax.all_gather(key_gain, ("blk", "wide"), axis=0, tiled=True),
        lax.all_gather(attn_gain, ("blk", "wide"), axis=0, tiled=True),
        lax.all_gather(mlp_gain, ("blk", "wide"), axis=0, tiled=True),
    )
    gate_local, up_local, down_local = (
        lax.all_gather(w_gate, "blk", axis=0, tiled=True),
        lax.all_gather(w_up, "blk", axis=0, tiled=True),
        lax.all_gather(w_down, "blk", axis=0, tiled=True),
    )
    positions = blk_pos * tok_rows + jnp.arange(tok_rows, dtype=jnp.int32)
    query = jnp.dot(inputs, full_query, preferred_element_type=jnp.float32)
    key_proj = jnp.dot(inputs, full_key, preferred_element_type=jnp.float32)
    value_b = jnp.dot(inputs, full_value, preferred_element_type=jnp.float32).astype(jnp.bfloat16)
    (query_rot, key_rot), prepare_back = jax.vjp(
        partial(prepare, positions),
        query,
        key_proj,
        gain_query.astype(jnp.float32),
        gain_key.astype(jnp.float32),
    )
    query_heads = query_rot.astype(jnp.bfloat16).reshape(tok_rows, -1, HEAD_DIM)
    key_b = key_rot.astype(jnp.bfloat16)
    key_prev, value_prev = passed_along((key_b, value_b), "blk", 1)
    keys_all = jnp.concatenate([key_prev, key_b], axis=0).reshape(2 * tok_rows, -1, HEAD_DIM)
    values_all = jnp.concatenate([value_prev, value_b], axis=0).reshape(2 * tok_rows, -1, HEAD_DIM)
    key_pos = jnp.concatenate([positions - tok_rows, positions])
    valid = (
        (key_pos[None, :] <= positions[:, None])
        & (key_pos[None, :] < length)
        & (key_pos[None, :] >= 0)
    )
    logits = masked_scores(query_heads, keys_all, valid)
    peak = jnp.max(logits, axis=-1, keepdims=True)
    powers = jnp.exp(logits - peak)
    totals = jnp.sum(powers, axis=-1, keepdims=True)
    chances = powers / totals
    log_total = peak + jnp.log(totals)
    attended = (
        jnp.einsum(
            "hqk,khd->qhd",
            chances.astype(jnp.bfloat16),
            values_all,
            preferred_element_type=jnp.float32,
        )
        .reshape(tok_rows, model_width)
        .astype(jnp.bfloat16)
    )
    branch = jnp.dot(attended, full_out, preferred_element_type=jnp.float32)
    normed, attn_back = jax.vjp(rms_scale, branch, gain_attn.astype(jnp.float32))
    hidden_state = inputs.astype(jnp.float32) + normed
    mlp_in = hidden_state.astype(jnp.bfloat16)
    piece = lax.all_gather(mlp_in, "wide", axis=0, tiled=True)
    stacked = jnp.stack(
        [
            jnp.dot(piece, gate_local, preferred_element_type=jnp.float32),
            jnp.dot(piece, up_local, preferred_element_type=jnp.float32),
        ]
    )
    product, act_back = jax.vjp(swiglu, stacked[0], stacked[1])
    product_b = product.astype(jnp.bfloat16)
    block = product_b
    mlp_out = lax.psum_scatter(
        contract(block, down_local, 1, 1), "wide", scatter_dimension=0, tiled=True
    )
    post, mlp_back = jax.vjp(rms_scale, mlp_out, gain_mlp.astype(jnp.float32))
    output = (hidden_state + post).astype(jnp.bfloat16)
    grad_out = grad_output[0].astype(jnp.float32)
    grad_mlp, grad_gain_mlp = mlp_back(grad_out)
    grad_mlp_b = grad_mlp.astype(jnp.bfloat16)
    piece = lax.all_gather(grad_mlp_b, "wide", axis=0, tiled=True)
    block = product_b
    down_acc = contract(piece, block, 0, 0)
    grad_prod = jnp.dot(piece, down_local, preferred_element_type=jnp.float32)
    grad_wd = down_acc
    grad_gate, grad_up = act_back(grad_prod)
    gate_b = grad_gate.astype(jnp.bfloat16)
    up_b = grad_up.astype(jnp.bfloat16)
    gate_part = gate_b
    up_part = up_b
    grad_mid = lax.psum_scatter(
        contract(gate_part, gate_local, 1, 1) + contract(up_part, up_local, 1, 1),
        "wide",
        scatter_dimension=0,
        tiled=True,
    )
    piece = lax.all_gather(mlp_in, "wide", axis=0, tiled=True)
    gate_part = gate_b
    up_part = up_b
    grad_wg = contract(piece, gate_part, 0, 0)
    grad_wu = contract(piece, up_part, 0, 0)
    grad_wg, grad_wu, grad_wd = (
        lax.psum_scatter(
            grad_wg.astype(jnp.bfloat16), "blk", scatter_dimension=0, tiled=True
        ).astype(jnp.float32),
        lax.psum_scatter(
            grad_wu.astype(jnp.bfloat16), "blk", scatter_dimension=0, tiled=True
        ).astype(jnp.float32),
        lax.psum_scatter(
            grad_wd.astype(jnp.bfloat16), "blk", scatter_dimension=0, tiled=True
        ).astype(jnp.float32),
    )
    grad_hidden = grad_out + grad_mid
    grad_branch, grad_gain_attn = attn_back(grad_hidden)
    branch_b = grad_branch.astype(jnp.bfloat16)
    grad_wo = contract(attended, branch_b, 0, 0)
    grad_att = (
        contract(branch_b, full_out, 1, 1).astype(jnp.bfloat16).reshape(tok_rows, -1, HEAD_DIM)
    )
    chances_again = jnp.exp(masked_scores(query_heads, keys_all, valid) - log_total)
    grad_chances = jnp.einsum(
        "qhd,khd->hqk", grad_att, values_all, preferred_element_type=jnp.float32
    )
    grad_values = jnp.einsum(
        "hqk,qhd->khd",
        chances_again.astype(jnp.bfloat16),
        grad_att,
        preferred_element_type=jnp.float32,
    ).reshape(2 * tok_rows, model_width)
    balance = jnp.sum(chances_again * grad_chances, axis=-1, keepdims=True)
    grad_logits = (chances_again * (grad_chances - balance)).astype(jnp.bfloat16)
    grad_query = jnp.einsum(
        "hqk,khd->qhd", grad_logits, keys_all, preferred_element_type=jnp.float32
    ).reshape(tok_rows, model_width) * HEAD_DIM ** (-0.5)
    grad_keys = jnp.einsum(
        "hqk,qhd->khd", grad_logits, query_heads, preferred_element_type=jnp.float32
    ).reshape(2 * tok_rows, model_width) * HEAD_DIM ** (-0.5)
    back_keys, back_values = (
        passed_along(grad_keys[:tok_rows].astype(jnp.bfloat16), "blk", -1).astype(jnp.float32),
        passed_along(grad_values[:tok_rows].astype(jnp.bfloat16), "blk", -1).astype(jnp.float32),
    )
    grad_key_rot = grad_keys[tok_rows:] + back_keys
    grad_value_b = (grad_values[tok_rows:] + back_values).astype(jnp.bfloat16)
    grad_q_in, grad_k_in, grad_gain_query, grad_gain_key = prepare_back(
        (rounded(grad_query), rounded(grad_key_rot))
    )
    grad_q_b = grad_q_in.astype(jnp.bfloat16)
    grad_k_b = grad_k_in.astype(jnp.bfloat16)
    grad_wq = contract(inputs, grad_q_b, 0, 0)
    grad_wk = contract(inputs, grad_k_b, 0, 0)
    grad_wv = contract(inputs, grad_value_b, 0, 0)
    grad_input = (
        grad_hidden
        + contract(grad_q_b, full_query, 1, 1)
        + contract(grad_k_b, full_key, 1, 1)
        + contract(grad_value_b, full_value, 1, 1)
    )
    totals_all = (
        lax.psum_scatter(grad_wq, ("blk", "wide"), scatter_dimension=0, tiled=True),
        lax.psum_scatter(grad_wk, ("blk", "wide"), scatter_dimension=0, tiled=True),
        lax.psum_scatter(grad_wv, ("blk", "wide"), scatter_dimension=0, tiled=True),
        lax.psum_scatter(grad_wo, ("blk", "wide"), scatter_dimension=0, tiled=True),
        lax.psum_scatter(grad_gain_query, ("blk", "wide"), scatter_dimension=0, tiled=True),
        lax.psum_scatter(grad_gain_key, ("blk", "wide"), scatter_dimension=0, tiled=True),
        lax.psum_scatter(grad_gain_attn, ("blk", "wide"), scatter_dimension=0, tiled=True),
        lax.psum_scatter(grad_gain_mlp, ("blk", "wide"), scatter_dimension=0, tiled=True),
    )
    return (
        output[None],
        grad_input.astype(jnp.bfloat16)[None],
        totals_all[0],
        totals_all[1],
        totals_all[2],
        totals_all[3],
        totals_all[4],
        totals_all[5],
        totals_all[6],
        totals_all[7],
        grad_wg,
        grad_wu,
        grad_wd,
    )


def solution(mesh):
    return jax.shard_map(
        body,
        mesh=mesh,
        in_specs=(
            P("wide", "blk", None),
            P("wide"),
            P(("blk", "wide"), None),
            P(("blk", "wide"), None),
            P(("blk", "wide"), None),
            P(("blk", "wide"), None),
            P(("blk", "wide")),
            P(("blk", "wide")),
            P(("blk", "wide")),
            P(("blk", "wide")),
            P("blk", "wide"),
            P("blk", "wide"),
            P("blk", "wide"),
            P("wide", "blk", None),
        ),
        out_specs=(
            P("wide", "blk", None),
            P("wide", "blk", None),
            P(("blk", "wide"), None),
            P(("blk", "wide"), None),
            P(("blk", "wide"), None),
            P(("blk", "wide"), None),
            P(("blk", "wide")),
            P(("blk", "wide")),
            P(("blk", "wide")),
            P(("blk", "wide")),
            P("blk", "wide"),
            P("blk", "wide"),
            P("blk", "wide"),
        ),
        check_vma=False,
    )
```

profile of v0, /device:TPU:0, one launch (start us, length us, event | category | flops | bytes accessed | tf_op | source)
XLA Modules:
  0.0 1869.4 jit_solution(9901952719976086102)
XLA Ops:
  12.4 42.8 %all-reduce.13 = (bf16[2048]{0:T(1024)(128)(2,1)S(1)}, bf16[2048]{0:T(1024)(128)(2,1)S(1)}, bf16[2048]{0:T(1024)(128)(2,1)S(1)}, bf16[2048]{0:T(1024)(128)(2,1)S(1)}) all-reduce(bf16[2048]{0:T(1024)(128)(2,1)S(1)} %dynamic-update-slice.1, bf16[2048]{0:T(1024)(128)(2,1)S(1)} %dynamic-update-slice, ...), channel_id=1, replica_groups=mesh['blk'=2,'wide'=16] {'blk','wide'}, use_global_device_ids=true, to_apply=%add.5 | all-reduce | flops 8192 | bytes 32768
  55.7 35.7 %all-gather.14.cloned.1.call-done = bf16[2048,2048]{1,0:T(8,128)(2,1)} async-done(((bf16[64,2048]{1,0:T(8,128)(2,1)}), bf16[2048,2048]{1,0:T(8,128)(2,1)}) %all-gather.14.cloned.1.call-update) | async-done | bytes 8388624 | tf_op jit(solution)/shard_map/all_gather | solution.py:95
  91.5 4.7 multiply_reduce_fusion.7
  97.5 73.0 %all-gather.12.cloned.1.call-done = bf16[2048,2048]{1,0:T(8,128)(2,1)} async-done(((bf16[64,2048]{1,0:T(8,128)(2,1)}), bf16[2048,2048]{1,0:T(8,128)(2,1)}) %all-gather.12.cloned.1.call-update) | async-done | bytes 8388624 | tf_op jit(solution)/shard_map/all_gather | solution.py:94
  170.5 4.7 multiply_reduce_fusion.8
  177.0 2.2 subtract_convert_fusion.1
  179.7 3.4 collective-permute-start.1
  183.1 67.8 %all-gather.10.cloned.1.call-done = bf16[2048,2048]{1,0:T(8,128)(2,1)} async-done(((bf16[64,2048]{1,0:T(8,128)(2,1)}), bf16[2048,2048]{1,0:T(8,128)(2,1)}) %all-gather.10.cloned.1.call-update) | async-done | bytes 8388624 | tf_op jit(solution)/shard_map/all_gather | solution.py:96
  250.9 4.6 convolution_convert_fusion.4
  255.6 3.8 collective-permute-start
  261.1 11.4 collective-permute-done
  274.6 56.6 %all-gather.16.cloned.1.call-done = bf16[2048,2048]{1,0:T(8,128)(2,1)} async-done(((bf16[64,2048]{1,0:T(8,128)(2,1)}), bf16[2048,2048]{1,0:T(8,128)(2,1)}) %all-gather.16.cloned.1.call-update) | async-done | bytes 8388624 | tf_op jit(solution)/shard_map/all_gather | solution.py:97
  331.2 4.7 multiply_reduce_fusion.6
  339.6 24.8 %all-gather.20.cloned.1.call-done = bf16[2048,512]{1,0:T(8,128)(2,1)} async-done(((bf16[1024,512]{1,0:T(8,128)(2,1)}), bf16[2048,512]{1,0:T(8,128)(2,1)}) %all-gather.20.cloned.1.call-update) | async-done | bytes 2097168 | tf_op jit(solution)/shard_map/all_gather | solution.py:104
  364.4 77.5 %all-gather.18.cloned.1.call-done = bf16[2048,2048]{1,0:T(8,128)(2,1)} async-done(((bf16[128,2048]{1,0:T(8,128)(2,1)}), bf16[2048,2048]{1,0:T(8,128)(2,1)}) %all-gather.18.cloned.1.call-update) | async-done | bytes 8388624 | tf_op jit(solution)/shard_map/all_gather | solution.py:150
  441.9 10.5 fusion.50
  452.4 22.4 %all-gather.22.cloned.1.call-done = bf16[2048,512]{1,0:T(8,128)(2,1)} async-done(((bf16[1024,512]{1,0:T(8,128)(2,1)}), bf16[2048,512]{1,0:T(8,128)(2,1)}) %all-gather.22.cloned.1.call-update) | async-done | bytes 2097168 | tf_op jit(solution)/shard_map/all_gather | solution.py:105
  474.8 12.9 multiply_convert_fusion.1
  487.8 21.8 %all-gather.24.cloned.1.call-done = bf16[2048,512]{1,0:T(8,128)(2,1)} async-done(((bf16[1024,512]{1,0:T(8,128)(2,1)}), bf16[2048,512]{1,0:T(8,128)(2,1)}) %all-gather.24.cloned.1.call-update) | async-done | bytes 2097168 | tf_op jit(solution)/shard_map/all_gather | solution.py:106
  509.5 20.4 %fusion.51 = f32[2048,2048]{1,0:T(8,128)} fusion(bf16[2048,512]{1,0:T(8,128)(2,1)} %get-tuple-element.104, bf16[2048,512]{1,0:T(8,128)(2,1)} %all-gather.24.cloned.1.call-done), kind=kOutput, calls=%fused_computation.135 | convolution fusion | flops 4294967296 | bytes 20971520 | tf_op jit(solution)/shard_map/dot_general | solution.py:60
  530.0 178.6 %reduce-scatter.16.cloned.1.call-done = f32[128,2048]{1,0:T(8,128)} async-done(((f32[2048,2048]{1,0:T(8,128)}), f32[128,2048]{1,0:T(8,128)}) %reduce-scatter.16.cloned.1.call-update) | async-done | bytes 1048592 | tf_op jit(solution)/shard_map/reduce_scatter | solution.py:160
  708.7 1.5 multiply_reduce_fusion.5
  710.1 2.1 fusion.16
  713.4 74.0 %all-gather.26.cloned.1.call-done = bf16[2048,2048]{1,0:T(8,128)(2,1)} async-done(((bf16[128,2048]{1,0:T(8,128)(2,1)}), bf16[2048,2048]{1,0:T(8,128)(2,1)}) %all-gather.26.cloned.1.call-update) | async-done | bytes 8388624 | tf_op jit(solution)/shard_map/all_gather | solution.py:168
  787.4 12.8 multiply_convert_fusion
  800.2 8.3 fusion.52
  808.5 11.6 convolution_add_fusion
  820.4 10.3 convolution_convert_fusion
  830.8 11.7 convolution_convert_fusion.1
  843.0 10.7 convolution_convert_fusion.2
  853.8 143.3 %reduce-scatter.18.cloned.1.call-done = f32[128,2048]{1,0:T(8,128)} async-done(((f32[2048,2048]{1,0:T(8,128)}), f32[128,2048]{1,0:T(8,128)}) %reduce-scatter.18.cloned.1.call-update) | async-done | bytes 1048592 | tf_op jit(solution)/shard_map/reduce_scatter | solution.py:178
  997.1 2.0 multiply_reduce_fusion.1
  999.3 2.7 fusion.13
  1002.8 8.1 fusion.53
  1011.0 7.3 convolution_convert_fusion.3
  1018.3 2.1 copy.98
  1020.4 1.6 convolution_bitcast_fusion.3
  1022.1 1.5 collective-permute-start.3
  1023.6 16.3 collective-permute-done.3
  1040.8 8.1 convolution_bitcast_fusion
  1048.9 17.6 copy.88
  1066.6 2.3 multiply_reduce_fusion
  1071.7 1.4 collective-permute-start.2
  1073.7 1.4 copy.94
  1075.1 1.3 copy.95
  1076.4 21.6 %collective-permute-done.2 = bf16[128,2048]{0,1:T(8,128)(2,1)} collective-permute-done((bf16[128,2048]{0,1:T(8,128)(2,1)}, bf16[128,2048]{0,1:T(8,128)(2,1)}, u32[]{:S(2)}, u32[]{:S(2)}) %collective-permute-start.2) | collective-permute-done | bytes 524320 | tf_op jit(solution)/shard_map/ppermute | solution.py:19
  1100.1 2.4 copy.96
  1103.9 3.6 multiply_add_fusion.1
  1109.4 8.1 convolution_bitcast_fusion.1
  1117.6 17.7 copy.86
  1136.5 1.7 fusion.19
  1139.6 8.2 convolution_bitcast_fusion.2
  1147.8 17.7 copy.84
  1165.6 2.8 convert_element_type.179
  1168.4 2.9 convert_element_type.177
  1171.3 3.0 convert_element_type.175
  1174.3 44.2 %all-reduce.12 = (f32[2048]{0:T(1024)S(1)}, f32[2048]{0:T(1024)S(1)}, f32[2048]{0:T(1024)S(1)}, f32[2048]{0:T(1024)S(1)}) all-reduce(f32[2048]{0:T(1024)S(1)} %get-tuple-element.56, f32[2048]{0:T(1024)S(1)} %get-tuple-element.54, f32[2048]{0:T(1024)S(1)} %get-tuple-element.52, ...), channel_id=8, replica_groups=mesh['blk'=2,'wide'=16] {'blk','wide'}, use_global_device_ids=true, to_apply=%region_18.19.clone | all-reduce | flops 8192 | bytes 65536
  1220.8 6.4 convolution_add_fusion.3
  1227.3 6.4 convolution_add_fusion.2
  1233.8 7.3 fusion.5
  1241.0 58.5 %reduce-scatter.20.cloned.1.call-done = f32[64,2048]{1,0:T(8,128)} async-done(((f32[2048,2048]{1,0:T(8,128)}), f32[64,2048]{1,0:T(8,128)}) %reduce-scatter.20.cloned.1.call-update) | async-done | bytes 524304 | tf_op jit(solution)/shard_map/reduce_scatter | solution.py:249
  1299.5 187.6 %reduce-scatter.32.cloned.1.call-done = f32[64,2048]{1,0:T(8,128)} async-done(((f32[2048,2048]{1,0:T(8,128)}), f32[64,2048]{1,0:T(8,128)}) %reduce-scatter.32.cloned.1.call-update) | async-done | bytes 524304
  1487.1 187.6 %reduce-scatter.30.cloned.1.call-done = f32[64,2048]{1,0:T(8,128)} async-done(((f32[2048,2048]{1,0:T(8,128)}), f32[64,2048]{1,0:T(8,128)}) %reduce-scatter.30.cloned.1.call-update) | async-done | bytes 524304
  1674.7 187.6 %reduce-scatter.28.cloned.1.call-done = f32[64,2048]{1,0:T(8,128)} async-done(((f32[2048,2048]{1,0:T(8,128)}), f32[64,2048]{1,0:T(8,128)}) %reduce-scatter.28.cloned.1.call-update) | async-done | bytes 524304
  (213 shorter events, 33.5 us)
Async XLA Ops:
  7.2 4.2 copy-start.51
  7.2 4.5 copy-start.52
  7.2 4.7 copy-start.53
  7.2 5.0 copy-start.54
  7.2 84.2 %copy-start = (bf16[1,128,2048]{2,1,0:T(8,128)(2,1)S(1)}, bf16[1,128,2048]{2,1,0:T(8,128)(2,1)}, u32[]{:S(2)}) copy-start(bf16[1,128,2048]{2,1,0:T(8,128)(2,1)} %param.14) | copy-start | bytes 1572868
  7.2 84.2 %all-gather.14.cloned.1.call-start = ((), (), s32[]{:S(2)}) async-start(), calls=%async_computation.11 | async-start | bytes 8650752 | tf_op jit(solution)/shard_map/all_gather | solution.py:95
  8.0 162.6 %all-gather.12.cloned.1.call-start = ((), (), s32[]{:S(2)}) async-start(), calls=%async_computation.10 | async-start | bytes 8650752 | tf_op jit(solution)/shard_map/all_gather | solution.py:94
  8.7 242.2 %all-gather.10.cloned.1.call-start = ((), (), s32[]{:S(2)}) async-start(), calls=%async_computation.9 | async-start | bytes 8650752 | tf_op jit(solution)/shard_map/all_gather | solution.py:96
  9.4 321.8 %all-gather.16.cloned.1.call-start = ((), (), s32[]{:S(2)}) async-start(), calls=%async_computation.12 | async-start | bytes 8650752 | tf_op jit(solution)/shard_map/all_gather | solution.py:97
  10.0 354.3 %all-gather.20.cloned.1.call-start = ((), (), s32[]{:S(2)}) async-start(), calls=%async_computation.14 | async-start | bytes 3145728 | tf_op jit(solution)/shard_map/all_gather | solution.py:104
  10.6 431.3 %all-gather.18.cloned.1.call-start = ((), (), s32[]{:S(2)}) async-start(), calls=%async_computation.13 | async-start | bytes 8912896 | tf_op jit(solution)/shard_map/all_gather | solution.py:150
  55.2 41.0 %copy-start.39 = (f32[2048]{0:T(1024)}, f32[2048]{0:T(1024)S(1)}, u32[]{:S(2)}) copy-start(f32[2048]{0:T(1024)S(1)} %convert_element_type.142) | copy-start | bytes 24580
  55.3 120.0 %copy-start.37 = (f32[2048]{0:T(1024)}, f32[2048]{0:T(1024)S(1)}, u32[]{:S(2)}) copy-start(f32[2048]{0:T(1024)S(1)} %convert_element_type.140) | copy-start | bytes 24580
  55.6 121.4 %copy-start.32 = (f32[128,64]{1,0:T(8,128)}, f32[128,64]{1,0:T(8,128)S(1)}, u32[]{:S(2)}) copy-start(f32[128,64]{1,0:T(8,128)S(1)} %get-tuple-element.94) | copy-start | bytes 98308
  55.6 121.4 %copy-start.34 = (f32[128,64]{1,0:T(8,128)}, f32[128,64]{1,0:T(8,128)S(1)}, u32[]{:S(2)}) copy-start(f32[128,64]{1,0:T(8,128)S(1)} %get-tuple-element.95) | copy-start | bytes 98308
  96.2 1.3 copy-start.48
  96.2 1.3 copy-start.44
  179.1 80.3 %copy-start.22 = (bf16[128,16,64]{2,0,1:T(8,128)(2,1)}, bf16[128,16,64]{2,0,1:T(8,128)(2,1)S(1)}, u32[]{:S(2)}) copy-start(bf16[128,16,64]{2,0,1:T(8,128)(2,1)S(1)} %get-tuple-element.74) | copy-start | bytes 786436
  179.7 79.6 %collective-permute-start.1 = (bf16[128,2048]{0,1:T(8,128)(2,1)S(1)}, bf16[128,2048]{0,1:T(8,128)(2,1)S(1)}, u32[]{:S(2)}, u32[]{:S(2)}) collective-permute-start(bf16[128,2048]{0,1:T(8,128)(2,1)S(1)} %bitcast.172), channel_id=1, source_target_pairs={{0,16},{1,17},{2,18},{3,19},{4,20},{5,21},{6,22},{7,23},{8,24},{9,... | collective-permute-start | bytes 1572872 | tf_op jit(solution)/shard_map/ppermute | solution.py:19
  255.5 17.0 copy-start.30
  255.5 3.9 copy-start.24
  255.6 16.9 collective-permute-start
  274.6 61.3 %copy-start.28 = (bf16[16,128,128]{2,1,0:T(8,128)(2,1)}, bf16[16,128,128]{2,1,0:T(8,128)(2,1)S(1)}, u32[]{:S(2)}) copy-start(bf16[16,128,128]{2,1,0:T(8,128)(2,1)S(1)} %convolution_convert_fusion.5) | copy-start | bytes 1572868
  338.0 136.8 %all-gather.22.cloned.1.call-start = ((), (), s32[]{:S(2)}) async-start(), calls=%async_computation.15 | async-start | bytes 3145728 | tf_op jit(solution)/shard_map/all_gather | solution.py:105
  338.8 170.8 %all-gather.24.cloned.1.call-start = ((), (), s32[]{:S(2)}) async-start(), calls=%async_computation.16 | async-start | bytes 3145728 | tf_op jit(solution)/shard_map/all_gather | solution.py:106
  339.5 369.1 %reduce-scatter.16.cloned.1.call-start = ((), (), s32[]{:S(2)}) async-start(), calls=%async_computation.17 | async-start | bytes 17825792 | tf_op jit(solution)/shard_map/reduce_scatter | solution.py:160
  529.9 180.2 %copy-start.9 = (bf16[1,128,2048]{2,1,0:T(8,128)(2,1)S(1)}, bf16[1,128,2048]{2,1,0:T(8,128)(2,1)}, u32[]{:S(2)}) copy-start(bf16[1,128,2048]{2,1,0:T(8,128)(2,1)} %param.27) | copy-start | bytes 1572868
  530.0 257.5 %all-gather.26.cloned.1.call-start = ((), (), s32[]{:S(2)}) async-start(), calls=%async_computation.18 | async-start | bytes 8912896 | tf_op jit(solution)/shard_map/all_gather | solution.py:168
  708.7 3.6 copy-start.7
  713.4 283.7 %reduce-scatter.18.cloned.1.call-start = ((), (), s32[]{:S(2)}) async-start(), calls=%async_computation.19 | async-start | bytes 17825792 | tf_op jit(solution)/shard_map/reduce_scatter | solution.py:178
  787.4 12.8 copy-start.50
  800.2 8.3 copy-start.55
  800.2 8.3 copy-start.26
  800.2 8.3 copy-start.31
  820.2 345.4 %reduce-scatter.26.cloned.1.call-start = ((), (), s32[]{:S(2)}) async-start(), calls=%async_computation.23 | async-start | bytes 3145728 | tf_op jit(solution)/shard_map/reduce_scatter | solution.py:196
  830.8 337.7 %reduce-scatter.24.cloned.1.call-start = ((), (), s32[]{:S(2)}) async-start(), calls=%async_computation.22 | async-start | bytes 3145728 | tf_op jit(solution)/shard_map/reduce_scatter | solution.py:193
  842.6 328.8 %reduce-scatter.22.cloned.1.call-start = ((), (), s32[]{:S(2)}) async-start(), calls=%async_computation.21 | async-start | bytes 3145728 | tf_op jit(solution)/shard_map/reduce_scatter | solution.py:190
  853.8 445.7 %reduce-scatter.20.cloned.1.call-start = ((), (), s32[]{:S(2)}) async-start(), calls=%async_computation.20 | async-start | bytes 17301504 | tf_op jit(solution)/shard_map/reduce_scatter | solution.py:249
  997.1 2.0 copy-start.2
  997.1 2.2 copy-start.8
  999.3 3.5 copy-start.29
  1010.9 476.2 %reduce-scatter.32.cloned.1.call-start = ((), (), s32[]{:S(2)}) async-start(), calls=%async_computation.26 | async-start | bytes 17301504
  1022.1 17.8 collective-permute-start.3
  1066.6 608.1 %reduce-scatter.30.cloned.1.call-start = ((), (), s32[]{:S(2)}) async-start(), calls=%async_computation.25 | async-start | bytes 17301504
  1070.8 2.8 copy-start.14
  1070.8 2.3 copy-start.11
  1071.7 26.3 %collective-permute-start.2 = (bf16[128,2048]{0,1:T(8,128)(2,1)}, bf16[128,2048]{0,1:T(8,128)(2,1)}, u32[]{:S(2)}, u32[]{:S(2)}) collective-permute-start(bf16[128,2048]{0,1:T(8,128)(2,1)} %bitcast.15), channel_id=1, source_target_pairs={{16,0},{17,1},{18,2},{19,3},{20,4},{21,5},{22,6},{23,7},{24,8},{25... | collective-permute-start | bytes 1572872 | tf_op jit(solution)/shard_map/ppermute | solution.py:19
  1073.7 24.3 %slice-start = ((f32[256,16,128]{0,2,1:T(8,128)}), f32[128,16,128]{0,2,1:T(8,128)S(1)}, s32[]{:S(2)}) async-start(f32[256,16,128]{0,2,1:T(8,128)} %copy-done.14), calls=%async_computation.27 | async-start | bytes 2097152 | tf_op jit(solution)/shard_map/slice | solution.py:229
  1100.1 3.8 copy-start.27
  1100.1 3.8 copy-start.33
  1100.1 3.8 copy-start.35
  1103.9 3.6 copy-start.6
  1103.9 3.6 copy-start.40
  1103.9 3.6 copy-start.45
  1135.3 1.2 copy-start.38
  1135.3 1.2 copy-start.43
  1135.3 2.9 copy-start.47
  1135.3 727.0 %reduce-scatter.28.cloned.1.call-start = ((), (), s32[]{:S(2)}) async-start(), calls=%async_computation.24 | async-start | bytes 17301504
  1135.6 2.7 copy-start.13
  1171.3 3.0 copy-start.41
  1171.3 49.5 %copy-start.12 = (f32[128,2048]{1,0:T(8,128)S(1)}, f32[128,2048]{1,0:T(8,128)}, u32[]{:S(2)}) copy-start(f32[128,2048]{1,0:T(8,128)} %reduce-scatter.18.cloned.1.call-done) | copy-start | bytes 3145732
  1171.3 49.5 %copy-start.18 = (bf16[128,2048]{1,0:T(8,128)(2,1)S(1)}, bf16[128,2048]{1,0:T(8,128)(2,1)}, u32[]{:S(2)}) copy-start(bf16[128,2048]{1,0:T(8,128)(2,1)} %copy-done.17) | copy-start | bytes 1572868
  1220.8 6.4 copy-start.20
  1227.3 6.4 copy-start.16
  (15 other events, 14.1 us)
Sparse Core Ops, SparseCore 0:
  10.9 80.4 all-gather.13
  94.3 76.1 all-gather.11
  173.4 77.4 all-gather.9
  253.6 77.5 all-gather.15
  332.6 31.7 all-gather.19
  367.0 74.8 all-gather.17
  443.4 31.3 all-gather.21
  476.4 33.1 all-gather.23
  530.1 178.5 reduce-scatter.15
  713.5 73.8 all-gather.25
  820.3 176.7 reduce-scatter.17
  999.2 32.9 reduce-scatter.25
  1034.5 33.2 reduce-scatter.23
  1070.5 40.9 reduce-scatter.21
  1114.2 185.1 reduce-scatter.19
  1302.3 184.7 reduce-scatter.31
  1489.9 184.7 reduce-scatter.29
  1677.5 184.7 reduce-scatter.27
where the time goes:
time: 1870 us
  waiting for transfers between devices  1450 us (78%)
  matrix products  195 us (10%)
  blocking collectives  87 us (5%)
  local copies, waits for them, and re-layouts  76.8 us (4%)
  other arithmetic  32 us (2%)
    unnamed x21, waiting for transfers between devices  568 us
    reduce_scatter x1, waiting for transfers between devices, body(): lax.psum_scatter(contract(block, down_local, 1, 1), 'wide', scatter_dimen...  179 us
    reduce_scatter x1, waiting for transfers between devices, body(): lax.psum_scatter(contract(gate_part, gate_local, 1, 1) + contract(up_part...  143 us
    dot_general x14, matrix products, contract(): lax.dot_general(left, right, (((left_dim,), (right_dim,)), ((), ())), pre...  133 us
    unnamed x2, blocking collectives  87 us
    all_gather x1, waiting for transfers between devices, body(): piece = lax.all_gather(mlp_in, 'wide', axis=0, tiled=True)  77.5 us
    all_gather x1, waiting for transfers between devices, body(): piece = lax.all_gather(grad_mlp_b, 'wide', axis=0, tiled=True)  74 us
    all_gather x1, waiting for transfers between devices, body(): lax.all_gather(w_query, ('blk', 'wide'), axis=0, tiled=True)  73 us
  transfers between devices with their start and end apart: 22, of which 18 were waited for; matrix products, arithmetic and copies ran while one was open for 13% of the time, Pallas kernels for 0%

commit v1 on v0

v1 whole, which is shorter than its diff:
```python
import math

import jax
import jax.numpy as jnp
from jax import lax
from jax.sharding import PartitionSpec as P

HEAD_DIM = 128
EPSILON = 1e-06
NEGATIVE = -1e30
BF16 = jnp.bfloat16
F32 = jnp.float32
AXES = ("blk", "wide")
NX, NY, NZ = 2, 2, 4


def rms_scale(values, gain):
    return values * lax.rsqrt(jnp.mean(values * values, axis=-1, keepdims=True) + EPSILON) * gain


def dot(left, right, left_dim, right_dim):
    return lax.dot_general(
        left, right, (((left_dim,), (right_dim,)), ((), ())), preferred_element_type=F32
    )


def flipped(values, axis, when):
    return jnp.where(when == 1, jnp.flip(values, axis), values)


def xored(values, axis, index):
    count = values.shape[axis]
    bits = count.bit_length() - 1
    shape = values.shape
    values = values.reshape(shape[:axis] + (2,) * bits + shape[axis + 1 :])
    for bit in range(bits):
        values = flipped(values, axis + bits - 1 - bit, (index >> bit) & 1)
    return values.reshape(shape)


def rolled(values, axis, start):
    size = values.shape[axis]
    return lax.dynamic_slice_in_dim(jnp.concatenate([values, values], axis), start, size, axis)


def make_body(wide):
    nc = wide // (NY * NZ)

    def send(value, x=0, y=0, z=0, c=0):
        pairs = []
        for sx in range(NX):
            for sz in range(NZ):
                for sy in range(NY):
                    for sc in range(nc):
                        source = sx * wide + (sz * NY + sy) * nc + sc
                        target = (sx ^ x) * wide
                        target += (((sz + z) % NZ) * NY + (sy ^ y)) * nc + (sc ^ c)
                        pairs.append((source, target))
        return lax.ppermute(value, AXES, pairs)

    def square_gather(first, second):
        first_x = send(first, x=1)
        second_y = send(second, y=1)
        first_y = send(first, y=1)
        second_x = send(second, x=1)
        first_xy = send(first_x, y=1)
        second_xy = send(second_y, x=1)
        return (
            ((first, first_y), (first_x, first_xy)),
            ((second, second_y), (second_x, second_xy)),
        )

    def square_scatter(first, second):
        def low(value):
            return value.astype(BF16)

        first_a = send(low(first[1][1]), x=1)
        second_a = send(low(second[1][1]), y=1)
        first_b = send(low(first[1][0]), x=1)
        second_b = send(low(second[0][1]), y=1)
        first_c = send(low(first[0][1].astype(F32) + first_a.astype(F32)), y=1)
        second_c = send(low(second[1][0].astype(F32) + second_a.astype(F32)), x=1)
        return (
            first[0][0].astype(F32) + first_b.astype(F32) + first_c.astype(F32),
            second[0][0].astype(F32) + second_b.astype(F32) + second_c.astype(F32),
        )

    def ring_gather(block):
        blocks = [block]
        for _ in range(NZ - 1):
            blocks.append(send(blocks[-1], z=-1))
        return blocks

    def core_gather(block):
        return [block] + [send(block, c=k) for k in range(1, nc)]

    def core_sum(parts):
        total = parts[0].astype(F32)
        for k in range(1, nc):
            total = total + send(parts[k].astype(BF16), c=k).astype(F32)
        return total

    def ring_sum(part_of):
        moving = None
        for s in list(range(1, NZ)) + [0]:
            total = part_of(s)
            if moving is not None:
                total = total + moving.astype(F32)
            if s == 0:
                return total
            moving = send(total.astype(BF16), z=-1)

    def body(
        layer_input,
        lengths,
        w_query,
        w_key,
        w_value,
        w_output,
        query_gain,
        key_gain,
        attn_gain,
        mlp_gain,
        w_gate,
        w_up,
        w_down,
        grad_output,
    ):
        x = lax.axis_index("blk")
        place = lax.axis_index("wide")
        z, y, c = place // (NY * nc), (place // nc) % NY, place % nc
        inputs = layer_input[0]
        tok, width = inputs.shape
        rows = w_query.shape[0]
        head_cols = NZ * HEAD_DIM
        group_tok = NX * NY * tok

        def pieces(weight):
            weight = weight.reshape(rows, NX, NZ, NY, HEAD_DIM)
            return flipped(flipped(weight, 1, x), 3, y)

        split = [pieces(weight) for weight in (w_query, w_key, w_value)]

        def piece(dx, dy):
            return jnp.concatenate(
                [part[:, dx, :, dy].reshape(rows, head_cols) for part in split], axis=1
            )

        received = [
            [piece(0, 0), send(piece(0, 1), y=1)],
            [send(piece(1, 0), x=1), send(piece(1, 1), x=1, y=1)],
        ]
        own_rows = jnp.stack([jnp.stack(row) for row in received])
        mine = rolled(inputs.reshape(tok, NX, NZ, NY * HEAD_DIM), 2, z).reshape(tok, width)
        upper, lower = square_gather(mine[: tok // 2], mine[tok // 2 :])

        def token_blocks(first, second):
            return jnp.concatenate(
                [
                    half
                    for dy in range(NY)
                    for dx in range(NX)
                    for half in (first[dx][dy], second[dx][dy])
                ],
                axis=0,
            )

        x_all = token_blocks(upper, lower).reshape(group_tok, NX, NZ, NY, HEAD_DIM)
        x_all = flipped(flipped(x_all, 1, x), 3, y)

        def x_part(s):
            return x_all[:, :, s].reshape(group_tok, NX * NY * HEAD_DIM)

        projected = 0.0
        w_parts = []
        for block in ring_gather(own_rows):
            w_part = jnp.stack(core_gather(block), axis=2)
            w_part = xored(w_part, 2, c).reshape(NX * NY * nc * rows, 3 * head_cols)
            w_parts.append(w_part)
        for s in range(NZ):
            projected = projected + dot(x_part(s), w_parts[s], 1, 0)
        query = projected[:, :head_cols]
        key_proj = projected[:, head_cols : 2 * head_cols]
        value_b = projected[:, 2 * head_cols :].astype(BF16)

        packed = jnp.stack([query_gain, key_gain, attn_gain, mlp_gain])
        by_z = jnp.stack([packed] + [send(packed, z=-s) for s in range(1, NZ)])
        by_z = rolled(by_z, 0, (NZ - z) % NZ)
        by_c = xored(jnp.stack(core_gather(by_z)), 0, c)
        group_gains = by_c.transpose(2, 1, 0, 3).reshape(4, head_cols).astype(F32)
        gain_query, gain_key = group_gains[0], group_gains[1]
        by_xy = jnp.stack(
            [
                jnp.stack([by_c, send(by_c, y=1)]),
                jnp.stack([send(by_c, x=1), send(by_c, x=1, y=1)]),
            ]
        )
        by_xy = flipped(flipped(by_xy, 0, x), 1, y)
        full_gains = by_xy.transpose(4, 0, 3, 1, 2, 5).reshape(4, width).astype(F32)
        gain_attn, gain_mlp = full_gains[2], full_gains[3]

        out_parts = [
            xored(jnp.stack(core_gather(block)), 0, c) for block in ring_gather(w_output)
        ]
        out_w = rolled(jnp.stack(out_parts), 0, (NZ - z) % NZ).reshape(head_cols, width)
        gate_parts, up_parts = square_gather(w_gate, w_up)
        half_hidden = w_down.shape[0] // 2
        down_first, down_second = square_gather(w_down[:half_hidden], w_down[half_hidden:])

        def joined(blocks):
            return jnp.concatenate([jnp.concatenate(row, axis=1) for row in blocks], axis=0)

        gate_w, up_w = joined(gate_parts), joined(up_parts)
        down_w = jnp.concatenate(
            [
                jnp.concatenate(row, axis=1)
                for dx in range(NX)
                for row in (down_first[dx], down_second[dx])
            ],
            axis=0,
        )

        positions = jnp.concatenate(
            [
                x * tok + jnp.arange(tok, dtype=jnp.int32),
                (1 - x) * tok + jnp.arange(tok, dtype=jnp.int32),
            ]
        )
        half = HEAD_DIM // 2
        frequency = jnp.exp(
            jnp.arange(half, dtype=F32) * (-2.0 * math.log(500000.0) / HEAD_DIM)
        )
        angles = positions.astype(F32)[:, None] * frequency[None, :]
        cosine = jnp.cos(angles)[None, :, None, :]
        sine = jnp.sin(angles)[None, :, None, :]

        def turn(values, sign):
            view = values.reshape(NY, NX * tok, NZ, HEAD_DIM)
            first, second = view[..., :half], view[..., half:]
            turned = jnp.concatenate(
                [first * cosine - sign * second * sine, second * cosine + sign * first * sine],
                axis=-1,
            )
            return turned.reshape(group_tok, head_cols)

        def group_sum(values):
            values = values.reshape(-1, NY, NX, tok)
            total = (
                values
                + jnp.flip(send(values, x=1), 2)
                + jnp.flip(send(values, y=1), 1)
                + jnp.flip(send(values, x=1, y=1), (1, 2))
            )
            return total.reshape(-1, group_tok)

        squares = group_sum(
            jnp.stack([jnp.sum(query * query, axis=1), jnp.sum(key_proj * key_proj, axis=1)])
        )
        scales = lax.rsqrt(squares / width + EPSILON)
        scale_q, scale_k = scales[0][:, None], scales[1][:, None]
        query_b = turn(query * scale_q * gain_query, 1.0).astype(BF16)
        key_b = turn(key_proj * scale_k * gain_key, 1.0).astype(BF16)

        def heads(values):
            return values.reshape(NY, NX * tok, NZ, HEAD_DIM)

        length = lengths.astype(F32)
        both = jnp.concatenate([length, send(length, y=1)]).astype(jnp.int32)
        valid = (positions[None, None, :] <= positions[None, :, None]) & (
            positions[None, None, :] < both[:, None, None]
        )
        logits = jnp.einsum(
            "sqhd,skhd->shqk", heads(query_b), heads(key_b), preferred_element_type=F32
        ) * HEAD_DIM ** (-0.5)
        logits = jnp.where(valid[:, None], logits, NEGATIVE)
        powers = jnp.exp(logits - jnp.max(logits, axis=-1, keepdims=True))
        chances = powers / jnp.sum(powers, axis=-1, keepdims=True)
        chances_b = chances.astype(BF16)
        attended = (
            jnp.einsum("shqk,skhd->sqhd", chances_b, heads(value_b), preferred_element_type=F32)
            .reshape(group_tok, head_cols)
            .astype(BF16)
        )

        branch_parts = dot(attended, out_w, 1, 0).astype(BF16).reshape(NY, NX, tok, width)

        def scatter_tokens(parts):
            return jnp.concatenate(
                square_scatter(
                    [[parts[dy, dx, : tok // 2] for dy in range(NY)] for dx in range(NX)],
                    [[parts[dy, dx, tok // 2 :] for dy in range(NY)] for dx in range(NX)],
                ),
                axis=0,
            )

        branch = scatter_tokens(branch_parts)
        normed, attn_back = jax.vjp(rms_scale, branch, gain_attn)
        hidden_state = inputs.astype(F32) + normed

        def half_order(values):
            return flipped(values.reshape(-1, NX, width // NX), 1, x).reshape(-1, width)

        def core_parts(values):
            values = values.reshape(nc, tok, width)
            return [values[k] for k in range(nc)]

        mlp_in = half_order(hidden_state.astype(BF16))
        mlp_blocks = []
        kept = []
        out_sums = []
        for block in ring_gather(mlp_in):
            block = jnp.concatenate(core_gather(block), axis=0)
            gate, up_proj = dot(block, gate_w, 1, 0), dot(block, up_w, 1, 0)
            product = (jax.nn.silu(gate) * up_proj).astype(BF16)
            mlp_blocks.append(block)
            kept.append((gate, up_proj, product))
            out_sums.append(core_sum(core_parts(dot(product, down_w, 1, 1))))
        mlp_out = half_order(ring_sum(lambda s: out_sums[s]))
        post, mlp_back = jax.vjp(rms_scale, mlp_out, gain_mlp)
        output = (hidden_state + post).astype(BF16)

        grad_out = grad_output[0].astype(F32)
        grad_mlp, grad_gain_mlp = mlp_back(grad_out)
        grad_blocks = []
        gate_grads = []
        up_grads = []
        mid_sums = []
        for s, block in enumerate(ring_gather(half_order(grad_mlp.astype(BF16)))):
            block = jnp.concatenate(core_gather(block), axis=0)
            gate, up_proj, product = kept[s]
            grad_prod = dot(block, down_w, 1, 0)
            chance = jax.nn.sigmoid(gate)
            grad_up = (grad_prod * gate * chance).astype(BF16)
            grad_gate = (
                grad_prod * up_proj * chance * (1.0 + gate * (1.0 - chance))
            ).astype(BF16)
            grad_blocks.append(block)
            gate_grads.append(grad_gate)
            up_grads.append(grad_up)
            mid_sums.append(
                core_sum(core_parts(dot(grad_gate, gate_w, 1, 1) + dot(grad_up, up_w, 1, 1)))
            )
        grad_mid = half_order(ring_sum(lambda s: mid_sums[s]))

        mlp_all = jnp.concatenate(mlp_blocks, axis=0)
        grad_all = jnp.concatenate(grad_blocks, axis=0)
        product_all = jnp.concatenate([entry[2] for entry in kept], axis=0)
        grad_wd = dot(grad_all, product_all, 0, 0).astype(BF16)
        grad_wg = dot(mlp_all, jnp.concatenate(gate_grads, axis=0), 0, 0).astype(BF16)
        grad_wu = dot(mlp_all, jnp.concatenate(up_grads, axis=0), 0, 0).astype(BF16)

        def quarters(values):
            height, span = values.shape[0] // NX, values.shape[1] // NY
            return [
                [
                    values[dx * height : (dx + 1) * height, dy * span : (dy + 1) * span]
                    for dy in range(NY)
                ]
                for dx in range(NX)
            ]

        grad_wd_parts = quarters(grad_wd)
        grad_wd = jnp.concatenate(
            square_scatter(
                [[part[:half_hidden] for part in row] for row in grad_wd_parts],
                [[part[half_hidden:] for part in row] for row in grad_wd_parts],
            ),
            axis=0,
        )
        grad_wg, grad_wu = square_scatter(quarters(grad_wg), quarters(grad_wu))

        grad_hidden = grad_out + grad_mid
        grad_branch, grad_gain_attn = attn_back(grad_hidden)
        branch_b = grad_branch.astype(BF16)
        branch_all = token_blocks(*square_gather(branch_b[: tok // 2], branch_b[tok // 2 :]))
        grad_att = dot(branch_all, out_w, 1, 1).astype(BF16)
        grad_wo = dot(attended, branch_all, 0, 0).astype(BF16).reshape(NZ, nc, rows, width)
        grad_wo = rolled(grad_wo, 0, z)
        grad_chances = jnp.einsum(
            "sqhd,skhd->shqk", heads(grad_att), heads(value_b), preferred_element_type=F32
        )
        grad_value = (
            jnp.einsum("shqk,sqhd->skhd", chances_b, heads(grad_att), preferred_element_type=F32)
            .reshape(group_tok, head_cols)
            .astype(BF16)
        )
        balance = jnp.sum(chances * grad_chances, axis=-1, keepdims=True)
        grad_logits = (chances * (grad_chances - balance)).astype(BF16)
        grad_query = jnp.einsum(
            "shqk,skhd->sqhd", grad_logits, heads(key_b), preferred_element_type=F32
        ).reshape(group_tok, head_cols) * HEAD_DIM ** (-0.5)
        grad_key = jnp.einsum(
            "shqk,sqhd->skhd", grad_logits, heads(query_b), preferred_element_type=F32
        ).reshape(group_tok, head_cols) * HEAD_DIM ** (-0.5)
        grad_query = turn(grad_query, -1.0)
        grad_key = turn(grad_key, -1.0)
        grad_gain_query = jnp.sum(grad_query * query * scale_q, axis=0)
        grad_gain_key = jnp.sum(grad_key * key_proj * scale_k, axis=0)
        grad_query = grad_query * gain_query
        grad_key = grad_key * gain_key
        means = (
            group_sum(
                jnp.stack(
                    [jnp.sum(grad_query * query, axis=1), jnp.sum(grad_key * key_proj, axis=1)]
                )
            )
            / width
        )
        grad_query = scale_q * (grad_query - query * (scale_q * scale_q * means[0][:, None]))
        grad_key = scale_k * (grad_key - key_proj * (scale_k * scale_k * means[1][:, None]))
        grads = jnp.concatenate(
            [grad_query.astype(BF16), grad_key.astype(BF16), grad_value], axis=1
        )

        grad_x = jnp.stack(
            [
                dot(grads, w_parts[s], 1, 1).astype(BF16).reshape(group_tok, NX, NY, HEAD_DIM)
                for s in range(NZ)
            ],
            axis=2,
        )
        grad_x = flipped(flipped(grad_x, 1, x), 3, y).reshape(NY, NX, tok, width)
        grad_x = scatter_tokens(grad_x).reshape(tok, NX, NZ, NY * HEAD_DIM)
        grad_x = rolled(grad_x, 2, (NZ - z) % NZ).reshape(tok, width)
        grad_input = (grad_hidden + grad_x).astype(BF16)

        def weight_part(s):
            part = dot(x_part(s), grads, 0, 0).astype(BF16)
            part = xored(part.reshape(NX * NY, nc, rows, 3 * head_cols), 1, c)
            return core_sum([part[:, k] for k in range(nc)])

        summed = ring_sum(weight_part).astype(BF16).reshape(NX, NY, rows, 3 * head_cols)
        blocks = jnp.stack(
            [
                jnp.stack([summed[0, 0], send(summed[0, 1], y=1)]),
                jnp.stack([send(summed[1, 0], x=1), send(summed[1, 1], x=1, y=1)]),
            ]
        )
        blocks = flipped(flipped(blocks, 0, x), 1, y)
        blocks = blocks.reshape(NX, NY, rows, 3, NZ, HEAD_DIM)
        blocks = blocks.transpose(3, 2, 0, 4, 1, 5)
        blocks = blocks.reshape(3, rows, width).astype(F32)

        def out_part(s):
            part = xored(grad_wo[s], 0, c)
            return core_sum([part[k] for k in range(nc)])

        grad_wo = ring_sum(out_part)

        wide_gains = jnp.stack([grad_gain_attn, grad_gain_mlp]).reshape(
            2, NX, NZ, NY, nc * rows
        )
        wide_gains = flipped(flipped(rolled(wide_gains, 2, z), 1, x), 3, y)
        own_gains = (
            wide_gains[:, 0, :, 0]
            + send(wide_gains[:, 1, :, 0], x=1)
            + send(wide_gains[:, 0, :, 1], y=1)
            + send(wide_gains[:, 1, :, 1], x=1, y=1)
        )
        head_gains = jnp.stack([grad_gain_query, grad_gain_key]).reshape(2, NZ, nc * rows)
        head_gains = rolled(head_gains, 1, z)
        gains = jnp.concatenate([head_gains, own_gains], axis=0).reshape(4, NZ, nc, rows)
        gains = xored(gains, 2, c)
        total = gains[:, :, 0]
        for k in range(1, nc):
            total = total + send(gains[:, :, k], c=k)
        gain_sums = total[:, 0]
        for s in range(1, NZ):
            gain_sums = gain_sums + send(total[:, s], z=s)

        return (
            output[None],
            grad_input[None],
            blocks[0],
            blocks[1],
            blocks[2],
            grad_wo,
            gain_sums[0],
            gain_sums[1],
            gain_sums[2],
            gain_sums[3],
            grad_wg,
            grad_wu,
            grad_wd,
        )

    return body


def solution(mesh):
    return jax.shard_map(
        make_body(mesh.shape["wide"]),
        mesh=mesh,
        in_specs=(
            P("wide", "blk", None),
            P("wide"),
            P(("blk", "wide"), None),
            P(("blk", "wide"), None),
            P(("blk", "wide"), None),
            P(("blk", "wide"), None),
            P(("blk", "wide")),
            P(("blk", "wide")),
            P(("blk", "wide")),
            P(("blk", "wide")),
            P("blk", "wide"),
            P("blk", "wide"),
            P("blk", "wide"),
            P("wide", "blk", None),
        ),
        out_specs=(
            P("wide", "blk", None),
            P("wide", "blk", None),
            P(("blk", "wide"), None),
            P(("blk", "wide"), None),
            P(("blk", "wide"), None),
            P(("blk", "wide"), None),
            P(("blk", "wide")),
            P(("blk", "wide")),
            P(("blk", "wide")),
            P(("blk", "wide")),
            P("blk", "wide"),
            P("blk", "wide"),
            P("blk", "wide"),
        ),
        check_vma=False,
    )
```

time: 1870 us -> 910 us (0.49)
  waiting for transfers between devices: 1450 us -> 316 us
  starting transfers between devices: 11.5 us -> 162 us
  other arithmetic: 32 us -> 143 us
  matrix products: 195 us -> 91.1 us
  local copies, waits for them, and re-layouts: 76.8 us -> 180 us
  blocking collectives: 87 us -> 0 us
    unnamed x21 -> x0, waiting for transfers between devices: 568 us -> none
    all_gather x9 -> x0, waiting for transfers between devices: 454 us -> none  [the longest x1 77.5 us: body(): piece = lax.all_gather(mlp_in, 'wide', axis=0, tiled=True)]
    reduce_scatter x6 -> x0, waiting for transfers between devices: 380 us -> none  [the longest x1 179 us: body(): lax.psum_scatter(contract(block, down_local, 1, 1), 'wide', scatter_dimen...]
    ppermute x4 -> x131, waiting for transfers between devices: 49.3 us -> 316 us  [send(): return lax.ppermute(value, AXES, pairs)]
    ppermute x4 -> x131, starting transfers between devices: 9.99 us -> 162 us  [send(): return lax.ppermute(value, AXES, pairs)]
    dot_general x27 -> x47, matrix products: 195 us -> 88.7 us  [the longest x42 83.6 us: dot(): lax.dot_general(left, right, (((left_dim,), (right_dim,)), ((), ())), pre...]
    unnamed x2 -> x0, blocking collectives: 87 us -> none
    rev x0 -> x12, local copies, waits for them, and re-layouts: none -> 55.3 us  [the longest x8 55.2 us: flipped(): return jnp.where(when == 1, jnp.flip(values, axis), values)]
  transfers between devices with their start and end apart: 22 -> 131, of which waited for: 18 -> 42; matrix products, arithmetic and copies ran while one was open for 13% -> 41% of each run, Pallas kernels for 0% -> 0%
where the time goes in v1:
time: 910 us; the launch traced here: 897 us
  waiting for transfers between devices  316 us (35%)
  local copies, waits for them, and re-layouts  180 us (20%)
  starting transfers between devices  162 us (18%)
  other arithmetic  143 us (16%)
  matrix products  91.1 us (10%)
    ppermute x131, waiting for transfers between devices, send(): return lax.ppermute(value, AXES, pairs)  316 us
    ppermute x131, starting transfers between devices, send(): return lax.ppermute(value, AXES, pairs)  162 us
    dot_general x42, matrix products, dot(): lax.dot_general(left, right, (((left_dim,), (right_dim,)), ((), ())), pre...  83.6 us
    rev x8, local copies, waits for them, and re-layouts, flipped(): return jnp.where(when == 1, jnp.flip(values, axis), values)  55.2 us
    unnamed x311, local copies, waits for them, and re-layouts  41.1 us
    select_n x27, other arithmetic, flipped(): return jnp.where(when == 1, jnp.flip(values, axis), values)  22.5 us
    concatenate x2, other arithmetic, joined(): jnp.concatenate([jnp.concatenate(row, axis=1) for row in blocks], axis=0)  18.3 us
  transfers between devices with their start and end apart: 131, of which 42 were waited for; matrix products, arithmetic and copies ran while one was open for 41% of the time, Pallas kernels for 0%

profile of v1, /device:TPU:0, one launch (start us, length us, event | category | flops | bytes accessed | tf_op | source)
XLA Modules:
  0.0 897.1 jit_solution(13821510536883013018)
XLA Ops:
  90.9 3.5 broadcast_select_fusion.1
  94.4 19.3 %rev.153 = bf16[512,2,4,2,128]{4,3,2,1,0:T(2,128)(2,1)} reverse(bf16[512,2,4,2,128]{4,3,2,1,0:T(2,128)(2,1)} %broadcast_select_fusion.1), dimensions={3} | reverse | bytes 4194304 | tf_op jit(solution)/shard_map/jit(_flip)/rev | solution.py:28
  113.7 3.2 broadcast_select_fusion.3
  139.4 14.5 %collective-permute-done.12 = bf16[2,2,64,1536]{3,2,1,0:T(8,128)(2,1)S(1)} collective-permute-done((bf16[2,2,64,1536]{3,2,1,0:T(8,128)(2,1)}, bf16[2,2,64,1536]{3,2,1,0:T(8,128)(2,1)S(1)}, u32[]{:S(2)}, u32[]{:S(2)}) %collective-permute-start.12) | collective-permute-done | bytes 786464 | tf_op jit(solution)/shard_map/ppermute | solution.py:59
  154.0 4.3 collective-permute-start.14
  160.5 14.5 %collective-permute-done.14 = bf16[2,2,64,1536]{3,2,1,0:T(8,128)(2,1)S(1)} collective-permute-done((bf16[2,2,64,1536]{3,2,1,0:T(8,128)(2,1)S(1)}, bf16[2,2,64,1536]{3,2,1,0:T(8,128)(2,1)S(1)}, u32[]{:S(2)}, u32[]{:S(2)}) %collective-permute-start.14) | collective-permute-done | bytes 786464 | tf_op jit(solution)/shard_map/ppermute | solution.py:59
  209.8 12.4 %collective-permute-done.32 = bf16[64,2048]{1,0:T(8,128)(2,1)S(1)} collective-permute-done((bf16[64,2048]{1,0:T(8,128)(2,1)S(1)}, bf16[64,2048]{1,0:T(8,128)(2,1)S(1)}, u32[]{:S(2)}, u32[]{:S(2)}) %collective-permute-start.32) | collective-permute-done | bytes 262176 | tf_op jit(solution)/shard_map/ppermute | solution.py:59
  223.8 9.6 %collective-permute-done.51 = bf16[512,512]{1,0:T(8,128)(2,1)S(1)} collective-permute-done((bf16[512,512]{1,0:T(8,128)(2,1)S(1)}, bf16[512,512]{1,0:T(8,128)(2,1)S(1)}, u32[]{:S(2)}, u32[]{:S(2)}) %collective-permute-start.51) | collective-permute-done | bytes 524320 | tf_op jit(solution)/shard_map/ppermute | solution.py:59
  235.5 3.4 collective-permute-done.50
  239.2 5.4 collective-permute-done.52
  246.7 15.2 %maximum_maximum_fusion.2 = bf16[2048,1024]{1,0:T(8,128)(2,1)} fusion(bf16[512,512]{1,0:T(8,128)(2,1)S(1)} %collective-permute-done.52, bf16[512,512]{1,0:T(8,128)(2,1)S(1)} %collective-permute-done.51, bf16[512,512]{1,0:T(8,128)(2,1)S(1)} %collective-permute-done.50, bf16[512,512]{1,0:T(8,128)(2,1)} %collective-permute-done.49, ...), kind=kLoop, calls=%fused_computation.3 | loop fusion | flops 33554432 | bytes 8388608 | tf_op jit(solution)/shard_map/concatenate | solution.py:214
  262.4 27.0 %collective-permute-done.35 = bf16[64,2048]{1,0:T(8,128)(2,1)S(1)} collective-permute-done((bf16[64,2048]{1,0:T(8,128)(2,1)}, bf16[64,2048]{1,0:T(8,128)(2,1)S(1)}, u32[]{:S(2)}, u32[]{:S(2)}) %collective-permute-start.35) | collective-permute-done | bytes 262176 | tf_op jit(solution)/shard_map/ppermute | solution.py:59
  289.8 3.9 collective-permute-done.33
  295.8 15.6 %maximum_maximum_fusion = bf16[2048,1024]{1,0:T(8,128)(2,1)} fusion(bf16[1024,512]{1,0:T(8,128)(2,1)S(1)} %collective-permute-done.43, bf16[1024,512]{1,0:T(8,128)(2,1)} %collective-permute-done.42, bf16[1024,512]{1,0:T(8,128)(2,1)S(1)} %collective-permute-done.41, bf16[1024,512]{1,0:T(8,128)(2,1)S(1)} %copy-done.79), kind=kLoop, calls=%fused_computation.1 | loop fusion | flops 16777216 | bytes 8388608 | tf_op jit(solution)/shard_map/concatenate | solution.py:211
  311.9 5.9 collective-permute-done.36
  324.7 4.3 collective-permute-start.54
  332.0 5.0 collective-permute-done.54
  337.0 4.4 collective-permute-start.55
  346.9 6.4 collective-permute-done.55
  355.3 4.3 collective-permute-start.56
  363.7 8.2 collective-permute-done.56
  378.4 3.8 collective-permute-done.63
  382.4 4.5 collective-permute-start.64
  394.3 3.2 collective-permute-done.64
  397.8 4.3 collective-permute-start.65
  403.4 8.3 collective-permute-done.65
  417.5 4.1 rev.175
  427.3 5.6 rev.176
  438.7 4.8 collective-permute-start.68
  446.3 4.2 multiply_convert_fusion.10
  451.8 3.9 collective-permute-done.68
  457.7 4.2 collective-permute-start.69
  467.5 5.8 collective-permute-done.69
  473.3 4.3 collective-permute-start.70
  480.9 8.5 collective-permute-done.70
  495.4 4.4 collective-permute-start.77
  503.9 4.9 convolution_convert_fusion.2
  508.9 8.5 convolution_convert_fusion.1
  521.9 7.0 convolution_convert_fusion
  534.5 9.8 %collective-permute-done.126 = bf16[512,512]{1,0:T(8,128)(2,1)S(1)} collective-permute-done((bf16[512,512]{1,0:T(8,128)(2,1)S(1)}, bf16[512,512]{1,0:T(8,128)(2,1)S(1)}, u32[]{:S(2)}, u32[]{:S(2)}) %collective-permute-start.126) | collective-permute-done | bytes 524320 | tf_op jit(solution)/shard_map/ppermute | solution.py:59
  548.4 9.5 %collective-permute-done.123 = bf16[1024,512]{1,0:T(8,128)(2,1)S(1)} collective-permute-done((bf16[1024,512]{1,0:T(8,128)(2,1)S(1)}, bf16[1024,512]{1,0:T(8,128)(2,1)S(1)}, u32[]{:S(2)}, u32[]{:S(2)}) %collective-permute-start.123) | collective-permute-done | bytes 1048608 | tf_op jit(solution)/shard_map/ppermute | solution.py:59
  559.3 11.1 %collective-permute-done.120 = bf16[1024,512]{1,0:T(8,128)(2,1)S(1)} collective-permute-done((bf16[1024,512]{1,0:T(8,128)(2,1)S(1)}, bf16[1024,512]{1,0:T(8,128)(2,1)S(1)}, u32[]{:S(2)}, u32[]{:S(2)}) %collective-permute-start.120) | collective-permute-done | bytes 1048608 | tf_op jit(solution)/shard_map/ppermute | solution.py:59
  579.2 4.1 rev.177
  583.2 3.8 multiply_reduce_fusion.2
  593.2 9.0 %collective-permute-done.127 = bf16[512,512]{1,0:T(8,128)(2,1)} collective-permute-done((bf16[512,512]{1,0:T(8,128)(2,1)}, bf16[512,512]{1,0:T(8,128)(2,1)}, u32[]{:S(2)}, u32[]{:S(2)}) %collective-permute-start.127) | collective-permute-done | bytes 524320 | tf_op jit(solution)/shard_map/ppermute | solution.py:59
  603.7 3.2 convert_add_fusion.7
  613.6 24.8 %collective-permute-done.81 = bf16[64,2048]{1,0:T(8,128)(2,1)S(1)} collective-permute-done((bf16[64,2048]{1,0:T(8,128)(2,1)S(1)}, bf16[64,2048]{1,0:T(8,128)(2,1)S(1)}, u32[]{:S(2)}, u32[]{:S(2)}) %collective-permute-start.81) | collective-permute-done | bytes 262176 | tf_op jit(solution)/shard_map/ppermute | solution.py:59
  643.3 12.5 %collective-permute-done.84 = bf16[64,2048]{1,0:T(8,128)(2,1)S(1)} collective-permute-done((bf16[64,2048]{1,0:T(8,128)(2,1)S(1)}, bf16[64,2048]{1,0:T(8,128)(2,1)S(1)}, u32[]{:S(2)}, u32[]{:S(2)}) %collective-permute-start.84) | collective-permute-done | bytes 262176 | tf_op jit(solution)/shard_map/ppermute | solution.py:59
  725.9 3.6 pad_maximum_fusion
  729.5 3.5 broadcast_select_fusion
  733.0 19.3 %rev.182 = bf16[512,2,4,2,128]{4,3,2,1,0:T(2,128)(2,1)} reverse(bf16[512,2,4,2,128]{4,3,2,1,0:T(2,128)(2,1)} %broadcast_select_fusion), dimensions={3} | reverse | bytes 4194304 | tf_op jit(solution)/shard_map/jit(_flip)/rev | solution.py:28
  752.3 4.6 broadcast_select_fusion.2
  756.8 3.4 reshape.727
  766.9 24.1 %collective-permute-done.90 = bf16[64,2048]{1,0:T(8,128)(2,1)S(1)} collective-permute-done((bf16[64,2048]{1,0:T(8,128)(2,1)S(1)}, bf16[64,2048]{1,0:T(8,128)(2,1)S(1)}, u32[]{:S(2)}, u32[]{:S(2)}) %collective-permute-start.90) | collective-permute-done | bytes 262176 | tf_op jit(solution)/shard_map/ppermute | solution.py:59
  791.8 3.3 convert_add_fusion
  798.8 3.3 convert_add_fusion.1
  803.9 6.3 collective-permute-done.109
  810.2 3.2 collective-permute-start.99
  814.8 14.5 %collective-permute-done.99 = bf16[4,64,1536]{2,1,0:T(8,128)(2,1)S(1)} collective-permute-done((bf16[4,64,1536]{2,1,0:T(8,128)(2,1)S(1)}, bf16[4,64,1536]{2,1,0:T(8,128)(2,1)S(1)}, u32[]{:S(2)}, u32[]{:S(2)}) %collective-permute-start.99) | collective-permute-done | bytes 786464 | tf_op jit(solution)/shard_map/ppermute | solution.py:59
  829.3 4.3 collective-permute-start.110
  837.5 4.3 collective-permute-start.100
  842.8 16.4 %collective-permute-done.100 = bf16[4,64,1536]{2,1,0:T(8,128)(2,1)S(1)} collective-permute-done((bf16[4,64,1536]{2,1,0:T(8,128)(2,1)S(1)}, bf16[4,64,1536]{2,1,0:T(8,128)(2,1)S(1)}, u32[]{:S(2)}, u32[]{:S(2)}) %collective-permute-start.100) | collective-permute-done | bytes 786464 | tf_op jit(solution)/shard_map/ppermute | solution.py:59
  860.4 4.5 collective-permute-start.101
  872.5 5.7 collective-permute-done.101
  (833 shorter events, 395.7 us)
Async XLA Ops:
  1.9 31.6 %collective-permute-start.22 = (bf16[4,64]{1,0:T(4,128)(2,1)}, bf16[4,64]{1,0:T(4,128)(2,1)}, u32[]{:S(2)}, u32[]{:S(2)}) collective-permute-start(bf16[4,64]{1,0:T(4,128)(2,1)} %get-tuple-element.33), channel_id=1, source_target_pairs={{0,4},{1,5},{2,6},{3,7},{4,8},{5,9},{6,10},{7,11},{8,12},{9,13},{1... | collective-permute-start | bytes 1544 | tf_op jit(solution)/shard_map/ppermute | solution.py:59
  4.9 27.9 %collective-permute-start.21 = (bf16[4,64]{1,0:T(4,128)(2,1)}, bf16[4,64]{1,0:T(4,128)(2,1)}, u32[]{:S(2)}, u32[]{:S(2)}) collective-permute-start(bf16[4,64]{1,0:T(4,128)(2,1)} %get-tuple-element.33), channel_id=1, source_target_pairs={{0,8},{1,9},{2,10},{3,11},{4,12},{5,13},{6,14},{7,15},{8,0},{9,1},... | collective-permute-start | bytes 1544 | tf_op jit(solution)/shard_map/ppermute | solution.py:59
  7.5 24.1 %collective-permute-start.20 = (bf16[4,64]{1,0:T(4,128)(2,1)}, bf16[4,64]{1,0:T(4,128)(2,1)}, u32[]{:S(2)}, u32[]{:S(2)}) collective-permute-start(bf16[4,64]{1,0:T(4,128)(2,1)} %get-tuple-element.33), channel_id=1, source_target_pairs={{0,12},{1,13},{2,14},{3,15},{4,0},{5,1},{6,2},{7,3},{8,4},{9,5},{1... | collective-permute-start | bytes 1544 | tf_op jit(solution)/shard_map/ppermute | solution.py:59
  9.5 20.4 %collective-permute-start.16 = (f32[1]{0:T(128)}, f32[1]{0:T(128)}, u32[]{:S(2)}, u32[]{:S(2)}) collective-permute-start(f32[1]{0:T(128)} %convert_element_type.552), channel_id=1, source_target_pairs={{0,2},{1,3},{2,0},{3,1},{4,6},{5,7},{6,4},{7,5},{8,10},{9,11},{10,... | collective-permute-start | bytes 20 | tf_op jit(solution)/shard_map/ppermute | solution.py:59
  12.4 68.8 %collective-permute-start.25 = (bf16[64,2048]{1,0:T(8,128)(2,1)}, bf16[64,2048]{1,0:T(8,128)(2,1)}, u32[]{:S(2)}, u32[]{:S(2)}) collective-permute-start(bf16[64,2048]{1,0:T(8,128)(2,1)} %param.19), channel_id=1, source_target_pairs={{0,12},{1,13},{2,14},{3,15},{4,0},{5,1},{6,2},{7,3},{8,4},{9,5},{1... | collective-permute-start | bytes 786440 | tf_op jit(solution)/shard_map/ppermute | solution.py:59
  30.0 29.4 %collective-permute-start.24 = (bf16[64,2048]{1,0:T(8,128)(2,1)}, bf16[64,2048]{1,0:T(8,128)(2,1)}, u32[]{:S(2)}, u32[]{:S(2)}) collective-permute-start(bf16[64,2048]{1,0:T(8,128)(2,1)} %param.19), channel_id=1, source_target_pairs={{0,1},{1,0},{2,3},{3,2},{4,5},{5,4},{6,7},{7,6},{8,9},{9,8},{10,11... | collective-permute-start | bytes 786440 | tf_op jit(solution)/shard_map/ppermute | solution.py:59
  49.9 23.7 %collective-permute-start.2 = (bf16[64,2048]{1,0:T(8,128)(2,1)}, bf16[64,2048]{1,0:T(8,128)(2,1)}, u32[]{:S(2)}, u32[]{:S(2)}) collective-permute-start(bf16[64,2048]{1,0:T(8,128)(2,1)} %slice.451), channel_id=1, source_target_pairs={{0,2},{1,3},{2,0},{3,1},{4,6},{5,7},{6,4},{7,5},{8,10},{9,11},{10,... | collective-permute-start | bytes 786440 | tf_op jit(solution)/shard_map/ppermute | solution.py:59
  63.0 144.2 %collective-permute-start.49 = (bf16[512,512]{1,0:T(8,128)(2,1)}, bf16[512,512]{1,0:T(8,128)(2,1)}, u32[]{:S(2)}, u32[]{:S(2)}) collective-permute-start(bf16[512,512]{1,0:T(8,128)(2,1)} %get-tuple-element.87), channel_id=1, source_target_pairs={{0,16},{1,17},{2,18},{3,19},{4,20},{5,21},{6,22},{7,23},{8,24},{9,... | collective-permute-start | bytes 1572872 | tf_op jit(solution)/shard_map/ppermute | solution.py:59
  73.6 62.6 %collective-permute-start.9 = (bf16[2,2,64,1536]{3,2,1,0:T(8,128)(2,1)}, bf16[2,2,64,1536]{3,2,1,0:T(8,128)(2,1)}, u32[]{:S(2)}, u32[]{:S(2)}) collective-permute-start(bf16[2,2,64,1536]{3,2,1,0:T(8,128)(2,1)} %get-tuple-element.98), channel_id=1, source_target_pairs={{0,1},{1,0},{2,3},{3,2},{4,5},{5,4},{6,7},{7,6},{8,9},{9,8},{10,11... | collective-permute-start | bytes 2359304 | tf_op jit(solution)/shard_map/ppermute | solution.py:59
  81.3 51.8 %collective-permute-start.10 = (bf16[2,2,64,1536]{3,2,1,0:T(8,128)(2,1)}, bf16[2,2,64,1536]{3,2,1,0:T(8,128)(2,1)}, u32[]{:S(2)}, u32[]{:S(2)}) collective-permute-start(bf16[2,2,64,1536]{3,2,1,0:T(8,128)(2,1)} %get-tuple-element.98), channel_id=1, source_target_pairs={{0,12},{1,13},{2,14},{3,15},{4,0},{5,1},{6,2},{7,3},{8,4},{9,5},{1... | collective-permute-start | bytes 2359304 | tf_op jit(solution)/shard_map/ppermute | solution.py:59
  82.7 36.3 %collective-permute-start.27 = (bf16[64,2048]{1,0:T(8,128)(2,1)}, bf16[64,2048]{1,0:T(8,128)(2,1)}, u32[]{:S(2)}, u32[]{:S(2)}) collective-permute-start(bf16[64,2048]{1,0:T(8,128)(2,1)} %collective-permute-done.25), channel_id=1, source_target_pairs={{0,12},{1,13},{2,14},{3,15},{4,0},{5,1},{6,2},{7,3},{8,4},{9,5},{1... | collective-permute-start | bytes 786440 | tf_op jit(solution)/shard_map/ppermute | solution.py:59
  87.9 29.0 %collective-permute-start.26 = (bf16[64,2048]{1,0:T(8,128)(2,1)}, bf16[64,2048]{1,0:T(8,128)(2,1)}, u32[]{:S(2)}, u32[]{:S(2)}) collective-permute-start(bf16[64,2048]{1,0:T(8,128)(2,1)} %collective-permute-done.25), channel_id=1, source_target_pairs={{0,1},{1,0},{2,3},{3,2},{4,5},{5,4},{6,7},{7,6},{8,9},{9,8},{10,11... | collective-permute-start | bytes 786440 | tf_op jit(solution)/shard_map/ppermute | solution.py:59
  127.9 81.0 %collective-permute-start.47 = (bf16[512,512]{1,0:T(8,128)(2,1)}, bf16[512,512]{1,0:T(8,128)(2,1)}, u32[]{:S(2)}, u32[]{:S(2)}) collective-permute-start(bf16[512,512]{1,0:T(8,128)(2,1)} %get-tuple-element.87), channel_id=1, source_target_pairs={{0,2},{1,3},{2,0},{3,1},{4,6},{5,7},{6,4},{7,5},{8,10},{9,11},{10,... | collective-permute-start | bytes 1572872 | tf_op jit(solution)/shard_map/ppermute | solution.py:59
  133.0 20.9 %collective-permute-start.12 = (bf16[2,2,64,1536]{3,2,1,0:T(8,128)(2,1)}, bf16[2,2,64,1536]{3,2,1,0:T(8,128)(2,1)S(1)}, u32[]{:S(2)}, u32[]{:S(2)}) collective-permute-start(bf16[2,2,64,1536]{3,2,1,0:T(8,128)(2,1)} %collective-permute-done.10), channel_id=1, source_target_pairs={{0,12},{1,13},{2,14},{3,15},{4,0},{5,1},{6,2},{7,3},{8,4},{9,5},{1... | collective-permute-start | bytes 2359304 | tf_op jit(solution)/shard_map/ppermute | solution.py:59
  136.2 22.1 %collective-permute-start.11 = (bf16[2,2,64,1536]{3,2,1,0:T(8,128)(2,1)}, bf16[2,2,64,1536]{3,2,1,0:T(8,128)(2,1)S(1)}, u32[]{:S(2)}, u32[]{:S(2)}) collective-permute-start(bf16[2,2,64,1536]{3,2,1,0:T(8,128)(2,1)} %collective-permute-done.10), channel_id=1, source_target_pairs={{0,1},{1,0},{2,3},{3,2},{4,5},{5,4},{6,7},{7,6},{8,9},{9,8},{10,11... | collective-permute-start | bytes 2359304 | tf_op jit(solution)/shard_map/ppermute | solution.py:59
  154.0 21.0 %collective-permute-start.14 = (bf16[2,2,64,1536]{3,2,1,0:T(8,128)(2,1)S(1)}, bf16[2,2,64,1536]{3,2,1,0:T(8,128)(2,1)S(1)}, u32[]{:S(2)}, u32[]{:S(2)}) collective-permute-start(bf16[2,2,64,1536]{3,2,1,0:T(8,128)(2,1)S(1)} %collective-permute-done.12), channel_id=1, source_target_pairs={{0,12},{1,13},{2,14},{3,15},{4,0},{5,1},{6,2},{7,3},{8,4},{9,5},{1... | collective-permute-start | bytes 2359304 | tf_op jit(solution)/shard_map/ppermute | solution.py:59
  190.2 45.2 %collective-permute-start.42 = (bf16[1024,512]{1,0:T(8,128)(2,1)}, bf16[1024,512]{1,0:T(8,128)(2,1)}, u32[]{:S(2)}, u32[]{:S(2)}) collective-permute-start(bf16[1024,512]{1,0:T(8,128)(2,1)} %param.24), channel_id=1, source_target_pairs={{0,16},{1,17},{2,18},{3,19},{4,20},{5,21},{6,22},{7,23},{8,24},{9,... | collective-permute-start | bytes 3145736 | tf_op jit(solution)/shard_map/ppermute | solution.py:59
  190.8 55.8 %collective-permute-start.44 = (bf16[1024,512]{1,0:T(8,128)(2,1)}, bf16[1024,512]{1,0:T(8,128)(2,1)}, u32[]{:S(2)}, u32[]{:S(2)}) collective-permute-start(bf16[1024,512]{1,0:T(8,128)(2,1)} %param.25), channel_id=1, source_target_pairs={{0,2},{1,3},{2,0},{3,1},{4,6},{5,7},{6,4},{7,5},{8,10},{9,11},{10,... | collective-permute-start | bytes 3145736 | tf_op jit(solution)/shard_map/ppermute | solution.py:59
  208.9 24.5 %collective-permute-start.51 = (bf16[512,512]{1,0:T(8,128)(2,1)S(1)}, bf16[512,512]{1,0:T(8,128)(2,1)S(1)}, u32[]{:S(2)}, u32[]{:S(2)}) collective-permute-start(bf16[512,512]{1,0:T(8,128)(2,1)S(1)} %copy-done.60), channel_id=1, source_target_pairs={{0,16},{1,17},{2,18},{3,19},{4,20},{5,21},{6,22},{7,23},{8,24},{9,... | collective-permute-start | bytes 1572872 | tf_op jit(solution)/shard_map/ppermute | solution.py:59
  209.4 29.4 %collective-permute-start.50 = (bf16[512,512]{1,0:T(8,128)(2,1)}, bf16[512,512]{1,0:T(8,128)(2,1)S(1)}, u32[]{:S(2)}, u32[]{:S(2)}) collective-permute-start(bf16[512,512]{1,0:T(8,128)(2,1)} %collective-permute-done.49), channel_id=1, source_target_pairs={{0,2},{1,3},{2,0},{3,1},{4,6},{5,7},{6,4},{7,5},{8,10},{9,11},{10,... | collective-permute-start | bytes 1572872 | tf_op jit(solution)/shard_map/ppermute | solution.py:59
  222.2 22.5 %collective-permute-start.52 = (bf16[512,512]{1,0:T(8,128)(2,1)}, bf16[512,512]{1,0:T(8,128)(2,1)S(1)}, u32[]{:S(2)}, u32[]{:S(2)}) collective-permute-start(bf16[512,512]{1,0:T(8,128)(2,1)} %collective-permute-done.48), channel_id=1, source_target_pairs={{0,16},{1,17},{2,18},{3,19},{4,20},{5,21},{6,22},{7,23},{8,24},{9,... | collective-permute-start | bytes 1572872 | tf_op jit(solution)/shard_map/ppermute | solution.py:59
  233.4 61.8 %collective-permute-start.41 = (bf16[1024,512]{1,0:T(8,128)(2,1)S(1)}, bf16[1024,512]{1,0:T(8,128)(2,1)S(1)}, u32[]{:S(2)}, u32[]{:S(2)}) collective-permute-start(bf16[1024,512]{1,0:T(8,128)(2,1)S(1)} %copy-done.79), channel_id=1, source_target_pairs={{0,2},{1,3},{2,0},{3,1},{4,6},{5,7},{6,4},{7,5},{8,10},{9,11},{10,... | collective-permute-start | bytes 3145736 | tf_op jit(solution)/shard_map/ppermute | solution.py:59
  235.4 60.4 %collective-permute-start.43 = (bf16[1024,512]{1,0:T(8,128)(2,1)}, bf16[1024,512]{1,0:T(8,128)(2,1)S(1)}, u32[]{:S(2)}, u32[]{:S(2)}) collective-permute-start(bf16[1024,512]{1,0:T(8,128)(2,1)} %collective-permute-done.42), channel_id=1, source_target_pairs={{0,2},{1,3},{2,0},{3,1},{4,6},{5,7},{6,4},{7,5},{8,10},{9,11},{10,... | collective-permute-start | bytes 3145736 | tf_op jit(solution)/shard_map/ppermute | solution.py:59
  238.8 23.0 %collective-permute-start.31 = (bf16[64,2048]{1,0:T(8,128)(2,1)}, bf16[64,2048]{1,0:T(8,128)(2,1)S(1)}, u32[]{:S(2)}, u32[]{:S(2)}) collective-permute-start(bf16[64,2048]{1,0:T(8,128)(2,1)} %get-tuple-element.72), channel_id=1, source_target_pairs={{0,16},{1,17},{2,18},{3,19},{4,20},{5,21},{6,22},{7,23},{8,24},{9,... | collective-permute-start | bytes 786440 | tf_op jit(solution)/shard_map/ppermute | solution.py:59
  244.6 44.8 %collective-permute-start.35 = (bf16[64,2048]{1,0:T(8,128)(2,1)}, bf16[64,2048]{1,0:T(8,128)(2,1)S(1)}, u32[]{:S(2)}, u32[]{:S(2)}) collective-permute-start(bf16[64,2048]{1,0:T(8,128)(2,1)} %get-tuple-element.73), channel_id=1, source_target_pairs={{0,2},{1,3},{2,0},{3,1},{4,6},{5,7},{6,4},{7,5},{8,10},{9,11},{10,... | collective-permute-start | bytes 786440 | tf_op jit(solution)/shard_map/ppermute | solution.py:59
  246.6 47.1 %collective-permute-start.33 = (bf16[64,2048]{1,0:T(8,128)(2,1)S(1)}, bf16[64,2048]{1,0:T(8,128)(2,1)S(1)}, u32[]{:S(2)}, u32[]{:S(2)}) collective-permute-start(bf16[64,2048]{1,0:T(8,128)(2,1)S(1)} %fusion.99), channel_id=1, source_target_pairs={{0,2},{1,3},{2,0},{3,1},{4,6},{5,7},{6,4},{7,5},{8,10},{9,11},{10,... | collective-permute-start | bytes 786440 | tf_op jit(solution)/shard_map/ppermute | solution.py:59
  261.9 67.2 %collective-permute-start.45 = (bf16[1024,512]{1,0:T(8,128)(2,1)}, bf16[1024,512]{1,0:T(8,128)(2,1)}, u32[]{:S(2)}, u32[]{:S(2)}) collective-permute-start(bf16[1024,512]{1,0:T(8,128)(2,1)} %param.25), channel_id=1, source_target_pairs={{0,16},{1,17},{2,18},{3,19},{4,20},{5,21},{6,22},{7,23},{8,24},{9,... | collective-permute-start | bytes 3145736 | tf_op jit(solution)/shard_map/ppermute | solution.py:59
  289.4 39.7 %collective-permute-start.46 = (bf16[1024,512]{1,0:T(8,128)(2,1)}, bf16[1024,512]{1,0:T(8,128)(2,1)}, u32[]{:S(2)}, u32[]{:S(2)}) collective-permute-start(bf16[1024,512]{1,0:T(8,128)(2,1)} %collective-permute-done.44), channel_id=1, source_target_pairs={{0,16},{1,17},{2,18},{3,19},{4,20},{5,21},{6,22},{7,23},{8,24},{9,... | collective-permute-start | bytes 3145736 | tf_op jit(solution)/shard_map/ppermute | solution.py:59
  295.2 22.5 %collective-permute-start.36 = (bf16[64,2048]{1,0:T(8,128)(2,1)S(1)}, bf16[64,2048]{1,0:T(8,128)(2,1)S(1)}, u32[]{:S(2)}, u32[]{:S(2)}) collective-permute-start(bf16[64,2048]{1,0:T(8,128)(2,1)S(1)} %get-tuple-element.71), channel_id=1, source_target_pairs={{0,16},{1,17},{2,18},{3,19},{4,20},{5,21},{6,22},{7,23},{8,24},{9,... | collective-permute-start | bytes 786440 | tf_op jit(solution)/shard_map/ppermute | solution.py:59
  361.2 21.0 %collective-permute-start.63 = (bf16[128,2048]{1,0:T(8,128)(2,1)S(1)}, bf16[128,2048]{1,0:T(8,128)(2,1)S(1)}, u32[]{:S(2)}, u32[]{:S(2)}) collective-permute-start(bf16[128,2048]{1,0:T(8,128)(2,1)S(1)} %fusion.48), channel_id=1, source_target_pairs={{0,12},{1,13},{2,14},{3,15},{4,0},{5,1},{6,2},{7,3},{8,4},{9,5},{1... | collective-permute-start | bytes 1572872 | tf_op jit(solution)/shard_map/ppermute | solution.py:59
  457.1 115.7 %collective-permute-start.67 = (bf16[128,2048]{1,0:T(8,128)(2,1)S(1)}, bf16[128,2048]{1,0:T(8,128)(2,1)}, u32[]{:S(2)}, u32[]{:S(2)}) collective-permute-start(bf16[128,2048]{1,0:T(8,128)(2,1)S(1)} %slice.851), channel_id=1, source_target_pairs={{0,1},{1,0},{2,3},{3,2},{4,5},{5,4},{6,7},{7,6},{8,9},{9,8},{10,11... | collective-permute-start | bytes 1572872 | tf_op jit(solution)/shard_map/ppermute | solution.py:59
  495.4 25.1 %collective-permute-start.77 = (bf16[128,2048]{1,0:T(8,128)(2,1)}, bf16[128,2048]{1,0:T(8,128)(2,1)S(1)}, u32[]{:S(2)}, u32[]{:S(2)}) collective-permute-start(bf16[128,2048]{1,0:T(8,128)(2,1)} %fusion.42), channel_id=1, source_target_pairs={{0,12},{1,13},{2,14},{3,15},{4,0},{5,1},{6,2},{7,3},{8,4},{9,5},{1... | collective-permute-start | bytes 1572872 | tf_op jit(solution)/shard_map/ppermute | solution.py:59
  499.8 20.6 %collective-permute-start.74 = (bf16[128,2048]{1,0:T(8,128)(2,1)}, bf16[128,2048]{1,0:T(8,128)(2,1)S(1)}, u32[]{:S(2)}, u32[]{:S(2)}) collective-permute-start(bf16[128,2048]{1,0:T(8,128)(2,1)} %slice.849), channel_id=1, source_target_pairs={{0,1},{1,0},{2,3},{3,2},{4,5},{5,4},{6,7},{7,6},{8,9},{9,8},{10,11... | collective-permute-start | bytes 1572872 | tf_op jit(solution)/shard_map/ppermute | solution.py:59
  520.1 25.5 %collective-permute-start.72 = (bf16[128,2048]{1,0:T(8,128)(2,1)S(1)}, bf16[128,2048]{1,0:T(8,128)(2,1)S(1)}, u32[]{:S(2)}, u32[]{:S(2)}) collective-permute-start(bf16[128,2048]{1,0:T(8,128)(2,1)S(1)} %slice.850), channel_id=1, source_target_pairs={{0,1},{1,0},{2,3},{3,2},{4,5},{5,4},{6,7},{7,6},{8,9},{9,8},{10,11... | collective-permute-start | bytes 1572872 | tf_op jit(solution)/shard_map/ppermute | solution.py:59
  520.7 26.4 %collective-permute-start.78 = (bf16[128,2048]{1,0:T(8,128)(2,1)S(1)}, bf16[128,2048]{1,0:T(8,128)(2,1)S(1)}, u32[]{:S(2)}, u32[]{:S(2)}) collective-permute-start(bf16[128,2048]{1,0:T(8,128)(2,1)S(1)} %fusion.44), channel_id=1, source_target_pairs={{0,12},{1,13},{2,14},{3,15},{4,0},{5,1},{6,2},{7,3},{8,4},{9,5},{1... | collective-permute-start | bytes 1572872 | tf_op jit(solution)/shard_map/ppermute | solution.py:59
  531.9 26.0 %collective-permute-start.123 = (bf16[1024,512]{1,0:T(8,128)(2,1)S(1)}, bf16[1024,512]{1,0:T(8,128)(2,1)S(1)}, u32[]{:S(2)}, u32[]{:S(2)}) collective-permute-start(bf16[1024,512]{1,0:T(8,128)(2,1)S(1)} %get-tuple-element.41), channel_id=1, source_target_pairs={{0,2},{1,3},{2,0},{3,1},{4,6},{5,7},{6,4},{7,5},{8,10},{9,11},{10,... | collective-permute-start | bytes 3145736 | tf_op jit(solution)/shard_map/ppermute | solution.py:59
  544.3 26.1 %collective-permute-start.120 = (bf16[1024,512]{1,0:T(8,128)(2,1)S(1)}, bf16[1024,512]{1,0:T(8,128)(2,1)S(1)}, u32[]{:S(2)}, u32[]{:S(2)}) collective-permute-start(bf16[1024,512]{1,0:T(8,128)(2,1)S(1)} %get-tuple-element.43), channel_id=1, source_target_pairs={{0,16},{1,17},{2,18},{3,19},{4,20},{5,21},{6,22},{7,23},{8,24},{9,... | collective-permute-start | bytes 3145736 | tf_op jit(solution)/shard_map/ppermute | solution.py:59
  545.7 245.5 %collective-permute-start.122 = (bf16[1024,512]{1,0:T(8,128)(2,1)}, bf16[1024,512]{1,0:T(8,128)(2,1)}, u32[]{:S(2)}, u32[]{:S(2)}) collective-permute-start(bf16[1024,512]{1,0:T(8,128)(2,1)} %get-tuple-element.40), channel_id=1, source_target_pairs={{0,2},{1,3},{2,0},{3,1},{4,6},{5,7},{6,4},{7,5},{8,10},{9,11},{10,... | collective-permute-start | bytes 3145736 | tf_op jit(solution)/shard_map/ppermute | solution.py:59
  547.1 42.2 %collective-permute-start.125 = (bf16[512,512]{1,0:T(8,128)(2,1)}, bf16[512,512]{1,0:T(8,128)(2,1)}, u32[]{:S(2)}, u32[]{:S(2)}) collective-permute-start(bf16[512,512]{1,0:T(8,128)(2,1)} %get-tuple-element.36), channel_id=1, source_target_pairs={{0,16},{1,17},{2,18},{3,19},{4,20},{5,21},{6,22},{7,23},{8,24},{9,... | collective-permute-start | bytes 1572872 | tf_op jit(solution)/shard_map/ppermute | solution.py:59
  570.4 21.4 %collective-permute-start.129 = (bf16[512,512]{1,0:T(8,128)(2,1)}, bf16[512,512]{1,0:T(8,128)(2,1)}, u32[]{:S(2)}, u32[]{:S(2)}) collective-permute-start(bf16[512,512]{1,0:T(8,128)(2,1)} %get-tuple-element.37), channel_id=1, source_target_pairs={{0,2},{1,3},{2,0},{3,1},{4,6},{5,7},{6,4},{7,5},{8,10},{9,11},{10,... | collective-permute-start | bytes 1572872 | tf_op jit(solution)/shard_map/ppermute | solution.py:59
  572.8 29.4 %collective-permute-start.127 = (bf16[512,512]{1,0:T(8,128)(2,1)}, bf16[512,512]{1,0:T(8,128)(2,1)}, u32[]{:S(2)}, u32[]{:S(2)}) collective-permute-start(bf16[512,512]{1,0:T(8,128)(2,1)} %add_convert_fusion.3), channel_id=1, source_target_pairs={{0,2},{1,3},{2,0},{3,1},{4,6},{5,7},{6,4},{7,5},{8,10},{9,11},{10,... | collective-permute-start | bytes 1572872 | tf_op jit(solution)/shard_map/ppermute | solution.py:59
  587.3 21.5 %collective-permute-start.112 = (f32[2,4,128]{2,1,0:T(4,128)S(1)}, f32[2,4,128]{2,1,0:T(4,128)S(1)}, u32[]{:S(2)}, u32[]{:S(2)}) collective-permute-start(f32[2,4,128]{2,1,0:T(4,128)S(1)} %bitcast.627), channel_id=1, source_target_pairs={{0,16},{1,17},{2,18},{3,19},{4,20},{5,21},{6,22},{7,23},{8,24},{9,... | collective-permute-start | bytes 12296 | tf_op jit(solution)/shard_map/ppermute | solution.py:59
  589.3 20.0 %collective-permute-start.114 = (f32[2,4,128]{2,1,0:T(4,128)S(1)}, f32[2,4,128]{2,1,0:T(4,128)S(1)}, u32[]{:S(2)}, u32[]{:S(2)}) collective-permute-start(f32[2,4,128]{2,1,0:T(4,128)S(1)} %bitcast.626), channel_id=1, source_target_pairs={{0,18},{1,19},{2,16},{3,17},{4,22},{5,23},{6,20},{7,21},{8,26},{9,... | collective-permute-start | bytes 12296 | tf_op jit(solution)/shard_map/ppermute | solution.py:59
  608.8 186.3 %collective-permute-start.119 = (bf16[1024,512]{1,0:T(8,128)(2,1)}, bf16[1024,512]{1,0:T(8,128)(2,1)}, u32[]{:S(2)}, u32[]{:S(2)}) collective-permute-start(bf16[1024,512]{1,0:T(8,128)(2,1)} %get-tuple-element.42), channel_id=1, source_target_pairs={{0,16},{1,17},{2,18},{3,19},{4,20},{5,21},{6,22},{7,23},{8,24},{9,... | collective-permute-start | bytes 3145736 | tf_op jit(solution)/shard_map/ppermute | solution.py:59
  609.3 30.7 %collective-permute-start.83 = (bf16[64,2048]{1,0:T(8,128)(2,1)S(1)}, bf16[64,2048]{1,0:T(8,128)(2,1)S(1)}, u32[]{:S(2)}, u32[]{:S(2)}) collective-permute-start(bf16[64,2048]{1,0:T(8,128)(2,1)S(1)} %get-tuple-element.115), channel_id=1, source_target_pairs={{0,2},{1,3},{2,0},{3,1},{4,6},{5,7},{6,4},{7,5},{8,10},{9,11},{10,... | collective-permute-start | bytes 786440 | tf_op jit(solution)/shard_map/ppermute | solution.py:59
  610.6 27.8 %collective-permute-start.81 = (bf16[64,2048]{1,0:T(8,128)(2,1)S(1)}, bf16[64,2048]{1,0:T(8,128)(2,1)S(1)}, u32[]{:S(2)}, u32[]{:S(2)}) collective-permute-start(bf16[64,2048]{1,0:T(8,128)(2,1)S(1)} %get-tuple-element.115), channel_id=1, source_target_pairs={{0,16},{1,17},{2,18},{3,19},{4,20},{5,21},{6,22},{7,23},{8,24},{9,... | collective-permute-start | bytes 786440 | tf_op jit(solution)/shard_map/ppermute | solution.py:59
  611.8 29.4 %collective-permute-start.82 = (bf16[64,2048]{1,0:T(8,128)(2,1)S(1)}, bf16[64,2048]{1,0:T(8,128)(2,1)S(1)}, u32[]{:S(2)}, u32[]{:S(2)}) collective-permute-start(bf16[64,2048]{1,0:T(8,128)(2,1)S(1)} %get-tuple-element.116), channel_id=1, source_target_pairs={{0,2},{1,3},{2,0},{3,1},{4,6},{5,7},{6,4},{7,5},{8,10},{9,11},{10,... | collective-permute-start | bytes 786440 | tf_op jit(solution)/shard_map/ppermute | solution.py:59
  638.4 44.2 %collective-permute-start.128 = (bf16[512,512]{1,0:T(8,128)(2,1)}, bf16[512,512]{1,0:T(8,128)(2,1)}, u32[]{:S(2)}, u32[]{:S(2)}) collective-permute-start(bf16[512,512]{1,0:T(8,128)(2,1)} %get-tuple-element.38), channel_id=1, source_target_pairs={{0,2},{1,3},{2,0},{3,1},{4,6},{5,7},{6,4},{7,5},{8,10},{9,11},{10,... | collective-permute-start | bytes 1572872 | tf_op jit(solution)/shard_map/ppermute | solution.py:59
  655.8 28.4 %collective-permute-start.130 = (bf16[512,512]{1,0:T(8,128)(2,1)}, bf16[512,512]{1,0:T(8,128)(2,1)}, u32[]{:S(2)}, u32[]{:S(2)}) collective-permute-start(bf16[512,512]{1,0:T(8,128)(2,1)} %get-tuple-element.35), channel_id=1, source_target_pairs={{0,16},{1,17},{2,18},{3,19},{4,20},{5,21},{6,22},{7,23},{8,24},{9,... | collective-permute-start | bytes 1572872 | tf_op jit(solution)/shard_map/ppermute | solution.py:59
  692.2 20.7 %collective-permute-start.115 = (f32[4,4,64]{2,1,0:T(4,128)S(1)}, f32[4,4,64]{2,1,0:T(4,128)S(1)}, u32[]{:S(2)}, u32[]{:S(2)}) collective-permute-start(f32[4,4,64]{2,1,0:T(4,128)S(1)} %bitcast.616), channel_id=1, source_target_pairs={{0,1},{1,0},{2,3},{3,2},{4,5},{5,4},{6,7},{7,6},{8,9},{9,8},{10,11... | collective-permute-start | bytes 12296 | tf_op jit(solution)/shard_map/ppermute | solution.py:59
  713.0 47.3 %collective-permute-start.116 = (f32[4,64]{1,0:T(4,128)S(1)}, f32[4,64]{1,0:T(4,128)S(1)}, u32[]{:S(2)}, u32[]{:S(2)}) collective-permute-start(f32[4,64]{1,0:T(4,128)S(1)} %bitcast.630), channel_id=1, source_target_pairs={{0,4},{1,5},{2,6},{3,7},{4,8},{5,9},{6,10},{7,11},{8,12},{9,13},{1... | collective-permute-start | bytes 3080 | tf_op jit(solution)/shard_map/ppermute | solution.py:59
  714.2 47.4 %collective-permute-start.118 = (f32[4,64]{1,0:T(4,128)S(1)}, f32[4,64]{1,0:T(4,128)S(1)}, u32[]{:S(2)}, u32[]{:S(2)}) collective-permute-start(f32[4,64]{1,0:T(4,128)S(1)} %bitcast.629), channel_id=1, source_target_pairs={{0,12},{1,13},{2,14},{3,15},{4,0},{5,1},{6,2},{7,3},{8,4},{9,5},{1... | collective-permute-start | bytes 3080 | tf_op jit(solution)/shard_map/ppermute | solution.py:59
  716.9 47.2 %collective-permute-start.117 = (f32[4,64]{1,0:T(4,128)S(1)}, f32[4,64]{1,0:T(4,128)S(1)}, u32[]{:S(2)}, u32[]{:S(2)}) collective-permute-start(f32[4,64]{1,0:T(4,128)S(1)} %bitcast.628), channel_id=1, source_target_pairs={{0,8},{1,9},{2,10},{3,11},{4,12},{5,13},{6,14},{7,15},{8,0},{9,1},... | collective-permute-start | bytes 3080 | tf_op jit(solution)/shard_map/ppermute | solution.py:59
  760.4 31.3 %collective-permute-start.124 = (bf16[1024,512]{1,0:T(8,128)(2,1)S(1)}, bf16[1024,512]{1,0:T(8,128)(2,1)S(1)}, u32[]{:S(2)}, u32[]{:S(2)}) collective-permute-start(bf16[1024,512]{1,0:T(8,128)(2,1)S(1)} %copy-done.77), channel_id=1, source_target_pairs={{0,16},{1,17},{2,18},{3,19},{4,20},{5,21},{6,22},{7,23},{8,24},{9,... | collective-permute-start | bytes 3145736 | tf_op jit(solution)/shard_map/ppermute | solution.py:59
  761.5 34.7 %collective-permute-start.121 = (bf16[1024,512]{1,0:T(8,128)(2,1)S(1)}, bf16[1024,512]{1,0:T(8,128)(2,1)S(1)}, u32[]{:S(2)}, u32[]{:S(2)}) collective-permute-start(bf16[1024,512]{1,0:T(8,128)(2,1)S(1)} %copy-done.76), channel_id=1, source_target_pairs={{0,2},{1,3},{2,0},{3,1},{4,6},{5,7},{6,4},{7,5},{8,10},{9,11},{10,... | collective-permute-start | bytes 3145736 | tf_op jit(solution)/shard_map/ppermute | solution.py:59
  765.8 25.2 %collective-permute-start.90 = (bf16[64,2048]{1,0:T(8,128)(2,1)S(1)}, bf16[64,2048]{1,0:T(8,128)(2,1)S(1)}, u32[]{:S(2)}, u32[]{:S(2)}) collective-permute-start(bf16[64,2048]{1,0:T(8,128)(2,1)S(1)} %get-tuple-element.61), channel_id=1, source_target_pairs={{0,16},{1,17},{2,18},{3,19},{4,20},{5,21},{6,22},{7,23},{8,24},{9,... | collective-permute-start | bytes 786440 | tf_op jit(solution)/shard_map/ppermute | solution.py:59
  791.7 22.6 %collective-permute-start.97 = (bf16[4,64,1536]{2,1,0:T(8,128)(2,1)S(1)}, bf16[4,64,1536]{2,1,0:T(8,128)(2,1)S(1)}, u32[]{:S(2)}, u32[]{:S(2)}) collective-permute-start(bf16[4,64,1536]{2,1,0:T(8,128)(2,1)S(1)} %copy-done.81), channel_id=1, source_target_pairs={{0,1},{1,0},{2,3},{3,2},{4,5},{5,4},{6,7},{7,6},{8,9},{9,8},{10,11... | collective-permute-start | bytes 2359304 | tf_op jit(solution)/shard_map/ppermute | solution.py:59
  813.5 69.6 %collective-permute-start.105 = (bf16[64,2048]{1,0:T(8,128)(2,1)}, bf16[64,2048]{1,0:T(8,128)(2,1)S(1)}, u32[]{:S(2)}, u32[]{:S(2)}) collective-permute-start(bf16[64,2048]{1,0:T(8,128)(2,1)} %slice_bitcast_fusion.18), channel_id=1, source_target_pairs={{0,1},{1,0},{2,3},{3,2},{4,5},{5,4},{6,7},{7,6},{8,9},{9,8},{10,11... | collective-permute-start | bytes 786440 | tf_op jit(solution)/shard_map/ppermute | solution.py:59
  813.6 20.3 %collective-permute-start.106 = (bf16[64,2048]{1,0:T(8,128)(2,1)S(1)}, bf16[64,2048]{1,0:T(8,128)(2,1)S(1)}, u32[]{:S(2)}, u32[]{:S(2)}) collective-permute-start(bf16[64,2048]{1,0:T(8,128)(2,1)S(1)} %copy-done.92), channel_id=1, source_target_pairs={{0,1},{1,0},{2,3},{3,2},{4,5},{5,4},{6,7},{7,6},{8,9},{9,8},{10,11... | collective-permute-start | bytes 786440 | tf_op jit(solution)/shard_map/ppermute | solution.py:59
  814.1 28.7 %collective-permute-start.96 = (bf16[4,64,1536]{2,1,0:T(8,128)(2,1)S(1)}, bf16[4,64,1536]{2,1,0:T(8,128)(2,1)S(1)}, u32[]{:S(2)}, u32[]{:S(2)}) collective-permute-start(bf16[4,64,1536]{2,1,0:T(8,128)(2,1)S(1)} %copy-done.80), channel_id=1, source_target_pairs={{0,1},{1,0},{2,3},{3,2},{4,5},{5,4},{6,7},{7,6},{8,9},{9,8},{10,11... | collective-permute-start | bytes 2359304 | tf_op jit(solution)/shard_map/ppermute | solution.py:59
  814.3 28.2 %collective-permute-start.92 = (bf16[64,2048]{1,0:T(8,128)(2,1)S(1)}, bf16[64,2048]{1,0:T(8,128)(2,1)S(1)}, u32[]{:S(2)}, u32[]{:S(2)}) collective-permute-start(bf16[64,2048]{1,0:T(8,128)(2,1)S(1)} %get-tuple-element.60), channel_id=1, source_target_pairs={{0,2},{1,3},{2,0},{3,1},{4,6},{5,7},{6,4},{7,5},{8,10},{9,11},{10,... | collective-permute-start | bytes 786440 | tf_op jit(solution)/shard_map/ppermute | solution.py:59
  837.5 21.7 %collective-permute-start.100 = (bf16[4,64,1536]{2,1,0:T(8,128)(2,1)S(1)}, bf16[4,64,1536]{2,1,0:T(8,128)(2,1)S(1)}, u32[]{:S(2)}, u32[]{:S(2)}) collective-permute-start(bf16[4,64,1536]{2,1,0:T(8,128)(2,1)S(1)} %fusion.26), channel_id=1, source_target_pairs={{0,12},{1,13},{2,14},{3,15},{4,0},{5,1},{6,2},{7,3},{8,4},{9,5},{1... | collective-permute-start | bytes 2359304 | tf_op jit(solution)/shard_map/ppermute | solution.py:59
  842.6 29.9 %collective-permute-start.95 = (bf16[4,64,1536]{2,1,0:T(8,128)(2,1)}, bf16[4,64,1536]{2,1,0:T(8,128)(2,1)}, u32[]{:S(2)}, u32[]{:S(2)}) collective-permute-start(bf16[4,64,1536]{2,1,0:T(8,128)(2,1)} %slice_bitcast_fusion.6), channel_id=1, source_target_pairs={{0,1},{1,0},{2,3},{3,2},{4,5},{5,4},{6,7},{7,6},{8,9},{9,8},{10,11... | collective-permute-start | bytes 2359304 | tf_op jit(solution)/shard_map/ppermute | solution.py:59
  842.6 40.4 %collective-permute-start.111 = (bf16[64,2048]{1,0:T(8,128)(2,1)}, bf16[64,2048]{1,0:T(8,128)(2,1)}, u32[]{:S(2)}, u32[]{:S(2)}) collective-permute-start(bf16[64,2048]{1,0:T(8,128)(2,1)} %fusion.91), channel_id=1, source_target_pairs={{0,12},{1,13},{2,14},{3,15},{4,0},{5,1},{6,2},{7,3},{8,4},{9,5},{1... | collective-permute-start | bytes 786440 | tf_op jit(solution)/shard_map/ppermute | solution.py:59
  (198 other events, 2205.1 us)

commit v2 on v0

v2 whole, which is shorter than its diff:
```python
import functools
import math

import jax
import jax.numpy as jnp
from jax import lax
from jax.experimental import pallas as pl
from jax.experimental.pallas import tpu as pltpu
from jax.sharding import PartitionSpec as P

HEAD_DIM = 128
EPSILON = 1e-06
NEGATIVE = -1e30
BF16 = jnp.bfloat16
F32 = jnp.float32
AXES = ("blk", "wide")
NX, NY, NZ = 2, 2, 4
GROUP = NX * NY
HEADS = NZ * HEAD_DIM
MIB = 1 << 20
SMEM = pl.BlockSpec(memory_space=pltpu.SMEM)
VMEM = pl.BlockSpec(memory_space=pltpu.VMEM)
ANY = pl.BlockSpec(memory_space=pl.ANY)
SQUARE = [(dx, dy) for dx in range(NX) for dy in range(NY)]
TOKEN_BLOCKS = [(dx, dy) for dy in range(NY) for dx in range(NX)]


def shaped(shape, dtype=BF16):
    return jax.ShapeDtypeStruct(tuple(shape), dtype)


def nn(left, right):
    return lax.dot_general(left, right, (((1,), (0,)), ((), ())), preferred_element_type=F32)


def nt(left, right):
    return lax.dot_general(left, right, (((1,), (1,)), ((), ())), preferred_element_type=F32)


def tn(left, right):
    return lax.dot_general(left, right, (((0,), (0,)), ((), ())), preferred_element_type=F32)


def run(body, outs, ins, specs=None, limit=32, **options):
    return pl.pallas_call(
        body,
        out_shape=outs,
        in_specs=specs or [VMEM] * len(ins),
        compiler_params=pltpu.CompilerParams(vmem_limit_bytes=limit * MIB),
        cost_estimate=pl.CostEstimate(flops=0, bytes_accessed=0, transcendentals=0),
        **options,
    )(*ins)


def place(pos):
    return pos[0], pos[1], pos[2], pos[3]


def column_of(x, z, y):
    return pl.multiple_of(((x * NZ + z) * NY + y) * HEAD_DIM, HEAD_DIM)


def split_kernel(pos, w_query, w_key, w_value, *outs):
    x, _, y, _ = place(pos)
    for (dx, dy), out in zip(SQUARE, outs):
        for i, weight in enumerate((w_query, w_key, w_value)):
            for head in range(NZ):
                start = column_of(x ^ dx, head, y ^ dy)
                at = i * HEADS + head * HEAD_DIM
                out[:, at : at + HEAD_DIM] = weight[:, pl.ds(start, HEAD_DIM)]


def join_kernel(*refs):
    *parts, out = refs
    rows = parts[0].shape[0]
    for i, part in enumerate(parts):
        out[i * rows : (i + 1) * rows] = part[...]


def gain_kernel(pos, *refs):
    *blocks, out = refs
    x, z, y, _ = place(pos)
    for (dx, dy), block in zip(SQUARE, blocks):
        for s in range(NZ):
            start = column_of(x ^ dx, (z + s) % NZ, y ^ dy)
            out[:, pl.ds(start, HEAD_DIM)] = block[s]


def row_stats(first, second):
    rows = lax.broadcasted_iota(jnp.int32, (8, first.shape[1]), 0)
    upper = jnp.where(rows < 4, 1.0, 0.0).astype(F32)
    high = functools.partial(
        lax.dot_general,
        dimension_numbers=(((1,), (1,)), ((), ())),
        preferred_element_type=F32,
        precision=lax.Precision.HIGHEST,
    )
    return high(upper, first) + high(1.0 - upper, second)


def group_total(stats, tok):
    blocks = []
    for dx, dy in TOKEN_BLOCKS:
        total = 0.0
        for (sx, sy), ref in zip(SQUARE, stats):
            at = ((dy ^ sy) * NX + (dx ^ sx)) * tok
            total = total + ref[:, at : at + tok]
        blocks.append(total)
    return jnp.concatenate(blocks, axis=1)


def project_kernel(nc, pos, *refs):
    x, z, y, c = place(pos)
    tokens, refs = refs[:GROUP], refs[GROUP:]
    weights, refs = refs[: NZ * nc], refs[NZ * nc :]
    query, key, value, stats, x_all, w_all, sems = refs
    tok = tokens[0].shape[0]
    rows = weights[0].shape[0] // GROUP
    copies = []
    for s in range(NZ):
        for k in range(nc):
            for i, (dx, dy) in enumerate(SQUARE):
                start = column_of(x ^ dx, (z + s) % NZ, y ^ dy) + (c ^ k) * rows
                copies.append(
                    pltpu.make_async_copy(
                        weights[s * nc + k].at[pl.ds(i * rows, rows)],
                        w_all.at[pl.ds(pl.multiple_of(start, rows), rows)],
                        sems.at[len(copies)],
                    )
                )
    for copy in copies:
        copy.start()
    for i, (dx, dy) in enumerate(TOKEN_BLOCKS):
        x_all[i * tok : (i + 1) * tok] = tokens[SQUARE.index((dx, dy))][...]
    for copy in copies:
        copy.wait()
    for out, at in ((query, 0), (key, HEADS), (value, 2 * HEADS)):
        for half in range(2):
            start = half * (HEADS // 2)
            columns = slice(at + start, at + start + HEADS // 2)
            result = nn(x_all[...], w_all[:, columns])
            out[:, start : start + HEADS // 2] = result.astype(out.dtype)
    stats[...] = row_stats(query[...] * query[...], key[...] * key[...])


def turn(values, cosine, sine):
    return values * cosine + pltpu.roll(values, HEAD_DIM // 2, 1) * sine


def valid_keys(x, length, tok):
    shape = (NX * tok, NX * tok)
    queries = lax.broadcasted_iota(jnp.int32, shape, 0)
    keys = lax.broadcasted_iota(jnp.int32, shape, 1)

    def at(index):
        return jnp.where(index < tok, x * tok + index, (1 - x) * tok + index - tok)

    return (at(keys) <= at(queries)) & (at(keys) < length)


def softmax(query, key, valid):
    logits = jnp.where(valid, nt(query, key) * HEAD_DIM ** (-0.5), NEGATIVE)
    powers = jnp.exp(logits - jnp.max(logits, axis=1, keepdims=True))
    return powers / jnp.sum(powers, axis=1, keepdims=True)


def attend_kernel(nc, pos, *refs):
    x, z, y, c = place(pos)
    stats, refs = refs[:GROUP], refs[GROUP:]
    query, key, value, gains, cosine, sine, *refs = refs
    out_parts, refs = refs[: NZ * nc], refs[NZ * nc :]
    query_r, key_r, scales, attended, out_w, *refs = refs
    pieces, sems = refs[:GROUP], refs[GROUP]
    tok = query.shape[0] // GROUP
    span = NX * tok
    rows = out_parts[0].shape[0]
    copies = []
    for s in range(NZ):
        for k in range(nc):
            start = ((z + s) % NZ) * HEAD_DIM + (c ^ k) * rows
            copies.append(
                pltpu.make_async_copy(
                    out_parts[s * nc + k],
                    out_w.at[pl.ds(pl.multiple_of(start, rows), rows)],
                    sems.at[len(copies)],
                )
            )
    for copy in copies:
        copy.start()
    width = out_w.shape[1]
    scale = lax.rsqrt(group_total(stats, tok) / width + EPSILON)
    scales[...] = scale
    for seq in range(NY):
        at = slice(seq * span, (seq + 1) * span)
        columns = jnp.transpose(scale[:, at])
        valid = valid_keys(x, pos[4 + seq], tok)
        for head in range(NZ):
            lanes = slice(head * HEAD_DIM, (head + 1) * HEAD_DIM)
            gain = pl.ds(column_of(x, head, y), HEAD_DIM)
            turned = []
            for row, (raw, out) in enumerate(((query, query_r), (key, key_r))):
                normed = raw[at, lanes] * columns[:, 4 * row : 4 * row + 1]
                normed = normed * gains[row : row + 1, gain]
                out[at, lanes] = turn(normed, cosine[...], sine[...]).astype(BF16)
            chances = softmax(query_r[at, lanes], key_r[at, lanes], valid)
            attended[at, lanes] = nn(chances.astype(BF16), value[at, lanes]).astype(BF16)
    for copy in copies:
        copy.wait()
    step = width // 4
    for part in range(4):
        columns = slice(part * step, (part + 1) * step)
        result = nn(attended[...], out_w[:, columns])
        for i, block in enumerate(TOKEN_BLOCKS):
            out = pieces[SQUARE.index(block)]
            out[:, columns] = result[i * tok : (i + 1) * tok].astype(out.dtype)


def in_halves(values, x, out):
    half = out.shape[1] // NX
    for dx in range(NX):
        start = pl.multiple_of((x ^ dx) * half, half)
        out[:, dx * half : (dx + 1) * half] = values[:, pl.ds(start, half)].astype(out.dtype)


def sum_of(refs):
    total = refs[0][...].astype(F32)
    for ref in refs[1:]:
        total = total + ref[...].astype(F32)
    return total


def branch_kernel(pos, *refs):
    parts, refs = refs[:GROUP], refs[GROUP:]
    inputs, gains, branch_out, hidden_out, mlp_in, scratch = refs
    branch = sum_of(parts)
    branch_out[...] = branch
    scale = lax.rsqrt(jnp.mean(branch * branch, axis=1, keepdims=True) + EPSILON)
    hidden = inputs[...].astype(F32) + branch * scale * gains[2:3, :]
    hidden_out[...] = hidden
    scratch[...] = hidden
    in_halves(scratch, pos[0], mlp_in)


def norm_back(values, gain, grad):
    scale = lax.rsqrt(jnp.mean(values * values, axis=1, keepdims=True) + EPSILON)
    normed = values * scale
    scaled = grad * gain
    mean = jnp.mean(scaled * normed, axis=1, keepdims=True)
    return scale * (scaled - normed * mean), jnp.sum(grad * normed, axis=0, keepdims=True)


def mlp_kernel(count, pos, *refs):
    parts, refs = refs[:count], refs[count:]
    hidden, gains, grad_output, output, grad_in, grad_gain, halves, mlp_out = refs
    halves[...] = sum_of(parts)
    in_halves(halves, pos[0], mlp_out)
    values = mlp_out[...]
    gain = gains[3:4, :]
    scale = lax.rsqrt(jnp.mean(values * values, axis=1, keepdims=True) + EPSILON)
    output[...] = (hidden[...] + values * scale * gain).astype(BF16)
    grad, by_gain = norm_back(values, gain, grad_output[...].astype(F32))
    halves[...] = grad
    in_halves(halves, pos[0], grad_in)
    grad_gain[...] = jnp.broadcast_to(by_gain, grad_gain.shape)


def branch_back_kernel(count, pos, *refs):
    parts, refs = refs[:count], refs[count:]
    branch, gains, grad_output, grad_hidden, grad_branch, grad_gain, halves, middle = refs
    halves[...] = sum_of(parts)
    in_halves(halves, pos[0], middle)
    total = grad_output[...].astype(F32) + middle[...]
    grad_hidden[...] = total
    grad, by_gain = norm_back(branch[...], gains[2:3, :], total)
    grad_branch[...] = grad.astype(BF16)
    grad_gain[...] = jnp.broadcast_to(by_gain, grad_gain.shape)


def attend_back_kernel(pos, *refs):
    blocks, refs = refs[:GROUP], refs[GROUP:]
    out_w, query_r, key_r, value, query, key, scales, gains, cosine, sine, *refs = refs
    branch_all, grad_query, grad_key, grad_value, stats, head_gains, grad_att = refs
    x, _, y, _ = place(pos)
    tok = blocks[0].shape[0]
    span = NX * tok
    for i, block in enumerate(TOKEN_BLOCKS):
        branch_all[i * tok : (i + 1) * tok] = blocks[SQUARE.index(block)][...]
    for half in range(2):
        lanes = slice(half * (HEADS // 2), (half + 1) * (HEADS // 2))
        grad_att[:, lanes] = nt(branch_all[...], out_w[lanes, :]).astype(BF16)
    head_gains[...] = jnp.zeros_like(head_gains)
    for seq in range(NY):
        at = slice(seq * span, (seq + 1) * span)
        columns = jnp.transpose(scales[:, at])
        valid = valid_keys(x, pos[4 + seq], tok)
        for head in range(NZ):
            lanes = slice(head * HEAD_DIM, (head + 1) * HEAD_DIM)
            gain = pl.ds(column_of(x, head, y), HEAD_DIM)
            queries, keys, values = query_r[at, lanes], key_r[at, lanes], value[at, lanes]
            chances = softmax(queries, keys, valid)
            incoming = grad_att[at, lanes]
            grad_chances = nt(incoming, values)
            grad_value[at, lanes] = tn(chances.astype(BF16), incoming).astype(BF16)
            balance = jnp.sum(chances * grad_chances, axis=1, keepdims=True)
            grad_logits = (chances * (grad_chances - balance)).astype(BF16)
            by_query = nn(grad_logits, keys) * HEAD_DIM ** (-0.5)
            by_key = tn(grad_logits, queries) * HEAD_DIM ** (-0.5)
            for row, (grad, raw, out) in enumerate(
                ((by_query, query, grad_query), (by_key, key, grad_key))
            ):
                back = turn(grad.astype(BF16).astype(F32), cosine[...], -sine[...])
                normed = raw[at, lanes] * columns[:, 4 * row : 4 * row + 1]
                head_gains[row : row + 1, lanes] += jnp.sum(back * normed, axis=0, keepdims=True)
                out[at, lanes] = back * gains[row : row + 1, gain]
    stats[...] = row_stats(grad_query[...] * query[...], grad_key[...] * key[...])


def input_back_kernel(*refs):
    stats, refs = refs[:GROUP], refs[GROUP:]
    grad_query, grad_key, grad_value, query, key, scales, w_all, *refs = refs
    grads, *pieces = refs
    tok = query.shape[0] // GROUP
    width = w_all.shape[0]
    means = jnp.transpose(group_total(stats, tok) / width)
    columns = jnp.transpose(scales[...])
    for row, (grad, raw) in enumerate(((grad_query, query), (grad_key, key))):
        scale = columns[:, 4 * row : 4 * row + 1]
        mean = means[:, 4 * row : 4 * row + 1]
        result = scale * (grad[...] - raw[...] * (scale * scale * mean))
        grads[:, row * HEADS : (row + 1) * HEADS] = result.astype(BF16)
    grads[:, 2 * HEADS :] = grad_value[...]
    step = width // 8
    for part in range(8):
        lanes = slice(part * step, (part + 1) * step)
        result = nt(grads[...], w_all[lanes, :])
        for i, block in enumerate(TOKEN_BLOCKS):
            out = pieces[SQUARE.index(block)]
            out[:, lanes] = result[i * tok : (i + 1) * tok].astype(out.dtype)


def weight_back_kernel(nc, s, pos, x_all, grads, *refs):
    *outs, columns, sums = refs
    x, z, y, c = place(pos)
    rows = outs[0].shape[0] // GROUP
    for i, (dx, dy) in enumerate(SQUARE):
        start = column_of(x ^ dx, (z + s) % NZ, y ^ dy)
        columns[:, i * HEAD_DIM : (i + 1) * HEAD_DIM] = x_all[:, pl.ds(start, HEAD_DIM)]
    step = grads.shape[1] // 3
    for part in range(3):
        lanes = slice(part * step, (part + 1) * step)
        sums[:, lanes] = tn(columns[...], grads[:, lanes]).astype(BF16)
    for k, out in enumerate(outs):
        for i in range(GROUP):
            start = pl.multiple_of(i * HEAD_DIM + (c ^ k) * rows, rows)
            out[i * rows : (i + 1) * rows] = sums[pl.ds(start, rows), :]


def pick_kernel(nc, pos, whole, *outs):
    _, z, _, c = place(pos)
    rows = outs[0].shape[0]
    for s in range(NZ):
        for k in range(nc):
            start = ((z + s) % NZ) * HEAD_DIM + (c ^ k) * rows
            outs[s * nc + k][...] = whole[pl.ds(pl.multiple_of(start, rows), rows), :]


def spread_kernel(pos, *refs):
    parts, outs = refs[:GROUP], refs[GROUP:]
    x, _, y, _ = place(pos)
    for (dx, dy), part in zip(SQUARE, parts):
        for i, out in enumerate(outs):
            for head in range(NZ):
                start = column_of(x ^ dx, head, y ^ dy)
                at = i * HEADS + head * HEAD_DIM
                out[:, pl.ds(start, HEAD_DIM)] = part[:, at : at + HEAD_DIM].astype(F32)


def gain_split_kernel(pos, attn, mlp, *outs):
    x, z, y, _ = place(pos)
    for (dx, dy), out in zip(SQUARE, outs):
        out[...] = jnp.zeros_like(out)
        for s in range(NZ):
            start = column_of(x ^ dx, (z + s) % NZ, y ^ dy)
            for row, grad in ((2, attn), (3, mlp)):
                out[s, row : row + 1, :] = grad[0:1, pl.ds(start, HEAD_DIM)]


def gain_sum_kernel(pos, *refs):
    parts, refs = refs[:GROUP], refs[GROUP:]
    heads, *outs = refs
    z = pos[1]
    for s, out in enumerate(outs):
        total = parts[0][s]
        for part in parts[1:]:
            total = total + part[s]
        out[...] = total
        start = pl.multiple_of(((z + s) % NZ) * HEAD_DIM, HEAD_DIM)
        out[0:2, :] = heads[0:2, pl.ds(start, HEAD_DIM)]


def mlp_forward_kernel(nc, per, *refs):
    blocks, refs = refs[:nc], refs[nc:]
    gates, ups, downs, refs = refs[:4], refs[4:8], refs[8:16], refs[16:]
    outs = refs[-(8 + nc + 1) :]
    products, by_gate, by_up, kept = outs[0:2], outs[2:4], outs[4:6], outs[6:8]
    sums, total = outs[8 : 8 + nc], outs[8 + nc]
    j = pl.program_id(0)
    tok = blocks[0].shape[0]
    half = kept[0].shape[1]

    @pl.when(j == 0)
    def _():
        for k, block in enumerate(blocks):
            for dx in range(NX):
                kept[dx][k * tok : (k + 1) * tok] = block[:, dx * half : (dx + 1) * half]

    for dy in range(NY):

        @pl.when(j // per == dy)
        def _(dy=dy):
            def through(weights):
                return nn(kept[0][...], weights[dy][...]) + nn(
                    kept[1][...], weights[NY + dy][...]
                )

            gate, up = through(gates), through(ups)
            chance = 1.0 / (1.0 + jnp.exp(-gate))
            silu = gate * chance
            product = (silu * up).astype(BF16)
            products[dy][...] = product
            by_up[dy][...] = silu.astype(BF16)
            by_gate[dy][...] = (up * (chance + silu * (1.0 - chance))).astype(BF16)
            quarter = half // 2
            for i in range(4):
                lanes = slice(i * quarter, (i + 1) * quarter)
                part = nt(product, downs[i * NY + dy][...])

                @pl.when(j == 0)
                def _(lanes=lanes, part=part):
                    total[:, lanes] = part

                @pl.when(j > 0)
                def _(lanes=lanes, part=part):
                    total[:, lanes] += part

    @pl.when(j == pl.num_programs(0) - 1)
    def _():
        for k, out in enumerate(sums):
            out[...] = total[k * tok : (k + 1) * tok].astype(out.dtype)


def mlp_back_kernel(nc, per, *refs):
    blocks, refs = refs[:nc], refs[nc:]
    gates, ups, downs, refs = refs[:4], refs[4:8], refs[8:16], refs[16:]
    by_gate, by_up = refs[0:2], refs[2:4]
    outs = refs[-(8 + nc + 1) :]
    grad_gates, grad_ups, kept = outs[0:2], outs[2:4], outs[4:8]
    sums, total = outs[8 : 8 + nc], outs[8 + nc]
    j = pl.program_id(0)
    tok = blocks[0].shape[0]
    quarter = kept[0].shape[1]

    @pl.when(j == 0)
    def _():
        for k, block in enumerate(blocks):
            for i in range(4):
                kept[i][k * tok : (k + 1) * tok] = block[:, i * quarter : (i + 1) * quarter]

    for dy in range(NY):

        @pl.when(j // per == dy)
        def _(dy=dy):
            grad = nn(kept[0][...], downs[dy][...])
            for i in range(1, 4):
                grad = grad + nn(kept[i][...], downs[i * NY + dy][...])
            grad_gate = (grad * by_gate[dy][...].astype(F32)).astype(BF16)
            grad_up = (grad * by_up[dy][...].astype(F32)).astype(BF16)
            grad_gates[dy][...] = grad_gate
            grad_ups[dy][...] = grad_up
            for i in range(4):
                lanes = slice(i * quarter, (i + 1) * quarter)
                dx, rows = i // 2, slice((i % 2) * quarter, (i % 2 + 1) * quarter)
                part = nt(grad_gate, gates[dx * NY + dy][rows, :]) + nt(
                    grad_up, ups[dx * NY + dy][rows, :]
                )

                @pl.when(j == 0)
                def _(lanes=lanes, part=part):
                    total[:, lanes] = part

                @pl.when(j > 0)
                def _(lanes=lanes, part=part):
                    total[:, lanes] += part

    @pl.when(j == pl.num_programs(0) - 1)
    def _():
        for k, out in enumerate(sums):
            out[...] = total[k * tok : (k + 1) * tok].astype(out.dtype)


def make_body(wide):
    nc = wide // (NY * NZ)

    def send(value, x=0, y=0, z=0, c=0):
        pairs = []
        for sx in range(NX):
            for sz in range(NZ):
                for sy in range(NY):
                    for sc in range(nc):
                        source = sx * wide + (sz * NY + sy) * nc + sc
                        target = (sx ^ x) * wide
                        target += (((sz + z) % NZ) * NY + (sy ^ y)) * nc + (sc ^ c)
                        pairs.append((source, target))
        return lax.ppermute(value, AXES, pairs)

    def square(parts):
        return [
            part if (dx, dy) == (0, 0) else send(part, x=dx, y=dy)
            for (dx, dy), part in zip(SQUARE, parts)
        ]

    def square_gather(first, second):
        first_x = send(first, x=1)
        second_y = send(second, y=1)
        first_y = send(first, y=1)
        second_x = send(second, x=1)
        first_xy = send(first_x, y=1)
        second_xy = send(second_y, x=1)
        return [first, first_y, first_x, first_xy], [second, second_y, second_x, second_xy]

    def square_scatter(first, second):
        first_a = send(first[3], x=1)
        second_a = send(second[3], y=1)
        first_b = send(first[2], x=1)
        second_b = send(second[1], y=1)
        first_c = send((first[1].astype(F32) + first_a.astype(F32)).astype(BF16), y=1)
        second_c = send((second[2].astype(F32) + second_a.astype(F32)).astype(BF16), x=1)
        return (
            first[0].astype(F32) + first_b.astype(F32) + first_c.astype(F32),
            second[0].astype(F32) + second_b.astype(F32) + second_c.astype(F32),
        )

    def ring_gather(block):
        blocks = [block]
        for _ in range(NZ - 1):
            blocks.append(send(blocks[-1], z=-1))
        return blocks

    def core_gather(block):
        return [block] + [send(block, c=k) for k in range(1, nc)]

    def core_parts(parts):
        return [parts[0]] + [send(parts[k], c=k) for k in range(1, nc)]

    def ring_parts(part_of):
        moving = []
        for s in list(range(1, NZ)) + [0]:
            parts = part_of(s) + moving
            if s == 0:
                return parts
            total = parts[0].astype(F32)
            for part in parts[1:]:
                total = total + part.astype(F32)
            moving = [send(total.astype(BF16), z=-1)]

    def body(
        layer_input,
        lengths,
        w_query,
        w_key,
        w_value,
        w_output,
        query_gain,
        key_gain,
        attn_gain,
        mlp_gain,
        w_gate,
        w_up,
        w_down,
        grad_output,
    ):
        x = lax.axis_index("blk")
        spot = lax.axis_index("wide")
        z, y, c = spot // (NY * nc), (spot // nc) % NY, spot % nc
        inputs = layer_input[0]
        tok, width = inputs.shape
        rows = w_query.shape[0]
        group_tok = GROUP * tok
        hidden = w_gate.shape[1]
        length = lengths.astype(F32)
        other = send(length, y=1)
        pos = jnp.concatenate(
            [jnp.stack([x, z, y, c]), length.astype(jnp.int32), other.astype(jnp.int32)]
        ).astype(jnp.int32)
        heads_shape = (group_tok, HEADS)

        pieces = run(
            split_kernel,
            [shaped((rows, 3 * HEADS))] * GROUP,
            (pos, w_query, w_key, w_value),
            [SMEM] + [VMEM] * 3,
        )
        own_rows = run(join_kernel, shaped((GROUP * rows, 3 * HEADS)), square(pieces))
        tokens = square([inputs] * GROUP)
        w_blocks = [part for block in ring_gather(own_rows) for part in core_gather(block)]
        query, key, value, stats, x_all, w_all = run(
            functools.partial(project_kernel, nc),
            [
                shaped(heads_shape, F32),
                shaped(heads_shape, F32),
                shaped(heads_shape),
                shaped((8, group_tok), F32),
                shaped((group_tok, width)),
                shaped((width, 3 * HEADS)),
            ],
            (pos, *tokens, *w_blocks),
            [SMEM] + [VMEM] * GROUP + [ANY] * len(w_blocks),
            scratch_shapes=[pltpu.SemaphoreType.DMA((GROUP * len(w_blocks),))],
        )

        packed = jnp.stack([query_gain, key_gain, attn_gain, mlp_gain]).astype(F32)
        by_c = jnp.stack(core_gather(packed))
        by_c = by_c[jnp.arange(nc) ^ c].transpose(1, 0, 2).reshape(4, HEAD_DIM)
        by_c = jnp.pad(by_c, ((0, 4), (0, 0)))
        by_z = jnp.stack([by_c] + [send(by_c, z=-s) for s in range(1, NZ)])
        gains = run(
            gain_kernel,
            shaped((8, width), F32),
            (pos, *square([by_z] * GROUP)),
            [SMEM] + [VMEM] * GROUP,
        )

        gate_w, up_w = square_gather(w_gate, w_up)
        down_rows = w_down.shape[0] // 2
        down_halves = square_gather(w_down[:down_rows], w_down[down_rows:])
        down_w = [
            down_halves[half][dx * NY + dy]
            for dx in range(NX)
            for half in range(2)
            for dy in range(NY)
        ]

        half = HEAD_DIM // 2
        order = jnp.concatenate([x * tok + jnp.arange(tok), (1 - x) * tok + jnp.arange(tok)])
        frequency = jnp.exp(
            jnp.arange(half, dtype=F32) * (-2.0 * math.log(500000.0) / HEAD_DIM)
        )
        angles = order.astype(F32)[:, None] * frequency[None, :]
        cosine = jnp.tile(jnp.cos(angles), (1, 2))
        sine = jnp.sin(angles)
        sine = jnp.concatenate([-sine, sine], axis=1)
        out_blocks = [part for block in ring_gather(w_output) for part in core_gather(block)]
        query_r, key_r, scales, attended, out_w, *parts = run(
            functools.partial(attend_kernel, nc),
            [
                shaped(heads_shape),
                shaped(heads_shape),
                shaped((8, group_tok), F32),
                shaped(heads_shape),
                shaped((HEADS, width)),
            ]
            + [shaped((tok, width))] * GROUP,
            (
                pos,
                *square([stats] * GROUP),
                query,
                key,
                value,
                gains,
                cosine,
                sine,
                *out_blocks,
            ),
            [SMEM] + [VMEM] * (GROUP + 6) + [ANY] * len(out_blocks),
            scratch_shapes=[pltpu.SemaphoreType.DMA((len(out_blocks),))],
        )
        branch, hidden_state, mlp_in = run(
            branch_kernel,
            [shaped((tok, width), F32), shaped((tok, width), F32), shaped((tok, width))],
            (pos, *square(parts), inputs, gains),
            [SMEM] + [VMEM] * (GROUP + 2),
            scratch_shapes=[pltpu.VMEM((tok, width), F32)],
        )

        m = nc * tok
        chunk = min(256, hidden)
        per = hidden // chunk
        steps = NY * per
        half_width = width // NX
        quarter = half_width // 2

        def chunk_of(dy):
            return lambda j: jnp.clip(j - dy * per, 0, per - 1)

        def weight_specs():
            specs = []
            for height, count in ((half_width, 4), (half_width, 4), (quarter, 8)):
                for i in range(count):
                    at = chunk_of(i % NY)
                    specs.append(pl.BlockSpec((height, chunk), lambda j, at=at: (0, at(j))))
            return specs

        def whole(shape):
            return pl.BlockSpec(shape, lambda j: (0, 0))

        def row_spec(s, dy):
            at = chunk_of(dy)
            return pl.BlockSpec((m, chunk), lambda j: (s, at(j)))

        def kept_spec(s, columns):
            return pl.BlockSpec((m, columns), lambda j: (s, 0))

        def mlp_call(kernel, s, block, extra, kept_columns, before):
            blocks = core_gather(block)
            ins = (*blocks, *gate_w, *up_w, *down_w, *extra)
            specs = [whole((tok, width))] * nc + weight_specs()
            specs += [row_spec(s, i % NY) for i in range(len(extra))]
            flat = 8 - len(kept_columns)
            outs = [shaped((NZ * m, hidden))] * flat
            outs += [shaped((NZ * m, columns)) for columns in kept_columns]
            aliases = {}
            if before is not None:
                aliases = {len(ins) + i: i for i in range(8)}
                ins = (*ins, *before)
                specs = specs + [ANY] * 8
            out_specs = [row_spec(s, i % NY) for i in range(flat)]
            out_specs += [kept_spec(s, columns) for columns in kept_columns]
            results = run(
                functools.partial(kernel, nc, per),
                outs + [shaped((tok, width), F32)] + [shaped((tok, width))] * (nc - 1),
                ins,
                specs,
                limit=56,
                grid=(steps,),
                out_specs=out_specs + [whole((tok, width))] * nc,
                input_output_aliases=aliases,
                scratch_shapes=[pltpu.VMEM((m, width), F32)],
            )
            return results[:8], core_parts(results[8:])

        kept = None
        sums = []
        for s, block in enumerate(ring_gather(mlp_in)):
            kept, parts = mlp_call(
                mlp_forward_kernel, s, block, (), (half_width, half_width), kept
            )
            sums.append(parts)
        products, by_gate, by_up, mlp_all = kept[0:2], kept[2:4], kept[4:6], kept[6:8]
        parts = ring_parts(lambda s: sums[s])
        output, grad_mlp, grad_gain_mlp = run(
            functools.partial(mlp_kernel, len(parts)),
            [shaped((tok, width)), shaped((tok, width)), shaped((8, width), F32)],
            (pos, *parts, hidden_state, gains, grad_output[0]),
            [SMEM] + [VMEM] * (len(parts) + 3),
            scratch_shapes=[pltpu.VMEM((tok, width), F32)] * 2,
        )
        kept = None
        sums = []
        for s, block in enumerate(ring_gather(grad_mlp)):
            kept, parts = mlp_call(
                mlp_back_kernel, s, block, (*by_gate, *by_up), (quarter,) * 4, kept
            )
            sums.append(parts)
        grad_gates, grad_ups, grad_all = kept[0:2], kept[2:4], kept[4:8]
        parts = ring_parts(lambda s: sums[s])
        grad_hidden, grad_branch, grad_gain_attn = run(
            functools.partial(branch_back_kernel, len(parts)),
            [shaped((tok, width), F32), shaped((tok, width)), shaped((8, width), F32)],
            (pos, *parts, branch, gains, grad_output[0]),
            [SMEM] + [VMEM] * (len(parts) + 3),
            scratch_shapes=[pltpu.VMEM((tok, width), F32)] * 2,
        )

        def products_of(left, right):
            return [tn(left[dx], right[dy]).astype(BF16) for dx, dy in SQUARE]

        grad_wg, grad_wu = square_scatter(
            products_of(mlp_all, grad_gates), products_of(mlp_all, grad_ups)
        )
        grad_wd = jnp.concatenate(
            square_scatter(
                products_of(grad_all[0::2], products), products_of(grad_all[1::2], products)
            ),
            axis=0,
        )

        branch_all, grad_query, grad_key, grad_value, stats, head_gains = run(
            attend_back_kernel,
            [
                shaped((group_tok, width)),
                shaped(heads_shape, F32),
                shaped(heads_shape, F32),
                shaped(heads_shape),
                shaped((8, group_tok), F32),
                shaped((8, HEADS), F32),
            ],
            (
                pos,
                *square([grad_branch] * GROUP),
                out_w,
                query_r,
                key_r,
                value,
                query,
                key,
                scales,
                gains,
                cosine,
                sine,
            ),
            [SMEM] + [VMEM] * (GROUP + 10),
            scratch_shapes=[pltpu.VMEM(heads_shape, BF16)],
        )
        grads, *parts = run(
            input_back_kernel,
            [shaped((group_tok, 3 * HEADS))] + [shaped((tok, width))] * GROUP,
            (
                *square([stats] * GROUP),
                grad_query,
                grad_key,
                grad_value,
                query,
                key,
                scales,
                w_all,
            ),
            limit=40,
        )
        grad_x = grad_hidden
        for part in square(parts):
            grad_x = grad_x + part.astype(F32)

        def weight_parts(s):
            return core_parts(
                run(
                    functools.partial(weight_back_kernel, nc, s),
                    [shaped((GROUP * rows, 3 * HEADS))] * nc,
                    (pos, x_all, grads),
                    [SMEM, VMEM, VMEM],
                    scratch_shapes=[
                        pltpu.VMEM((group_tok, GROUP * HEAD_DIM), BF16),
                        pltpu.VMEM((GROUP * HEAD_DIM, 3 * HEADS), BF16),
                    ],
                )
            )

        total = 0.0
        for part in ring_parts(weight_parts):
            total = total + part.astype(F32)
        total = total.astype(BF16).reshape(GROUP, rows, 3 * HEADS)
        grad_wq, grad_wk, grad_wv = run(
            spread_kernel,
            [shaped((rows, width), F32)] * 3,
            (pos, *square([total[i] for i in range(GROUP)])),
            [SMEM] + [VMEM] * GROUP,
        )
        picked = run(
            functools.partial(pick_kernel, nc),
            [shaped((rows, width))] * (NZ * nc),
            (pos, tn(attended, branch_all).astype(BF16)),
            [SMEM, VMEM],
        )
        grad_wo = 0.0
        for part in ring_parts(lambda s: core_parts(picked[s * nc : (s + 1) * nc])):
            grad_wo = grad_wo + part.astype(F32)

        wide_gains = run(
            gain_split_kernel,
            [shaped((NZ, 8, HEAD_DIM), F32)] * GROUP,
            (pos, grad_gain_attn, grad_gain_mlp),
            [SMEM, VMEM, VMEM],
        )
        gain_parts = run(
            gain_sum_kernel,
            [shaped((8, HEAD_DIM), F32)] * NZ,
            (pos, *square(wide_gains), head_gains),
            [SMEM] + [VMEM] * (GROUP + 1),
        )
        gain_sums = gain_parts[0]
        for s in range(1, NZ):
            gain_sums = gain_sums + send(gain_parts[s], z=s)
        total_gains = gain_sums
        for k in range(1, nc):
            total_gains = total_gains + send(gain_sums, c=k)
        total_gains = lax.dynamic_slice_in_dim(total_gains, c * rows, rows, 1)

        return (
            output[None],
            grad_x.astype(BF16)[None],
            grad_wq,
            grad_wk,
            grad_wv,
            grad_wo,
            total_gains[0],
            total_gains[1],
            total_gains[2],
            total_gains[3],
            grad_wg,
            grad_wu,
            grad_wd,
        )

    return body


def solution(mesh):
    return jax.shard_map(
        make_body(mesh.shape["wide"]),
        mesh=mesh,
        in_specs=(
            P("wide", "blk", None),
            P("wide"),
            P(("blk", "wide"), None),
            P(("blk", "wide"), None),
            P(("blk", "wide"), None),
            P(("blk", "wide"), None),
            P(("blk", "wide")),
            P(("blk", "wide")),
            P(("blk", "wide")),
            P(("blk", "wide")),
            P("blk", "wide"),
            P("blk", "wide"),
            P("blk", "wide"),
            P("wide", "blk", None),
        ),
        out_specs=(
            P("wide", "blk", None),
            P("wide", "blk", None),
            P(("blk", "wide"), None),
            P(("blk", "wide"), None),
            P(("blk", "wide"), None),
            P(("blk", "wide"), None),
            P(("blk", "wide")),
            P(("blk", "wide")),
            P(("blk", "wide")),
            P(("blk", "wide")),
            P("blk", "wide"),
            P("blk", "wide"),
            P("blk", "wide"),
        ),
        check_vma=False,
    )
```

time: 1870 us -> 729 us (0.39)
  waiting for transfers between devices: 1450 us -> 343 us
  matrix products: 195 us -> 21 us
  Pallas kernels: 0 us -> 162 us
  starting transfers between devices: 11.5 us -> 137 us
  blocking collectives: 87 us -> 0 us
  local copies, waits for them, and re-layouts: 76.8 us -> 40.8 us
    unnamed x21 -> x0, waiting for transfers between devices: 568 us -> none
    all_gather x9 -> x0, waiting for transfers between devices: 454 us -> none  [the longest x1 77.5 us: body(): piece = lax.all_gather(mlp_in, 'wide', axis=0, tiled=True)]
    reduce_scatter x6 -> x0, waiting for transfers between devices: 380 us -> none  [the longest x1 179 us: body(): lax.psum_scatter(contract(block, down_local, 1, 1), 'wide', scatter_dimen...]
    ppermute x4 -> x119, waiting for transfers between devices: 49.3 us -> 343 us  [send(): return lax.ppermute(value, AXES, pairs)]
    dot_general x27 -> x17, matrix products: 195 us -> 21 us  [tn(): lax.dot_general(left, right, (((0,), (0,)), ((), ())), preferred_element_...]
    pallas_call x0 -> x26, Pallas kernels: none -> 162 us  [run(): pl.pallas_call(body, out_shape=outs, in_specs=specs or [VMEM] * len(ins),...]
    ppermute x4 -> x119, starting transfers between devices: 9.99 us -> 137 us  [send(): return lax.ppermute(value, AXES, pairs)]
    unnamed x2 -> x0, blocking collectives: 87 us -> none
  transfers between devices with their start and end apart: 22 -> 119, of which waited for: 18 -> 39; matrix products, arithmetic and copies ran while one was open for 13% -> 6% of each run, Pallas kernels for 0% -> 22%
where the time goes in v2:
time: 729 us; the launch traced here: 726 us
  waiting for transfers between devices  343 us (47%)
  Pallas kernels  162 us (22%)
  starting transfers between devices  137 us (19%)
  local copies, waits for them, and re-layouts  40.8 us (6%)
  matrix products  21 us (3%)
  other arithmetic  18.4 us (3%)
    ppermute x119, waiting for transfers between devices, send(): return lax.ppermute(value, AXES, pairs)  343 us
    pallas_call x26, Pallas kernels, run(): pl.pallas_call(body, out_shape=outs, in_specs=specs or [VMEM] * len(ins),...  162 us
    ppermute x119, starting transfers between devices, send(): return lax.ppermute(value, AXES, pairs)  137 us
    unnamed x194, local copies, waits for them, and re-layouts  34.5 us
    dot_general x17, matrix products, tn(): lax.dot_general(left, right, (((0,), (0,)), ((), ())), preferred_element_...  21 us
  transfers between devices with their start and end apart: 119, of which 39 were waited for; matrix products, arithmetic and copies ran while one was open for 6% of the time, Pallas kernels for 22%

profile of v2, /device:TPU:0, one launch (start us, length us, event | category | flops | bytes accessed | tf_op | source)
XLA Modules:
  0.0 725.7 jit_solution(8087080931884003194)
XLA Ops:
  1.4 4.3 collective-permute-start
  13.9 3.0 collective-permute-done.4.refs_1_
  16.9 2.9 collective-permute-done.5.refs_2_
  21.8 3.8 collective-permute-start.8
  25.7 14.4 %collective-permute-done.8.refs_6_ = bf16[256,1536]{1,0:T(8,128)(2,1)S(1)} collective-permute-done((bf16[256,1536]{1,0:T(8,128)(2,1)S(1)}, bf16[256,1536]{1,0:T(8,128)(2,1)S(1)}, u32[]{:S(2)}, u32[]{:S(2)}) %collective-permute-start.8) | collective-permute-done | bytes 786464 | tf_op jit(solution)/shard_map/ppermute | solution.py:514
  40.1 4.3 collective-permute-start.10
  47.3 10.5 %collective-permute-done.10.refs_8_ = bf16[256,1536]{1,0:T(8,128)(2,1)S(1)} collective-permute-done((bf16[256,1536]{1,0:T(8,128)(2,1)S(1)}, bf16[256,1536]{1,0:T(8,128)(2,1)S(1)}, u32[]{:S(2)}, u32[]{:S(2)}) %collective-permute-start.10) | collective-permute-done | bytes 786464 | tf_op jit(solution)/shard_map/ppermute | solution.py:514
  57.9 4.4 collective-permute-start.12
  63.5 12.1 %collective-permute-done.20 = f32[8,128]{1,0:T(8,128)S(1)} collective-permute-done((f32[8,128]{1,0:T(8,128)S(1)}, f32[8,128]{1,0:T(8,128)S(1)}, u32[]{:S(2)}, u32[]{:S(2)}) %collective-permute-start.20) | collective-permute-done | bytes 4128 | tf_op jit(solution)/shard_map/ppermute | solution.py:514
  75.7 3.6 collective-permute-done.18
  82.0 2.8 collective-permute-done.21.refs_1_
  88.2 6.5 collective-permute-done.25.refs_12_
  100.2 6.6 collective-permute-done.27.refs_14_
  106.9 4.2 collective-permute-start.29
  111.0 2.2 fusion.15
  113.3 3.0 collective-permute-done.29.refs_16_
  122.7 11.6 %shard_map.239 = (f32[512,512]{1,0:T(8,128)S(1)}, f32[512,512]{1,0:T(8,128)S(1)}, bf16[512,512]{1,0:T(8,128)(2,1)S(1)}, f32[8,512]{1,0:T(8,128)S(1)}, bf16[512,2...) custom-call(s32[6]{0:T(128)S(1)} %concatenate.23.pos, bf16[128,2048]{1,0:T(8,128)(2,1)S(1)} %bitcast.72, ...), custom_call_target="tpu_custom_call" | custom-call | tf_op jit(solution)/shard_map/pallas_call | solution.py:45
  135.3 2.6 copy-done.3
  158.2 7.2 shard_map.241
  170.6 5.6 collective-permute-done.42.refs_13_
  179.0 19.6 %collective-permute-done.31.refs_1_ = bf16[128,2048]{1,0:T(8,128)(2,1)S(1)} collective-permute-done((bf16[128,2048]{1,0:T(8,128)(2,1)S(1)}, bf16[128,2048]{1,0:T(8,128)(2,1)S(1)}, u32[]{:S(2)}, u32[]{:S(2)}) %collective-permute-start.31) | collective-permute-done | bytes 524320 | tf_op jit(solution)/shard_map/ppermute | solution.py:514
  204.1 43.9 %collective-permute-done.45.refs_16_ = bf16[512,512]{1,0:T(8,128)(2,1)S(1)} collective-permute-done((bf16[512,512]{1,0:T(8,128)(2,1)S(1)}, bf16[512,512]{1,0:T(8,128)(2,1)S(1)}, u32[]{:S(2)}, u32[]{:S(2)}) %collective-permute-start.45) | collective-permute-done | bytes 524320 | tf_op jit(solution)/shard_map/ppermute | solution.py:514
  250.6 4.3 collective-permute-start.48
  256.4 6.5 collective-permute-done.44.refs_15_
  263.4 19.6 %collective-permute-done.46.refs_17_ = bf16[512,512]{1,0:T(8,128)(2,1)S(1)} collective-permute-done((bf16[512,512]{1,0:T(8,128)(2,1)S(1)}, bf16[512,512]{1,0:T(8,128)(2,1)S(1)}, u32[]{:S(2)}, u32[]{:S(2)}) %collective-permute-start.46) | collective-permute-done | bytes 524320 | tf_op jit(solution)/shard_map/ppermute | solution.py:514
  283.0 4.4 collective-permute-start.49
  290.2 13.0 %shard_map.243 = (bf16[1024,512]{1,0:T(8,128)(2,1)}, bf16[1024,512]{1,0:T(8,128)(2,1)}, bf16[1024,512]{1,0:T(8,128)(2,1)}, bf16[1024,512]{1,0:T(8,128)(2,1)}, bf...) custom-call(bf16[128,2048]{1,0:T(8,128)(2,1)} %copy-done.33, ...), custom_call_target="tpu_custom_call" | custom-call | tf_op jit(solution)/shard_map/pallas_call | solution.py:45
  304.0 13.0 %shard_map.244 = (bf16[1024,512]{1,0:T(8,128)(2,1)}, bf16[1024,512]{1,0:T(8,128)(2,1)}, bf16[1024,512]{1,0:T(8,128)(2,1)}, bf16[1024,512]{1,0:T(8,128)(2,1)}, bf...) custom-call(bf16[128,2048]{1,0:T(8,128)(2,1)} %collective-permute-do, ...), custom_call_target="tpu_custom_call", output_to_operand_aliasing={{0}: (18, {}), {1}: (19, {}), {2}: (20, {}), {3}: (21, {}),... | custom-call | tf_op jit(solution)/shard_map/pallas_call | solution.py:45
  321.4 13.0 %shard_map.245 = (bf16[1024,512]{1,0:T(8,128)(2,1)}, bf16[1024,512]{1,0:T(8,128)(2,1)}, bf16[1024,512]{1,0:T(8,128)(2,1)}, bf16[1024,512]{1,0:T(8,128)(2,1)}, bf...) custom-call(bf16[128,2048]{1,0:T(8,128)(2,1)} %copy-done.82, ...), custom_call_target="tpu_custom_call", output_to_operand_aliasing={{0}: (18, {}), {1}: (19, {}), {2}: (20, {}), {3}: (21, {}),... | custom-call | tf_op jit(solution)/shard_map/pallas_call | solution.py:45
  335.0 7.8 %collective-permute-done.57 = bf16[128,2048]{1,0:T(8,128)(2,1)S(1)} collective-permute-done((bf16[128,2048]{1,0:T(8,128)(2,1)S(1)}, bf16[128,2048]{1,0:T(8,128)(2,1)S(1)}, u32[]{:S(2)}, u32[]{:S(2)}) %collective-permute-start.57) | collective-permute-done | bytes 524320 | tf_op jit(solution)/shard_map/ppermute | solution.py:514
  344.2 2.5 collective-permute-start.58
  347.5 13.0 %shard_map.246 = (bf16[1024,512]{1,0:T(8,128)(2,1)}, bf16[1024,512]{1,0:T(8,128)(2,1)}, bf16[1024,512]{1,0:T(8,128)(2,1)}, bf16[1024,512]{1,0:T(8,128)(2,1)}, bf...) custom-call(bf16[128,2048]{1,0:T(8,128)(2,1)} %copy-done.83, ...), custom_call_target="tpu_custom_call", output_to_operand_aliasing={{0}: (18, {}), {1}: (19, {}), {2}: (20, {}), {3}: (21, {}),... | custom-call | tf_op jit(solution)/shard_map/pallas_call | solution.py:45
  364.3 13.9 %collective-permute-done.59.refs_2_ = bf16[128,2048]{1,0:T(8,128)(2,1)S(1)} collective-permute-done((bf16[128,2048]{1,0:T(8,128)(2,1)S(1)}, bf16[128,2048]{1,0:T(8,128)(2,1)S(1)}, u32[]{:S(2)}, u32[]{:S(2)}) %collective-permute-start.59) | collective-permute-done | bytes 524320 | tf_op jit(solution)/shard_map/ppermute | solution.py:514
  383.0 11.1 %collective-permute-done.62.refs_0_ = bf16[128,2048]{1,0:T(8,128)(2,1)S(1)} collective-permute-done((bf16[128,2048]{1,0:T(8,128)(2,1)S(1)}, bf16[128,2048]{1,0:T(8,128)(2,1)S(1)}, u32[]{:S(2)}, u32[]{:S(2)}) %collective-permute-start.62) | collective-permute-done | bytes 524320 | tf_op jit(solution)/shard_map/ppermute | solution.py:514
  394.0 4.2 collective-permute-start.63
  398.7 9.6 %collective-permute-done.63.refs_0_ = bf16[128,2048]{1,0:T(8,128)(2,1)} collective-permute-done((bf16[128,2048]{1,0:T(8,128)(2,1)S(1)}, bf16[128,2048]{1,0:T(8,128)(2,1)}, u32[]{:S(2)}, u32[]{:S(2)}) %collective-permute-start.63) | collective-permute-done | bytes 524320 | tf_op jit(solution)/shard_map/ppermute | solution.py:514
  408.3 4.4 collective-permute-start.64
  413.5 14.9 %shard_map.248 = (bf16[1024,512]{1,0:T(8,128)(2,1)}, bf16[1024,512]{1,0:T(8,128)(2,1)}, bf16[1024,512]{1,0:T(8,128)(2,1)}, bf16[1024,512]{1,0:T(8,128)(2,1)}, bf...) custom-call(bf16[128,2048]{1,0:T(8,128)(2,1)} %copy-done.32, ...), custom_call_target="tpu_custom_call" | custom-call | tf_op jit(solution)/shard_map/pallas_call | solution.py:45
  429.2 14.9 %shard_map.249 = (bf16[1024,512]{1,0:T(8,128)(2,1)}, bf16[1024,512]{1,0:T(8,128)(2,1)}, bf16[1024,512]{1,0:T(8,128)(2,1)}, bf16[1024,512]{1,0:T(8,128)(2,1)}, bf...) custom-call(bf16[128,2048]{1,0:T(8,128)(2,1)} %copy-done.84, ...), custom_call_target="tpu_custom_call", output_to_operand_aliasing={{0}: (22, {}), {1}: (23, {}), {2}: (24, {}), {3}: (25, {}),... | custom-call | tf_op jit(solution)/shard_map/pallas_call | solution.py:45
  446.4 2.3 add_convert_fusion.9
  448.8 14.9 %shard_map.250 = (bf16[1024,512]{1,0:T(8,128)(2,1)}, bf16[1024,512]{1,0:T(8,128)(2,1)}, bf16[1024,512]{1,0:T(8,128)(2,1)}, bf16[1024,512]{1,0:T(8,128)(2,1)}, bf...) custom-call(bf16[128,2048]{1,0:T(8,128)(2,1)} %collective-permute-do, ...), custom_call_target="tpu_custom_call", output_to_operand_aliasing={{0}: (22, {}), {1}: (23, {}), {2}: (24, {}), {3}: (25, {}),... | custom-call | tf_op jit(solution)/shard_map/pallas_call | solution.py:45
  464.0 15.1 %shard_map.251 = (bf16[1024,512]{1,0:T(8,128)(2,1)}, bf16[1024,512]{1,0:T(8,128)(2,1)}, bf16[1024,512]{1,0:T(8,128)(2,1)}, bf16[1024,512]{1,0:T(8,128)(2,1)}, bf...) custom-call(bf16[128,2048]{1,0:T(8,128)(2,1)} %collective-permute-do, ...), custom_call_target="tpu_custom_call", output_to_operand_aliasing={{0}: (22, {}), {1}: (23, {}), {2}: (24, {}), {3}: (25, {}),... | custom-call | tf_op jit(solution)/shard_map/pallas_call | solution.py:45
  479.1 2.7 convolution_convert_fusion.5
  483.1 2.3 convolution_convert_fusion.7
  488.0 2.3 convolution_convert_fusion.3
  500.4 9.7 %collective-permute-done.117 = bf16[512,512]{1,0:T(8,128)(2,1)S(1)} collective-permute-done((bf16[512,512]{1,0:T(8,128)(2,1)S(1)}, bf16[512,512]{1,0:T(8,128)(2,1)S(1)}, u32[]{:S(2)}, u32[]{:S(2)}) %collective-permute-start.117) | collective-permute-done | bytes 524320 | tf_op jit(solution)/shard_map/ppermute | solution.py:514
  514.7 16.8 %collective-permute-done.114 = bf16[512,512]{1,0:T(8,128)(2,1)S(1)} collective-permute-done((bf16[512,512]{1,0:T(8,128)(2,1)S(1)}, bf16[512,512]{1,0:T(8,128)(2,1)S(1)}, u32[]{:S(2)}, u32[]{:S(2)}) %collective-permute-start.114) | collective-permute-done | bytes 524320 | tf_op jit(solution)/shard_map/ppermute | solution.py:514
  535.5 9.8 %collective-permute-done.73.refs_2_ = bf16[128,2048]{1,0:T(8,128)(2,1)S(1)} collective-permute-done((bf16[128,2048]{1,0:T(8,128)(2,1)S(1)}, bf16[128,2048]{1,0:T(8,128)(2,1)S(1)}, u32[]{:S(2)}, u32[]{:S(2)}) %collective-permute-start.73) | collective-permute-done | bytes 524320 | tf_op jit(solution)/shard_map/ppermute | solution.py:514
  549.8 2.2 collective-permute-start.76
  553.7 27.6 %collective-permute-done.74.refs_1_ = bf16[128,2048]{1,0:T(8,128)(2,1)S(1)} collective-permute-done((bf16[128,2048]{1,0:T(8,128)(2,1)S(1)}, bf16[128,2048]{1,0:T(8,128)(2,1)S(1)}, u32[]{:S(2)}, u32[]{:S(2)}) %collective-permute-start.74) | collective-permute-done | bytes 524320 | tf_op jit(solution)/shard_map/ppermute | solution.py:514
  584.7 7.9 %shard_map.253 = (bf16[512,2048]{1,0:T(8,128)(2,1)S(1)}, f32[512,512]{1,0:T(8,128)S(1)}, f32[512,512]{1,0:T(8,128)S(1)}, bf16[512,512]{1,0:T(8,128)(2,1)S(1)}, f...) custom-call(s32[6]{0:T(128)S(1)} %concatenate.23.pos, bf16[128,2048]{1,0:T(8,128)(2,1)S(1)} %get-tuple-element.245.refs_0_, ...), custom_call_target="tpu_custom_call" | custom-call | tf_op jit(solution)/shard_map/pallas_call | solution.py:45
  594.8 2.2 collective-permute-start.79
  598.0 3.2 collective-permute-start.104
  606.1 6.5 shard_map.254
  625.9 5.1 collective-permute-done.107
  633.0 16.1 %collective-permute-done.109 = bf16[1024,512]{1,0:T(8,128)(2,1)S(1)} collective-permute-done((bf16[1024,512]{1,0:T(8,128)(2,1)S(1)}, bf16[1024,512]{1,0:T(8,128)(2,1)S(1)}, u32[]{:S(2)}, u32[]{:S(2)}) %collective-permute-start.109) | collective-permute-done | bytes 1048608 | tf_op jit(solution)/shard_map/ppermute | solution.py:514
  651.7 3.3 collective-permute-start.97
  657.1 4.6 collective-permute-done.97
  663.8 14.3 %collective-permute-done.88 = bf16[256,1536]{1,0:T(8,128)(2,1)S(1)} collective-permute-done((bf16[256,1536]{1,0:T(8,128)(2,1)S(1)}, bf16[256,1536]{1,0:T(8,128)(2,1)S(1)}, u32[]{:S(2)}, u32[]{:S(2)}) %collective-permute-start.88) | collective-permute-done | bytes 786464 | tf_op jit(solution)/shard_map/ppermute | solution.py:514
  679.1 7.0 collective-permute-done.81
  686.1 4.3 collective-permute-start.98
  691.7 4.3 collective-permute-start.89
  699.0 15.0 %collective-permute-done.89 = bf16[256,1536]{1,0:T(8,128)(2,1)S(1)} collective-permute-done((bf16[256,1536]{1,0:T(8,128)(2,1)S(1)}, bf16[256,1536]{1,0:T(8,128)(2,1)S(1)}, u32[]{:S(2)}, u32[]{:S(2)}) %collective-permute-start.89) | collective-permute-done | bytes 786464 | tf_op jit(solution)/shard_map/ppermute | solution.py:514
  720.6 3.0 collective-permute-done.92.refs_3_
  (456 shorter events, 170.3 us)
Async XLA Ops:
  21.8 18.3 %collective-permute-start.8 = (bf16[256,1536]{1,0:T(8,128)(2,1)S(1)}, bf16[256,1536]{1,0:T(8,128)(2,1)S(1)}, u32[]{:S(2)}, u32[]{:S(2)}) collective-permute-start(bf16[256,1536]{1,0:T(8,128)(2,1)S(1)} %shard_map.238.refs_4_), channel_id=1, source_target_pairs={{0,12},{1,13},{2,14},{3,15},{4,0},{5,1},{6,2},{7,3},{8,4},{9,5},{1... | collective-permute-start | bytes 2359304 | tf_op jit(solution)/shard_map/ppermute | solution.py:514
  40.1 17.8 %collective-permute-start.10 = (bf16[256,1536]{1,0:T(8,128)(2,1)S(1)}, bf16[256,1536]{1,0:T(8,128)(2,1)S(1)}, u32[]{:S(2)}, u32[]{:S(2)}) collective-permute-start(bf16[256,1536]{1,0:T(8,128)(2,1)S(1)} %collective-permute-done.8.refs_6_), channel_id=1, source_target_pairs={{0,12},{1,13},{2,14},{3,15},{4,0},{5,1},{6,2},{7,3},{8,4},{9,5},{1... | collective-permute-start | bytes 2359304 | tf_op jit(solution)/shard_map/ppermute | solution.py:514
  44.4 50.4 %collective-permute-start.1 = (bf16[128,2048]{1,0:T(8,128)(2,1)S(1)}, bf16[128,2048]{1,0:T(8,128)(2,1)S(1)}, u32[]{:S(2)}, u32[]{:S(2)}) collective-permute-start(bf16[128,2048]{1,0:T(8,128)(2,1)S(1)} %bitcast.69), channel_id=1, source_target_pairs={{0,2},{1,3},{2,0},{3,1},{4,6},{5,7},{6,4},{7,5},{8,10},{9,11},{10,... | collective-permute-start | bytes 1572872 | tf_op jit(solution)/shard_map/ppermute | solution.py:514
  45.7 50.3 %collective-permute-start.2 = (bf16[128,2048]{1,0:T(8,128)(2,1)S(1)}, bf16[128,2048]{1,0:T(8,128)(2,1)}, u32[]{:S(2)}, u32[]{:S(2)}) collective-permute-start(bf16[128,2048]{1,0:T(8,128)(2,1)S(1)} %bitcast.70), channel_id=1, source_target_pairs={{0,16},{1,17},{2,18},{3,19},{4,20},{5,21},{6,22},{7,23},{8,24},{9,... | collective-permute-start | bytes 1572872 | tf_op jit(solution)/shard_map/ppermute | solution.py:514
  57.9 39.1 %collective-permute-start.12 = (bf16[256,1536]{1,0:T(8,128)(2,1)S(1)}, bf16[256,1536]{1,0:T(8,128)(2,1)}, u32[]{:S(2)}, u32[]{:S(2)}) collective-permute-start(bf16[256,1536]{1,0:T(8,128)(2,1)S(1)} %collective-permute-done.10.refs_8_), channel_id=1, source_target_pairs={{0,12},{1,13},{2,14},{3,15},{4,0},{5,1},{6,2},{7,3},{8,4},{9,5},{1... | collective-permute-start | bytes 2359304 | tf_op jit(solution)/shard_map/ppermute | solution.py:514
  94.7 21.6 %collective-permute-start.7 = (bf16[256,1536]{1,0:T(8,128)(2,1)S(1)}, bf16[256,1536]{1,0:T(8,128)(2,1)}, u32[]{:S(2)}, u32[]{:S(2)}) collective-permute-start(bf16[256,1536]{1,0:T(8,128)(2,1)S(1)} %shard_map.238.refs_4_), channel_id=1, source_target_pairs={{0,1},{1,0},{2,3},{3,2},{4,5},{5,4},{6,7},{7,6},{8,9},{9,8},{10,11... | collective-permute-start | bytes 2359304 | tf_op jit(solution)/shard_map/ppermute | solution.py:514
  95.5 21.3 %collective-permute-start.9 = (bf16[256,1536]{1,0:T(8,128)(2,1)S(1)}, bf16[256,1536]{1,0:T(8,128)(2,1)}, u32[]{:S(2)}, u32[]{:S(2)}) collective-permute-start(bf16[256,1536]{1,0:T(8,128)(2,1)S(1)} %collective-permute-done.8.refs_6_), channel_id=1, source_target_pairs={{0,1},{1,0},{2,3},{3,2},{4,5},{5,4},{6,7},{7,6},{8,9},{9,8},{10,11... | collective-permute-start | bytes 2359304 | tf_op jit(solution)/shard_map/ppermute | solution.py:514
  96.0 21.6 %collective-permute-start.11 = (bf16[256,1536]{1,0:T(8,128)(2,1)S(1)}, bf16[256,1536]{1,0:T(8,128)(2,1)}, u32[]{:S(2)}, u32[]{:S(2)}) collective-permute-start(bf16[256,1536]{1,0:T(8,128)(2,1)S(1)} %collective-permute-done.10.refs_8_), channel_id=1, source_target_pairs={{0,1},{1,0},{2,3},{3,2},{4,5},{5,4},{6,7},{7,6},{8,9},{9,8},{10,11... | collective-permute-start | bytes 2359304 | tf_op jit(solution)/shard_map/ppermute | solution.py:514
  97.0 20.7 %collective-permute-start.13 = (bf16[256,1536]{1,0:T(8,128)(2,1)}, bf16[256,1536]{1,0:T(8,128)(2,1)}, u32[]{:S(2)}, u32[]{:S(2)}) collective-permute-start(bf16[256,1536]{1,0:T(8,128)(2,1)} %collective-permute-done.12.refs_10_), channel_id=1, source_target_pairs={{0,1},{1,0},{2,3},{3,2},{4,5},{5,4},{6,7},{7,6},{8,9},{9,8},{10,11... | collective-permute-start | bytes 2359304 | tf_op jit(solution)/shard_map/ppermute | solution.py:514
  116.3 24.3 %collective-permute-start.24 = (bf16[64,2048]{1,0:T(8,128)(2,1)S(1)}, bf16[64,2048]{1,0:T(8,128)(2,1)S(1)}, u32[]{:S(2)}, u32[]{:S(2)}) collective-permute-start(bf16[64,2048]{1,0:T(8,128)(2,1)S(1)} %copy-done.37), channel_id=1, source_target_pairs={{0,1},{1,0},{2,3},{3,2},{4,5},{5,4},{6,7},{7,6},{8,9},{9,8},{10,11... | collective-permute-start | bytes 786440 | tf_op jit(solution)/shard_map/ppermute | solution.py:514
  116.3 26.5 %collective-permute-start.26 = (bf16[64,2048]{1,0:T(8,128)(2,1)}, bf16[64,2048]{1,0:T(8,128)(2,1)S(1)}, u32[]{:S(2)}, u32[]{:S(2)}) collective-permute-start(bf16[64,2048]{1,0:T(8,128)(2,1)} %collective-permute-done.25.refs_12_), channel_id=1, source_target_pairs={{0,1},{1,0},{2,3},{3,2},{4,5},{5,4},{6,7},{7,6},{8,9},{9,8},{10,11... | collective-permute-start | bytes 786440 | tf_op jit(solution)/shard_map/ppermute | solution.py:514
  116.8 21.9 %collective-permute-start.23 = (f32[4,8,128]{2,1,0:T(8,128)S(1)}, f32[4,8,128]{2,1,0:T(8,128)S(1)}, u32[]{:S(2)}, u32[]{:S(2)}) collective-permute-start(f32[4,8,128]{2,1,0:T(8,128)S(1)} %pad_maximum_fusion.2.refs_0_), channel_id=1, source_target_pairs={{0,18},{1,19},{2,16},{3,17},{4,22},{5,23},{6,20},{7,21},{8,26},{9,... | collective-permute-start | bytes 49160 | tf_op jit(solution)/shard_map/ppermute | solution.py:514
  117.6 32.1 %collective-permute-start.28 = (bf16[64,2048]{1,0:T(8,128)(2,1)}, bf16[64,2048]{1,0:T(8,128)(2,1)}, u32[]{:S(2)}, u32[]{:S(2)}) collective-permute-start(bf16[64,2048]{1,0:T(8,128)(2,1)} %collective-permute-done.27.refs_14_), channel_id=1, source_target_pairs={{0,1},{1,0},{2,3},{3,2},{4,5},{5,4},{6,7},{7,6},{8,9},{9,8},{10,11... | collective-permute-start | bytes 786440 | tf_op jit(solution)/shard_map/ppermute | solution.py:514
  117.7 33.5 %collective-permute-start.30 = (bf16[64,2048]{1,0:T(8,128)(2,1)}, bf16[64,2048]{1,0:T(8,128)(2,1)}, u32[]{:S(2)}, u32[]{:S(2)}) collective-permute-start(bf16[64,2048]{1,0:T(8,128)(2,1)} %collective-permute-done.29.refs_16_), channel_id=1, source_target_pairs={{0,1},{1,0},{2,3},{3,2},{4,5},{5,4},{6,7},{7,6},{8,9},{9,8},{10,11... | collective-permute-start | bytes 786440 | tf_op jit(solution)/shard_map/ppermute | solution.py:514
  149.8 19.4 %collective-permute-start.41 = (bf16[512,512]{1,0:T(8,128)(2,1)}, bf16[512,512]{1,0:T(8,128)(2,1)S(1)}, u32[]{:S(2)}, u32[]{:S(2)}) collective-permute-start(bf16[512,512]{1,0:T(8,128)(2,1)} %get-tuple-element.306.refs_10_), channel_id=1, source_target_pairs={{0,2},{1,3},{2,0},{3,1},{4,6},{5,7},{6,4},{7,5},{8,10},{9,11},{10,... | collective-permute-start | bytes 1572872 | tf_op jit(solution)/shard_map/ppermute | solution.py:514
  151.1 26.3 %collective-permute-start.43 = (bf16[512,512]{1,0:T(8,128)(2,1)}, bf16[512,512]{1,0:T(8,128)(2,1)S(1)}, u32[]{:S(2)}, u32[]{:S(2)}) collective-permute-start(bf16[512,512]{1,0:T(8,128)(2,1)} %get-tuple-element.306.refs_10_), channel_id=1, source_target_pairs={{0,16},{1,17},{2,18},{3,19},{4,20},{5,21},{6,22},{7,23},{8,24},{9,... | collective-permute-start | bytes 1572872 | tf_op jit(solution)/shard_map/ppermute | solution.py:514
  152.6 23.5 %collective-permute-start.42 = (bf16[512,512]{1,0:T(8,128)(2,1)}, bf16[512,512]{1,0:T(8,128)(2,1)S(1)}, u32[]{:S(2)}, u32[]{:S(2)}) collective-permute-start(bf16[512,512]{1,0:T(8,128)(2,1)} %get-tuple-element.305.refs_12_), channel_id=1, source_target_pairs={{0,2},{1,3},{2,0},{3,1},{4,6},{5,7},{6,4},{7,5},{8,10},{9,11},{10,... | collective-permute-start | bytes 1572872 | tf_op jit(solution)/shard_map/ppermute | solution.py:514
  167.1 31.5 %collective-permute-start.31 = (bf16[128,2048]{1,0:T(8,128)(2,1)S(1)}, bf16[128,2048]{1,0:T(8,128)(2,1)S(1)}, u32[]{:S(2)}, u32[]{:S(2)}) collective-permute-start(bf16[128,2048]{1,0:T(8,128)(2,1)S(1)} %get-tuple-element.168), channel_id=1, source_target_pairs={{0,2},{1,3},{2,0},{3,1},{4,6},{5,7},{6,4},{7,5},{8,10},{9,11},{10,... | collective-permute-start | bytes 1572872 | tf_op jit(solution)/shard_map/ppermute | solution.py:514
  168.6 31.3 %collective-permute-start.32 = (bf16[128,2048]{1,0:T(8,128)(2,1)S(1)}, bf16[128,2048]{1,0:T(8,128)(2,1)S(1)}, u32[]{:S(2)}, u32[]{:S(2)}) collective-permute-start(bf16[128,2048]{1,0:T(8,128)(2,1)S(1)} %get-tuple-element.169), channel_id=1, source_target_pairs={{0,16},{1,17},{2,18},{3,19},{4,20},{5,21},{6,22},{7,23},{8,24},{9,... | collective-permute-start | bytes 1572872 | tf_op jit(solution)/shard_map/ppermute | solution.py:514
  169.2 32.2 %collective-permute-start.33 = (bf16[128,2048]{1,0:T(8,128)(2,1)S(1)}, bf16[128,2048]{1,0:T(8,128)(2,1)S(1)}, u32[]{:S(2)}, u32[]{:S(2)}) collective-permute-start(bf16[128,2048]{1,0:T(8,128)(2,1)S(1)} %get-tuple-element.170), channel_id=1, source_target_pairs={{0,18},{1,19},{2,16},{3,17},{4,22},{5,23},{6,20},{7,21},{8,26},{9,... | collective-permute-start | bytes 1572872 | tf_op jit(solution)/shard_map/ppermute | solution.py:514
  176.1 72.4 %collective-permute-start.36 = (bf16[1024,512]{1,0:T(8,128)(2,1)S(1)}, bf16[1024,512]{1,0:T(8,128)(2,1)S(1)}, u32[]{:S(2)}, u32[]{:S(2)}) collective-permute-start(bf16[1024,512]{1,0:T(8,128)(2,1)S(1)} %copy-done.53), channel_id=1, source_target_pairs={{0,16},{1,17},{2,18},{3,19},{4,20},{5,21},{6,22},{7,23},{8,24},{9,... | collective-permute-start | bytes 3145736 | tf_op jit(solution)/shard_map/ppermute | solution.py:514
  177.4 72.7 %collective-permute-start.38 = (bf16[1024,512]{1,0:T(8,128)(2,1)S(1)}, bf16[1024,512]{1,0:T(8,128)(2,1)S(1)}, u32[]{:S(2)}, u32[]{:S(2)}) collective-permute-start(bf16[1024,512]{1,0:T(8,128)(2,1)S(1)} %copy-done.54), channel_id=1, source_target_pairs={{0,2},{1,3},{2,0},{3,1},{4,6},{5,7},{6,4},{7,5},{8,10},{9,11},{10,... | collective-permute-start | bytes 3145736 | tf_op jit(solution)/shard_map/ppermute | solution.py:514
  198.6 52.0 %collective-permute-start.35 = (bf16[1024,512]{1,0:T(8,128)(2,1)S(1)}, bf16[1024,512]{1,0:T(8,128)(2,1)S(1)}, u32[]{:S(2)}, u32[]{:S(2)}) collective-permute-start(bf16[1024,512]{1,0:T(8,128)(2,1)S(1)} %copy-done.53), channel_id=1, source_target_pairs={{0,2},{1,3},{2,0},{3,1},{4,6},{5,7},{6,4},{7,5},{8,10},{9,11},{10,... | collective-permute-start | bytes 3145736 | tf_op jit(solution)/shard_map/ppermute | solution.py:514
  199.9 55.0 %collective-permute-start.39 = (bf16[1024,512]{1,0:T(8,128)(2,1)S(1)}, bf16[1024,512]{1,0:T(8,128)(2,1)S(1)}, u32[]{:S(2)}, u32[]{:S(2)}) collective-permute-start(bf16[1024,512]{1,0:T(8,128)(2,1)S(1)} %copy-done.54), channel_id=1, source_target_pairs={{0,16},{1,17},{2,18},{3,19},{4,20},{5,21},{6,22},{7,23},{8,24},{9,... | collective-permute-start | bytes 3145736 | tf_op jit(solution)/shard_map/ppermute | solution.py:514
  201.4 46.6 %collective-permute-start.45 = (bf16[512,512]{1,0:T(8,128)(2,1)S(1)}, bf16[512,512]{1,0:T(8,128)(2,1)S(1)}, u32[]{:S(2)}, u32[]{:S(2)}) collective-permute-start(bf16[512,512]{1,0:T(8,128)(2,1)S(1)} %copy-done.61), channel_id=1, source_target_pairs={{0,16},{1,17},{2,18},{3,19},{4,20},{5,21},{6,22},{7,23},{8,24},{9,... | collective-permute-start | bytes 1572872 | tf_op jit(solution)/shard_map/ppermute | solution.py:514
  248.5 38.9 %collective-permute-start.37 = (bf16[1024,512]{1,0:T(8,128)(2,1)S(1)}, bf16[1024,512]{1,0:T(8,128)(2,1)S(1)}, u32[]{:S(2)}, u32[]{:S(2)}) collective-permute-start(bf16[1024,512]{1,0:T(8,128)(2,1)S(1)} %collective-permute-done.36.refs_4_), channel_id=1, source_target_pairs={{0,2},{1,3},{2,0},{3,1},{4,6},{5,7},{6,4},{7,5},{8,10},{9,11},{10,... | collective-permute-start | bytes 3145736 | tf_op jit(solution)/shard_map/ppermute | solution.py:514
  250.1 37.4 %collective-permute-start.40 = (bf16[1024,512]{1,0:T(8,128)(2,1)S(1)}, bf16[1024,512]{1,0:T(8,128)(2,1)S(1)}, u32[]{:S(2)}, u32[]{:S(2)}) collective-permute-start(bf16[1024,512]{1,0:T(8,128)(2,1)S(1)} %collective-permute-done.38.refs_7_), channel_id=1, source_target_pairs={{0,16},{1,17},{2,18},{3,19},{4,20},{5,21},{6,22},{7,23},{8,24},{9,... | collective-permute-start | bytes 3145736 | tf_op jit(solution)/shard_map/ppermute | solution.py:514
  254.9 28.1 %collective-permute-start.46 = (bf16[512,512]{1,0:T(8,128)(2,1)S(1)}, bf16[512,512]{1,0:T(8,128)(2,1)S(1)}, u32[]{:S(2)}, u32[]{:S(2)}) collective-permute-start(bf16[512,512]{1,0:T(8,128)(2,1)S(1)} %collective-permute-done.42.refs_13_), channel_id=1, source_target_pairs={{0,16},{1,17},{2,18},{3,19},{4,20},{5,21},{6,22},{7,23},{8,24},{9,... | collective-permute-start | bytes 1572872 | tf_op jit(solution)/shard_map/ppermute | solution.py:514
  262.9 26.5 %collective-permute-start.34 = (bf16[128,2048]{1,0:T(8,128)(2,1)S(1)}, bf16[128,2048]{1,0:T(8,128)(2,1)S(1)}, u32[]{:S(2)}, u32[]{:S(2)}) collective-permute-start(bf16[128,2048]{1,0:T(8,128)(2,1)S(1)} %get-tuple-element.171.refs_0_), channel_id=1, source_target_pairs={{0,1},{1,0},{2,3},{3,2},{4,5},{5,4},{6,7},{7,6},{8,9},{9,8},{10,11... | collective-permute-start | bytes 1572872 | tf_op jit(solution)/shard_map/ppermute | solution.py:514
  262.9 40.3 %collective-permute-start.53 = (bf16[128,2048]{1,0:T(8,128)(2,1)}, bf16[128,2048]{1,0:T(8,128)(2,1)S(1)}, u32[]{:S(2)}, u32[]{:S(2)}) collective-permute-start(bf16[128,2048]{1,0:T(8,128)(2,1)} %collective-permute-done.48.refs_0_), channel_id=1, source_target_pairs={{0,1},{1,0},{2,3},{3,2},{4,5},{5,4},{6,7},{7,6},{8,9},{9,8},{10,11... | collective-permute-start | bytes 1572872 | tf_op jit(solution)/shard_map/ppermute | solution.py:514
  283.0 34.1 %collective-permute-start.49 = (bf16[128,2048]{1,0:T(8,128)(2,1)}, bf16[128,2048]{1,0:T(8,128)(2,1)S(1)}, u32[]{:S(2)}, u32[]{:S(2)}) collective-permute-start(bf16[128,2048]{1,0:T(8,128)(2,1)} %collective-permute-done.48.refs_0_), channel_id=1, source_target_pairs={{0,12},{1,13},{2,14},{3,15},{4,0},{5,1},{6,2},{7,3},{8,4},{9,5},{1... | collective-permute-start | bytes 1572872 | tf_op jit(solution)/shard_map/ppermute | solution.py:514
  320.5 22.2 %collective-permute-start.57 = (bf16[128,2048]{1,0:T(8,128)(2,1)S(1)}, bf16[128,2048]{1,0:T(8,128)(2,1)S(1)}, u32[]{:S(2)}, u32[]{:S(2)}) collective-permute-start(bf16[128,2048]{1,0:T(8,128)(2,1)S(1)} %add_convert_fusion.12), channel_id=1, source_target_pairs={{0,12},{1,13},{2,14},{3,15},{4,0},{5,1},{6,2},{7,3},{8,4},{9,5},{1... | collective-permute-start | bytes 1572872 | tf_op jit(solution)/shard_map/ppermute | solution.py:514
  398.2 30.2 %collective-permute-start.67 = (bf16[128,2048]{1,0:T(8,128)(2,1)S(1)}, bf16[128,2048]{1,0:T(8,128)(2,1)S(1)}, u32[]{:S(2)}, u32[]{:S(2)}) collective-permute-start(bf16[128,2048]{1,0:T(8,128)(2,1)S(1)} %collective-permute-done.62.refs_0_), channel_id=1, source_target_pairs={{0,1},{1,0},{2,3},{3,2},{4,5},{5,4},{6,7},{7,6},{8,9},{9,8},{10,11... | collective-permute-start | bytes 1572872 | tf_op jit(solution)/shard_map/ppermute | solution.py:514
  408.3 36.4 %collective-permute-start.64 = (bf16[128,2048]{1,0:T(8,128)(2,1)}, bf16[128,2048]{1,0:T(8,128)(2,1)}, u32[]{:S(2)}, u32[]{:S(2)}) collective-permute-start(bf16[128,2048]{1,0:T(8,128)(2,1)} %collective-permute-done.63.refs_0_), channel_id=1, source_target_pairs={{0,12},{1,13},{2,14},{3,15},{4,0},{5,1},{6,2},{7,3},{8,4},{9,5},{1... | collective-permute-start | bytes 1572872 | tf_op jit(solution)/shard_map/ppermute | solution.py:514
  444.6 19.3 %collective-permute-start.65 = (bf16[128,2048]{1,0:T(8,128)(2,1)}, bf16[128,2048]{1,0:T(8,128)(2,1)}, u32[]{:S(2)}, u32[]{:S(2)}) collective-permute-start(bf16[128,2048]{1,0:T(8,128)(2,1)} %collective-permute-done.64.refs_0_), channel_id=1, source_target_pairs={{0,1},{1,0},{2,3},{3,2},{4,5},{5,4},{6,7},{7,6},{8,9},{9,8},{10,11... | collective-permute-start | bytes 1572872 | tf_op jit(solution)/shard_map/ppermute | solution.py:514
  444.7 89.2 %collective-permute-start.61 = (bf16[128,2048]{1,0:T(8,128)(2,1)}, bf16[128,2048]{1,0:T(8,128)(2,1)S(1)}, u32[]{:S(2)}, u32[]{:S(2)}) collective-permute-start(bf16[128,2048]{1,0:T(8,128)(2,1)} %get-tuple-element.212), channel_id=1, source_target_pairs={{0,1},{1,0},{2,3},{3,2},{4,5},{5,4},{6,7},{7,6},{8,9},{9,8},{10,11... | collective-permute-start | bytes 1572872 | tf_op jit(solution)/shard_map/ppermute | solution.py:514
  448.6 44.4 %collective-permute-start.71 = (bf16[128,2048]{1,0:T(8,128)(2,1)}, bf16[128,2048]{1,0:T(8,128)(2,1)}, u32[]{:S(2)}, u32[]{:S(2)}) collective-permute-start(bf16[128,2048]{1,0:T(8,128)(2,1)} %add_convert_fusion.9), channel_id=1, source_target_pairs={{0,12},{1,13},{2,14},{3,15},{4,0},{5,1},{6,2},{7,3},{8,4},{9,5},{1... | collective-permute-start | bytes 1572872 | tf_op jit(solution)/shard_map/ppermute | solution.py:514
  463.8 29.3 %collective-permute-start.69 = (bf16[128,2048]{1,0:T(8,128)(2,1)}, bf16[128,2048]{1,0:T(8,128)(2,1)}, u32[]{:S(2)}, u32[]{:S(2)}) collective-permute-start(bf16[128,2048]{1,0:T(8,128)(2,1)} %get-tuple-element.240), channel_id=1, source_target_pairs={{0,1},{1,0},{2,3},{3,2},{4,5},{5,4},{6,7},{7,6},{8,9},{9,8},{10,11... | collective-permute-start | bytes 1572872 | tf_op jit(solution)/shard_map/ppermute | solution.py:514
  494.6 17.8 %collective-permute-start.72 = (bf16[128,2048]{1,0:T(8,128)(2,1)S(1)}, bf16[128,2048]{1,0:T(8,128)(2,1)S(1)}, u32[]{:S(2)}, u32[]{:S(2)}) collective-permute-start(bf16[128,2048]{1,0:T(8,128)(2,1)S(1)} %add_convert_fusion.8), channel_id=1, source_target_pairs={{0,12},{1,13},{2,14},{3,15},{4,0},{5,1},{6,2},{7,3},{8,4},{9,5},{1... | collective-permute-start | bytes 1572872 | tf_op jit(solution)/shard_map/ppermute | solution.py:514
  494.7 18.3 %collective-permute-start.68 = (bf16[128,2048]{1,0:T(8,128)(2,1)S(1)}, bf16[128,2048]{1,0:T(8,128)(2,1)S(1)}, u32[]{:S(2)}, u32[]{:S(2)}) collective-permute-start(bf16[128,2048]{1,0:T(8,128)(2,1)S(1)} %copy-done.96), channel_id=1, source_target_pairs={{0,1},{1,0},{2,3},{3,2},{4,5},{5,4},{6,7},{7,6},{8,9},{9,8},{10,11... | collective-permute-start | bytes 1572872 | tf_op jit(solution)/shard_map/ppermute | solution.py:514
  495.1 37.2 %collective-permute-start.108 = (bf16[1024,512]{1,0:T(8,128)(2,1)S(1)}, bf16[1024,512]{1,0:T(8,128)(2,1)S(1)}, u32[]{:S(2)}, u32[]{:S(2)}) collective-permute-start(bf16[1024,512]{1,0:T(8,128)(2,1)S(1)} %convolution_convert_fusion.5), channel_id=1, source_target_pairs={{0,16},{1,17},{2,18},{3,19},{4,20},{5,21},{6,22},{7,23},{8,24},{9,... | collective-permute-start | bytes 3145736 | tf_op jit(solution)/shard_map/ppermute | solution.py:514
  510.1 21.4 %collective-permute-start.114 = (bf16[512,512]{1,0:T(8,128)(2,1)S(1)}, bf16[512,512]{1,0:T(8,128)(2,1)S(1)}, u32[]{:S(2)}, u32[]{:S(2)}) collective-permute-start(bf16[512,512]{1,0:T(8,128)(2,1)S(1)} %convolution_convert_fusion.13), channel_id=1, source_target_pairs={{0,16},{1,17},{2,18},{3,19},{4,20},{5,21},{6,22},{7,23},{8,24},{9,... | collective-permute-start | bytes 1572872 | tf_op jit(solution)/shard_map/ppermute | solution.py:514
  512.4 36.6 %collective-permute-start.111 = (bf16[1024,512]{1,0:T(8,128)(2,1)S(1)}, bf16[1024,512]{1,0:T(8,128)(2,1)S(1)}, u32[]{:S(2)}, u32[]{:S(2)}) collective-permute-start(bf16[1024,512]{1,0:T(8,128)(2,1)S(1)} %convolution_convert_fusion.1), channel_id=1, source_target_pairs={{0,2},{1,3},{2,0},{3,1},{4,6},{5,7},{6,4},{7,5},{8,10},{9,11},{10,... | collective-permute-start | bytes 3145736 | tf_op jit(solution)/shard_map/ppermute | solution.py:514
  513.0 35.5 %collective-permute-start.116 = (bf16[512,512]{1,0:T(8,128)(2,1)S(1)}, bf16[512,512]{1,0:T(8,128)(2,1)S(1)}, u32[]{:S(2)}, u32[]{:S(2)}) collective-permute-start(bf16[512,512]{1,0:T(8,128)(2,1)S(1)} %convolution_convert_fusion.11), channel_id=1, source_target_pairs={{0,2},{1,3},{2,0},{3,1},{4,6},{5,7},{6,4},{7,5},{8,10},{9,11},{10,... | collective-permute-start | bytes 1572872 | tf_op jit(solution)/shard_map/ppermute | solution.py:514
  532.3 17.5 %collective-permute-start.118 = (bf16[512,512]{1,0:T(8,128)(2,1)S(1)}, bf16[512,512]{1,0:T(8,128)(2,1)S(1)}, u32[]{:S(2)}, u32[]{:S(2)}) collective-permute-start(bf16[512,512]{1,0:T(8,128)(2,1)S(1)} %fusion.2), channel_id=1, source_target_pairs={{0,16},{1,17},{2,18},{3,19},{4,20},{5,21},{6,22},{7,23},{8,24},{9,... | collective-permute-start | bytes 1572872 | tf_op jit(solution)/shard_map/ppermute | solution.py:514
  533.9 58.7 %collective-permute-start.113 = (bf16[512,512]{1,0:T(8,128)(2,1)S(1)}, bf16[512,512]{1,0:T(8,128)(2,1)S(1)}, u32[]{:S(2)}, u32[]{:S(2)}) collective-permute-start(bf16[512,512]{1,0:T(8,128)(2,1)S(1)} %convolution_convert_fusion.15), channel_id=1, source_target_pairs={{0,16},{1,17},{2,18},{3,19},{4,20},{5,21},{6,22},{7,23},{8,24},{9,... | collective-permute-start | bytes 1572872 | tf_op jit(solution)/shard_map/ppermute | solution.py:514
  545.3 47.9 %collective-permute-start.115 = (bf16[512,512]{1,0:T(8,128)(2,1)S(1)}, bf16[512,512]{1,0:T(8,128)(2,1)S(1)}, u32[]{:S(2)}, u32[]{:S(2)}) collective-permute-start(bf16[512,512]{1,0:T(8,128)(2,1)S(1)} %fusion.8), channel_id=1, source_target_pairs={{0,2},{1,3},{2,0},{3,1},{4,6},{5,7},{6,4},{7,5},{8,10},{9,11},{10,... | collective-permute-start | bytes 1572872 | tf_op jit(solution)/shard_map/ppermute | solution.py:514
  548.5 32.7 %collective-permute-start.74 = (bf16[128,2048]{1,0:T(8,128)(2,1)S(1)}, bf16[128,2048]{1,0:T(8,128)(2,1)S(1)}, u32[]{:S(2)}, u32[]{:S(2)}) collective-permute-start(bf16[128,2048]{1,0:T(8,128)(2,1)S(1)} %get-tuple-element.245.refs_0_), channel_id=1, source_target_pairs={{0,2},{1,3},{2,0},{3,1},{4,6},{5,7},{6,4},{7,5},{8,10},{9,11},{10,... | collective-permute-start | bytes 1572872 | tf_op jit(solution)/shard_map/ppermute | solution.py:514
  549.0 32.7 %collective-permute-start.75 = (bf16[128,2048]{1,0:T(8,128)(2,1)S(1)}, bf16[128,2048]{1,0:T(8,128)(2,1)S(1)}, u32[]{:S(2)}, u32[]{:S(2)}) collective-permute-start(bf16[128,2048]{1,0:T(8,128)(2,1)S(1)} %get-tuple-element.245.refs_0_), channel_id=1, source_target_pairs={{0,16},{1,17},{2,18},{3,19},{4,20},{5,21},{6,22},{7,23},{8,24},{9,... | collective-permute-start | bytes 1572872 | tf_op jit(solution)/shard_map/ppermute | solution.py:514
  549.8 32.7 %collective-permute-start.76 = (bf16[128,2048]{1,0:T(8,128)(2,1)S(1)}, bf16[128,2048]{1,0:T(8,128)(2,1)S(1)}, u32[]{:S(2)}, u32[]{:S(2)}) collective-permute-start(bf16[128,2048]{1,0:T(8,128)(2,1)S(1)} %get-tuple-element.245.refs_0_), channel_id=1, source_target_pairs={{0,18},{1,19},{2,16},{3,17},{4,22},{5,23},{6,20},{7,21},{8,26},{9,... | collective-permute-start | bytes 1572872 | tf_op jit(solution)/shard_map/ppermute | solution.py:514
  598.0 17.7 %collective-permute-start.104 = (f32[8,128]{1,0:T(8,128)S(1)}, f32[8,128]{1,0:T(8,128)S(1)}, u32[]{:S(2)}, u32[]{:S(2)}) collective-permute-start(f32[8,128]{1,0:T(8,128)S(1)} %get-tuple-element.291), channel_id=1, source_target_pairs={{0,8},{1,9},{2,10},{3,11},{4,12},{5,13},{6,14},{7,15},{8,0},{9,1},... | collective-permute-start | bytes 12296 | tf_op jit(solution)/shard_map/ppermute | solution.py:514
  604.8 26.3 %collective-permute-start.107 = (bf16[1024,512]{1,0:T(8,128)(2,1)}, bf16[1024,512]{1,0:T(8,128)(2,1)S(1)}, u32[]{:S(2)}, u32[]{:S(2)}) collective-permute-start(bf16[1024,512]{1,0:T(8,128)(2,1)} %convolution_convert_fusion.7), channel_id=1, source_target_pairs={{0,16},{1,17},{2,18},{3,19},{4,20},{5,21},{6,22},{7,23},{8,24},{9,... | collective-permute-start | bytes 3145736 | tf_op jit(solution)/shard_map/ppermute | solution.py:514
  605.3 46.5 %collective-permute-start.110 = (bf16[1024,512]{1,0:T(8,128)(2,1)}, bf16[1024,512]{1,0:T(8,128)(2,1)S(1)}, u32[]{:S(2)}, u32[]{:S(2)}) collective-permute-start(bf16[1024,512]{1,0:T(8,128)(2,1)} %convolution_convert_fusion.3), channel_id=1, source_target_pairs={{0,2},{1,3},{2,0},{3,1},{4,6},{5,7},{6,4},{7,5},{8,10},{9,11},{10,... | collective-permute-start | bytes 3145736 | tf_op jit(solution)/shard_map/ppermute | solution.py:514
  614.4 34.7 %collective-permute-start.109 = (bf16[1024,512]{1,0:T(8,128)(2,1)S(1)}, bf16[1024,512]{1,0:T(8,128)(2,1)S(1)}, u32[]{:S(2)}, u32[]{:S(2)}) collective-permute-start(bf16[1024,512]{1,0:T(8,128)(2,1)S(1)} %add_convert_fusion.1), channel_id=1, source_target_pairs={{0,2},{1,3},{2,0},{3,1},{4,6},{5,7},{6,4},{7,5},{8,10},{9,11},{10,... | collective-permute-start | bytes 3145736 | tf_op jit(solution)/shard_map/ppermute | solution.py:514
  618.3 36.8 %collective-permute-start.112 = (bf16[1024,512]{1,0:T(8,128)(2,1)S(1)}, bf16[1024,512]{1,0:T(8,128)(2,1)S(1)}, u32[]{:S(2)}, u32[]{:S(2)}) collective-permute-start(bf16[1024,512]{1,0:T(8,128)(2,1)S(1)} %add_convert_fusion), channel_id=1, source_target_pairs={{0,16},{1,17},{2,18},{3,19},{4,20},{5,21},{6,22},{7,23},{8,24},{9,... | collective-permute-start | bytes 3145736 | tf_op jit(solution)/shard_map/ppermute | solution.py:514
  631.1 19.8 %collective-permute-start.85 = (bf16[256,1536]{1,0:T(8,128)(2,1)S(1)}, bf16[256,1536]{1,0:T(8,128)(2,1)S(1)}, u32[]{:S(2)}, u32[]{:S(2)}) collective-permute-start(bf16[256,1536]{1,0:T(8,128)(2,1)S(1)} %get-tuple-element.266), channel_id=1, source_target_pairs={{0,1},{1,0},{2,3},{3,2},{4,5},{5,4},{6,7},{7,6},{8,9},{9,8},{10,11... | collective-permute-start | bytes 2359304 | tf_op jit(solution)/shard_map/ppermute | solution.py:514
  631.1 20.3 %collective-permute-start.87 = (bf16[256,1536]{1,0:T(8,128)(2,1)S(1)}, bf16[256,1536]{1,0:T(8,128)(2,1)S(1)}, u32[]{:S(2)}, u32[]{:S(2)}) collective-permute-start(bf16[256,1536]{1,0:T(8,128)(2,1)S(1)} %add_convert_fusion.5), channel_id=1, source_target_pairs={{0,12},{1,13},{2,14},{3,15},{4,0},{5,1},{6,2},{7,3},{8,4},{9,5},{1... | collective-permute-start | bytes 2359304 | tf_op jit(solution)/shard_map/ppermute | solution.py:514
  650.9 46.3 %collective-permute-start.94 = (bf16[64,2048]{1,0:T(8,128)(2,1)S(1)}, bf16[64,2048]{1,0:T(8,128)(2,1)S(1)}, u32[]{:S(2)}, u32[]{:S(2)}) collective-permute-start(bf16[64,2048]{1,0:T(8,128)(2,1)S(1)} %get-tuple-element.277), channel_id=1, source_target_pairs={{0,1},{1,0},{2,3},{3,2},{4,5},{5,4},{6,7},{7,6},{8,9},{9,8},{10,11... | collective-permute-start | bytes 786440 | tf_op jit(solution)/shard_map/ppermute | solution.py:514
  655.1 23.1 %collective-permute-start.88 = (bf16[256,1536]{1,0:T(8,128)(2,1)S(1)}, bf16[256,1536]{1,0:T(8,128)(2,1)S(1)}, u32[]{:S(2)}, u32[]{:S(2)}) collective-permute-start(bf16[256,1536]{1,0:T(8,128)(2,1)S(1)} %add_convert_fusion.4), channel_id=1, source_target_pairs={{0,12},{1,13},{2,14},{3,15},{4,0},{5,1},{6,2},{7,3},{8,4},{9,5},{1... | collective-permute-start | bytes 2359304 | tf_op jit(solution)/shard_map/ppermute | solution.py:514
  656.8 61.1 %collective-permute-start.93 = (bf16[64,2048]{1,0:T(8,128)(2,1)S(1)}, bf16[64,2048]{1,0:T(8,128)(2,1)S(1)}, u32[]{:S(2)}, u32[]{:S(2)}) collective-permute-start(bf16[64,2048]{1,0:T(8,128)(2,1)S(1)} %get-tuple-element.275), channel_id=1, source_target_pairs={{0,1},{1,0},{2,3},{3,2},{4,5},{5,4},{6,7},{7,6},{8,9},{9,8},{10,11... | collective-permute-start | bytes 786440 | tf_op jit(solution)/shard_map/ppermute | solution.py:514
  662.5 23.5 %collective-permute-start.81 = (bf16[128,2048]{1,0:T(8,128)(2,1)S(1)}, bf16[128,2048]{1,0:T(8,128)(2,1)S(1)}, u32[]{:S(2)}, u32[]{:S(2)}) collective-permute-start(bf16[128,2048]{1,0:T(8,128)(2,1)S(1)} %get-tuple-element.257), channel_id=1, source_target_pairs={{0,16},{1,17},{2,18},{3,19},{4,20},{5,21},{6,22},{7,23},{8,24},{9,... | collective-permute-start | bytes 1572872 | tf_op jit(solution)/shard_map/ppermute | solution.py:514
  679.0 20.0 %collective-permute-start.83 = (bf16[256,1536]{1,0:T(8,128)(2,1)S(1)}, bf16[256,1536]{1,0:T(8,128)(2,1)S(1)}, u32[]{:S(2)}, u32[]{:S(2)}) collective-permute-start(bf16[256,1536]{1,0:T(8,128)(2,1)S(1)} %get-tuple-element.262), channel_id=1, source_target_pairs={{0,1},{1,0},{2,3},{3,2},{4,5},{5,4},{6,7},{7,6},{8,9},{9,8},{10,11... | collective-permute-start | bytes 2359304 | tf_op jit(solution)/shard_map/ppermute | solution.py:514
  691.7 22.3 %collective-permute-start.89 = (bf16[256,1536]{1,0:T(8,128)(2,1)S(1)}, bf16[256,1536]{1,0:T(8,128)(2,1)S(1)}, u32[]{:S(2)}, u32[]{:S(2)}) collective-permute-start(bf16[256,1536]{1,0:T(8,128)(2,1)S(1)} %add_convert_fusion.3), channel_id=1, source_target_pairs={{0,12},{1,13},{2,14},{3,15},{4,0},{5,1},{6,2},{7,3},{8,4},{9,5},{1... | collective-permute-start | bytes 2359304 | tf_op jit(solution)/shard_map/ppermute | solution.py:514
  697.3 20.6 %collective-permute-start.99 = (bf16[64,2048]{1,0:T(8,128)(2,1)S(1)}, bf16[64,2048]{1,0:T(8,128)(2,1)S(1)}, u32[]{:S(2)}, u32[]{:S(2)}) collective-permute-start(bf16[64,2048]{1,0:T(8,128)(2,1)S(1)} %add_convert_fusion.13), channel_id=1, source_target_pairs={{0,12},{1,13},{2,14},{3,15},{4,0},{5,1},{6,2},{7,3},{8,4},{9,5},{1... | collective-permute-start | bytes 786440 | tf_op jit(solution)/shard_map/ppermute | solution.py:514
  (152 other events, 2205.6 us)

commit v3 on v2

v3 whole, which is shorter than its diff:
```python
import functools
import math

import jax
import jax.numpy as jnp
from jax import lax
from jax.experimental import pallas as pl
from jax.experimental.pallas import tpu as pltpu
from jax.sharding import PartitionSpec as P

HEAD_DIM = 128
EPSILON = 1e-06
NEGATIVE = -1e30
BF16 = jnp.bfloat16
F32 = jnp.float32
AXES = ("blk", "wide")
NX, NY, NZ = 2, 2, 4
GROUP = NX * NY
HEADS = NZ * HEAD_DIM
MIB = 1 << 20
SMEM = pl.BlockSpec(memory_space=pltpu.SMEM)
VMEM = pl.BlockSpec(memory_space=pltpu.VMEM)
HBM = pl.BlockSpec(memory_space=pltpu.HBM)
EXTRA = 16
SQUARE = [(dx, dy) for dx in range(NX) for dy in range(NY)]
TOKEN_BLOCKS = [(dx, dy) for dy in range(NY) for dx in range(NX)]


def shaped(shape, dtype=BF16):
    return jax.ShapeDtypeStruct(tuple(shape), dtype)


def nn(left, right):
    return lax.dot_general(left, right, (((1,), (0,)), ((), ())), preferred_element_type=F32)


def nt(left, right):
    return lax.dot_general(left, right, (((1,), (1,)), ((), ())), preferred_element_type=F32)


def tn(left, right):
    return lax.dot_general(left, right, (((0,), (0,)), ((), ())), preferred_element_type=F32)


def auto(array):
    return pl.BlockSpec(array.shape, lambda i: (0,) * len(array.shape))


def run(body, outs, ins, limit=12, **options):
    return pl.pallas_call(
        body,
        grid=(1,),
        out_shape=[out for out, _ in outs],
        out_specs=[spec if isinstance(spec, pl.BlockSpec) else spec(out) for out, spec in outs],
        in_specs=[spec if isinstance(spec, pl.BlockSpec) else spec(array) for array, spec in ins],
        compiler_params=pltpu.CompilerParams(vmem_limit_bytes=limit * MIB),
        **options,
    )(*[array for array, _ in ins])


def each(arrays, spec):
    return [(array, spec) for array in arrays]


def after(value, *others):
    return lax.optimization_barrier((value, others))[0]


class Copies:
    def __init__(self, sems):
        self.sems, self.count = sems, 0

    def start(self, source, target):
        copy = pltpu.make_async_copy(source, target, self.sems.at[self.count])
        self.count += 1
        copy.start()
        return copy


def finish(copies):
    for copy in copies:
        copy.wait()


def place(pos):
    return pos[0], pos[1], pos[2], pos[3]


def gray(index):
    return index ^ (index >> 1)


def ring(r, s):
    return gray((r + s) % NZ)


def column_of(x, z, y):
    return pl.multiple_of(((x * NZ + z) * NY + y) * HEAD_DIM, HEAD_DIM)


def extra_rows(blocks):
    used = sum(block.shape[0] for block in blocks)
    if used < EXTRA:
        blocks = [*blocks, jnp.zeros((EXTRA - used, HEAD_DIM), F32)]
    return jnp.concatenate(blocks, axis=0)


def put_extra(out, start, values):
    out[start : start + EXTRA, :HEAD_DIM] = values.astype(BF16)
    out[start : start + EXTRA, HEAD_DIM:] = jnp.zeros((EXTRA, out.shape[1] - HEAD_DIM), BF16)


def split_kernel(pos, gains, w_query, w_key, w_value, *outs):
    x, _, y, _ = place(pos)
    rows = w_query.shape[0]
    own = gains[...].astype(F32)
    own = jnp.concatenate([own, jnp.zeros((4, HEAD_DIM - rows), F32)], axis=1)
    length = jnp.full((1, HEAD_DIM), pos[4]).astype(F32)
    for (dx, dy), out in zip(SQUARE, outs):
        for i, weight in enumerate((w_query, w_key, w_value)):
            for head in range(NZ):
                start = column_of(x ^ dx, head, y ^ dy)
                at = i * HEADS + head * HEAD_DIM
                out[:rows, at : at + HEAD_DIM] = weight[:, pl.ds(start, HEAD_DIM)]
        put_extra(out, rows, extra_rows([own, length]))


def join_kernel(*refs):
    *parts, out, lengths = refs
    rows = parts[0].shape[0] - EXTRA
    extras = []
    for i, part in enumerate(parts):
        out[i * rows : (i + 1) * rows] = part[:rows]
        extras.append(part[rows:, :HEAD_DIM].astype(F32))
    put_extra(out, GROUP * rows, extra_rows([extra[:4] for extra in extras]))
    lengths[...] = jnp.concatenate(
        [extras[0][4:5], extras[1][4:5], jnp.zeros((6, HEAD_DIM), F32)], axis=0
    )


def row_stats(first, second):
    shape = (first.shape[0], HEAD_DIM)
    upper = lax.broadcasted_iota(jnp.int32, shape, 1) < 4
    sums = jnp.where(
        upper,
        jnp.sum(first, axis=1, keepdims=True),
        jnp.sum(second, axis=1, keepdims=True),
    )
    return jnp.transpose(sums)[:8]


def group_total(stats, tok):
    blocks = []
    for dx, dy in TOKEN_BLOCKS:
        total = 0.0
        for (sx, sy), ref in zip(SQUARE, stats):
            at = ((dy ^ sy) * NX + (dx ^ sx)) * tok
            total = total + ref[:, at : at + tok]
        blocks.append(total)
    return jnp.concatenate(blocks, axis=1)


def gather_kernel(*refs):
    blocks, (whole, kept, sem) = refs[:GROUP], refs[GROUP:]
    tok = blocks[0].shape[0]
    for i, block in enumerate(TOKEN_BLOCKS):
        whole[i * tok : (i + 1) * tok] = blocks[SQUARE.index(block)][...]
    copy = pltpu.make_async_copy(whole, kept, sem)
    copy.start()
    copy.wait()


def out_rows_kernel(nc, pos, *refs):
    *parts, out_w, kept, sem = refs
    _, r, _, c = place(pos)
    rows = parts[0].shape[0]
    for s in range(NZ):
        for k in range(nc):
            start = ring(r, s) * HEAD_DIM + (c ^ k) * rows
            out_w[pl.ds(pl.multiple_of(start, rows), rows)] = parts[s * nc + k][...]
    copy = pltpu.make_async_copy(out_w, kept, sem)
    copy.start()
    copy.wait()


def project_kernel(nc, s, pos, x_all, *refs):
    weights, refs = refs[:nc], refs[nc:]
    if s > 0:
        refs = refs[2:] if s < NZ - 1 else (refs[0], *refs[2:])
    x, r, y, c = place(pos)
    rows = (weights[0].shape[0] - EXTRA) // GROUP
    if s < NZ - 1:
        total, gains, w_rows, columns, w_part, sems = refs
    else:
        before, gains, w_rows, query, key, value, query_h, key_h, value_h, stats, *refs = refs
        total, columns, w_part, sems = refs
    z = ring(r, s)
    extras = [weight[GROUP * rows :, :HEAD_DIM].astype(F32) for weight in weights]
    lanes = []
    for place_c in range(nc):
        chosen = 0.0
        for k, part in enumerate(extras):
            chosen = chosen + jnp.where((c ^ k) == place_c, part[:, :rows], 0.0)
        lanes.append(chosen)
    ordered = jnp.concatenate(lanes, axis=1)
    for i, (dx, dy) in enumerate(SQUARE):
        start = column_of(x ^ dx, z, y ^ dy)
        gains[:, pl.ds(start, HEAD_DIM)] = jnp.concatenate(
            [ordered[4 * i : 4 * i + 4], jnp.zeros((4, HEAD_DIM), F32)], axis=0
        )
        columns[:, i * HEAD_DIM : (i + 1) * HEAD_DIM] = x_all[:, pl.ds(start, HEAD_DIM)]
        for k, weight in enumerate(weights):
            at = pl.multiple_of(i * HEAD_DIM + (c ^ k) * rows, rows)
            w_part[pl.ds(at, rows)] = weight[i * rows : (i + 1) * rows]
    copies = Copies(sems)
    put = [copies.start(w_part, w_rows)]
    step = HEADS // 2
    for part in range(6):
        at = slice(part * step, (part + 1) * step)
        result = nn(columns[...], w_part[:, at])
        if s == 0:
            total[:, at] = result
        elif s < NZ - 1:
            total[:, at] += result
        else:
            result = before[:, at] + result
            out = (query, key, value)[part // 2]
            out[:, (part % 2) * step : (part % 2 + 1) * step] = result.astype(out.dtype)
    if s == NZ - 1:
        stats[...] = row_stats(query[...] * query[...], key[...] * key[...])
        put += [
            copies.start(*pair)
            for pair in ((query, query_h), (key, key_h), (value, value_h))
        ]
    finish(put)


def turn(values, cosine, sine):
    return values * cosine + pltpu.roll(values, HEAD_DIM // 2, 1) * sine


def valid_keys(x, length, tok):
    shape = (NX * tok, NX * tok)
    queries = lax.broadcasted_iota(jnp.int32, shape, 0)
    keys = lax.broadcasted_iota(jnp.int32, shape, 1)

    def at(index):
        return jnp.where(index < tok, x * tok + index, (1 - x) * tok + index - tok)

    return (at(keys) <= at(queries)) & (at(keys).astype(F32) < length)


def softmax(query, key, valid):
    logits = jnp.where(valid, nt(query, key) * HEAD_DIM ** (-0.5), NEGATIVE)
    powers = jnp.exp(logits - jnp.max(logits, axis=1, keepdims=True))
    return powers / jnp.sum(powers, axis=1, keepdims=True)


def attend_kernel(pos, *refs):
    x, _, y, _ = place(pos)
    stats, refs = refs[:GROUP], refs[GROUP:]
    lengths, gains, cosine, sine, query, key, value, out_w, *refs = refs
    query_out, key_out, attended_out, scales, *refs = refs
    pieces, refs = refs[:GROUP], refs[GROUP:]
    query_r, key_r, attended, sems = refs
    copies = Copies(sems)
    tok = query.shape[0] // GROUP
    span = NX * tok
    width = out_w.shape[1]
    scale = lax.rsqrt(group_total(stats, tok) / width + EPSILON)
    scales[...] = scale
    for seq in range(NY):
        at = slice(seq * span, (seq + 1) * span)
        columns = jnp.transpose(scale[:, at])
        valid = valid_keys(x, lengths[seq : seq + 1, 0:1], tok)
        for head in range(NZ):
            lanes = slice(head * HEAD_DIM, (head + 1) * HEAD_DIM)
            gain = pl.ds(column_of(x, head, y), HEAD_DIM)
            for row, (raw, out) in enumerate(((query, query_r), (key, key_r))):
                normed = raw[at, lanes] * columns[:, 4 * row : 4 * row + 1]
                normed = normed * gains[row : row + 1, gain]
                out[at, lanes] = turn(normed, cosine[...], sine[...]).astype(BF16)
            chances = softmax(query_r[at, lanes], key_r[at, lanes], valid)
            attended[at, lanes] = nn(chances.astype(BF16), value[at, lanes]).astype(BF16)
    put = [
        copies.start(*pair)
        for pair in ((query_r, query_out), (key_r, key_out), (attended, attended_out))
    ]
    step = width // 4
    for part in range(4):
        columns = slice(part * step, (part + 1) * step)
        result = nn(attended[...], out_w[:, columns])
        for i, block in enumerate(TOKEN_BLOCKS):
            out = pieces[SQUARE.index(block)]
            out[:, columns] = result[i * tok : (i + 1) * tok].astype(out.dtype)
    finish(put)


def in_halves(values, x, out):
    half = out.shape[1] // NX
    for dx in range(NX):
        start = pl.multiple_of((x ^ dx) * half, half)
        out[:, dx * half : (dx + 1) * half] = values[:, pl.ds(start, half)].astype(out.dtype)


def sum_of(refs):
    total = refs[0][...].astype(F32)
    for ref in refs[1:]:
        total = total + ref[...].astype(F32)
    return total


def branch_kernel(pos, *refs):
    parts, refs = refs[:GROUP], refs[GROUP:]
    inputs, gains, branch_out, hidden_out, mlp_in = refs
    branch = sum_of(parts)
    branch_out[...] = branch
    scale = lax.rsqrt(jnp.mean(branch * branch, axis=1, keepdims=True) + EPSILON)
    hidden_out[...] = inputs[...].astype(F32) + branch * scale * gains[2:3, :]
    in_halves(hidden_out, pos[0], mlp_in)


def norm_back(values, gain, grad):
    scale = lax.rsqrt(jnp.mean(values * values, axis=1, keepdims=True) + EPSILON)
    normed = values * scale
    scaled = grad * gain
    mean = jnp.mean(scaled * normed, axis=1, keepdims=True)
    return scale * (scaled - normed * mean), jnp.sum(grad * normed, axis=0, keepdims=True)


def mlp_kernel(count, pos, *refs):
    parts, refs = refs[:count], refs[count:]
    hidden, gains, grad_output, output, grad_in, grad_gain, halves, mlp_out = refs
    halves[...] = sum_of(parts)
    in_halves(halves, pos[0], mlp_out)
    values = mlp_out[...]
    gain = gains[3:4, :]
    scale = lax.rsqrt(jnp.mean(values * values, axis=1, keepdims=True) + EPSILON)
    output[...] = (hidden[...] + values * scale * gain).astype(BF16)
    grad, by_gain = norm_back(values, gain, grad_output[...].astype(F32))
    halves[...] = grad
    in_halves(halves, pos[0], grad_in)
    grad_gain[...] = jnp.broadcast_to(by_gain, grad_gain.shape)


def branch_back_kernel(count, pos, *refs):
    parts, refs = refs[:count], refs[count:]
    branch, gains, grad_output, grad_hidden, grad_branch, grad_gain, halves, middle = refs
    halves[...] = sum_of(parts)
    in_halves(halves, pos[0], middle)
    total = grad_output[...].astype(F32) + middle[...]
    grad_hidden[...] = total
    grad, by_gain = norm_back(branch[...], gains[2:3, :], total)
    grad_branch[...] = grad.astype(BF16)
    grad_gain[...] = jnp.broadcast_to(by_gain, grad_gain.shape)


def out_back_kernel(nc, pos, *refs):
    blocks, refs = refs[:GROUP], refs[GROUP:]
    attended, branch_all, *outs, sums = refs
    _, r, _, c = place(pos)
    tok = blocks[0].shape[0]
    rows = outs[0].shape[0] // NZ
    for i, block in enumerate(TOKEN_BLOCKS):
        branch_all[i * tok : (i + 1) * tok] = blocks[SQUARE.index(block)][...]
    for s in range(NZ):
        start = pl.multiple_of(ring(r, s) * HEAD_DIM, HEAD_DIM)
        sums[...] = tn(attended[:, pl.ds(start, HEAD_DIM)], branch_all[...]).astype(BF16)
        for k in range(nc):
            at = pl.ds(pl.multiple_of((c ^ k) * rows, rows), rows)
            outs[k][s * rows : (s + 1) * rows] = sums[at, :]


def attend_back_kernel(pos, *refs):
    lengths, scales, gains, cosine, sine, branch_all, out_w, *refs = refs
    held, refs = refs[:5], refs[5:]
    query_out, key_out, grad_value, stats, head_gains, *refs = refs
    query_r, key_r, value, query, key, *refs = refs
    grad_query, grad_key, grad_att, sems = refs
    x, _, y, _ = place(pos)
    tok = branch_all.shape[0] // GROUP
    span = NX * tok
    copies = Copies(sems)
    later = [
        copies.start(*pair) for pair in zip(held, (query_r, key_r, value, query, key))
    ]
    for half in range(2):
        lanes = slice(half * (HEADS // 2), (half + 1) * (HEADS // 2))
        grad_att[:, lanes] = nt(branch_all[...], out_w[lanes, :]).astype(BF16)
    head_gains[...] = jnp.zeros_like(head_gains)
    finish(later)
    for seq in range(NY):
        at = slice(seq * span, (seq + 1) * span)
        columns = jnp.transpose(scales[:, at])
        valid = valid_keys(x, lengths[seq : seq + 1, 0:1], tok)
        for head in range(NZ):
            lanes = slice(head * HEAD_DIM, (head + 1) * HEAD_DIM)
            gain = pl.ds(column_of(x, head, y), HEAD_DIM)
            queries, keys, values = query_r[at, lanes], key_r[at, lanes], value[at, lanes]
            chances = softmax(queries, keys, valid)
            incoming = grad_att[at, lanes]
            grad_chances = nt(incoming, values)
            grad_value[at, lanes] = tn(chances.astype(BF16), incoming).astype(BF16)
            balance = jnp.sum(chances * grad_chances, axis=1, keepdims=True)
            grad_logits = (chances * (grad_chances - balance)).astype(BF16)
            by_query = nn(grad_logits, keys) * HEAD_DIM ** (-0.5)
            by_key = tn(grad_logits, queries) * HEAD_DIM ** (-0.5)
            for row, (grad, raw, out) in enumerate(
                ((by_query, query, grad_query), (by_key, key, grad_key))
            ):
                back = turn(grad.astype(BF16).astype(F32), cosine[...], -sine[...])
                normed = raw[at, lanes] * columns[:, 4 * row : 4 * row + 1]
                head_gains[row : row + 1, lanes] += jnp.sum(back * normed, axis=0, keepdims=True)
                out[at, lanes] = back * gains[row : row + 1, gain]
    query_out[...] = grad_query[...]
    key_out[...] = grad_key[...]
    stats[...] = row_stats(grad_query[...] * query[...], grad_key[...] * key[...])


def project_back_kernel(*refs):
    stats, refs = refs[:GROUP], refs[GROUP:]
    scales, grad_query, grad_key, grad_value, query, key, grads = refs
    tok = query.shape[0] // GROUP
    width = NX * NY * HEADS
    means = jnp.transpose(group_total(stats, tok) / width)
    columns = jnp.transpose(scales[...])
    for row, (grad, raw) in enumerate(((grad_query, query), (grad_key, key))):
        scale = columns[:, 4 * row : 4 * row + 1]
        mean = means[:, 4 * row : 4 * row + 1]
        result = scale * (grad[...] - raw[...] * (scale * scale * mean))
        grads[:, row * HEADS : (row + 1) * HEADS] = result.astype(BF16)
    grads[:, 2 * HEADS :] = grad_value[...]


def input_back_kernel(pos, grads, *refs):
    weights, refs = refs[:NZ], refs[NZ:]
    *pieces, results = refs
    x, r, y, _ = place(pos)
    tok = grads.shape[0] // GROUP
    for s, weight in enumerate(weights):
        for half in range(2):
            result = nt(grads[...], weight[half * HEADS // 2 : (half + 1) * HEADS // 2, :])
            results[:, half * HEADS // 2 : (half + 1) * HEADS // 2] = result.astype(BF16)
        for j, (dx, dy) in enumerate(SQUARE):
            start = column_of(x ^ dx, ring(r, s), y ^ dy)
            for i, block in enumerate(TOKEN_BLOCKS):
                out = pieces[SQUARE.index(block)]
                out[:, pl.ds(start, HEAD_DIM)] = results[
                    i * tok : (i + 1) * tok, j * HEAD_DIM : (j + 1) * HEAD_DIM
                ]


def weight_back_kernel(nc, places, pos, *refs):
    for i, s in enumerate(places):
        weight_back_part(nc, s, i, pos, *refs)


def weight_back_part(nc, s, slot, pos, x_all, grads, attn_gain, mlp_gain, head_gains, *refs):
    *outs, columns, sums = refs
    x, r, y, c = place(pos)
    rows = HEAD_DIM // nc
    base = slot * (GROUP * rows + EXTRA)
    z = ring(r, s)
    gains = []
    for i, (dx, dy) in enumerate(SQUARE):
        start = column_of(x ^ dx, z, y ^ dy)
        columns[:, i * HEAD_DIM : (i + 1) * HEAD_DIM] = x_all[:, pl.ds(start, HEAD_DIM)]
        if i == 0:
            heads = pl.ds(pl.multiple_of(z * HEAD_DIM, HEAD_DIM), HEAD_DIM)
            gains.append(head_gains[0:2, heads])
        else:
            gains.append(jnp.zeros((2, HEAD_DIM), F32))
        gains.append(attn_gain[0:1, pl.ds(start, HEAD_DIM)])
        gains.append(mlp_gain[0:1, pl.ds(start, HEAD_DIM)])
    gains = jnp.concatenate(gains, axis=0)
    step = grads.shape[1] // 3
    for part in range(3):
        lanes = slice(part * step, (part + 1) * step)
        sums[:, lanes] = tn(columns[...], grads[:, lanes]).astype(BF16)
    for k, out in enumerate(outs):
        for i in range(GROUP):
            start = pl.multiple_of(i * HEAD_DIM + (c ^ k) * rows, rows)
            out[base + i * rows : base + (i + 1) * rows] = sums[pl.ds(start, rows), :]
        chosen = 0.0
        for place_c in range(nc):
            part = gains[:, place_c * rows : (place_c + 1) * rows]
            chosen = chosen + jnp.where((c ^ k) == place_c, part, 0.0)
        chosen = jnp.concatenate([chosen, jnp.zeros((EXTRA, HEAD_DIM - rows), F32)], axis=1)
        put_extra(out, base + GROUP * rows, chosen)


def collect_kernel(count, *refs):
    parts, outs = refs[:count], refs[count:]
    rows = (parts[0].shape[0] - EXTRA) // GROUP

    def total(at, lanes=slice(None)):
        result = parts[0][at, lanes].astype(F32)
        for part in parts[1:]:
            result = result + part[at, lanes].astype(F32)
        return result

    extra = total(slice(GROUP * rows, GROUP * rows + EXTRA), slice(0, HEAD_DIM))
    for i, out in enumerate(outs):
        out[:rows] = total(slice(i * rows, (i + 1) * rows)).astype(BF16)
        put_extra(out, rows, extra_rows([extra[4 * i : 4 * i + 4]]))


def spread_kernel(pos, *refs):
    parts, (*outs, gains) = refs[:GROUP], refs[GROUP:]
    x, _, y, _ = place(pos)
    rows = parts[0].shape[0] - EXTRA
    total = 0.0
    for (dx, dy), part in zip(SQUARE, parts):
        total = total + part[rows:, :HEAD_DIM].astype(F32)
        for i, out in enumerate(outs):
            for head in range(NZ):
                start = column_of(x ^ dx, head, y ^ dy)
                at = i * HEADS + head * HEAD_DIM
                out[:, pl.ds(start, HEAD_DIM)] = part[:rows, at : at + HEAD_DIM].astype(F32)
    gains[...] = total[:8]


def mlp_forward_kernel(nc, *refs):
    blocks, refs = refs[:nc], refs[nc:]
    gates, ups, downs, refs = refs[:4], refs[4:8], refs[8:16], refs[16:]
    outs = refs[-(8 + nc + 1) :]
    products, by_gate, by_up, kept = outs[0:2], outs[2:4], outs[4:6], outs[6:8]
    sums, total = outs[8 : 8 + nc], outs[8 + nc]
    tok = blocks[0].shape[0]
    half = kept[0].shape[1]
    quarter = half // 2
    for k, block in enumerate(blocks):
        for dx in range(NX):
            kept[dx][k * tok : (k + 1) * tok] = block[:, dx * half : (dx + 1) * half]
    for dy in range(NY):

        def through(weights):
            return nn(kept[0][...], weights[dy][...]) + nn(kept[1][...], weights[NY + dy][...])

        gate, up = through(gates), through(ups)
        chance = 1.0 / (1.0 + jnp.exp(-gate))
        silu = gate * chance
        product = (silu * up).astype(BF16)
        products[dy][...] = product
        by_up[dy][...] = silu.astype(BF16)
        by_gate[dy][...] = (up * (chance + silu * (1.0 - chance))).astype(BF16)
        for i in range(4):
            lanes = slice(i * quarter, (i + 1) * quarter)
            part = nt(product, downs[i * NY + dy][...])
            if dy == 0:
                total[:, lanes] = part
            else:
                part = total[:, lanes] + part
                for k, out in enumerate(sums):
                    out[:, lanes] = part[k * tok : (k + 1) * tok].astype(out.dtype)


def mlp_back_kernel(nc, *refs):
    blocks, refs = refs[:nc], refs[nc:]
    gates, ups, downs, refs = refs[:4], refs[4:8], refs[8:16], refs[16:]
    by_gate, by_up = refs[0:2], refs[2:4]
    outs = refs[-(8 + nc + 1) :]
    grad_gates, grad_ups, kept = outs[0:2], outs[2:4], outs[4:8]
    sums, total = outs[8 : 8 + nc], outs[8 + nc]
    tok = blocks[0].shape[0]
    quarter = kept[0].shape[1]
    for k, block in enumerate(blocks):
        for i in range(4):
            kept[i][k * tok : (k + 1) * tok] = block[:, i * quarter : (i + 1) * quarter]
    for dy in range(NY):
        grad = nn(kept[0][...], downs[dy][...])
        for i in range(1, 4):
            grad = grad + nn(kept[i][...], downs[i * NY + dy][...])
        grad_gate = (grad * by_gate[dy][...].astype(F32)).astype(BF16)
        grad_up = (grad * by_up[dy][...].astype(F32)).astype(BF16)
        grad_gates[dy][...] = grad_gate
        grad_ups[dy][...] = grad_up
        for i in range(4):
            lanes = slice(i * quarter, (i + 1) * quarter)
            dx, rows = i // 2, slice((i % 2) * quarter, (i % 2 + 1) * quarter)
            part = nt(grad_gate, gates[dx * NY + dy][rows, :]) + nt(
                grad_up, ups[dx * NY + dy][rows, :]
            )
            if dy == 0:
                total[:, lanes] = part
            else:
                part = total[:, lanes] + part
                for k, out in enumerate(sums):
                    out[:, lanes] = part[k * tok : (k + 1) * tok].astype(out.dtype)


def make_body(wide):
    nc = wide // (NY * NZ)

    def send(value, x=0, y=0, r=0, c=0):
        pairs = []
        for sx in range(NX):
            for sz in range(NZ):
                for sy in range(NY):
                    for sc in range(nc):
                        source = sx * wide + (sz * NY + sy) * nc + sc
                        target = (sx ^ x) * wide
                        target += (ring(gray(sz), r) * NY + (sy ^ y)) * nc + (sc ^ c)
                        pairs.append((source, target))
        return lax.ppermute(value, AXES, pairs)

    def square(parts):
        return [
            part if (dx, dy) == (0, 0) else send(part, x=dx, y=dy)
            for (dx, dy), part in zip(SQUARE, parts)
        ]

    def square_gather(first, second):
        first_x = send(first, x=1)
        second_y = send(second, y=1)
        first_y = send(first, y=1)
        second_x = send(second, x=1)
        first_xy = send(first_x, y=1)
        second_xy = send(second_y, x=1)
        return [first, first_y, first_x, first_xy], [second, second_y, second_x, second_xy]

    def scatter_far(first, second):
        return send(first[3], x=1), send(second[3], y=1)

    def scatter_near(first, second):
        return send(first[2], x=1), send(second[1], y=1)

    def scatter_rest(first, second, far, near):
        first_c = send((first[1].astype(F32) + far[0].astype(F32)).astype(BF16), y=1)
        second_c = send((second[2].astype(F32) + far[1].astype(F32)).astype(BF16), x=1)
        return (
            first[0].astype(F32) + near[0].astype(F32) + first_c.astype(F32),
            second[0].astype(F32) + near[1].astype(F32) + second_c.astype(F32),
        )

    def ring_gather(block):
        blocks = [block]
        for _ in range(NZ - 1):
            blocks.append(send(blocks[-1], r=-1))
        return blocks

    def core_gather(block):
        return [block] + [send(block, c=k) for k in range(1, nc)]

    def core_parts(parts):
        return [parts[0]] + [send(parts[k], c=k) for k in range(1, nc)]

    def ring_parts(part_of, hold=None):
        moving, sent = [], []
        for s in list(range(1, NZ)) + [0]:
            parts = part_of(s)
            if moving and hold is not None:
                moving = [after(moving[0], hold(s))]
            parts = parts + moving
            if s == 0:
                return parts, sent
            total = parts[0].astype(F32)
            for part in parts[1:]:
                total = total + part.astype(F32)
            sent.append(total.astype(BF16))
            moving = [send(sent[-1], r=-1)]

    def body(
        layer_input,
        lengths,
        w_query,
        w_key,
        w_value,
        w_output,
        query_gain,
        key_gain,
        attn_gain,
        mlp_gain,
        w_gate,
        w_up,
        w_down,
        grad_output,
    ):
        x = lax.axis_index("blk")
        spot = lax.axis_index("wide")
        z, y, c = spot // (NY * nc), (spot // nc) % NY, spot % nc
        inputs, grad_out = layer_input[0], grad_output[0]
        tok, width = inputs.shape
        rows = w_query.shape[0]
        group_tok = GROUP * tok
        hidden = w_gate.shape[1]
        pos = jnp.stack([x, gray(z), y, c, lengths[0]]).astype(jnp.int32)
        wide_small = shaped((8, width), F32)
        by_head = shaped((group_tok, HEADS))
        by_head_wide = shaped((group_tok, HEADS), F32)
        by_token = shaped((8, group_tok), F32)
        tokens_shape = shaped((tok, width))
        tokens_wide = shaped((tok, width), F32)
        message = shaped((GROUP * rows + EXTRA, 3 * HEADS))
        piece = shaped((rows + EXTRA, 3 * HEADS))

        def dma(count):
            return pltpu.SemaphoreType.DMA((count,))

        def held(shape):
            return pltpu.VMEM(shape.shape, shape.dtype)

        gains = jnp.stack([query_gain, key_gain, attn_gain, mlp_gain])
        pieces = run(
            split_kernel,
            each([piece] * GROUP, VMEM),
            [(pos, SMEM), (gains, VMEM), (w_query, auto), (w_key, auto), (w_value, auto)],
        )
        out_ring = [w_output, send(after(w_output, pieces), r=-1)]
        down_rows = w_down.shape[0] // 2
        down_halves = after(w_down, pieces)
        down_halves = down_halves[:down_rows], down_halves[down_rows:]
        far_down = send(down_halves[0], x=1), send(down_halves[1], y=1)
        received = square(pieces)
        own_rows, lengths_row = run(
            join_kernel,
            [(message, VMEM), (shaped((8, HEAD_DIM), F32), VMEM)],
            each(received, VMEM),
        )
        half = HEAD_DIM // 2
        order = jnp.concatenate([x * tok + jnp.arange(tok), (1 - x) * tok + jnp.arange(tok)])
        frequency = jnp.exp(
            jnp.arange(half, dtype=F32) * (-2.0 * math.log(500000.0) / HEAD_DIM)
        )
        angles = order.astype(F32)[:, None] * frequency[None, :]
        cosine = jnp.tile(jnp.cos(angles), (1, 2))
        sine = jnp.sin(angles)
        sine = jnp.concatenate([-sine, sine], axis=1)
        tokens = square([after(inputs, own_rows)] * GROUP)
        w_ring = [own_rows, send(own_rows, r=-1)]
        out_ring.append(send(out_ring[1], r=-1))
        ready = cosine, sine, far_down, out_ring[2], tokens[1], tokens[2]
        w_ring.append(send(after(w_ring[1], ready), r=-1))
        x_all, x_kept = run(
            gather_kernel,
            [(shaped((group_tok, width)), VMEM), (shaped((group_tok, width)), HBM)],
            each(tokens, VMEM),
            scratch_shapes=[pltpu.SemaphoreType.DMA],
        )
        far_gate = send(after(w_gate, x_all), x=1)
        far_up = send(after(w_up, x_all), y=1)
        near_gate = send(after(w_gate, far_gate), y=1)
        near_up = send(after(w_up, far_up), x=1)
        total, gains = None, None
        totals = []
        w_parts = []
        w_shape = shaped((GROUP * HEAD_DIM, 3 * HEADS))
        for s in range(NZ):
            if s == NZ - 1:
                w_ring.append(send(after(w_ring[2], totals[1]), r=-1))
                out_ring.append(send(after(out_ring[2], w_ring[3]), r=-1))
            blocks = core_gather(w_ring[s])
            ins = [(pos, SMEM), (x_all, VMEM), *each(blocks, VMEM)]
            outs = [(wide_small, VMEM), (w_shape, HBM)]
            aliases = {}
            if s > 0:
                if s == NZ - 1:
                    total, gains = after((total, gains), far_gate, far_up)
                aliases = {len(ins) + 1: 1 if s < NZ - 1 else 0}
                ins += [(total, VMEM), (gains, VMEM)]
            if s < NZ - 1:
                outs = [(shaped((group_tok, 3 * HEADS), F32), VMEM)] + outs
                if s > 0:
                    aliases[len(ins) - 2] = 0
            else:
                outs += [(by_head_wide, VMEM), (by_head_wide, VMEM), (by_head, VMEM)]
                outs += [(by_head_wide, HBM), (by_head_wide, HBM), (by_head, HBM)]
                outs += [(by_token, VMEM)]
            results = run(
                functools.partial(project_kernel, nc, s),
                outs,
                ins,
                input_output_aliases=aliases,
                scratch_shapes=([pltpu.VMEM((8, HEAD_DIM), F32)] if s == NZ - 1 else [])
                + [
                    pltpu.VMEM((group_tok, GROUP * HEAD_DIM), BF16),
                    pltpu.VMEM((GROUP * HEAD_DIM, 3 * HEADS), BF16),
                    dma(4),
                ],
            )
            if s < NZ - 1:
                total, gains, w_part = results
                totals.append(total)
            else:
                gains, w_part, query, key, value, query_h, key_h, value_h, stats = results
            w_parts.append(w_part)
        out_w, out_kept = run(
            functools.partial(out_rows_kernel, nc),
            [(shaped((HEADS, width)), VMEM), (shaped((HEADS, width)), HBM)],
            [
                (pos, SMEM),
                *each([part for block in out_ring for part in core_gather(block)], VMEM),
            ],
            scratch_shapes=[pltpu.SemaphoreType.DMA],
        )
        group_stats = square([stats] * GROUP)
        last_gate = send(after(far_gate, group_stats), y=1)
        last_up = send(after(far_up, group_stats), x=1)
        gate_w = [w_gate, near_gate, far_gate, last_gate]
        up_w = [w_up, far_up, near_up, last_up]

        query_r, key_r, attended, scales, *parts = run(
            attend_kernel,
            [(by_head, HBM)] * 3 + [(by_token, VMEM)] + [(tokens_shape, VMEM)] * GROUP,
            [
                (pos, SMEM),
                *each(group_stats, VMEM),
                *each((lengths_row, gains, cosine, sine), VMEM),
                *each((query, key, value, out_w), VMEM),
            ],
            scratch_shapes=[held(by_head), held(by_head), held(by_head), dma(3)],
        )
        parts = square(after(parts, gate_w, up_w))
        first, second = after(down_halves, parts)
        first_x, second_y = after(far_down, parts)
        down_first = first, send(first, y=1), first_x, send(first_x, y=1)
        down_second = second, second_y, send(second, x=1), send(second_y, x=1)
        down_w = [
            half[dx * NY + dy]
            for dx in range(NX)
            for half in (down_first, down_second)
            for dy in range(NY)
        ]
        branch, hidden_state, mlp_in = run(
            branch_kernel,
            [(tokens_wide, auto), (tokens_wide, auto), (tokens_shape, VMEM)],
            [(pos, SMEM), *each(parts, auto), (inputs, auto), (gains, VMEM)],
        )

        half_width = width // NX
        quarter = half_width // 2
        m = nc * tok

        def mlp_call(kernel, s, block, extra, kept_columns, before):
            def rows_of(array):
                return pl.BlockSpec((m, array.shape[1]), lambda i: (s, 0))

            ins = each(core_gather(block), auto)
            ins += each((*gate_w, *up_w, *down_w), VMEM) + each(extra, rows_of)
            columns = [hidden] * (8 - len(kept_columns)) + list(kept_columns)
            outs = each([shaped((NZ * m, count)) for count in columns], rows_of)
            outs += [(tokens_wide, VMEM)] + [(tokens_shape, VMEM)] * (nc - 1)
            aliases = {}
            if before is not None:
                aliases = {len(ins) + i: i for i in range(8)}
                ins += each(before, HBM)
            results = run(
                functools.partial(kernel, nc),
                outs,
                ins,
                limit=20 if nc == 2 else 56,
                input_output_aliases=aliases,
                scratch_shapes=[pltpu.VMEM((m, width), F32)],
            )
            return results[:8], core_parts(results[8:])

        kept = None
        sums = []
        for s, block in enumerate(ring_gather(mlp_in)):
            kept, parts = mlp_call(
                mlp_forward_kernel, s, block, (), (half_width, half_width), kept
            )
            sums.append(parts)

        def hold(s):
            return sums[(s + 1) % NZ][0]

        products, by_gate, by_up, mlp_all = kept[0:2], kept[2:4], kept[4:6], kept[6:8]
        parts, _ = ring_parts(lambda s: sums[s], hold)
        output, grad_mlp, grad_gain_mlp = run(
            functools.partial(mlp_kernel, len(parts)),
            [(tokens_shape, auto), (tokens_shape, VMEM), (wide_small, VMEM)],
            [
                (pos, SMEM),
                *each(parts, auto),
                (hidden_state, auto),
                (gains, VMEM),
                (grad_out, auto),
            ],
            scratch_shapes=[held(tokens_wide)] * 2,
        )
        kept = None
        sums = []
        for s, block in enumerate(ring_gather(grad_mlp)):
            kept, parts = mlp_call(
                mlp_back_kernel, s, block, (*by_gate, *by_up), (quarter,) * 4, kept
            )
            sums.append(parts)
        grad_gates, grad_ups, grad_all = kept[0:2], kept[2:4], kept[4:8]
        parts, sent = ring_parts(lambda s: sums[s], hold)
        grad_hidden, grad_branch, grad_gain_attn = run(
            functools.partial(branch_back_kernel, len(parts)),
            [(tokens_wide, auto), (tokens_shape, VMEM), (wide_small, VMEM)],
            [
                (pos, SMEM),
                *each(parts, auto),
                (branch, auto),
                (gains, VMEM),
                (grad_out, auto),
            ],
            scratch_shapes=[held(tokens_wide)] * 2,
        )

        def products_of(left, right):
            return [tn(left[dx], right[dy]).astype(BF16) for dx, dy in SQUARE]

        grad_all = after(grad_all, sent[1])
        wd_pair = products_of(grad_all[0::2], products), products_of(grad_all[1::2], products)
        wd_far = scatter_far(*wd_pair)
        wd_near = scatter_near(*after(wd_pair, wd_far))
        grad_branch = after(grad_branch, wd_far)
        grad_wd = jnp.concatenate(scatter_rest(*wd_pair, wd_far, wd_near), axis=0)
        mlp_all = after(mlp_all, sent[2])
        grad_wg = products_of(mlp_all, grad_gates)
        grad_wu = products_of(mlp_all, grad_ups)

        blocks = square([grad_branch] * GROUP)
        w_pair = after((grad_wg, grad_wu), blocks)
        w_far = scatter_far(*w_pair)
        branch_all, *picked = run(
            functools.partial(out_back_kernel, nc),
            [(shaped((group_tok, width)), VMEM)] + [(shaped((NZ * rows, width)), VMEM)] * nc,
            [(pos, SMEM), *each(blocks, VMEM), (attended, VMEM)],
            scratch_shapes=[pltpu.VMEM((HEAD_DIM, width), BF16)],
        )
        picked = core_parts(picked)

        def out_part(s):
            return [part[s * rows : (s + 1) * rows] for part in picked]

        def summed(parts):
            total = parts[0].astype(F32)
            for part in parts[1:]:
                total = total + part.astype(F32)
            return total

        out_moving = send(summed(out_part(1)).astype(BF16), r=-1)
        branch_all = after(branch_all, w_pair)
        grad_query, grad_key, grad_value, stats, head_gains = run(
            attend_back_kernel,
            [
                (by_head_wide, VMEM),
                (by_head_wide, VMEM),
                (by_head, VMEM),
                (by_token, VMEM),
                (shaped((8, HEADS), F32), VMEM),
            ],
            [
                (pos, SMEM),
                *each((lengths_row, scales, gains, cosine, sine, branch_all, out_kept), VMEM),
                *each((query_r, key_r, value_h, query_h, key_h), HBM),
            ],
            limit=16,
            scratch_shapes=[
                held(by_head),
                held(by_head),
                held(by_head),
                held(by_head_wide),
                held(by_head_wide),
                held(by_head_wide),
                held(by_head_wide),
                held(by_head),
                dma(5),
            ],
        )
        (grads,) = run(
            project_back_kernel,
            [(shaped((group_tok, 3 * HEADS)), VMEM)],
            [
                *each(square([stats] * GROUP), VMEM),
                (scales, VMEM),
                *each((grad_query, grad_key, grad_value, query_h, key_h), VMEM),
            ],
        )
        grads = after(grads, out_moving)
        w_near = scatter_near(*after(w_pair, grads))

        def weight_parts(places):
            height = message.shape[0]
            results = run(
                functools.partial(weight_back_kernel, nc, places),
                [(shaped((len(places) * height, 3 * HEADS)), VMEM)] * nc,
                [
                    (pos, SMEM),
                    (x_kept, VMEM),
                    *each((grads, grad_gain_attn, grad_gain_mlp, head_gains), VMEM),
                ],
                scratch_shapes=[
                    pltpu.VMEM((group_tok, GROUP * HEAD_DIM), BF16),
                    pltpu.VMEM((GROUP * HEAD_DIM, 3 * HEADS), BF16),
                ],
            )
            results = core_parts(results)
            return [
                [part[i * height : (i + 1) * height] for part in results]
                for i in range(len(places))
            ]

        (first,) = weight_parts((1,))
        out_second = summed(out_part(2) + [out_moving]).astype(BF16)
        w_moving = send(after(summed(first).astype(BF16), w_far, out_second), r=-1)
        out_moving = send(out_second, r=-1)
        second, third, own = weight_parts((2, 3, 0))
        out_third = summed(out_part(3) + [out_moving]).astype(BF16)
        sent = summed(second + [w_moving]).astype(BF16)
        w_moving = send(after(sent, own, out_third, w_near), r=-1)
        out_moving = send(out_third, r=-1)
        grad_wg, grad_wu = scatter_rest(*w_pair, *after((w_far, w_near), sent))
        sent = summed(third + [w_moving]).astype(BF16)
        w_moving = send(sent, r=-1)
        parts = own + [w_moving]
        messages = run(
            functools.partial(collect_kernel, len(parts)),
            [(piece, VMEM)] * GROUP,
            each(parts, auto),
        )
        grad_wq, grad_wk, grad_wv, total_gains = run(
            spread_kernel,
            [(shaped((rows, width), F32), auto)] * 3 + [(shaped((8, HEAD_DIM), F32), VMEM)],
            [(pos, SMEM), *each(square(messages), auto)],
        )
        grad_wo = summed(out_part(0) + [out_moving])

        parts = run(
            input_back_kernel,
            [(tokens_shape, VMEM)] * GROUP,
            [(pos, SMEM), (after(grads, sent), VMEM), *each(w_parts, VMEM)],
            scratch_shapes=[pltpu.VMEM((group_tok, GROUP * HEAD_DIM), BF16)],
        )
        grad_x = summed([grad_hidden, *square(parts)])

        return (
            output[None],
            grad_x.astype(BF16)[None],
            grad_wq,
            grad_wk,
            grad_wv,
            grad_wo,
            total_gains[0, :rows],
            total_gains[1, :rows],
            total_gains[2, :rows],
            total_gains[3, :rows],
            grad_wg,
            grad_wu,
            grad_wd,
        )

    return body


def solution(mesh):
    return jax.shard_map(
        make_body(mesh.shape["wide"]),
        mesh=mesh,
        in_specs=(
            P("wide", "blk", None),
            P("wide"),
            P(("blk", "wide"), None),
            P(("blk", "wide"), None),
            P(("blk", "wide"), None),
            P(("blk", "wide"), None),
            P(("blk", "wide")),
            P(("blk", "wide")),
            P(("blk", "wide")),
            P(("blk", "wide")),
            P("blk", "wide"),
            P("blk", "wide"),
            P("blk", "wide"),
            P("wide", "blk", None),
        ),
        out_specs=(
            P("wide", "blk", None),
            P("wide", "blk", None),
            P(("blk", "wide"), None),
            P(("blk", "wide"), None),
            P(("blk", "wide"), None),
            P(("blk", "wide"), None),
            P(("blk", "wide")),
            P(("blk", "wide")),
            P(("blk", "wide")),
            P(("blk", "wide")),
            P("blk", "wide"),
            P("blk", "wide"),
            P("blk", "wide"),
        ),
        check_vma=False,
    )
```

time: 729 us -> 567 us (0.78)
  Pallas kernels: 162 us -> 97 us
  starting transfers between devices: 137 us -> 97.3 us
  waiting for transfers between devices: 343 us -> 312 us
  local copies, waits for them, and re-layouts: 40.8 us -> 22.6 us
    pallas_call x26 -> x28, Pallas kernels: 162 us -> 97 us  [run(): pl.pallas_call(body, grid=(1,), out_shape=[out for out, _ in outs], out_s...]
    ppermute x119 -> x99, starting transfers between devices: 137 us -> 97.3 us  [send(): return lax.ppermute(value, AXES, pairs)]
    ppermute x119 -> x99, waiting for transfers between devices: 343 us -> 312 us  [send(): return lax.ppermute(value, AXES, pairs)]
    unnamed x194 -> x100, local copies, waits for them, and re-layouts: 34.5 us -> 19.2 us
    convert_element_type x17 -> x14, other arithmetic: 10.1 us -> 2.67 us  [the longest x6 0.95 us: ring_parts(): sent.append(total.astype(BF16))]
    dot_general x17 -> x16, matrix products: 21 us -> 16.1 us  [tn(): lax.dot_general(left, right, (((0,), (0,)), ((), ())), preferred_element_...]
  transfers between devices with their start and end apart: 119 -> 99, of which waited for: 39 -> 48; matrix products, arithmetic and copies ran while one was open for 6% -> 6% of each run, Pallas kernels for 22% -> 15%
where the time goes in v3:
time: 567 us; the launch traced here: 561 us
  waiting for transfers between devices  312 us (55%)
  starting transfers between devices  97.3 us (17%)
  Pallas kernels  97 us (17%)
  local copies, waits for them, and re-layouts  22.6 us (4%)
  matrix products  16.1 us (3%)
  other arithmetic  13.2 us (2%)
    ppermute x99, waiting for transfers between devices, send(): return lax.ppermute(value, AXES, pairs)  312 us
    ppermute x99, starting transfers between devices, send(): return lax.ppermute(value, AXES, pairs)  97.3 us
    pallas_call x28, Pallas kernels, run(): pl.pallas_call(body, grid=(1,), out_shape=[out for out, _ in outs], out_s...  97 us
    unnamed x100, local copies, waits for them, and re-layouts  19.2 us
    dot_general x16, matrix products, tn(): lax.dot_general(left, right, (((0,), (0,)), ((), ())), preferred_element_...  16.1 us
  transfers between devices with their start and end apart: 99, of which 48 were waited for; matrix products, arithmetic and copies ran while one was open for 6% of the time, Pallas kernels for 15%

profile of v3, /device:TPU:0, one launch (start us, length us, event | category | flops | bytes accessed | tf_op | source)
XLA Modules:
  0.0 560.7 jit_solution(6033497581046316005)
XLA Ops:
  5.8 4.1 collective-permute-start.9
  13.4 4.5 collective-permute-done.refs_1_
  17.9 2.4 collective-permute-done.1.refs_2_
  20.3 3.4 collective-permute-done.2.refs_3_
  30.4 19.1 %collective-permute-done.10.refs_4_ = bf16[64,2048]{1,0:T(8,128)(2,1)} collective-permute-done((bf16[64,2048]{1,0:T(8,128)(2,1)S(1)}, bf16[64,2048]{1,0:T(8,128)(2,1)}, u32[]{:S(2)}, u32[]{:S(2)}) %collective-permute-start.10) | collective-permute-done | bytes 262176 | tf_op jit(solution)/shard_map/ppermute | solution.py:605
  55.0 5.8 %collective-permute-done.3.refs_1_ = bf16[128,2048]{1,0:T(8,128)(2,1)} collective-permute-done((bf16[128,2048]{1,0:T(8,128)(2,1)S(1)}, bf16[128,2048]{1,0:T(8,128)(2,1)}, u32[]{:S(2)}, u32[]{:S(2)}) %collective-permute-start.3) | collective-permute-done | bytes 524320 | tf_op jit(solution)/shard_map/ppermute | solution.py:605
  61.5 2.5 collective-permute-start.11
  64.0 2.4 collective-permute-start.5
  66.4 8.5 %collective-permute-done.5.refs_3_ = bf16[128,2048]{1,0:T(8,128)(2,1)S(1)} collective-permute-done((bf16[128,2048]{1,0:T(8,128)(2,1)S(1)}, bf16[128,2048]{1,0:T(8,128)(2,1)S(1)}, u32[]{:S(2)}, u32[]{:S(2)}) %collective-permute-start.5) | collective-permute-done | bytes 524320 | tf_op jit(solution)/shard_map/ppermute | solution.py:605
  77.6 2.5 shard_map.240
  80.3 3.2 shard_map.241
  86.8 12.5 %collective-permute-done.14.refs_0_ = bf16[272,1536]{1,0:T(8,128)(2,1)S(1)} collective-permute-done((bf16[272,1536]{1,0:T(8,128)(2,1)S(1)}, bf16[272,1536]{1,0:T(8,128)(2,1)S(1)}, u32[]{:S(2)}, u32[]{:S(2)}) %collective-permute-start.14) | collective-permute-done | bytes 835616 | tf_op jit(solution)/shard_map/ppermute | solution.py:605
  99.9 2.0 shard_map.242
  101.8 2.4 collective-permute-done.17.refs_4_
  105.5 2.2 shard_map.243
  127.5 8.2 %collective-permute-done.25.refs_6_ = bf16[64,2048]{1,0:T(8,128)(2,1)} collective-permute-done((bf16[64,2048]{1,0:T(8,128)(2,1)}, bf16[64,2048]{1,0:T(8,128)(2,1)}, u32[]{:S(2)}, u32[]{:S(2)}) %collective-permute-start.25) | collective-permute-done | bytes 262176 | tf_op jit(solution)/shard_map/ppermute | solution.py:605
  144.9 6.1 %shard_map.245 = (bf16[512,512]{1,0:T(8,128)(2,1)S(1)}, bf16[512,512]{1,0:T(8,128)(2,1)S(1)}, bf16[512,512]{1,0:T(8,128)(2,1)S(1)}, f32[8,512]{1,0:T(8,128)S(1)}...) custom-call(s32[5]{0:T(128)S(1)} %stack.34.pos, ...), custom_call_target="tpu_custom_call" | custom-call | tf_op jit(solution)/shard_map/pallas_call | solution.py:50
  151.1 15.0 %collective-permute-done.28.refs_5_ = bf16[1024,512]{1,0:T(8,128)(2,1)} collective-permute-done((bf16[1024,512]{1,0:T(8,128)(2,1)S(1)}, bf16[1024,512]{1,0:T(8,128)(2,1)}, u32[]{:S(2)}, u32[]{:S(2)}) %collective-permute-start.28) | collective-permute-done | bytes 1048608 | tf_op jit(solution)/shard_map/ppermute | solution.py:605
  168.3 2.4 collective-permute-start.33
  170.7 10.5 %collective-permute-done.31.refs_1_ = bf16[128,2048]{1,0:T(8,128)(2,1)S(1)} collective-permute-done((bf16[128,2048]{1,0:T(8,128)(2,1)S(1)}, bf16[128,2048]{1,0:T(8,128)(2,1)S(1)}, u32[]{:S(2)}, u32[]{:S(2)}) %collective-permute-start.31) | collective-permute-done | bytes 524320 | tf_op jit(solution)/shard_map/ppermute | solution.py:605
  182.7 9.0 %collective-permute-done.33.refs_3_ = bf16[128,2048]{1,0:T(8,128)(2,1)S(1)} collective-permute-done((bf16[128,2048]{1,0:T(8,128)(2,1)S(1)}, bf16[128,2048]{1,0:T(8,128)(2,1)S(1)}, u32[]{:S(2)}, u32[]{:S(2)}) %collective-permute-start.33) | collective-permute-done | bytes 524320 | tf_op jit(solution)/shard_map/ppermute | solution.py:605
  197.4 9.2 %collective-permute-done.35.refs_11_ = bf16[512,512]{1,0:T(8,128)(2,1)S(1)} collective-permute-done((bf16[512,512]{1,0:T(8,128)(2,1)S(1)}, bf16[512,512]{1,0:T(8,128)(2,1)S(1)}, u32[]{:S(2)}, u32[]{:S(2)}) %collective-permute-start.35) | collective-permute-done | bytes 524320 | tf_op jit(solution)/shard_map/ppermute | solution.py:605
  207.0 1.8 collective-permute-done.37.refs_16_
  208.8 6.6 %collective-permute-done.38.refs_17_ = bf16[512,512]{1,0:T(8,128)(2,1)S(1)} collective-permute-done((bf16[512,512]{1,0:T(8,128)(2,1)S(1)}, bf16[512,512]{1,0:T(8,128)(2,1)S(1)}, u32[]{:S(2)}, u32[]{:S(2)}) %collective-permute-start.38) | collective-permute-done | bytes 524320 | tf_op jit(solution)/shard_map/ppermute | solution.py:605
  215.3 6.1 %shard_map.247 = (bf16[1024,512]{1,0:T(8,128)(2,1)S(1)}, bf16[1024,512]{1,0:T(8,128)(2,1)S(1)}, bf16[1024,512]{1,0:T(8,128)(2,1)S(1)}, bf16[1024,512]{1,0:T(8,12...) custom-call(bf16[128,2048]{1,0:T(8,128)(2,1)S(1)} %get-tuple-element, ...), custom_call_target="tpu_custom_call" | custom-call | tf_op jit(solution)/shard_map/pallas_call | solution.py:50
  221.5 1.8 collective-permute-start.42
  223.3 6.1 %shard_map.248 = (bf16[1024,512]{1,0:T(8,128)(2,1)S(1)}, bf16[1024,512]{1,0:T(8,128)(2,1)S(1)}, bf16[1024,512]{1,0:T(8,128)(2,1)S(1)}, bf16[1024,512]{1,0:T(8,12...) custom-call(bf16[128,2048]{1,0:T(8,128)(2,1)S(1)} %collective-permut, ...), custom_call_target="tpu_custom_call", output_to_operand_aliasing={{0}: (18, {}), {1}: (19, {}), {2}: (20, {}), {3}: (21, {}),... | custom-call | tf_op jit(solution)/shard_map/pallas_call | solution.py:50
  230.0 5.3 collective-permute-done.42.refs_0_
  237.0 6.1 %shard_map.249 = (bf16[1024,512]{1,0:T(8,128)(2,1)S(1)}, bf16[1024,512]{1,0:T(8,128)(2,1)S(1)}, bf16[1024,512]{1,0:T(8,128)(2,1)S(1)}, bf16[1024,512]{1,0:T(8,12...) custom-call(bf16[128,2048]{1,0:T(8,128)(2,1)S(1)} %collective-permut, ...), custom_call_target="tpu_custom_call", output_to_operand_aliasing={{0}: (18, {}), {1}: (19, {}), {2}: (20, {}), {3}: (21, {}),... | custom-call | tf_op jit(solution)/shard_map/pallas_call | solution.py:50
  243.4 6.1 %shard_map.250 = (bf16[1024,512]{1,0:T(8,128)(2,1)S(1)}, bf16[1024,512]{1,0:T(8,128)(2,1)S(1)}, bf16[1024,512]{1,0:T(8,128)(2,1)S(1)}, bf16[1024,512]{1,0:T(8,12...) custom-call(bf16[128,2048]{1,0:T(8,128)(2,1)S(1)} %collective-permut, ...), custom_call_target="tpu_custom_call", output_to_operand_aliasing={{0}: (18, {}), {1}: (19, {}), {2}: (20, {}), {3}: (21, {}),... | custom-call | tf_op jit(solution)/shard_map/pallas_call | solution.py:50
  252.5 12.9 %collective-permute-done.50 = bf16[128,2048]{1,0:T(8,128)(2,1)S(1)} collective-permute-done((bf16[128,2048]{1,0:T(8,128)(2,1)S(1)}, bf16[128,2048]{1,0:T(8,128)(2,1)S(1)}, u32[]{:S(2)}, u32[]{:S(2)}) %collective-permute-start.50) | collective-permute-done | bytes 524320 | tf_op jit(solution)/shard_map/ppermute | solution.py:605
  267.2 12.0 %collective-permute-done.51.refs_2_ = bf16[128,2048]{1,0:T(8,128)(2,1)S(1)} collective-permute-done((bf16[128,2048]{1,0:T(8,128)(2,1)S(1)}, bf16[128,2048]{1,0:T(8,128)(2,1)S(1)}, u32[]{:S(2)}, u32[]{:S(2)}) %collective-permute-start.51) | collective-permute-done | bytes 524320 | tf_op jit(solution)/shard_map/ppermute | solution.py:605
  279.2 2.1 shard_map.251
  282.8 11.1 %collective-permute-done.54.refs_0_ = bf16[128,2048]{1,0:T(8,128)(2,1)S(1)} collective-permute-done((bf16[128,2048]{1,0:T(8,128)(2,1)S(1)}, bf16[128,2048]{1,0:T(8,128)(2,1)S(1)}, u32[]{:S(2)}, u32[]{:S(2)}) %collective-permute-start.54) | collective-permute-done | bytes 524320 | tf_op jit(solution)/shard_map/ppermute | solution.py:605
  293.9 2.0 collective-permute-start.55
  295.9 6.1 %shard_map.252 = (bf16[1024,512]{1,0:T(8,128)(2,1)S(1)}, bf16[1024,512]{1,0:T(8,128)(2,1)S(1)}, bf16[1024,512]{1,0:T(8,128)(2,1)S(1)}, bf16[1024,512]{1,0:T(8,12...) custom-call(bf16[128,2048]{1,0:T(8,128)(2,1)S(1)} %get-tuple-element, ...), custom_call_target="tpu_custom_call" | custom-call | tf_op jit(solution)/shard_map/pallas_call | solution.py:50
  302.0 4.4 collective-permute-done.55.refs_0_
  307.9 6.1 %shard_map.253 = (bf16[1024,512]{1,0:T(8,128)(2,1)S(1)}, bf16[1024,512]{1,0:T(8,128)(2,1)S(1)}, bf16[1024,512]{1,0:T(8,128)(2,1)S(1)}, bf16[1024,512]{1,0:T(8,12...) custom-call(bf16[128,2048]{1,0:T(8,128)(2,1)S(1)} %collective-permut, ...), custom_call_target="tpu_custom_call", output_to_operand_aliasing={{0}: (22, {}), {1}: (23, {}), {2}: (24, {}), {3}: (25, {}),... | custom-call | tf_op jit(solution)/shard_map/pallas_call | solution.py:50
  314.7 2.6 collective-permute-done.56.refs_0_
  319.0 6.1 %shard_map.254 = (bf16[1024,512]{1,0:T(8,128)(2,1)S(1)}, bf16[1024,512]{1,0:T(8,128)(2,1)S(1)}, bf16[1024,512]{1,0:T(8,128)(2,1)S(1)}, bf16[1024,512]{1,0:T(8,12...) custom-call(bf16[128,2048]{1,0:T(8,128)(2,1)S(1)} %collective-permut, ...), custom_call_target="tpu_custom_call", output_to_operand_aliasing={{0}: (22, {}), {1}: (23, {}), {2}: (24, {}), {3}: (25, {}),... | custom-call | tf_op jit(solution)/shard_map/pallas_call | solution.py:50
  325.7 6.1 %shard_map.255 = (bf16[1024,512]{1,0:T(8,128)(2,1)S(1)}, bf16[1024,512]{1,0:T(8,128)(2,1)S(1)}, bf16[1024,512]{1,0:T(8,128)(2,1)S(1)}, bf16[1024,512]{1,0:T(8,12...) custom-call(bf16[128,2048]{1,0:T(8,128)(2,1)S(1)} %collective-permut, ...), custom_call_target="tpu_custom_call", output_to_operand_aliasing={{0}: (22, {}), {1}: (23, {}), {2}: (24, {}), {3}: (25, {}),... | custom-call | tf_op jit(solution)/shard_map/pallas_call | solution.py:50
  332.8 1.8 collective-permute-start.64
  339.6 7.9 %collective-permute-done.64 = bf16[128,2048]{1,0:T(8,128)(2,1)S(1)} collective-permute-done((bf16[128,2048]{1,0:T(8,128)(2,1)S(1)}, bf16[128,2048]{1,0:T(8,128)(2,1)S(1)}, u32[]{:S(2)}, u32[]{:S(2)}) %collective-permute-start.64) | collective-permute-done | bytes 524320 | tf_op jit(solution)/shard_map/ppermute | solution.py:605
  353.2 8.1 %collective-permute-done.65.refs_2_ = bf16[128,2048]{1,0:T(8,128)(2,1)S(1)} collective-permute-done((bf16[128,2048]{1,0:T(8,128)(2,1)S(1)}, bf16[128,2048]{1,0:T(8,128)(2,1)S(1)}, u32[]{:S(2)}, u32[]{:S(2)}) %collective-permute-start.65) | collective-permute-done | bytes 524320 | tf_op jit(solution)/shard_map/ppermute | solution.py:605
  369.0 9.7 %collective-permute-done.70.refs_3_ = bf16[128,2048]{1,0:T(8,128)(2,1)S(1)} collective-permute-done((bf16[128,2048]{1,0:T(8,128)(2,1)S(1)}, bf16[128,2048]{1,0:T(8,128)(2,1)S(1)}, u32[]{:S(2)}, u32[]{:S(2)}) %collective-permute-start.70) | collective-permute-done | bytes 524320 | tf_op jit(solution)/shard_map/ppermute | solution.py:605
  378.7 7.5 %collective-permute-done.69.refs_2_ = bf16[128,2048]{1,0:T(8,128)(2,1)S(1)} collective-permute-done((bf16[128,2048]{1,0:T(8,128)(2,1)S(1)}, bf16[128,2048]{1,0:T(8,128)(2,1)S(1)}, u32[]{:S(2)}, u32[]{:S(2)}) %collective-permute-start.69) | collective-permute-done | bytes 524320 | tf_op jit(solution)/shard_map/ppermute | solution.py:605
  387.1 2.0 shard_map.257
  393.4 8.1 %shard_map.258 = (f32[512,512]{1,0:T(8,128)S(1)}, f32[512,512]{1,0:T(8,128)S(1)}, bf16[512,512]{1,0:T(8,128)(2,1)S(1)}, f32[8,512]{1,0:T(8,128)S(1)}, f32[8,512]{1,0:T(8,128)S(1)}) custom-call(s32[5]{0:T(128)S(1)} %stack.34.pos, f32[8,128]{1,0:T(8,128)S(1)} %get-tuple-element.240.refs_4_.refs_0_, f32[8,512]{1,0:T(8,128)S(1)} %get-tuple-element.343.refs_1_.refs_4_, ...), custom_call_target="tpu_custom_call" | custom-call | tf_op jit(solution)/shard_map/pallas_call | solution.py:50
  408.5 5.5 collective-permute-done.75
  413.9 3.7 shard_map.260
  426.8 31.1 %collective-permute-done.78 = bf16[1024,512]{1,0:T(8,128)(2,1)S(1)} collective-permute-done((bf16[1024,512]{1,0:T(8,128)(2,1)S(1)}, bf16[1024,512]{1,0:T(8,128)(2,1)S(1)}, u32[]{:S(2)}, u32[]{:S(2)}) %collective-permute-start.78) | collective-permute-done | bytes 1048608 | tf_op jit(solution)/shard_map/ppermute | solution.py:605
  461.9 22.2 %collective-permute-done.81 = bf16[64,2048]{1,0:T(8,128)(2,1)S(1)} collective-permute-done((bf16[64,2048]{1,0:T(8,128)(2,1)S(1)}, bf16[64,2048]{1,0:T(8,128)(2,1)S(1)}, u32[]{:S(2)}, u32[]{:S(2)}) %collective-permute-start.81) | collective-permute-done | bytes 262176 | tf_op jit(solution)/shard_map/ppermute | solution.py:605
  485.8 2.5 collective-permute-start.84
  488.3 8.2 %collective-permute-done.95 = bf16[512,512]{1,0:T(8,128)(2,1)S(1)} collective-permute-done((bf16[512,512]{1,0:T(8,128)(2,1)S(1)}, bf16[512,512]{1,0:T(8,128)(2,1)S(1)}, u32[]{:S(2)}, u32[]{:S(2)}) %collective-permute-start.95) | collective-permute-done | bytes 524320 | tf_op jit(solution)/shard_map/ppermute | solution.py:605
  498.6 1.8 collective-permute-start.92
  503.3 4.8 collective-permute-done.84
  508.4 3.0 collective-permute-start.88
  511.4 2.3 collective-permute-done.92
  514.6 4.3 shard_map.262
  521.8 5.0 collective-permute-done.93
  534.2 11.1 %collective-permute-done.85 = bf16[128,2048]{1,0:T(8,128)(2,1)S(1)} collective-permute-done((bf16[128,2048]{1,0:T(8,128)(2,1)S(1)}, bf16[128,2048]{1,0:T(8,128)(2,1)S(1)}, u32[]{:S(2)}, u32[]{:S(2)}) %collective-permute-start.85) | collective-permute-done | bytes 524320 | tf_op jit(solution)/shard_map/ppermute | solution.py:605
  546.4 4.8 collective-permute-done.87
  554.3 3.5 collective-permute-done.91.refs_3_
  557.8 1.8 shard_map.264
  (313 shorter events, 147.6 us)
Async XLA Ops:
  5.8 20.5 %collective-permute-start.9 = (bf16[64,2048]{1,0:T(8,128)(2,1)}, bf16[64,2048]{1,0:T(8,128)(2,1)S(1)}, u32[]{:S(2)}, u32[]{:S(2)}) collective-permute-start(bf16[64,2048]{1,0:T(8,128)(2,1)} %refs_0_.1), channel_id=1, source_target_pairs={{0,8},{1,9},{2,10},{3,11},{4,0},{5,1},{6,2},{7,3},{8,12},{9,13},{1... | collective-permute-start | bytes 786440 | tf_op jit(solution)/shard_map/ppermute | solution.py:605
  24.7 29.8 %collective-permute-start.6 = (bf16[272,1536]{1,0:T(8,128)(2,1)}, bf16[272,1536]{1,0:T(8,128)(2,1)}, u32[]{:S(2)}, u32[]{:S(2)}) collective-permute-start(bf16[272,1536]{1,0:T(8,128)(2,1)} %get-tuple-element.222.refs_0_), channel_id=1, source_target_pairs={{0,8},{1,9},{2,10},{3,11},{4,0},{5,1},{6,2},{7,3},{8,12},{9,13},{1... | collective-permute-start | bytes 2506760 | tf_op jit(solution)/shard_map/ppermute | solution.py:605
  26.3 23.2 %collective-permute-start.10 = (bf16[64,2048]{1,0:T(8,128)(2,1)S(1)}, bf16[64,2048]{1,0:T(8,128)(2,1)}, u32[]{:S(2)}, u32[]{:S(2)}) collective-permute-start(bf16[64,2048]{1,0:T(8,128)(2,1)S(1)} %collective-permute-done.9.refs_2_), channel_id=1, source_target_pairs={{0,8},{1,9},{2,10},{3,11},{4,0},{5,1},{6,2},{7,3},{8,12},{9,13},{1... | collective-permute-start | bytes 786440 | tf_op jit(solution)/shard_map/ppermute | solution.py:605
  26.8 27.6 %collective-permute-start.8 = (bf16[512,512]{1,0:T(8,128)(2,1)S(1)}, bf16[512,512]{1,0:T(8,128)(2,1)S(1)}, u32[]{:S(2)}, u32[]{:S(2)}) collective-permute-start(bf16[512,512]{1,0:T(8,128)(2,1)S(1)} %get-tuple-element.261.refs_12_), channel_id=1, source_target_pairs={{0,2},{1,3},{2,0},{3,1},{4,6},{5,7},{6,4},{7,5},{8,10},{9,11},{10,... | collective-permute-start | bytes 1572872 | tf_op jit(solution)/shard_map/ppermute | solution.py:605
  28.4 26.7 %collective-permute-start.7 = (bf16[512,512]{1,0:T(8,128)(2,1)S(1)}, bf16[512,512]{1,0:T(8,128)(2,1)S(1)}, u32[]{:S(2)}, u32[]{:S(2)}) collective-permute-start(bf16[512,512]{1,0:T(8,128)(2,1)S(1)} %get-tuple-element.260.refs_10_), channel_id=1, source_target_pairs={{0,16},{1,17},{2,18},{3,19},{4,20},{5,21},{6,22},{7,23},{8,24},{9,... | collective-permute-start | bytes 1572872 | tf_op jit(solution)/shard_map/ppermute | solution.py:605
  29.9 25.2 %collective-permute-start.4 = (bf16[128,2048]{1,0:T(8,128)(2,1)S(1)}, bf16[128,2048]{1,0:T(8,128)(2,1)S(1)}, u32[]{:S(2)}, u32[]{:S(2)}) collective-permute-start(bf16[128,2048]{1,0:T(8,128)(2,1)S(1)} %bitcast.54), channel_id=1, source_target_pairs={{0,16},{1,17},{2,18},{3,19},{4,20},{5,21},{6,22},{7,23},{8,24},{9,... | collective-permute-start | bytes 1572872 | tf_op jit(solution)/shard_map/ppermute | solution.py:605
  54.4 23.2 %collective-permute-start.13 = (bf16[272,1536]{1,0:T(8,128)(2,1)}, bf16[272,1536]{1,0:T(8,128)(2,1)S(1)}, u32[]{:S(2)}, u32[]{:S(2)}) collective-permute-start(bf16[272,1536]{1,0:T(8,128)(2,1)} %get-tuple-element.222.refs_0_), channel_id=1, source_target_pairs={{0,1},{1,0},{2,3},{3,2},{4,5},{5,4},{6,7},{7,6},{8,9},{9,8},{10,11... | collective-permute-start | bytes 2506760 | tf_op jit(solution)/shard_map/ppermute | solution.py:605
  54.5 25.7 %collective-permute-start.12 = (bf16[272,1536]{1,0:T(8,128)(2,1)}, bf16[272,1536]{1,0:T(8,128)(2,1)S(1)}, u32[]{:S(2)}, u32[]{:S(2)}) collective-permute-start(bf16[272,1536]{1,0:T(8,128)(2,1)} %collective-permute-done.6.refs_0_), channel_id=1, source_target_pairs={{0,1},{1,0},{2,3},{3,2},{4,5},{5,4},{6,7},{7,6},{8,9},{9,8},{10,11... | collective-permute-start | bytes 2506760 | tf_op jit(solution)/shard_map/ppermute | solution.py:605
  61.5 22.0 %collective-permute-start.11 = (bf16[272,1536]{1,0:T(8,128)(2,1)}, bf16[272,1536]{1,0:T(8,128)(2,1)S(1)}, u32[]{:S(2)}, u32[]{:S(2)}) collective-permute-start(bf16[272,1536]{1,0:T(8,128)(2,1)} %collective-permute-done.6.refs_0_), channel_id=1, source_target_pairs={{0,8},{1,9},{2,10},{3,11},{4,0},{5,1},{6,2},{7,3},{8,12},{9,13},{1... | collective-permute-start | bytes 2506760 | tf_op jit(solution)/shard_map/ppermute | solution.py:605
  83.5 15.9 %collective-permute-start.14 = (bf16[272,1536]{1,0:T(8,128)(2,1)S(1)}, bf16[272,1536]{1,0:T(8,128)(2,1)S(1)}, u32[]{:S(2)}, u32[]{:S(2)}) collective-permute-start(bf16[272,1536]{1,0:T(8,128)(2,1)S(1)} %collective-permute-done.11.refs_0_), channel_id=1, source_target_pairs={{0,8},{1,9},{2,10},{3,11},{4,0},{5,1},{6,2},{7,3},{8,12},{9,13},{1... | collective-permute-start | bytes 2506760 | tf_op jit(solution)/shard_map/ppermute | solution.py:605
  83.8 20.4 %collective-permute-start.17 = (bf16[1024,512]{1,0:T(8,128)(2,1)S(1)}, bf16[1024,512]{1,0:T(8,128)(2,1)S(1)}, u32[]{:S(2)}, u32[]{:S(2)}) collective-permute-start(bf16[1024,512]{1,0:T(8,128)(2,1)S(1)} %copy-done), channel_id=1, source_target_pairs={{0,16},{1,17},{2,18},{3,19},{4,20},{5,21},{6,22},{7,23},{8,24},{9,... | collective-permute-start | bytes 3145736 | tf_op jit(solution)/shard_map/ppermute | solution.py:605
  85.3 20.2 %collective-permute-start.18 = (bf16[1024,512]{1,0:T(8,128)(2,1)S(1)}, bf16[1024,512]{1,0:T(8,128)(2,1)}, u32[]{:S(2)}, u32[]{:S(2)}) collective-permute-start(bf16[1024,512]{1,0:T(8,128)(2,1)S(1)} %copy-done.1), channel_id=1, source_target_pairs={{0,2},{1,3},{2,0},{3,1},{4,6},{5,7},{6,4},{7,5},{8,10},{9,11},{10,... | collective-permute-start | bytes 3145736 | tf_op jit(solution)/shard_map/ppermute | solution.py:605
  86.8 13.0 %collective-permute-start.16 = (bf16[272,1536]{1,0:T(8,128)(2,1)S(1)}, bf16[272,1536]{1,0:T(8,128)(2,1)S(1)}, u32[]{:S(2)}, u32[]{:S(2)}) collective-permute-start(bf16[272,1536]{1,0:T(8,128)(2,1)S(1)} %collective-permute-done.11.refs_0_), channel_id=1, source_target_pairs={{0,1},{1,0},{2,3},{3,2},{4,5},{5,4},{6,7},{7,6},{8,9},{9,8},{10,11... | collective-permute-start | bytes 2506760 | tf_op jit(solution)/shard_map/ppermute | solution.py:605
  99.3 22.3 %collective-permute-start.22 = (bf16[64,2048]{1,0:T(8,128)(2,1)S(1)}, bf16[64,2048]{1,0:T(8,128)(2,1)S(1)}, u32[]{:S(2)}, u32[]{:S(2)}) collective-permute-start(bf16[64,2048]{1,0:T(8,128)(2,1)S(1)} %copy-done.35), channel_id=1, source_target_pairs={{0,1},{1,0},{2,3},{3,2},{4,5},{5,4},{6,7},{7,6},{8,9},{9,8},{10,11... | collective-permute-start | bytes 786440 | tf_op jit(solution)/shard_map/ppermute | solution.py:605
  119.0 32.1 %collective-permute-start.27 = (bf16[1024,512]{1,0:T(8,128)(2,1)S(1)}, bf16[1024,512]{1,0:T(8,128)(2,1)}, u32[]{:S(2)}, u32[]{:S(2)}) collective-permute-start(bf16[1024,512]{1,0:T(8,128)(2,1)S(1)} %copy-done), channel_id=1, source_target_pairs={{0,2},{1,3},{2,0},{3,1},{4,6},{5,7},{6,4},{7,5},{8,10},{9,11},{10,... | collective-permute-start | bytes 3145736 | tf_op jit(solution)/shard_map/ppermute | solution.py:605
  120.5 30.6 %collective-permute-start.29 = (bf16[1024,512]{1,0:T(8,128)(2,1)S(1)}, bf16[1024,512]{1,0:T(8,128)(2,1)}, u32[]{:S(2)}, u32[]{:S(2)}) collective-permute-start(bf16[1024,512]{1,0:T(8,128)(2,1)S(1)} %copy-done.1), channel_id=1, source_target_pairs={{0,16},{1,17},{2,18},{3,19},{4,20},{5,21},{6,22},{7,23},{8,24},{9,... | collective-permute-start | bytes 3145736 | tf_op jit(solution)/shard_map/ppermute | solution.py:605
  121.2 45.0 %collective-permute-start.28 = (bf16[1024,512]{1,0:T(8,128)(2,1)S(1)}, bf16[1024,512]{1,0:T(8,128)(2,1)}, u32[]{:S(2)}, u32[]{:S(2)}) collective-permute-start(bf16[1024,512]{1,0:T(8,128)(2,1)S(1)} %collective-permute-done.17.refs_4_), channel_id=1, source_target_pairs={{0,2},{1,3},{2,0},{3,1},{4,6},{5,7},{6,4},{7,5},{8,10},{9,11},{10,... | collective-permute-start | bytes 3145736 | tf_op jit(solution)/shard_map/ppermute | solution.py:605
  122.3 44.9 %collective-permute-start.30 = (bf16[1024,512]{1,0:T(8,128)(2,1)}, bf16[1024,512]{1,0:T(8,128)(2,1)}, u32[]{:S(2)}, u32[]{:S(2)}) collective-permute-start(bf16[1024,512]{1,0:T(8,128)(2,1)} %collective-permute-done.18.refs_7_), channel_id=1, source_target_pairs={{0,16},{1,17},{2,18},{3,19},{4,20},{5,21},{6,22},{7,23},{8,24},{9,... | collective-permute-start | bytes 3145736 | tf_op jit(solution)/shard_map/ppermute | solution.py:605
  167.3 14.0 %collective-permute-start.31 = (bf16[128,2048]{1,0:T(8,128)(2,1)S(1)}, bf16[128,2048]{1,0:T(8,128)(2,1)S(1)}, u32[]{:S(2)}, u32[]{:S(2)}) collective-permute-start(bf16[128,2048]{1,0:T(8,128)(2,1)S(1)} %get-tuple-element.256), channel_id=1, source_target_pairs={{0,2},{1,3},{2,0},{3,1},{4,6},{5,7},{6,4},{7,5},{8,10},{9,11},{10,... | collective-permute-start | bytes 1572872 | tf_op jit(solution)/shard_map/ppermute | solution.py:605
  167.8 14.9 %collective-permute-start.32 = (bf16[128,2048]{1,0:T(8,128)(2,1)S(1)}, bf16[128,2048]{1,0:T(8,128)(2,1)S(1)}, u32[]{:S(2)}, u32[]{:S(2)}) collective-permute-start(bf16[128,2048]{1,0:T(8,128)(2,1)S(1)} %get-tuple-element.257), channel_id=1, source_target_pairs={{0,16},{1,17},{2,18},{3,19},{4,20},{5,21},{6,22},{7,23},{8,24},{9,... | collective-permute-start | bytes 1572872 | tf_op jit(solution)/shard_map/ppermute | solution.py:605
  168.3 23.4 %collective-permute-start.33 = (bf16[128,2048]{1,0:T(8,128)(2,1)S(1)}, bf16[128,2048]{1,0:T(8,128)(2,1)S(1)}, u32[]{:S(2)}, u32[]{:S(2)}) collective-permute-start(bf16[128,2048]{1,0:T(8,128)(2,1)S(1)} %get-tuple-element.258), channel_id=1, source_target_pairs={{0,18},{1,19},{2,16},{3,17},{4,22},{5,23},{6,20},{7,21},{8,26},{9,... | collective-permute-start | bytes 1572872 | tf_op jit(solution)/shard_map/ppermute | solution.py:605
  191.7 14.9 %collective-permute-start.35 = (bf16[512,512]{1,0:T(8,128)(2,1)S(1)}, bf16[512,512]{1,0:T(8,128)(2,1)S(1)}, u32[]{:S(2)}, u32[]{:S(2)}) collective-permute-start(bf16[512,512]{1,0:T(8,128)(2,1)S(1)} %copy-done.5), channel_id=1, source_target_pairs={{0,2},{1,3},{2,0},{3,1},{4,6},{5,7},{6,4},{7,5},{8,10},{9,11},{10,... | collective-permute-start | bytes 1572872 | tf_op jit(solution)/shard_map/ppermute | solution.py:605
  193.5 13.1 %collective-permute-start.40 = (bf16[128,2048]{1,0:T(8,128)(2,1)S(1)}, bf16[128,2048]{1,0:T(8,128)(2,1)S(1)}, u32[]{:S(2)}, u32[]{:S(2)}) collective-permute-start(bf16[128,2048]{1,0:T(8,128)(2,1)S(1)} %get-tuple-element.259.refs_0_), channel_id=1, source_target_pairs={{0,8},{1,9},{2,10},{3,11},{4,0},{5,1},{6,2},{7,3},{8,12},{9,13},{1... | collective-permute-start | bytes 1572872 | tf_op jit(solution)/shard_map/ppermute | solution.py:605
  193.9 14.9 %collective-permute-start.37 = (bf16[512,512]{1,0:T(8,128)(2,1)S(1)}, bf16[512,512]{1,0:T(8,128)(2,1)S(1)}, u32[]{:S(2)}, u32[]{:S(2)}) collective-permute-start(bf16[512,512]{1,0:T(8,128)(2,1)S(1)} %copy-done.3), channel_id=1, source_target_pairs={{0,16},{1,17},{2,18},{3,19},{4,20},{5,21},{6,22},{7,23},{8,24},{9,... | collective-permute-start | bytes 1572872 | tf_op jit(solution)/shard_map/ppermute | solution.py:605
  195.3 20.0 %collective-permute-start.38 = (bf16[512,512]{1,0:T(8,128)(2,1)S(1)}, bf16[512,512]{1,0:T(8,128)(2,1)S(1)}, u32[]{:S(2)}, u32[]{:S(2)}) collective-permute-start(bf16[512,512]{1,0:T(8,128)(2,1)S(1)} %copy-done.7), channel_id=1, source_target_pairs={{0,16},{1,17},{2,18},{3,19},{4,20},{5,21},{6,22},{7,23},{8,24},{9,... | collective-permute-start | bytes 1572872 | tf_op jit(solution)/shard_map/ppermute | solution.py:605
  195.9 19.4 %collective-permute-start.36 = (bf16[512,512]{1,0:T(8,128)(2,1)S(1)}, bf16[512,512]{1,0:T(8,128)(2,1)S(1)}, u32[]{:S(2)}, u32[]{:S(2)}) collective-permute-start(bf16[512,512]{1,0:T(8,128)(2,1)S(1)} %copy-done.9), channel_id=1, source_target_pairs={{0,2},{1,3},{2,0},{3,1},{4,6},{5,7},{6,4},{7,5},{8,10},{9,11},{10,... | collective-permute-start | bytes 1572872 | tf_op jit(solution)/shard_map/ppermute | solution.py:605
  206.6 14.9 %collective-permute-start.41 = (bf16[128,2048]{1,0:T(8,128)(2,1)S(1)}, bf16[128,2048]{1,0:T(8,128)(2,1)S(1)}, u32[]{:S(2)}, u32[]{:S(2)}) collective-permute-start(bf16[128,2048]{1,0:T(8,128)(2,1)S(1)} %collective-permute-done.40.refs_0_), channel_id=1, source_target_pairs={{0,8},{1,9},{2,10},{3,11},{4,0},{5,1},{6,2},{7,3},{8,12},{9,13},{1... | collective-permute-start | bytes 1572872 | tf_op jit(solution)/shard_map/ppermute | solution.py:605
  208.7 14.5 %collective-permute-start.45 = (bf16[128,2048]{1,0:T(8,128)(2,1)S(1)}, bf16[128,2048]{1,0:T(8,128)(2,1)S(1)}, u32[]{:S(2)}, u32[]{:S(2)}) collective-permute-start(bf16[128,2048]{1,0:T(8,128)(2,1)S(1)} %collective-permute-done.40.refs_0_), channel_id=1, source_target_pairs={{0,1},{1,0},{2,3},{3,2},{4,5},{5,4},{6,7},{7,6},{8,9},{9,8},{10,11... | collective-permute-start | bytes 1572872 | tf_op jit(solution)/shard_map/ppermute | solution.py:605
  221.5 13.8 %collective-permute-start.42 = (bf16[128,2048]{1,0:T(8,128)(2,1)S(1)}, bf16[128,2048]{1,0:T(8,128)(2,1)S(1)}, u32[]{:S(2)}, u32[]{:S(2)}) collective-permute-start(bf16[128,2048]{1,0:T(8,128)(2,1)S(1)} %collective-permute-done.41.refs_0_), channel_id=1, source_target_pairs={{0,8},{1,9},{2,10},{3,11},{4,0},{5,1},{6,2},{7,3},{8,12},{9,13},{1... | collective-permute-start | bytes 1572872 | tf_op jit(solution)/shard_map/ppermute | solution.py:605
  235.4 15.3 %collective-permute-start.49 = (bf16[128,2048]{1,0:T(8,128)(2,1)S(1)}, bf16[128,2048]{1,0:T(8,128)(2,1)S(1)}, u32[]{:S(2)}, u32[]{:S(2)}) collective-permute-start(bf16[128,2048]{1,0:T(8,128)(2,1)S(1)} %add_convert_fusion.13), channel_id=1, source_target_pairs={{0,8},{1,9},{2,10},{3,11},{4,0},{5,1},{6,2},{7,3},{8,12},{9,13},{1... | collective-permute-start | bytes 1572872 | tf_op jit(solution)/shard_map/ppermute | solution.py:605
  250.9 14.5 %collective-permute-start.50 = (bf16[128,2048]{1,0:T(8,128)(2,1)S(1)}, bf16[128,2048]{1,0:T(8,128)(2,1)S(1)}, u32[]{:S(2)}, u32[]{:S(2)}) collective-permute-start(bf16[128,2048]{1,0:T(8,128)(2,1)S(1)} %add_convert_fusion.12), channel_id=1, source_target_pairs={{0,8},{1,9},{2,10},{3,11},{4,0},{5,1},{6,2},{7,3},{8,12},{9,13},{1... | collective-permute-start | bytes 1572872 | tf_op jit(solution)/shard_map/ppermute | solution.py:605
  252.5 12.9 %collective-permute-start.46 = (bf16[128,2048]{1,0:T(8,128)(2,1)S(1)}, bf16[128,2048]{1,0:T(8,128)(2,1)S(1)}, u32[]{:S(2)}, u32[]{:S(2)}) collective-permute-start(bf16[128,2048]{1,0:T(8,128)(2,1)S(1)} %get-tuple-element.291), channel_id=1, source_target_pairs={{0,1},{1,0},{2,3},{3,2},{4,5},{5,4},{6,7},{7,6},{8,9},{9,8},{10,11... | collective-permute-start | bytes 1572872 | tf_op jit(solution)/shard_map/ppermute | solution.py:605
  265.6 13.6 %collective-permute-start.51 = (bf16[128,2048]{1,0:T(8,128)(2,1)S(1)}, bf16[128,2048]{1,0:T(8,128)(2,1)S(1)}, u32[]{:S(2)}, u32[]{:S(2)}) collective-permute-start(bf16[128,2048]{1,0:T(8,128)(2,1)S(1)} %add_convert_fusion.11), channel_id=1, source_target_pairs={{0,8},{1,9},{2,10},{3,11},{4,0},{5,1},{6,2},{7,3},{8,12},{9,13},{1... | collective-permute-start | bytes 1572872 | tf_op jit(solution)/shard_map/ppermute | solution.py:605
  282.8 13.0 %collective-permute-start.52 = (bf16[128,2048]{1,0:T(8,128)(2,1)S(1)}, bf16[128,2048]{1,0:T(8,128)(2,1)S(1)}, u32[]{:S(2)}, u32[]{:S(2)}) collective-permute-start(bf16[128,2048]{1,0:T(8,128)(2,1)S(1)} %get-tuple-element.301.refs_0_), channel_id=1, source_target_pairs={{0,1},{1,0},{2,3},{3,2},{4,5},{5,4},{6,7},{7,6},{8,9},{9,8},{10,11... | collective-permute-start | bytes 1572872 | tf_op jit(solution)/shard_map/ppermute | solution.py:605
  317.4 15.3 %collective-permute-start.63 = (bf16[128,2048]{1,0:T(8,128)(2,1)S(1)}, bf16[128,2048]{1,0:T(8,128)(2,1)S(1)}, u32[]{:S(2)}, u32[]{:S(2)}) collective-permute-start(bf16[128,2048]{1,0:T(8,128)(2,1)S(1)} %add_convert_fusion.10), channel_id=1, source_target_pairs={{0,8},{1,9},{2,10},{3,11},{4,0},{5,1},{6,2},{7,3},{8,12},{9,13},{1... | collective-permute-start | bytes 1572872 | tf_op jit(solution)/shard_map/ppermute | solution.py:605
  325.4 35.9 %collective-permute-start.53 = (bf16[128,2048]{1,0:T(8,128)(2,1)S(1)}, bf16[128,2048]{1,0:T(8,128)(2,1)S(1)}, u32[]{:S(2)}, u32[]{:S(2)}) collective-permute-start(bf16[128,2048]{1,0:T(8,128)(2,1)S(1)} %get-tuple-element.307), channel_id=1, source_target_pairs={{0,1},{1,0},{2,3},{3,2},{4,5},{5,4},{6,7},{7,6},{8,9},{9,8},{10,11... | collective-permute-start | bytes 1572872 | tf_op jit(solution)/shard_map/ppermute | solution.py:605
  331.8 15.7 %collective-permute-start.60 = (bf16[128,2048]{1,0:T(8,128)(2,1)S(1)}, bf16[128,2048]{1,0:T(8,128)(2,1)S(1)}, u32[]{:S(2)}, u32[]{:S(2)}) collective-permute-start(bf16[128,2048]{1,0:T(8,128)(2,1)S(1)} %get-tuple-element.333), channel_id=1, source_target_pairs={{0,1},{1,0},{2,3},{3,2},{4,5},{5,4},{6,7},{7,6},{8,9},{9,8},{10,11... | collective-permute-start | bytes 1572872 | tf_op jit(solution)/shard_map/ppermute | solution.py:605
  332.8 14.7 %collective-permute-start.64 = (bf16[128,2048]{1,0:T(8,128)(2,1)S(1)}, bf16[128,2048]{1,0:T(8,128)(2,1)S(1)}, u32[]{:S(2)}, u32[]{:S(2)}) collective-permute-start(bf16[128,2048]{1,0:T(8,128)(2,1)S(1)} %add_convert_fusion.9), channel_id=1, source_target_pairs={{0,8},{1,9},{2,10},{3,11},{4,0},{5,1},{6,2},{7,3},{8,12},{9,13},{1... | collective-permute-start | bytes 1572872 | tf_op jit(solution)/shard_map/ppermute | solution.py:605
  336.1 26.7 %collective-permute-start.67 = (bf16[512,512]{1,0:T(8,128)(2,1)S(1)}, bf16[512,512]{1,0:T(8,128)(2,1)S(1)}, u32[]{:S(2)}, u32[]{:S(2)}) collective-permute-start(bf16[512,512]{1,0:T(8,128)(2,1)S(1)} %convolution_convert_fusion.14), channel_id=1, source_target_pairs={{0,2},{1,3},{2,0},{3,1},{4,6},{5,7},{6,4},{7,5},{8,10},{9,11},{10,... | collective-permute-start | bytes 1572872 | tf_op jit(solution)/shard_map/ppermute | solution.py:605
  336.7 26.1 %collective-permute-start.66 = (bf16[512,512]{1,0:T(8,128)(2,1)S(1)}, bf16[512,512]{1,0:T(8,128)(2,1)S(1)}, u32[]{:S(2)}, u32[]{:S(2)}) collective-permute-start(bf16[512,512]{1,0:T(8,128)(2,1)S(1)} %convolution_convert_fusion.15), channel_id=1, source_target_pairs={{0,16},{1,17},{2,18},{3,19},{4,20},{5,21},{6,22},{7,23},{8,24},{9,... | collective-permute-start | bytes 1572872 | tf_op jit(solution)/shard_map/ppermute | solution.py:605
  347.7 13.6 %collective-permute-start.65 = (bf16[128,2048]{1,0:T(8,128)(2,1)S(1)}, bf16[128,2048]{1,0:T(8,128)(2,1)S(1)}, u32[]{:S(2)}, u32[]{:S(2)}) collective-permute-start(bf16[128,2048]{1,0:T(8,128)(2,1)S(1)} %add_convert_fusion.8), channel_id=1, source_target_pairs={{0,8},{1,9},{2,10},{3,11},{4,0},{5,1},{6,2},{7,3},{8,12},{9,13},{1... | collective-permute-start | bytes 1572872 | tf_op jit(solution)/shard_map/ppermute | solution.py:605
  362.8 15.8 %collective-permute-start.70 = (bf16[128,2048]{1,0:T(8,128)(2,1)S(1)}, bf16[128,2048]{1,0:T(8,128)(2,1)S(1)}, u32[]{:S(2)}, u32[]{:S(2)}) collective-permute-start(bf16[128,2048]{1,0:T(8,128)(2,1)S(1)} %get-tuple-element.352.refs_0_), channel_id=1, source_target_pairs={{0,18},{1,19},{2,16},{3,17},{4,22},{5,23},{6,20},{7,21},{8,26},{9,... | collective-permute-start | bytes 1572872 | tf_op jit(solution)/shard_map/ppermute | solution.py:605
  363.4 22.8 %collective-permute-start.69 = (bf16[128,2048]{1,0:T(8,128)(2,1)S(1)}, bf16[128,2048]{1,0:T(8,128)(2,1)S(1)}, u32[]{:S(2)}, u32[]{:S(2)}) collective-permute-start(bf16[128,2048]{1,0:T(8,128)(2,1)S(1)} %get-tuple-element.352.refs_0_), channel_id=1, source_target_pairs={{0,16},{1,17},{2,18},{3,19},{4,20},{5,21},{6,22},{7,23},{8,24},{9,... | collective-permute-start | bytes 1572872 | tf_op jit(solution)/shard_map/ppermute | solution.py:605
  364.9 22.1 %collective-permute-start.68 = (bf16[128,2048]{1,0:T(8,128)(2,1)S(1)}, bf16[128,2048]{1,0:T(8,128)(2,1)S(1)}, u32[]{:S(2)}, u32[]{:S(2)}) collective-permute-start(bf16[128,2048]{1,0:T(8,128)(2,1)S(1)} %get-tuple-element.352.refs_0_), channel_id=1, source_target_pairs={{0,2},{1,3},{2,0},{3,1},{4,6},{5,7},{6,4},{7,5},{8,10},{9,11},{10,... | collective-permute-start | bytes 1572872 | tf_op jit(solution)/shard_map/ppermute | solution.py:605
  389.1 16.0 %collective-permute-start.74 = (bf16[256,2048]{1,0:T(8,128)(2,1)S(1)}, bf16[256,2048]{1,0:T(8,128)(2,1)S(1)}, u32[]{:S(2)}, u32[]{:S(2)}) collective-permute-start(bf16[256,2048]{1,0:T(8,128)(2,1)S(1)} %get-tuple-element.383), channel_id=1, source_target_pairs={{0,1},{1,0},{2,3},{3,2},{4,5},{5,4},{6,7},{7,6},{8,9},{9,8},{10,11... | collective-permute-start | bytes 3145736 | tf_op jit(solution)/shard_map/ppermute | solution.py:605
  417.7 67.1 %collective-permute-start.76 = (bf16[816,1536]{1,0:T(8,128)(2,1)S(1)}, bf16[816,1536]{1,0:T(8,128)(2,1)S(1)}, u32[]{:S(2)}, u32[]{:S(2)}) collective-permute-start(bf16[816,1536]{1,0:T(8,128)(2,1)S(1)} %get-tuple-element.390), channel_id=1, source_target_pairs={{0,1},{1,0},{2,3},{3,2},{4,5},{5,4},{6,7},{7,6},{8,9},{9,8},{10,11... | collective-permute-start | bytes 7520264 | tf_op jit(solution)/shard_map/ppermute | solution.py:605
  421.6 39.0 %collective-permute-start.98 = (bf16[512,512]{1,0:T(8,128)(2,1)S(1)}, bf16[512,512]{1,0:T(8,128)(2,1)S(1)}, u32[]{:S(2)}, u32[]{:S(2)}) collective-permute-start(bf16[512,512]{1,0:T(8,128)(2,1)S(1)} %add_convert_fusion.5), channel_id=1, source_target_pairs={{0,16},{1,17},{2,18},{3,19},{4,20},{5,21},{6,22},{7,23},{8,24},{9,... | collective-permute-start | bytes 1572872 | tf_op jit(solution)/shard_map/ppermute | solution.py:605
  422.1 35.8 %collective-permute-start.78 = (bf16[1024,512]{1,0:T(8,128)(2,1)S(1)}, bf16[1024,512]{1,0:T(8,128)(2,1)S(1)}, u32[]{:S(2)}, u32[]{:S(2)}) collective-permute-start(bf16[1024,512]{1,0:T(8,128)(2,1)S(1)} %convolution_convert_fusion.4), channel_id=1, source_target_pairs={{0,16},{1,17},{2,18},{3,19},{4,20},{5,21},{6,22},{7,23},{8,24},{9,... | collective-permute-start | bytes 3145736 | tf_op jit(solution)/shard_map/ppermute | solution.py:605
  423.6 34.3 %collective-permute-start.79 = (bf16[1024,512]{1,0:T(8,128)(2,1)S(1)}, bf16[1024,512]{1,0:T(8,128)(2,1)S(1)}, u32[]{:S(2)}, u32[]{:S(2)}) collective-permute-start(bf16[1024,512]{1,0:T(8,128)(2,1)S(1)} %convolution_convert_fusion), channel_id=1, source_target_pairs={{0,2},{1,3},{2,0},{3,1},{4,6},{5,7},{6,4},{7,5},{8,10},{9,11},{10,... | collective-permute-start | bytes 3145736 | tf_op jit(solution)/shard_map/ppermute | solution.py:605
  425.1 35.9 %collective-permute-start.97 = (bf16[512,512]{1,0:T(8,128)(2,1)S(1)}, bf16[512,512]{1,0:T(8,128)(2,1)S(1)}, u32[]{:S(2)}, u32[]{:S(2)}) collective-permute-start(bf16[512,512]{1,0:T(8,128)(2,1)S(1)} %convolution_convert_fusion.9), channel_id=1, source_target_pairs={{0,2},{1,3},{2,0},{3,1},{4,6},{5,7},{6,4},{7,5},{8,10},{9,11},{10,... | collective-permute-start | bytes 1572872 | tf_op jit(solution)/shard_map/ppermute | solution.py:605
  457.9 27.6 %collective-permute-start.80 = (bf16[272,1536]{1,0:T(8,128)(2,1)S(1)}, bf16[272,1536]{1,0:T(8,128)(2,1)S(1)}, u32[]{:S(2)}, u32[]{:S(2)}) collective-permute-start(bf16[272,1536]{1,0:T(8,128)(2,1)S(1)} %add_convert_fusion.4), channel_id=1, source_target_pairs={{0,8},{1,9},{2,10},{3,11},{4,0},{5,1},{6,2},{7,3},{8,12},{9,13},{1... | collective-permute-start | bytes 2506760 | tf_op jit(solution)/shard_map/ppermute | solution.py:605
  459.6 24.5 %collective-permute-start.81 = (bf16[64,2048]{1,0:T(8,128)(2,1)S(1)}, bf16[64,2048]{1,0:T(8,128)(2,1)S(1)}, u32[]{:S(2)}, u32[]{:S(2)}) collective-permute-start(bf16[64,2048]{1,0:T(8,128)(2,1)S(1)} %add_convert_fusion.15), channel_id=1, source_target_pairs={{0,8},{1,9},{2,10},{3,11},{4,0},{5,1},{6,2},{7,3},{8,12},{9,13},{1... | collective-permute-start | bytes 786440 | tf_op jit(solution)/shard_map/ppermute | solution.py:605
  460.6 25.3 %collective-permute-start.82 = (bf16[1024,512]{1,0:T(8,128)(2,1)S(1)}, bf16[1024,512]{1,0:T(8,128)(2,1)S(1)}, u32[]{:S(2)}, u32[]{:S(2)}) collective-permute-start(bf16[1024,512]{1,0:T(8,128)(2,1)S(1)} %convolution_convert_fusion.5), channel_id=1, source_target_pairs={{0,16},{1,17},{2,18},{3,19},{4,20},{5,21},{6,22},{7,23},{8,24},{9,... | collective-permute-start | bytes 3145736 | tf_op jit(solution)/shard_map/ppermute | solution.py:605
  461.1 24.8 %collective-permute-start.83 = (bf16[1024,512]{1,0:T(8,128)(2,1)S(1)}, bf16[1024,512]{1,0:T(8,128)(2,1)S(1)}, u32[]{:S(2)}, u32[]{:S(2)}) collective-permute-start(bf16[1024,512]{1,0:T(8,128)(2,1)S(1)} %convolution_convert_fusion.2), channel_id=1, source_target_pairs={{0,2},{1,3},{2,0},{3,1},{4,6},{5,7},{6,4},{7,5},{8,10},{9,11},{10,... | collective-permute-start | bytes 3145736 | tf_op jit(solution)/shard_map/ppermute | solution.py:605
  485.8 22.2 %collective-permute-start.84 = (bf16[272,1536]{1,0:T(8,128)(2,1)S(1)}, bf16[272,1536]{1,0:T(8,128)(2,1)S(1)}, u32[]{:S(2)}, u32[]{:S(2)}) collective-permute-start(bf16[272,1536]{1,0:T(8,128)(2,1)S(1)} %add_convert_fusion.3), channel_id=1, source_target_pairs={{0,8},{1,9},{2,10},{3,11},{4,0},{5,1},{6,2},{7,3},{8,12},{9,13},{1... | collective-permute-start | bytes 2506760 | tf_op jit(solution)/shard_map/ppermute | solution.py:605
  498.6 15.1 %collective-permute-start.92 = (bf16[64,2048]{1,0:T(8,128)(2,1)S(1)}, bf16[64,2048]{1,0:T(8,128)(2,1)S(1)}, u32[]{:S(2)}, u32[]{:S(2)}) collective-permute-start(bf16[64,2048]{1,0:T(8,128)(2,1)S(1)} %add_convert_fusion.14), channel_id=1, source_target_pairs={{0,8},{1,9},{2,10},{3,11},{4,0},{5,1},{6,2},{7,3},{8,12},{9,13},{1... | collective-permute-start | bytes 786440 | tf_op jit(solution)/shard_map/ppermute | solution.py:605
  500.7 26.2 %collective-permute-start.93 = (bf16[1024,512]{1,0:T(8,128)(2,1)S(1)}, bf16[1024,512]{1,0:T(8,128)(2,1)S(1)}, u32[]{:S(2)}, u32[]{:S(2)}) collective-permute-start(bf16[1024,512]{1,0:T(8,128)(2,1)S(1)} %add_convert_fusion.1), channel_id=1, source_target_pairs={{0,2},{1,3},{2,0},{3,1},{4,6},{5,7},{6,4},{7,5},{8,10},{9,11},{10,... | collective-permute-start | bytes 3145736 | tf_op jit(solution)/shard_map/ppermute | solution.py:605
  502.1 28.0 %collective-permute-start.94 = (bf16[1024,512]{1,0:T(8,128)(2,1)S(1)}, bf16[1024,512]{1,0:T(8,128)(2,1)S(1)}, u32[]{:S(2)}, u32[]{:S(2)}) collective-permute-start(bf16[1024,512]{1,0:T(8,128)(2,1)S(1)} %add_convert_fusion), channel_id=1, source_target_pairs={{0,16},{1,17},{2,18},{3,19},{4,20},{5,21},{6,22},{7,23},{8,24},{9,... | collective-permute-start | bytes 3145736 | tf_op jit(solution)/shard_map/ppermute | solution.py:605
  508.4 23.5 %collective-permute-start.88 = (bf16[272,1536]{1,0:T(8,128)(2,1)S(1)}, bf16[272,1536]{1,0:T(8,128)(2,1)S(1)}, u32[]{:S(2)}, u32[]{:S(2)}) collective-permute-start(bf16[272,1536]{1,0:T(8,128)(2,1)S(1)} %add_convert_fusion.2), channel_id=1, source_target_pairs={{0,8},{1,9},{2,10},{3,11},{4,0},{5,1},{6,2},{7,3},{8,12},{9,13},{1... | collective-permute-start | bytes 2506760 | tf_op jit(solution)/shard_map/ppermute | solution.py:605
  518.9 26.4 %collective-permute-start.85 = (bf16[128,2048]{1,0:T(8,128)(2,1)S(1)}, bf16[128,2048]{1,0:T(8,128)(2,1)S(1)}, u32[]{:S(2)}, u32[]{:S(2)}) collective-permute-start(bf16[128,2048]{1,0:T(8,128)(2,1)S(1)} %get-tuple-element.403), channel_id=1, source_target_pairs={{0,2},{1,3},{2,0},{3,1},{4,6},{5,7},{6,4},{7,5},{8,10},{9,11},{10,... | collective-permute-start | bytes 1572872 | tf_op jit(solution)/shard_map/ppermute | solution.py:605
  520.3 26.1 %collective-permute-start.86 = (bf16[128,2048]{1,0:T(8,128)(2,1)S(1)}, bf16[128,2048]{1,0:T(8,128)(2,1)S(1)}, u32[]{:S(2)}, u32[]{:S(2)}) collective-permute-start(bf16[128,2048]{1,0:T(8,128)(2,1)S(1)} %get-tuple-element.404), channel_id=1, source_target_pairs={{0,16},{1,17},{2,18},{3,19},{4,20},{5,21},{6,22},{7,23},{8,24},{9,... | collective-permute-start | bytes 1572872 | tf_op jit(solution)/shard_map/ppermute | solution.py:605
  526.8 24.4 %collective-permute-start.87 = (bf16[128,2048]{1,0:T(8,128)(2,1)S(1)}, bf16[128,2048]{1,0:T(8,128)(2,1)S(1)}, u32[]{:S(2)}, u32[]{:S(2)}) collective-permute-start(bf16[128,2048]{1,0:T(8,128)(2,1)S(1)} %get-tuple-element.405), channel_id=1, source_target_pairs={{0,18},{1,19},{2,16},{3,17},{4,22},{5,23},{6,20},{7,21},{8,26},{9,... | collective-permute-start | bytes 1572872 | tf_op jit(solution)/shard_map/ppermute | solution.py:605
  532.2 21.0 %collective-permute-start.89 = (bf16[80,1536]{1,0:T(8,128)(2,1)S(1)}, bf16[80,1536]{1,0:T(8,128)(2,1)S(1)}, u32[]{:S(2)}, u32[]{:S(2)}) collective-permute-start(bf16[80,1536]{1,0:T(8,128)(2,1)S(1)} %get-tuple-element.407), channel_id=1, source_target_pairs={{0,2},{1,3},{2,0},{3,1},{4,6},{5,7},{6,4},{7,5},{8,10},{9,11},{10,... | collective-permute-start | bytes 737288 | tf_op jit(solution)/shard_map/ppermute | solution.py:605
  533.6 20.7 %collective-permute-start.90 = (bf16[80,1536]{1,0:T(8,128)(2,1)S(1)}, bf16[80,1536]{1,0:T(8,128)(2,1)S(1)}, u32[]{:S(2)}, u32[]{:S(2)}) collective-permute-start(bf16[80,1536]{1,0:T(8,128)(2,1)S(1)} %get-tuple-element.408), channel_id=1, source_target_pairs={{0,16},{1,17},{2,18},{3,19},{4,20},{5,21},{6,22},{7,23},{8,24},{9,... | collective-permute-start | bytes 737288 | tf_op jit(solution)/shard_map/ppermute | solution.py:605
  (85 other events, 928.0 us)

commit v4 on v3

--- a/solution.py
+++ b/solution.py
@@ -50,7 +50,9 @@
     return pl.pallas_call(
         body,
         grid=(1,),
-        out_shape=[out for out, _ in outs],
+        out_shape=[
+            pltpu.HBM(out.shape, out.dtype) if spec is HBM else out for out, spec in outs
+        ],
         out_specs=[spec if isinstance(spec, pl.BlockSpec) else spec(out) for out, spec in outs],
         in_specs=[spec if isinstance(spec, pl.BlockSpec) else spec(array) for array, spec in ins],
         compiler_params=pltpu.CompilerParams(vmem_limit_bytes=limit * MIB),
@@ -126,13 +128,17 @@
 
 
 def join_kernel(*refs):
-    *parts, out, lengths = refs
+    *parts, w_output, out, lengths = refs
     rows = parts[0].shape[0] - EXTRA
     extras = []
     for i, part in enumerate(parts):
-        out[i * rows : (i + 1) * rows] = part[:rows]
+        for j in range(3):
+            at = (j * GROUP + i) * rows
+            out[at : at + rows] = part[:rows, j * HEADS : (j + 1) * HEADS]
+        at = (3 * GROUP + i) * rows
+        out[at : at + rows] = w_output[:, i * HEADS : (i + 1) * HEADS]
         extras.append(part[rows:, :HEAD_DIM].astype(F32))
-    put_extra(out, GROUP * rows, extra_rows([extra[:4] for extra in extras]))
+    put_extra(out, 4 * GROUP * rows, extra_rows([extra[:4] for extra in extras]))
     lengths[...] = jnp.concatenate(
         [extras[0][4:5], extras[1][4:5], jnp.zeros((6, HEAD_DIM), F32)], axis=0
     )
@@ -149,88 +155,80 @@
     return jnp.transpose(sums)[:8]
 
 
-def group_total(stats, tok):
-    blocks = []
-    for dx, dy in TOKEN_BLOCKS:
-        total = 0.0
-        for (sx, sy), ref in zip(SQUARE, stats):
-            at = ((dy ^ sy) * NX + (dx ^ sx)) * tok
-            total = total + ref[:, at : at + tok]
-        blocks.append(total)
-    return jnp.concatenate(blocks, axis=1)
-
-
 def gather_kernel(*refs):
-    blocks, (whole, kept, sem) = refs[:GROUP], refs[GROUP:]
-    tok = blocks[0].shape[0]
-    for i, block in enumerate(TOKEN_BLOCKS):
-        whole[i * tok : (i + 1) * tok] = blocks[SQUARE.index(block)][...]
+    blocks, (whole, kept, sem) = refs[:-3], refs[-3:]
+    start = 0
+    for block in blocks:
+        whole[start : start + block.shape[0]] = block[...]
+        start += block.shape[0]
     copy = pltpu.make_async_copy(whole, kept, sem)
     copy.start()
     copy.wait()
 
 
-def out_rows_kernel(nc, pos, *refs):
-    *parts, out_w, kept, sem = refs
-    _, r, _, c = place(pos)
-    rows = parts[0].shape[0]
-    for s in range(NZ):
-        for k in range(nc):
-            start = ring(r, s) * HEAD_DIM + (c ^ k) * rows
-            out_w[pl.ds(pl.multiple_of(start, rows), rows)] = parts[s * nc + k][...]
-    copy = pltpu.make_async_copy(out_w, kept, sem)
-    copy.start()
-    copy.wait()
-
-
-def project_kernel(nc, s, pos, x_all, *refs):
-    weights, refs = refs[:nc], refs[nc:]
-    if s > 0:
-        refs = refs[2:] if s < NZ - 1 else (refs[0], *refs[2:])
+def project_kernel(nc, places, pos, x_all, *refs):
+    weights, refs = refs[: nc * len(places)], refs[nc * len(places) :]
+    last = places[-1] == NZ - 1
+    if last:
+        before, _, _, *refs = refs
+    gains, out_w, *refs = refs
+    w_rows, refs = refs[: len(places)], refs[len(places) :]
+    if last:
+        query, key, value, query_h, key_h, value_h, out_kept, stats, *refs = refs
+    else:
+        total, *refs = refs
+    columns, w_part, sems = refs
     x, r, y, c = place(pos)
-    rows = (weights[0].shape[0] - EXTRA) // GROUP
-    if s < NZ - 1:
-        total, gains, w_rows, columns, w_part, sems = refs
-    else:
-        before, gains, w_rows, query, key, value, query_h, key_h, value_h, stats, *refs = refs
-        total, columns, w_part, sems = refs
-    z = ring(r, s)
-    extras = [weight[GROUP * rows :, :HEAD_DIM].astype(F32) for weight in weights]
-    lanes = []
-    for place_c in range(nc):
-        chosen = 0.0
-        for k, part in enumerate(extras):
-            chosen = chosen + jnp.where((c ^ k) == place_c, part[:, :rows], 0.0)
-        lanes.append(chosen)
-    ordered = jnp.concatenate(lanes, axis=1)
-    for i, (dx, dy) in enumerate(SQUARE):
-        start = column_of(x ^ dx, z, y ^ dy)
-        gains[:, pl.ds(start, HEAD_DIM)] = jnp.concatenate(
-            [ordered[4 * i : 4 * i + 4], jnp.zeros((4, HEAD_DIM), F32)], axis=0
-        )
-        columns[:, i * HEAD_DIM : (i + 1) * HEAD_DIM] = x_all[:, pl.ds(start, HEAD_DIM)]
-        for k, weight in enumerate(weights):
-            at = pl.multiple_of(i * HEAD_DIM + (c ^ k) * rows, rows)
-            w_part[pl.ds(at, rows)] = weight[i * rows : (i + 1) * rows]
+    rows = (weights[0].shape[0] - EXTRA) // (4 * GROUP)
     copies = Copies(sems)
-    put = [copies.start(w_part, w_rows)]
+    put = []
+    for slot, s in enumerate(places):
+        blocks = weights[slot * nc : (slot + 1) * nc]
+        z = ring(r, s)
+        extras = [block[4 * GROUP * rows :, :HEAD_DIM].astype(F32) for block in blocks]
+        lanes = []
+        for place_c in range(nc):
+            chosen = 0.0
+            for k, part in enumerate(extras):
+                chosen = chosen + jnp.where((c ^ k) == place_c, part[:, :rows], 0.0)
+            lanes.append(chosen)
+        ordered = jnp.concatenate(lanes, axis=1)
+        base = slot * GROUP * HEAD_DIM
+        for i, (dx, dy) in enumerate(SQUARE):
+            start = column_of(x ^ dx, z, y ^ dy)
+            gains[:, pl.ds(start, HEAD_DIM)] = jnp.concatenate(
+                [ordered[4 * i : 4 * i + 4], jnp.zeros((4, HEAD_DIM), F32)], axis=0
+            )
+            to = base + i * HEAD_DIM
+            columns[:, to : to + HEAD_DIM] = x_all[:, pl.ds(start, HEAD_DIM)]
+            for k, block in enumerate(blocks):
+                at = pl.multiple_of(to + (c ^ k) * rows, rows)
+                for j in range(3):
+                    got = (j * GROUP + i) * rows
+                    lanes = slice(j * HEADS, (j + 1) * HEADS)
+                    w_part[pl.ds(at, rows), lanes] = block[got : got + rows]
+                got = (3 * GROUP + i) * rows
+                at = pl.multiple_of(z * HEAD_DIM + (c ^ k) * rows, rows)
+                lanes = slice(i * HEADS, (i + 1) * HEADS)
+                out_w[pl.ds(at, rows), lanes] = block[got : got + rows]
+        put.append(
+            copies.start(w_part.at[pl.ds(base, GROUP * HEAD_DIM)], w_rows[slot])
+        )
     step = HEADS // 2
     for part in range(6):
         at = slice(part * step, (part + 1) * step)
         result = nn(columns[...], w_part[:, at])
-        if s == 0:
-            total[:, at] = result
-        elif s < NZ - 1:
-            total[:, at] += result
-        else:
+        if last:
             result = before[:, at] + result
             out = (query, key, value)[part // 2]
             out[:, (part % 2) * step : (part % 2 + 1) * step] = result.astype(out.dtype)
-    if s == NZ - 1:
+        else:
+            total[:, at] = result
+    if last:
         stats[...] = row_stats(query[...] * query[...], key[...] * key[...])
         put += [
             copies.start(*pair)
-            for pair in ((query, query_h), (key, key_h), (value, value_h))
+            for pair in ((query, query_h), (key, key_h), (value, value_h), (out_w, out_kept))
         ]
     finish(put)
 
@@ -258,7 +256,7 @@
 
 def attend_kernel(pos, *refs):
     x, _, y, _ = place(pos)
-    stats, refs = refs[:GROUP], refs[GROUP:]
+    stats, *refs = refs
     lengths, gains, cosine, sine, query, key, value, out_w, *refs = refs
     query_out, key_out, attended_out, scales, *refs = refs
     pieces, refs = refs[:GROUP], refs[GROUP:]
@@ -267,7 +265,7 @@
     tok = query.shape[0] // GROUP
     span = NX * tok
     width = out_w.shape[1]
-    scale = lax.rsqrt(group_total(stats, tok) / width + EPSILON)
+    scale = lax.rsqrt(stats[...] / width + EPSILON)
     scales[...] = scale
     for seq in range(NY):
         at = slice(seq * span, (seq + 1) * span)
@@ -355,35 +353,22 @@
     grad_gain[...] = jnp.broadcast_to(by_gain, grad_gain.shape)
 
 
-def out_back_kernel(nc, pos, *refs):
+def attend_back_kernel(pos, *refs):
+    lengths, scales, gains, cosine, sine, out_w, *refs = refs
     blocks, refs = refs[:GROUP], refs[GROUP:]
-    attended, branch_all, *outs, sums = refs
-    _, r, _, c = place(pos)
-    tok = blocks[0].shape[0]
-    rows = outs[0].shape[0] // NZ
-    for i, block in enumerate(TOKEN_BLOCKS):
-        branch_all[i * tok : (i + 1) * tok] = blocks[SQUARE.index(block)][...]
-    for s in range(NZ):
-        start = pl.multiple_of(ring(r, s) * HEAD_DIM, HEAD_DIM)
-        sums[...] = tn(attended[:, pl.ds(start, HEAD_DIM)], branch_all[...]).astype(BF16)
-        for k in range(nc):
-            at = pl.ds(pl.multiple_of((c ^ k) * rows, rows), rows)
-            outs[k][s * rows : (s + 1) * rows] = sums[at, :]
-
-
-def attend_back_kernel(pos, *refs):
-    lengths, scales, gains, cosine, sine, branch_all, out_w, *refs = refs
     held, refs = refs[:5], refs[5:]
-    query_out, key_out, grad_value, stats, head_gains, *refs = refs
+    query_out, key_out, grad_value, stats, head_gains, branch_all, *refs = refs
     query_r, key_r, value, query, key, *refs = refs
     grad_query, grad_key, grad_att, sems = refs
     x, _, y, _ = place(pos)
-    tok = branch_all.shape[0] // GROUP
+    tok = blocks[0].shape[0]
     span = NX * tok
     copies = Copies(sems)
     later = [
         copies.start(*pair) for pair in zip(held, (query_r, key_r, value, query, key))
     ]
+    for i, block in enumerate(TOKEN_BLOCKS):
+        branch_all[i * tok : (i + 1) * tok] = blocks[SQUARE.index(block)][...]
     for half in range(2):
         lanes = slice(half * (HEADS // 2), (half + 1) * (HEADS // 2))
         grad_att[:, lanes] = nt(branch_all[...], out_w[lanes, :]).astype(BF16)
@@ -418,11 +403,10 @@
 
 
 def project_back_kernel(*refs):
-    stats, refs = refs[:GROUP], refs[GROUP:]
+    stats, *refs = refs
     scales, grad_query, grad_key, grad_value, query, key, grads = refs
-    tok = query.shape[0] // GROUP
     width = NX * NY * HEADS
-    means = jnp.transpose(group_total(stats, tok) / width)
+    means = jnp.transpose(stats[...] / width)
     columns = jnp.transpose(scales[...])
     for row, (grad, raw) in enumerate(((grad_query, query), (grad_key, key))):
         scale = columns[:, 4 * row : 4 * row + 1]
@@ -455,11 +439,11 @@
         weight_back_part(nc, s, i, pos, *refs)
 
 
-def weight_back_part(nc, s, slot, pos, x_all, grads, attn_gain, mlp_gain, head_gains, *refs):
-    *outs, columns, sums = refs
+def weight_back_part(nc, s, slot, pos, x_all, grads, attended, branch_all, *refs):
+    attn_gain, mlp_gain, head_gains, *outs, columns, sums, out_sums = refs
     x, r, y, c = place(pos)
     rows = HEAD_DIM // nc
-    base = slot * (GROUP * rows + EXTRA)
+    base = slot * (4 * GROUP * rows + EXTRA)
     z = ring(r, s)
     gains = []
     for i, (dx, dy) in enumerate(SQUARE):
@@ -477,31 +461,43 @@
     for part in range(3):
         lanes = slice(part * step, (part + 1) * step)
         sums[:, lanes] = tn(columns[...], grads[:, lanes]).astype(BF16)
+    heads = pl.ds(pl.multiple_of(z * HEAD_DIM, HEAD_DIM), HEAD_DIM)
+    out_sums[...] = tn(attended[:, heads], branch_all[...]).astype(BF16)
     for k, out in enumerate(outs):
         for i in range(GROUP):
             start = pl.multiple_of(i * HEAD_DIM + (c ^ k) * rows, rows)
-            out[base + i * rows : base + (i + 1) * rows] = sums[pl.ds(start, rows), :]
+            for j in range(3):
+                at = base + (j * GROUP + i) * rows
+                lanes = slice(j * HEADS, (j + 1) * HEADS)
+                out[at : at + rows] = sums[pl.ds(start, rows), lanes]
+            start = pl.multiple_of((c ^ k) * rows, rows)
+            at = base + (3 * GROUP + i) * rows
+            lanes = slice(i * HEADS, (i + 1) * HEADS)
+            out[at : at + rows] = out_sums[pl.ds(start, rows), lanes]
         chosen = 0.0
         for place_c in range(nc):
             part = gains[:, place_c * rows : (place_c + 1) * rows]
             chosen = chosen + jnp.where((c ^ k) == place_c, part, 0.0)
         chosen = jnp.concatenate([chosen, jnp.zeros((EXTRA, HEAD_DIM - rows), F32)], axis=1)
-        put_extra(out, base + GROUP * rows, chosen)
+        put_extra(out, base + 4 * GROUP * rows, chosen)
 
 
 def collect_kernel(count, *refs):
-    parts, outs = refs[:count], refs[count:]
-    rows = (parts[0].shape[0] - EXTRA) // GROUP
-
-    def total(at, lanes=slice(None)):
-        result = parts[0][at, lanes].astype(F32)
+    parts, (grad_wo, *outs) = refs[:count], refs[count:]
+    rows = (parts[0].shape[0] - EXTRA) // (4 * GROUP)
+
+    def total(at, height, lanes=slice(None)):
+        result = parts[0][at : at + height, lanes].astype(F32)
         for part in parts[1:]:
-            result = result + part[at, lanes].astype(F32)
+            result = result + part[at : at + height, lanes].astype(F32)
         return result
 
-    extra = total(slice(GROUP * rows, GROUP * rows + EXTRA), slice(0, HEAD_DIM))
+    extra = total(4 * GROUP * rows, EXTRA, slice(0, HEAD_DIM))
     for i, out in enumerate(outs):
-        out[:rows] = total(slice(i * rows, (i + 1) * rows)).astype(BF16)
+        for j in range(3):
+            part = total((j * GROUP + i) * rows, rows)
+            out[:rows, j * HEADS : (j + 1) * HEADS] = part.astype(BF16)
+        grad_wo[:, i * HEADS : (i + 1) * HEADS] = total((3 * GROUP + i) * rows, rows)
         put_extra(out, rows, extra_rows([extra[4 * i : 4 * i + 4]]))
 
 
@@ -633,32 +629,11 @@
             second[0].astype(F32) + near[1].astype(F32) + second_c.astype(F32),
         )
 
-    def ring_gather(block):
-        blocks = [block]
-        for _ in range(NZ - 1):
-            blocks.append(send(blocks[-1], r=-1))
-        return blocks
-
     def core_gather(block):
         return [block] + [send(block, c=k) for k in range(1, nc)]
 
     def core_parts(parts):
         return [parts[0]] + [send(parts[k], c=k) for k in range(1, nc)]
-
-    def ring_parts(part_of, hold=None):
-        moving, sent = [], []
-        for s in list(range(1, NZ)) + [0]:
-            parts = part_of(s)
-            if moving and hold is not None:
-                moving = [after(moving[0], hold(s))]
-            parts = parts + moving
-            if s == 0:
-                return parts, sent
-            total = parts[0].astype(F32)
-            for part in parts[1:]:
-                total = total + part.astype(F32)
-            sent.append(total.astype(BF16))
-            moving = [send(sent[-1], r=-1)]
 
     def body(
         layer_input,
@@ -691,8 +666,19 @@
         by_token = shaped((8, group_tok), F32)
         tokens_shape = shaped((tok, width))
         tokens_wide = shaped((tok, width), F32)
-        message = shaped((GROUP * rows + EXTRA, 3 * HEADS))
+        message = shaped((4 * GROUP * rows + EXTRA, HEADS))
         piece = shaped((rows + EXTRA, 3 * HEADS))
+
+        def group_sum(stats, *ready):
+            blocks = [stats[:, i * tok : (i + 1) * tok] for i in range(GROUP)]
+            for flip, way in ((1, {"x": 1}), (2, {"y": 1})):
+                total = jnp.concatenate(blocks, axis=1)
+                if flip == 2 and ready:
+                    total = after(total, ready)
+                got = send(total, **way)
+                got = [got[:, i * tok : (i + 1) * tok] for i in range(GROUP)]
+                blocks = [block + got[i ^ flip] for i, block in enumerate(blocks)]
+            return jnp.concatenate(blocks, axis=1)
 
         def dma(count):
             return pltpu.SemaphoreType.DMA((count,))
@@ -706,96 +692,75 @@
             each([piece] * GROUP, VMEM),
             [(pos, SMEM), (gains, VMEM), (w_query, auto), (w_key, auto), (w_value, auto)],
         )
-        out_ring = [w_output, send(after(w_output, pieces), r=-1)]
         down_rows = w_down.shape[0] // 2
-        down_halves = after(w_down, pieces)
-        down_halves = down_halves[:down_rows], down_halves[down_rows:]
+        down_halves = w_down[:down_rows], w_down[down_rows:]
         far_down = send(down_halves[0], x=1), send(down_halves[1], y=1)
-        received = square(pieces)
+        received = after(square(pieces), far_down)
         own_rows, lengths_row = run(
             join_kernel,
             [(message, VMEM), (shaped((8, HEAD_DIM), F32), VMEM)],
-            each(received, VMEM),
-        )
+            each((*received, w_output), VMEM),
+        )
+        lane = jnp.arange(HEAD_DIM)[None, :]
+        row = jnp.arange(NX * tok)[:, None]
+        row = jnp.where(row < tok, x * tok + row, (1 - x) * tok + row - tok).astype(F32)
         half = HEAD_DIM // 2
-        order = jnp.concatenate([x * tok + jnp.arange(tok), (1 - x) * tok + jnp.arange(tok)])
-        frequency = jnp.exp(
-            jnp.arange(half, dtype=F32) * (-2.0 * math.log(500000.0) / HEAD_DIM)
-        )
-        angles = order.astype(F32)[:, None] * frequency[None, :]
-        cosine = jnp.tile(jnp.cos(angles), (1, 2))
-        sine = jnp.sin(angles)
-        sine = jnp.concatenate([-sine, sine], axis=1)
-        tokens = square([after(inputs, own_rows)] * GROUP)
+        frequency = jnp.exp((lane % half).astype(F32) * (-2.0 * math.log(500000.0) / HEAD_DIM))
+        cosine = jnp.cos(row * frequency)
+        sine = jnp.sin(row * jnp.where(lane < half, -frequency, frequency))
         w_ring = [own_rows, send(own_rows, r=-1)]
-        out_ring.append(send(out_ring[1], r=-1))
-        ready = cosine, sine, far_down, out_ring[2], tokens[1], tokens[2]
-        w_ring.append(send(after(w_ring[1], ready), r=-1))
+        far_gate = send(after(w_gate, own_rows), x=1)
+        far_up = send(after(w_up, own_rows), y=1)
+        from_x = send(after(inputs, far_gate), x=1)
+        from_y = send(after(inputs, far_up), y=1)
+        half_tok = tok // 2
+        from_xy = send(from_x[:half_tok], y=1), send(from_y[half_tok:], x=1)
+        near_gate = send(after(w_gate, from_xy[0]), y=1)
+        near_up = send(after(w_up, from_xy[1]), x=1)
+        w_ring.append(send(after(w_ring[1], cosine, sine, far_gate, far_up), r=-1))
+        w_ring.append(send(after(w_ring[2], from_xy), r=-1))
         x_all, x_kept = run(
             gather_kernel,
             [(shaped((group_tok, width)), VMEM), (shaped((group_tok, width)), HBM)],
-            each(tokens, VMEM),
+            each([inputs, from_x, from_y, *from_xy], VMEM),
             scratch_shapes=[pltpu.SemaphoreType.DMA],
         )
-        far_gate = send(after(w_gate, x_all), x=1)
-        far_up = send(after(w_up, x_all), y=1)
-        near_gate = send(after(w_gate, far_gate), y=1)
-        near_up = send(after(w_up, far_up), x=1)
-        total, gains = None, None
-        totals = []
-        w_parts = []
+        w_ring[3] = after(w_ring[3], near_gate, near_up)
+        w_blocks = [core_gather(block) for block in w_ring]
         w_shape = shaped((GROUP * HEAD_DIM, 3 * HEADS))
-        for s in range(NZ):
-            if s == NZ - 1:
-                w_ring.append(send(after(w_ring[2], totals[1]), r=-1))
-                out_ring.append(send(after(out_ring[2], w_ring[3]), r=-1))
-            blocks = core_gather(w_ring[s])
-            ins = [(pos, SMEM), (x_all, VMEM), *each(blocks, VMEM)]
-            outs = [(wide_small, VMEM), (w_shape, HBM)]
-            aliases = {}
-            if s > 0:
-                if s == NZ - 1:
-                    total, gains = after((total, gains), far_gate, far_up)
-                aliases = {len(ins) + 1: 1 if s < NZ - 1 else 0}
-                ins += [(total, VMEM), (gains, VMEM)]
-            if s < NZ - 1:
-                outs = [(shaped((group_tok, 3 * HEADS), F32), VMEM)] + outs
-                if s > 0:
-                    aliases[len(ins) - 2] = 0
-            else:
-                outs += [(by_head_wide, VMEM), (by_head_wide, VMEM), (by_head, VMEM)]
-                outs += [(by_head_wide, HBM), (by_head_wide, HBM), (by_head, HBM)]
-                outs += [(by_token, VMEM)]
-            results = run(
-                functools.partial(project_kernel, nc, s),
-                outs,
+        by_three = shaped((group_tok, 3 * HEADS), F32)
+        out_shape = shaped((HEADS, width))
+
+        def project(places, blocks, before, outs):
+            ins = [(pos, SMEM), (x_all, VMEM), *each(blocks, VMEM), *each(before, VMEM)]
+            depth = len(places) * GROUP * HEAD_DIM
+            return run(
+                functools.partial(project_kernel, nc, places),
+                [(wide_small, VMEM), (out_shape, VMEM)] + [(w_shape, HBM)] * len(places) + outs,
                 ins,
-                input_output_aliases=aliases,
-                scratch_shapes=([pltpu.VMEM((8, HEAD_DIM), F32)] if s == NZ - 1 else [])
-                + [
-                    pltpu.VMEM((group_tok, GROUP * HEAD_DIM), BF16),
-                    pltpu.VMEM((GROUP * HEAD_DIM, 3 * HEADS), BF16),
-                    dma(4),
+                limit=16,
+                input_output_aliases={len(ins) - 2: 0, len(ins) - 1: 1} if before else {},
+                scratch_shapes=[
+                    pltpu.VMEM((group_tok, depth), BF16),
+                    pltpu.VMEM((depth, 3 * HEADS), BF16),
+                    dma(len(places) + 4),
                 ],
             )
-            if s < NZ - 1:
-                total, gains, w_part = results
-                totals.append(total)
-            else:
-                gains, w_part, query, key, value, query_h, key_h, value_h, stats = results
-            w_parts.append(w_part)
-        out_w, out_kept = run(
-            functools.partial(out_rows_kernel, nc),
-            [(shaped((HEADS, width)), VMEM), (shaped((HEADS, width)), HBM)],
-            [
-                (pos, SMEM),
-                *each([part for block in out_ring for part in core_gather(block)], VMEM),
-            ],
-            scratch_shapes=[pltpu.SemaphoreType.DMA],
-        )
-        group_stats = square([stats] * GROUP)
-        last_gate = send(after(far_gate, group_stats), y=1)
-        last_up = send(after(far_up, group_stats), x=1)
+
+        blocks = w_blocks[0] + w_blocks[1] + w_blocks[2]
+        gains, out_w, *w_parts, total = project((0, 1, 2), blocks, (), [(by_three, VMEM)])
+        gains, out_w, w_part, query, key, value, query_h, key_h, value_h, out_kept, stats = project(
+            (3,),
+            w_blocks[3],
+            (total, gains, out_w),
+            [(by_head_wide, VMEM), (by_head_wide, VMEM), (by_head, VMEM)]
+            + [(by_head_wide, HBM), (by_head_wide, HBM), (by_head, HBM)]
+            + [(out_shape, HBM), (by_token, VMEM)],
+        )
+        w_parts.append(w_part)
+        group_stats = group_sum(stats, near_gate, near_up)
+        last_gate = send(after(far_gate, group_stats, near_gate), y=1)
+        last_up = send(after(far_up, group_stats, near_up), x=1)
         gate_w = [w_gate, near_gate, far_gate, last_gate]
         up_w = [w_up, far_up, near_up, last_up]
 
@@ -804,7 +769,7 @@
             [(by_head, HBM)] * 3 + [(by_token, VMEM)] + [(tokens_shape, VMEM)] * GROUP,
             [
                 (pos, SMEM),
-                *each(group_stats, VMEM),
+                (group_stats, VMEM),
                 *each((lengths_row, gains, cosine, sine), VMEM),
                 *each((query, key, value, out_w), VMEM),
             ],
@@ -854,19 +819,29 @@
             )
             return results[:8], core_parts(results[8:])
 
-        kept = None
-        sums = []
-        for s, block in enumerate(ring_gather(mlp_in)):
-            kept, parts = mlp_call(
-                mlp_forward_kernel, s, block, (), (half_width, half_width), kept
-            )
-            sums.append(parts)
-
-        def hold(s):
-            return sums[(s + 1) % NZ][0]
+        def summed(parts):
+            total = parts[0].astype(F32)
+            for part in parts[1:]:
+                total = total + part.astype(F32)
+            return total
+
+        def mlp_pass(kernel, block, extra, kept_columns):
+            near = send(block, r=-1)
+            kept, first = mlp_call(kernel, 1, near, extra, kept_columns, None)
+            middle = send(near, r=-1)
+            moving = send(summed(first).astype(BF16), r=-1)
+            kept, own = mlp_call(kernel, 0, block, extra, kept_columns, kept)
+            far = send(after(middle, first[0]), r=-1)
+            kept, second = mlp_call(kernel, 2, middle, extra, kept_columns, kept)
+            far = after(far, moving)
+            kept, third = mlp_call(kernel, 3, far, extra, kept_columns, kept)
+            sent = [summed(second + [moving]).astype(BF16)]
+            sent.append(summed(third + [send(sent[0], r=-1)]).astype(BF16))
+            return kept, own + [send(sent[1], r=-1)], sent
+
+        kept, parts, _ = mlp_pass(mlp_forward_kernel, mlp_in, (), (half_width, half_width))
 
         products, by_gate, by_up, mlp_all = kept[0:2], kept[2:4], kept[4:6], kept[6:8]
-        parts, _ = ring_parts(lambda s: sums[s], hold)
         output, grad_mlp, grad_gain_mlp = run(
             functools.partial(mlp_kernel, len(parts)),
             [(tokens_shape, auto), (tokens_shape, VMEM), (wide_small, VMEM)],
@@ -879,15 +854,9 @@
             ],
             scratch_shapes=[held(tokens_wide)] * 2,
         )
-        kept = None
-        sums = []
-        for s, block in enumerate(ring_gather(grad_mlp)):
-            kept, parts = mlp_call(
-                mlp_back_kernel, s, block, (*by_gate, *by_up), (quarter,) * 4, kept
-            )
-            sums.append(parts)
+        extra = *by_gate, *by_up
+        kept, parts, sent = mlp_pass(mlp_back_kernel, grad_mlp, extra, (quarter,) * 4)
         grad_gates, grad_ups, grad_all = kept[0:2], kept[2:4], kept[4:8]
-        parts, sent = ring_parts(lambda s: sums[s], hold)
         grad_hidden, grad_branch, grad_gain_attn = run(
             functools.partial(branch_back_kernel, len(parts)),
             [(tokens_wide, auto), (tokens_shape, VMEM), (wide_small, VMEM)],
@@ -904,39 +873,20 @@
         def products_of(left, right):
             return [tn(left[dx], right[dy]).astype(BF16) for dx, dy in SQUARE]
 
-        grad_all = after(grad_all, sent[1])
+        grad_all = after(grad_all, sent[0])
         wd_pair = products_of(grad_all[0::2], products), products_of(grad_all[1::2], products)
         wd_far = scatter_far(*wd_pair)
         wd_near = scatter_near(*after(wd_pair, wd_far))
-        grad_branch = after(grad_branch, wd_far)
-        grad_wd = jnp.concatenate(scatter_rest(*wd_pair, wd_far, wd_near), axis=0)
-        mlp_all = after(mlp_all, sent[2])
+        grad_branch = after(grad_branch, wd_near)
+        mlp_all = after(mlp_all, sent[1])
         grad_wg = products_of(mlp_all, grad_gates)
         grad_wu = products_of(mlp_all, grad_ups)
 
         blocks = square([grad_branch] * GROUP)
-        w_pair = after((grad_wg, grad_wu), blocks)
-        w_far = scatter_far(*w_pair)
-        branch_all, *picked = run(
-            functools.partial(out_back_kernel, nc),
-            [(shaped((group_tok, width)), VMEM)] + [(shaped((NZ * rows, width)), VMEM)] * nc,
-            [(pos, SMEM), *each(blocks, VMEM), (attended, VMEM)],
-            scratch_shapes=[pltpu.VMEM((HEAD_DIM, width), BF16)],
-        )
-        picked = core_parts(picked)
-
-        def out_part(s):
-            return [part[s * rows : (s + 1) * rows] for part in picked]
-
-        def summed(parts):
-            total = parts[0].astype(F32)
-            for part in parts[1:]:
-                total = total + part.astype(F32)
-            return total
-
-        out_moving = send(summed(out_part(1)).astype(BF16), r=-1)
-        branch_all = after(branch_all, w_pair)
-        grad_query, grad_key, grad_value, stats, head_gains = run(
+        w_pair = grad_wg, grad_wu
+        blocks = after(blocks, w_pair)
+        w_far = scatter_far(*after(w_pair, blocks))
+        grad_query, grad_key, grad_value, stats, head_gains, branch_all = run(
             attend_back_kernel,
             [
                 (by_head_wide, VMEM),
@@ -944,10 +894,11 @@
                 (by_head, VMEM),
                 (by_token, VMEM),
                 (shaped((8, HEADS), F32), VMEM),
+                (shaped((group_tok, width)), VMEM),
             ],
             [
                 (pos, SMEM),
-                *each((lengths_row, scales, gains, cosine, sine, branch_all, out_kept), VMEM),
+                *each((lengths_row, scales, gains, cosine, sine, out_kept, *blocks), VMEM),
                 *each((query_r, key_r, value_h, query_h, key_h), HBM),
             ],
             limit=16,
@@ -967,27 +918,27 @@
             project_back_kernel,
             [(shaped((group_tok, 3 * HEADS)), VMEM)],
             [
-                *each(square([stats] * GROUP), VMEM),
+                (after(group_sum(stats), w_far), VMEM),
                 (scales, VMEM),
                 *each((grad_query, grad_key, grad_value, query_h, key_h), VMEM),
             ],
         )
-        grads = after(grads, out_moving)
         w_near = scatter_near(*after(w_pair, grads))
 
         def weight_parts(places):
             height = message.shape[0]
             results = run(
                 functools.partial(weight_back_kernel, nc, places),
-                [(shaped((len(places) * height, 3 * HEADS)), VMEM)] * nc,
+                [(shaped((len(places) * height, HEADS)), VMEM)] * nc,
                 [
                     (pos, SMEM),
-                    (x_kept, VMEM),
-                    *each((grads, grad_gain_attn, grad_gain_mlp, head_gains), VMEM),
+                    *each((x_kept, grads, attended, branch_all), VMEM),
+                    *each((grad_gain_attn, grad_gain_mlp, head_gains), VMEM),
                 ],
                 scratch_shapes=[
                     pltpu.VMEM((group_tok, GROUP * HEAD_DIM), BF16),
                     pltpu.VMEM((GROUP * HEAD_DIM, 3 * HEADS), BF16),
+                    pltpu.VMEM((HEAD_DIM, width), BF16),
                 ],
             )
             results = core_parts(results)
@@ -997,21 +948,20 @@
             ]
 
         (first,) = weight_parts((1,))
-        out_second = summed(out_part(2) + [out_moving]).astype(BF16)
-        w_moving = send(after(summed(first).astype(BF16), w_far, out_second), r=-1)
-        out_moving = send(out_second, r=-1)
+        w_moving = send(after(summed(first).astype(BF16), w_far), r=-1)
+        grads = after(grads, first)
         second, third, own = weight_parts((2, 3, 0))
-        out_third = summed(out_part(3) + [out_moving]).astype(BF16)
         sent = summed(second + [w_moving]).astype(BF16)
-        w_moving = send(after(sent, own, out_third, w_near), r=-1)
-        out_moving = send(out_third, r=-1)
+        w_moving = send(after(sent, own, w_near), r=-1)
         grad_wg, grad_wu = scatter_rest(*w_pair, *after((w_far, w_near), sent))
+        wd_far, wd_near = after((wd_far, wd_near), grad_wg, grad_wu)
+        grad_wd = jnp.concatenate(scatter_rest(*wd_pair, wd_far, wd_near), axis=0)
         sent = summed(third + [w_moving]).astype(BF16)
         w_moving = send(sent, r=-1)
         parts = own + [w_moving]
-        messages = run(
+        grad_wo, *messages = run(
             functools.partial(collect_kernel, len(parts)),
-            [(piece, VMEM)] * GROUP,
+            [(shaped((rows, width), F32), auto)] + [(piece, VMEM)] * GROUP,
             each(parts, auto),
         )
         grad_wq, grad_wk, grad_wv, total_gains = run(
@@ -1019,15 +969,13 @@
             [(shaped((rows, width), F32), auto)] * 3 + [(shaped((8, HEAD_DIM), F32), VMEM)],
             [(pos, SMEM), *each(square(messages), auto)],
         )
-        grad_wo = summed(out_part(0) + [out_moving])
-
         parts = run(
             input_back_kernel,
             [(tokens_shape, VMEM)] * GROUP,
             [(pos, SMEM), (after(grads, sent), VMEM), *each(w_parts, VMEM)],
             scratch_shapes=[pltpu.VMEM((group_tok, GROUP * HEAD_DIM), BF16)],
         )
-        grad_x = summed([grad_hidden, *square(parts)])
+        grad_x = summed([grad_hidden, *square(after(parts, messages))])
 
         return (
             output[None],

time: 567 us -> 538 us (0.949)
  local copies, waits for them, and re-layouts: 22.6 us -> 7.02 us
  Pallas kernels: 97 us -> 87.9 us
  waiting for transfers between devices: 312 us -> 321 us
  starting transfers between devices: 97.3 us -> 89.5 us
    unnamed x100 -> x50, local copies, waits for them, and re-layouts: 19.2 us -> 4.81 us
    ppermute x99 -> x87, waiting for transfers between devices: 312 us -> 321 us  [send(): return lax.ppermute(value, AXES, pairs)]
    pallas_call x28 -> x24, Pallas kernels: 97 us -> 87.9 us  [run(): pl.pallas_call(body, grid=(1,), out_shape=[pltpu.HBM(out.shape, out.dtype...]
    ppermute x99 -> x87, starting transfers between devices: 97.3 us -> 89.5 us  [send(): return lax.ppermute(value, AXES, pairs)]
  transfers between devices with their start and end apart: 99 -> 87, of which waited for: 48 -> 45; matrix products, arithmetic and copies ran while one was open for 6% -> 5% of each run, Pallas kernels for 15% -> 14%
where the time goes in v4:
time: 538 us; the launch traced here: 535 us
  waiting for transfers between devices  321 us (60%)
  starting transfers between devices  89.5 us (17%)
  Pallas kernels  87.9 us (16%)
  matrix products  16.1 us (3%)
  other arithmetic  11.1 us (2%)
  local copies, waits for them, and re-layouts  7.02 us (1%)
    ppermute x87, waiting for transfers between devices, send(): return lax.ppermute(value, AXES, pairs)  321 us
    ppermute x87, starting transfers between devices, send(): return lax.ppermute(value, AXES, pairs)  89.5 us
    pallas_call x24, Pallas kernels, run(): pl.pallas_call(body, grid=(1,), out_shape=[pltpu.HBM(out.shape, out.dtype...  87.9 us
    dot_general x16, matrix products, tn(): lax.dot_general(left, right, (((0,), (0,)), ((), ())), preferred_element_...  16.1 us
  transfers between devices with their start and end apart: 87, of which 45 were waited for; matrix products, arithmetic and copies ran while one was open for 5% of the time, Pallas kernels for 14%

profile of v4, /device:TPU:0, one launch (start us, length us, event | category | flops | bytes accessed | tf_op | source)
XLA Modules:
  0.0 535.2 jit_solution(10568798281625313705)
XLA Ops:
  2.1 3.0 collective-permute-start.3
  12.4 2.9 collective-permute-start.2
  15.3 13.8 %collective-permute-done.refs_1_ = bf16[80,1536]{1,0:T(8,128)(2,1)S(1)} collective-permute-done((bf16[80,1536]{1,0:T(8,128)(2,1)S(1)}, bf16[80,1536]{1,0:T(8,128)(2,1)S(1)}, u32[]{:S(2)}, u32[]{:S(2)}) %collective-permute-start) | collective-permute-done | bytes 245792 | tf_op jit(solution)/shard_map/ppermute | solution.py:601
  30.1 2.6 collective-permute-start.11
  35.7 20.5 %collective-permute-done.5.refs_4_ = bf16[1024,512]{1,0:T(8,128)(2,1)S(1)} collective-permute-done((bf16[1024,512]{1,0:T(8,128)(2,1)S(1)}, bf16[1024,512]{1,0:T(8,128)(2,1)S(1)}, u32[]{:S(2)}, u32[]{:S(2)}) %collective-permute-start.5) | collective-permute-done | bytes 1048608 | tf_op jit(solution)/shard_map/ppermute | solution.py:601
  60.2 10.3 %collective-permute-done.6.refs_1_ = bf16[128,2048]{1,0:T(8,128)(2,1)S(1)} collective-permute-done((bf16[128,2048]{1,0:T(8,128)(2,1)}, bf16[128,2048]{1,0:T(8,128)(2,1)S(1)}, u32[]{:S(2)}, u32[]{:S(2)}) %collective-permute-start.6) | collective-permute-done | bytes 524320 | tf_op jit(solution)/shard_map/ppermute | solution.py:601
  70.7 2.0 collective-permute-done.8.refs_2_
  73.5 3.4 collective-permute-done.9.refs_3_
  76.9 2.3 collective-permute-done.10.refs_4_
  79.2 2.0 collective-permute-done.12.refs_4_
  81.2 2.1 collective-permute-start.13
  85.1 19.6 %collective-permute-done.14.refs_3_ = bf16[1024,512]{1,0:T(8,128)(2,1)S(1)} collective-permute-done((bf16[1024,512]{1,0:T(8,128)(2,1)S(1)}, bf16[1024,512]{1,0:T(8,128)(2,1)S(1)}, u32[]{:S(2)}, u32[]{:S(2)}) %collective-permute-start.14) | collective-permute-done | bytes 1048608 | tf_op jit(solution)/shard_map/ppermute | solution.py:601
  107.7 5.8 %shard_map.240 = (f32[8,2048]{1,0:T(8,128)S(1)}, bf16[512,2048]{1,0:T(8,128)(2,1)S(1)}, bf16[512,1536]{1,0:T(8,128)(2,1)}, bf16[512,1536]{1,0:T(8,128)(2,1)}, bf...) custom-call(s32[5]{0:T(128)S(1)} %stack.34.pos, bf16[512,2048]{1,0:T(8,128)(2,1)S(1)} %get-tuple-element.233.x_all, ...), custom_call_target="tpu_custom_call" | custom-call | tf_op jit(solution)/shard_map/pallas_call | solution.py:50
  113.5 3.8 shard_map.241
  118.7 2.3 collective-permute-done.20
  122.4 2.5 collective-permute-done.21
  127.6 6.2 %shard_map.242 = (bf16[512,512]{1,0:T(8,128)(2,1)}, bf16[512,512]{1,0:T(8,128)(2,1)}, bf16[512,512]{1,0:T(8,128)(2,1)}, f32[8,512]{1,0:T(8,128)S(1)}, bf16[128,2...) custom-call(s32[5]{0:T(128)S(1)} %stack.34.pos, ...), custom_call_target="tpu_custom_call" | custom-call | tf_op jit(solution)/shard_map/pallas_call | solution.py:50
  133.8 13.9 %collective-permute-done.22.refs_5_ = bf16[1024,512]{1,0:T(8,128)(2,1)S(1)} collective-permute-done((bf16[1024,512]{1,0:T(8,128)(2,1)S(1)}, bf16[1024,512]{1,0:T(8,128)(2,1)S(1)}, u32[]{:S(2)}, u32[]{:S(2)}) %collective-permute-start.22) | collective-permute-done | bytes 1048608 | tf_op jit(solution)/shard_map/ppermute | solution.py:601
  153.2 10.5 %collective-permute-done.24.refs_1_ = bf16[128,2048]{1,0:T(8,128)(2,1)S(1)} collective-permute-done((bf16[128,2048]{1,0:T(8,128)(2,1)S(1)}, bf16[128,2048]{1,0:T(8,128)(2,1)S(1)}, u32[]{:S(2)}, u32[]{:S(2)}) %collective-permute-start.24) | collective-permute-done | bytes 524320 | tf_op jit(solution)/shard_map/ppermute | solution.py:601
  164.6 8.0 %collective-permute-done.26.refs_3_ = bf16[128,2048]{1,0:T(8,128)(2,1)S(1)} collective-permute-done((bf16[128,2048]{1,0:T(8,128)(2,1)S(1)}, bf16[128,2048]{1,0:T(8,128)(2,1)S(1)}, u32[]{:S(2)}, u32[]{:S(2)}) %collective-permute-start.26) | collective-permute-done | bytes 524320 | tf_op jit(solution)/shard_map/ppermute | solution.py:601
  178.4 4.9 collective-permute-done.32.refs_0_
  183.3 5.9 %collective-permute-done.28.refs_11_ = bf16[512,512]{1,0:T(8,128)(2,1)S(1)} collective-permute-done((bf16[512,512]{1,0:T(8,128)(2,1)S(1)}, bf16[512,512]{1,0:T(8,128)(2,1)S(1)}, u32[]{:S(2)}, u32[]{:S(2)}) %collective-permute-start.28) | collective-permute-done | bytes 524320 | tf_op jit(solution)/shard_map/ppermute | solution.py:601
  190.6 4.5 collective-permute-done.29.refs_15_
  196.5 5.2 shard_map.244
  204.8 5.1 shard_map.245
  209.9 5.2 shard_map.246
  217.0 10.8 %collective-permute-done.38 = bf16[128,2048]{1,0:T(8,128)(2,1)S(1)} collective-permute-done((bf16[128,2048]{1,0:T(8,128)(2,1)S(1)}, bf16[128,2048]{1,0:T(8,128)(2,1)S(1)}, u32[]{:S(2)}, u32[]{:S(2)}) %collective-permute-start.38) | collective-permute-done | bytes 524320 | tf_op jit(solution)/shard_map/ppermute | solution.py:601
  228.0 2.2 collective-permute-start.43
  230.3 5.1 shard_map.247
  236.0 7.1 %collective-permute-done.43 = bf16[128,2048]{1,0:T(8,128)(2,1)S(1)} collective-permute-done((bf16[128,2048]{1,0:T(8,128)(2,1)S(1)}, bf16[128,2048]{1,0:T(8,128)(2,1)S(1)}, u32[]{:S(2)}, u32[]{:S(2)}) %collective-permute-start.43) | collective-permute-done | bytes 524320 | tf_op jit(solution)/shard_map/ppermute | solution.py:601
  243.3 2.4 collective-permute-start.44
  245.7 12.1 %collective-permute-done.44.refs_2_ = bf16[128,2048]{1,0:T(8,128)(2,1)S(1)} collective-permute-done((bf16[128,2048]{1,0:T(8,128)(2,1)S(1)}, bf16[128,2048]{1,0:T(8,128)(2,1)S(1)}, u32[]{:S(2)}, u32[]{:S(2)}) %collective-permute-start.44) | collective-permute-done | bytes 524320 | tf_op jit(solution)/shard_map/ppermute | solution.py:601
  257.8 2.0 shard_map.248
  259.9 2.4 collective-permute-start.46
  262.2 11.2 %collective-permute-done.46.refs_0_ = bf16[128,2048]{1,0:T(8,128)(2,1)S(1)} collective-permute-done((bf16[128,2048]{1,0:T(8,128)(2,1)S(1)}, bf16[128,2048]{1,0:T(8,128)(2,1)S(1)}, u32[]{:S(2)}, u32[]{:S(2)}) %collective-permute-start.46) | collective-permute-done | bytes 524320 | tf_op jit(solution)/shard_map/ppermute | solution.py:601
  273.4 2.4 collective-permute-start.49
  275.8 5.1 shard_map.249
  281.5 7.1 %collective-permute-done.49.refs_0_ = bf16[128,2048]{1,0:T(8,128)(2,1)S(1)} collective-permute-done((bf16[128,2048]{1,0:T(8,128)(2,1)S(1)}, bf16[128,2048]{1,0:T(8,128)(2,1)S(1)}, u32[]{:S(2)}, u32[]{:S(2)}) %collective-permute-start.49) | collective-permute-done | bytes 524320 | tf_op jit(solution)/shard_map/ppermute | solution.py:601
  288.7 2.4 collective-permute-start.50
  291.8 5.2 shard_map.250
  297.0 5.2 shard_map.251
  304.1 11.1 %collective-permute-done.52 = bf16[128,2048]{1,0:T(8,128)(2,1)S(1)} collective-permute-done((bf16[128,2048]{1,0:T(8,128)(2,1)S(1)}, bf16[128,2048]{1,0:T(8,128)(2,1)S(1)}, u32[]{:S(2)}, u32[]{:S(2)}) %collective-permute-start.52) | collective-permute-done | bytes 524320 | tf_op jit(solution)/shard_map/ppermute | solution.py:601
  315.9 2.6 collective-permute-start.57
  318.4 5.1 shard_map.252
  339.3 3.2 collective-permute-done.59
  349.6 7.5 %collective-permute-done.61 = bf16[512,512]{1,0:T(8,128)(2,1)S(1)} collective-permute-done((bf16[512,512]{1,0:T(8,128)(2,1)S(1)}, bf16[512,512]{1,0:T(8,128)(2,1)S(1)}, u32[]{:S(2)}, u32[]{:S(2)}) %collective-permute-start.61) | collective-permute-done | bytes 524320 | tf_op jit(solution)/shard_map/ppermute | solution.py:601
  363.6 7.8 %collective-permute-done.63.refs_7_ = bf16[128,2048]{1,0:T(8,128)(2,1)S(1)} collective-permute-done((bf16[128,2048]{1,0:T(8,128)(2,1)S(1)}, bf16[128,2048]{1,0:T(8,128)(2,1)S(1)}, u32[]{:S(2)}, u32[]{:S(2)}) %collective-permute-start.63) | collective-permute-done | bytes 524320 | tf_op jit(solution)/shard_map/ppermute | solution.py:601
  371.4 2.2 collective-permute-done.64.refs_8_
  373.6 8.6 %collective-permute-done.65.refs_9_ = bf16[128,2048]{1,0:T(8,128)(2,1)S(1)} collective-permute-done((bf16[128,2048]{1,0:T(8,128)(2,1)S(1)}, bf16[128,2048]{1,0:T(8,128)(2,1)S(1)}, u32[]{:S(2)}, u32[]{:S(2)}) %collective-permute-start.65) | collective-permute-done | bytes 524320 | tf_op jit(solution)/shard_map/ppermute | solution.py:601
  384.8 8.2 %shard_map.254 = (f32[512,512]{1,0:T(8,128)S(1)}, f32[512,512]{1,0:T(8,128)S(1)}, bf16[512,512]{1,0:T(8,128)(2,1)S(1)}, f32[8,512]{1,0:T(8,128)S(1)}, f32[8,512]...) custom-call(s32[5]{0:T(128)S(1)} %stack.34.pos, f32[8,128]{1,0:T(8,128)S(1)} %get-tuple-element.244.refs_1_.refs_0_, ...), custom_call_target="tpu_custom_call" | custom-call | tf_op jit(solution)/shard_map/pallas_call | solution.py:50
  393.7 11.1 %collective-permute-done.66 = f32[8,512]{1,0:T(8,128)S(1)} collective-permute-done((f32[8,512]{1,0:T(8,128)S(1)}, f32[8,512]{1,0:T(8,128)S(1)}, u32[]{:S(2)}, u32[]{:S(2)}) %collective-permute-start.66) | collective-permute-done | bytes 16416 | tf_op jit(solution)/shard_map/ppermute | solution.py:601
  406.1 2.5 collective-permute-done.67
  410.3 2.1 shard_map.256
  412.5 2.7 collective-permute-done.70
  415.2 4.6 shard_map.257
  423.3 23.1 %collective-permute-done.72 = bf16[1040,512]{1,0:T(8,128)(2,1)S(1)} collective-permute-done((bf16[1040,512]{1,0:T(8,128)(2,1)S(1)}, bf16[1040,512]{1,0:T(8,128)(2,1)S(1)}, u32[]{:S(2)}, u32[]{:S(2)}) %collective-permute-start.72) | collective-permute-done | bytes 1064992 | tf_op jit(solution)/shard_map/ppermute | solution.py:601
  448.7 2.4 collective-permute-start.75
  452.1 19.7 %collective-permute-done.83 = bf16[1024,512]{1,0:T(8,128)(2,1)S(1)} collective-permute-done((bf16[1024,512]{1,0:T(8,128)(2,1)S(1)}, bf16[1024,512]{1,0:T(8,128)(2,1)S(1)}, u32[]{:S(2)}, u32[]{:S(2)}) %collective-permute-start.83) | collective-permute-done | bytes 1048608 | tf_op jit(solution)/shard_map/ppermute | solution.py:601
  473.9 2.6 collective-permute-start.76
  480.4 4.3 shard_map.258
  484.7 12.9 %collective-permute-done.76.refs_2_ = bf16[1040,512]{1,0:T(8,128)(2,1)S(1)} collective-permute-done((bf16[1040,512]{1,0:T(8,128)(2,1)S(1)}, bf16[1040,512]{1,0:T(8,128)(2,1)S(1)}, u32[]{:S(2)}, u32[]{:S(2)}) %collective-permute-start.76) | collective-permute-done | bytes 1064992 | tf_op jit(solution)/shard_map/ppermute | solution.py:601
  502.4 2.0 collective-permute-start.79
  505.5 14.9 %collective-permute-done.80.refs_1_ = bf16[80,1536]{1,0:T(8,128)(2,1)S(1)} collective-permute-done((bf16[80,1536]{1,0:T(8,128)(2,1)S(1)}, bf16[80,1536]{1,0:T(8,128)(2,1)S(1)}, u32[]{:S(2)}, u32[]{:S(2)}) %collective-permute-start.80) | collective-permute-done | bytes 245792 | tf_op jit(solution)/shard_map/ppermute | solution.py:601
  526.1 7.5 %collective-permute-done.78 = bf16[128,2048]{1,0:T(8,128)(2,1)S(1)} collective-permute-done((bf16[128,2048]{1,0:T(8,128)(2,1)S(1)}, bf16[128,2048]{1,0:T(8,128)(2,1)S(1)}, u32[]{:S(2)}, u32[]{:S(2)}) %collective-permute-start.78) | collective-permute-done | bytes 524320 | tf_op jit(solution)/shard_map/ppermute | solution.py:601
  (238 shorter events, 113.2 us)
Async XLA Ops:
  2.1 26.9 %collective-permute-start.3 = (bf16[512,512]{1,0:T(8,128)(2,1)S(1)}, bf16[512,512]{1,0:T(8,128)(2,1)}, u32[]{:S(2)}, u32[]{:S(2)}) collective-permute-start(bf16[512,512]{1,0:T(8,128)(2,1)S(1)} %get-tuple-element.261.refs_10_), channel_id=1, source_target_pairs={{0,16},{1,17},{2,18},{3,19},{4,20},{5,21},{6,22},{7,23},{8,24},{9,... | collective-permute-start | bytes 1572872 | tf_op jit(solution)/shard_map/ppermute | solution.py:601
  5.1 23.9 %collective-permute-start.4 = (bf16[512,512]{1,0:T(8,128)(2,1)S(1)}, bf16[512,512]{1,0:T(8,128)(2,1)}, u32[]{:S(2)}, u32[]{:S(2)}) collective-permute-start(bf16[512,512]{1,0:T(8,128)(2,1)S(1)} %get-tuple-element.262.refs_12_), channel_id=1, source_target_pairs={{0,2},{1,3},{2,0},{3,1},{4,6},{5,7},{6,4},{7,5},{8,10},{9,11},{10,... | collective-permute-start | bytes 1572872 | tf_op jit(solution)/shard_map/ppermute | solution.py:601
  11.7 17.3 %collective-permute-start = (bf16[80,1536]{1,0:T(8,128)(2,1)S(1)}, bf16[80,1536]{1,0:T(8,128)(2,1)S(1)}, u32[]{:S(2)}, u32[]{:S(2)}) collective-permute-start(bf16[80,1536]{1,0:T(8,128)(2,1)S(1)} %get-tuple-element.221), channel_id=1, source_target_pairs={{0,2},{1,3},{2,0},{3,1},{4,6},{5,7},{6,4},{7,5},{8,10},{9,11},{10,... | collective-permute-start | bytes 737288 | tf_op jit(solution)/shard_map/ppermute | solution.py:601
  12.3 16.8 %collective-permute-start.1 = (bf16[80,1536]{1,0:T(8,128)(2,1)S(1)}, bf16[80,1536]{1,0:T(8,128)(2,1)S(1)}, u32[]{:S(2)}, u32[]{:S(2)}) collective-permute-start(bf16[80,1536]{1,0:T(8,128)(2,1)S(1)} %get-tuple-element.222), channel_id=1, source_target_pairs={{0,16},{1,17},{2,18},{3,19},{4,20},{5,21},{6,22},{7,23},{8,24},{9,... | collective-permute-start | bytes 737288 | tf_op jit(solution)/shard_map/ppermute | solution.py:601
  12.4 16.7 %collective-permute-start.2 = (bf16[80,1536]{1,0:T(8,128)(2,1)S(1)}, bf16[80,1536]{1,0:T(8,128)(2,1)S(1)}, u32[]{:S(2)}, u32[]{:S(2)}) collective-permute-start(bf16[80,1536]{1,0:T(8,128)(2,1)S(1)} %get-tuple-element.223), channel_id=1, source_target_pairs={{0,18},{1,19},{2,16},{3,17},{4,22},{5,23},{6,20},{7,21},{8,26},{9,... | collective-permute-start | bytes 737288 | tf_op jit(solution)/shard_map/ppermute | solution.py:601
  30.1 27.4 %collective-permute-start.11 = (bf16[1040,512]{1,0:T(8,128)(2,1)}, bf16[1040,512]{1,0:T(8,128)(2,1)}, u32[]{:S(2)}, u32[]{:S(2)}) collective-permute-start(bf16[1040,512]{1,0:T(8,128)(2,1)} %get-tuple-element.228.refs_0_), channel_id=1, source_target_pairs={{0,8},{1,9},{2,10},{3,11},{4,0},{5,1},{6,2},{7,3},{8,12},{9,13},{1... | collective-permute-start | bytes 3194888 | tf_op jit(solution)/shard_map/ppermute | solution.py:601
  32.7 23.5 %collective-permute-start.5 = (bf16[1024,512]{1,0:T(8,128)(2,1)S(1)}, bf16[1024,512]{1,0:T(8,128)(2,1)S(1)}, u32[]{:S(2)}, u32[]{:S(2)}) collective-permute-start(bf16[1024,512]{1,0:T(8,128)(2,1)S(1)} %copy-done), channel_id=1, source_target_pairs={{0,16},{1,17},{2,18},{3,19},{4,20},{5,21},{6,22},{7,23},{8,24},{9,... | collective-permute-start | bytes 3145736 | tf_op jit(solution)/shard_map/ppermute | solution.py:601
  33.9 23.6 %collective-permute-start.7 = (bf16[1024,512]{1,0:T(8,128)(2,1)S(1)}, bf16[1024,512]{1,0:T(8,128)(2,1)}, u32[]{:S(2)}, u32[]{:S(2)}) collective-permute-start(bf16[1024,512]{1,0:T(8,128)(2,1)S(1)} %copy-done.1), channel_id=1, source_target_pairs={{0,2},{1,3},{2,0},{3,1},{4,6},{5,7},{6,4},{7,5},{8,10},{9,11},{10,... | collective-permute-start | bytes 3145736 | tf_op jit(solution)/shard_map/ppermute | solution.py:601
  57.5 23.7 %collective-permute-start.12 = (bf16[1040,512]{1,0:T(8,128)(2,1)}, bf16[1040,512]{1,0:T(8,128)(2,1)S(1)}, u32[]{:S(2)}, u32[]{:S(2)}) collective-permute-start(bf16[1040,512]{1,0:T(8,128)(2,1)} %collective-permute-done.11.refs_2_), channel_id=1, source_target_pairs={{0,8},{1,9},{2,10},{3,11},{4,0},{5,1},{6,2},{7,3},{8,12},{9,13},{1... | collective-permute-start | bytes 3194888 | tf_op jit(solution)/shard_map/ppermute | solution.py:601
  59.7 13.1 %collective-permute-start.8 = (bf16[128,2048]{1,0:T(8,128)(2,1)}, bf16[128,2048]{1,0:T(8,128)(2,1)S(1)}, u32[]{:S(2)}, u32[]{:S(2)}) collective-permute-start(bf16[128,2048]{1,0:T(8,128)(2,1)} %bitcast.54), channel_id=1, source_target_pairs={{0,2},{1,3},{2,0},{3,1},{4,6},{5,7},{6,4},{7,5},{8,10},{9,11},{10,... | collective-permute-start | bytes 1572872 | tf_op jit(solution)/shard_map/ppermute | solution.py:601
  81.2 23.4 %collective-permute-start.13 = (bf16[1040,512]{1,0:T(8,128)(2,1)S(1)}, bf16[1040,512]{1,0:T(8,128)(2,1)S(1)}, u32[]{:S(2)}, u32[]{:S(2)}) collective-permute-start(bf16[1040,512]{1,0:T(8,128)(2,1)S(1)} %collective-permute-done.12.refs_4_), channel_id=1, source_target_pairs={{0,8},{1,9},{2,10},{3,11},{4,0},{5,1},{6,2},{7,3},{8,12},{9,13},{1... | collective-permute-start | bytes 3194888 | tf_op jit(solution)/shard_map/ppermute | solution.py:601
  83.3 21.3 %collective-permute-start.14 = (bf16[1024,512]{1,0:T(8,128)(2,1)S(1)}, bf16[1024,512]{1,0:T(8,128)(2,1)S(1)}, u32[]{:S(2)}, u32[]{:S(2)}) collective-permute-start(bf16[1024,512]{1,0:T(8,128)(2,1)S(1)} %copy-done), channel_id=1, source_target_pairs={{0,2},{1,3},{2,0},{3,1},{4,6},{5,7},{6,4},{7,5},{8,10},{9,11},{10,... | collective-permute-start | bytes 3145736 | tf_op jit(solution)/shard_map/ppermute | solution.py:601
  83.6 21.1 %collective-permute-start.15 = (bf16[1024,512]{1,0:T(8,128)(2,1)S(1)}, bf16[1024,512]{1,0:T(8,128)(2,1)S(1)}, u32[]{:S(2)}, u32[]{:S(2)}) collective-permute-start(bf16[1024,512]{1,0:T(8,128)(2,1)S(1)} %copy-done.1), channel_id=1, source_target_pairs={{0,16},{1,17},{2,18},{3,19},{4,20},{5,21},{6,22},{7,23},{8,24},{9,... | collective-permute-start | bytes 3145736 | tf_op jit(solution)/shard_map/ppermute | solution.py:601
  84.6 23.1 %collective-permute-start.17 = (bf16[1040,512]{1,0:T(8,128)(2,1)}, bf16[1040,512]{1,0:T(8,128)(2,1)S(1)}, u32[]{:S(2)}, u32[]{:S(2)}) collective-permute-start(bf16[1040,512]{1,0:T(8,128)(2,1)} %get-tuple-element.228.refs_0_), channel_id=1, source_target_pairs={{0,1},{1,0},{2,3},{3,2},{4,5},{5,4},{6,7},{7,6},{8,9},{9,8},{10,11... | collective-permute-start | bytes 3194888 | tf_op jit(solution)/shard_map/ppermute | solution.py:601
  84.6 23.1 %collective-permute-start.18 = (bf16[1040,512]{1,0:T(8,128)(2,1)}, bf16[1040,512]{1,0:T(8,128)(2,1)S(1)}, u32[]{:S(2)}, u32[]{:S(2)}) collective-permute-start(bf16[1040,512]{1,0:T(8,128)(2,1)} %collective-permute-done.11.refs_2_), channel_id=1, source_target_pairs={{0,1},{1,0},{2,3},{3,2},{4,5},{5,4},{6,7},{7,6},{8,9},{9,8},{10,11... | collective-permute-start | bytes 3194888 | tf_op jit(solution)/shard_map/ppermute | solution.py:601
  124.9 22.9 %collective-permute-start.22 = (bf16[1024,512]{1,0:T(8,128)(2,1)S(1)}, bf16[1024,512]{1,0:T(8,128)(2,1)S(1)}, u32[]{:S(2)}, u32[]{:S(2)}) collective-permute-start(bf16[1024,512]{1,0:T(8,128)(2,1)S(1)} %collective-permute-done.5.refs_4_), channel_id=1, source_target_pairs={{0,2},{1,3},{2,0},{3,1},{4,6},{5,7},{6,4},{7,5},{8,10},{9,11},{10,... | collective-permute-start | bytes 3145736 | tf_op jit(solution)/shard_map/ppermute | solution.py:601
  126.2 23.5 %collective-permute-start.23 = (bf16[1024,512]{1,0:T(8,128)(2,1)}, bf16[1024,512]{1,0:T(8,128)(2,1)S(1)}, u32[]{:S(2)}, u32[]{:S(2)}) collective-permute-start(bf16[1024,512]{1,0:T(8,128)(2,1)} %collective-permute-done.7.refs_7_), channel_id=1, source_target_pairs={{0,16},{1,17},{2,18},{3,19},{4,20},{5,21},{6,22},{7,23},{8,24},{9,... | collective-permute-start | bytes 3145736 | tf_op jit(solution)/shard_map/ppermute | solution.py:601
  149.7 14.0 %collective-permute-start.24 = (bf16[128,2048]{1,0:T(8,128)(2,1)S(1)}, bf16[128,2048]{1,0:T(8,128)(2,1)S(1)}, u32[]{:S(2)}, u32[]{:S(2)}) collective-permute-start(bf16[128,2048]{1,0:T(8,128)(2,1)S(1)} %get-tuple-element.257), channel_id=1, source_target_pairs={{0,2},{1,3},{2,0},{3,1},{4,6},{5,7},{6,4},{7,5},{8,10},{9,11},{10,... | collective-permute-start | bytes 1572872 | tf_op jit(solution)/shard_map/ppermute | solution.py:601
  149.8 14.9 %collective-permute-start.25 = (bf16[128,2048]{1,0:T(8,128)(2,1)S(1)}, bf16[128,2048]{1,0:T(8,128)(2,1)S(1)}, u32[]{:S(2)}, u32[]{:S(2)}) collective-permute-start(bf16[128,2048]{1,0:T(8,128)(2,1)S(1)} %get-tuple-element.258), channel_id=1, source_target_pairs={{0,16},{1,17},{2,18},{3,19},{4,20},{5,21},{6,22},{7,23},{8,24},{9,... | collective-permute-start | bytes 1572872 | tf_op jit(solution)/shard_map/ppermute | solution.py:601
  151.2 21.5 %collective-permute-start.26 = (bf16[128,2048]{1,0:T(8,128)(2,1)S(1)}, bf16[128,2048]{1,0:T(8,128)(2,1)S(1)}, u32[]{:S(2)}, u32[]{:S(2)}) collective-permute-start(bf16[128,2048]{1,0:T(8,128)(2,1)S(1)} %get-tuple-element.259), channel_id=1, source_target_pairs={{0,18},{1,19},{2,16},{3,17},{4,22},{5,23},{6,20},{7,21},{8,26},{9,... | collective-permute-start | bytes 1572872 | tf_op jit(solution)/shard_map/ppermute | solution.py:601
  174.3 14.9 %collective-permute-start.28 = (bf16[512,512]{1,0:T(8,128)(2,1)S(1)}, bf16[512,512]{1,0:T(8,128)(2,1)S(1)}, u32[]{:S(2)}, u32[]{:S(2)}) collective-permute-start(bf16[512,512]{1,0:T(8,128)(2,1)S(1)} %copy-done.5), channel_id=1, source_target_pairs={{0,2},{1,3},{2,0},{3,1},{4,6},{5,7},{6,4},{7,5},{8,10},{9,11},{10,... | collective-permute-start | bytes 1572872 | tf_op jit(solution)/shard_map/ppermute | solution.py:601
  175.7 19.4 %collective-permute-start.29 = (bf16[512,512]{1,0:T(8,128)(2,1)}, bf16[512,512]{1,0:T(8,128)(2,1)S(1)}, u32[]{:S(2)}, u32[]{:S(2)}) collective-permute-start(bf16[512,512]{1,0:T(8,128)(2,1)} %collective-permute-done.3.refs_14_), channel_id=1, source_target_pairs={{0,2},{1,3},{2,0},{3,1},{4,6},{5,7},{6,4},{7,5},{8,10},{9,11},{10,... | collective-permute-start | bytes 1572872 | tf_op jit(solution)/shard_map/ppermute | solution.py:601
  176.4 18.8 %collective-permute-start.30 = (bf16[512,512]{1,0:T(8,128)(2,1)S(1)}, bf16[512,512]{1,0:T(8,128)(2,1)S(1)}, u32[]{:S(2)}, u32[]{:S(2)}) collective-permute-start(bf16[512,512]{1,0:T(8,128)(2,1)S(1)} %copy-done.3), channel_id=1, source_target_pairs={{0,16},{1,17},{2,18},{3,19},{4,20},{5,21},{6,22},{7,23},{8,24},{9,... | collective-permute-start | bytes 1572872 | tf_op jit(solution)/shard_map/ppermute | solution.py:601
  177.8 18.7 %collective-permute-start.31 = (bf16[512,512]{1,0:T(8,128)(2,1)}, bf16[512,512]{1,0:T(8,128)(2,1)S(1)}, u32[]{:S(2)}, u32[]{:S(2)}) collective-permute-start(bf16[512,512]{1,0:T(8,128)(2,1)} %collective-permute-done.4.refs_13_), channel_id=1, source_target_pairs={{0,16},{1,17},{2,18},{3,19},{4,20},{5,21},{6,22},{7,23},{8,24},{9,... | collective-permute-start | bytes 1572872 | tf_op jit(solution)/shard_map/ppermute | solution.py:601
  183.3 13.2 %collective-permute-start.33 = (bf16[128,2048]{1,0:T(8,128)(2,1)S(1)}, bf16[128,2048]{1,0:T(8,128)(2,1)S(1)}, u32[]{:S(2)}, u32[]{:S(2)}) collective-permute-start(bf16[128,2048]{1,0:T(8,128)(2,1)S(1)} %collective-permute-done.32.refs_0_), channel_id=1, source_target_pairs={{0,1},{1,0},{2,3},{3,2},{4,5},{5,4},{6,7},{7,6},{8,9},{9,8},{10,11... | collective-permute-start | bytes 1572872 | tf_op jit(solution)/shard_map/ppermute | solution.py:601
  189.2 13.0 %collective-permute-start.35 = (bf16[128,2048]{1,0:T(8,128)(2,1)S(1)}, bf16[128,2048]{1,0:T(8,128)(2,1)S(1)}, u32[]{:S(2)}, u32[]{:S(2)}) collective-permute-start(bf16[128,2048]{1,0:T(8,128)(2,1)S(1)} %collective-permute-done.32.refs_0_), channel_id=1, source_target_pairs={{0,8},{1,9},{2,10},{3,11},{4,0},{5,1},{6,2},{7,3},{8,12},{9,13},{1... | collective-permute-start | bytes 1572872 | tf_op jit(solution)/shard_map/ppermute | solution.py:601
  202.3 14.7 %collective-permute-start.36 = (bf16[128,2048]{1,0:T(8,128)(2,1)S(1)}, bf16[128,2048]{1,0:T(8,128)(2,1)S(1)}, u32[]{:S(2)}, u32[]{:S(2)}) collective-permute-start(bf16[128,2048]{1,0:T(8,128)(2,1)S(1)} %collective-permute-done.35.refs_0_), channel_id=1, source_target_pairs={{0,8},{1,9},{2,10},{3,11},{4,0},{5,1},{6,2},{7,3},{8,12},{9,13},{1... | collective-permute-start | bytes 1572872 | tf_op jit(solution)/shard_map/ppermute | solution.py:601
  203.7 24.1 %collective-permute-start.38 = (bf16[128,2048]{1,0:T(8,128)(2,1)S(1)}, bf16[128,2048]{1,0:T(8,128)(2,1)S(1)}, u32[]{:S(2)}, u32[]{:S(2)}) collective-permute-start(bf16[128,2048]{1,0:T(8,128)(2,1)S(1)} %add_convert_fusion.13), channel_id=1, source_target_pairs={{0,8},{1,9},{2,10},{3,11},{4,0},{5,1},{6,2},{7,3},{8,12},{9,13},{1... | collective-permute-start | bytes 1572872 | tf_op jit(solution)/shard_map/ppermute | solution.py:601
  215.1 12.7 %collective-permute-start.42 = (bf16[128,2048]{1,0:T(8,128)(2,1)S(1)}, bf16[128,2048]{1,0:T(8,128)(2,1)S(1)}, u32[]{:S(2)}, u32[]{:S(2)}) collective-permute-start(bf16[128,2048]{1,0:T(8,128)(2,1)S(1)} %get-tuple-element.298), channel_id=1, source_target_pairs={{0,1},{1,0},{2,3},{3,2},{4,5},{5,4},{6,7},{7,6},{8,9},{9,8},{10,11... | collective-permute-start | bytes 1572872 | tf_op jit(solution)/shard_map/ppermute | solution.py:601
  228.0 15.1 %collective-permute-start.43 = (bf16[128,2048]{1,0:T(8,128)(2,1)S(1)}, bf16[128,2048]{1,0:T(8,128)(2,1)S(1)}, u32[]{:S(2)}, u32[]{:S(2)}) collective-permute-start(bf16[128,2048]{1,0:T(8,128)(2,1)S(1)} %add_convert_fusion.12), channel_id=1, source_target_pairs={{0,8},{1,9},{2,10},{3,11},{4,0},{5,1},{6,2},{7,3},{8,12},{9,13},{1... | collective-permute-start | bytes 1572872 | tf_op jit(solution)/shard_map/ppermute | solution.py:601
  243.3 14.5 %collective-permute-start.44 = (bf16[128,2048]{1,0:T(8,128)(2,1)S(1)}, bf16[128,2048]{1,0:T(8,128)(2,1)S(1)}, u32[]{:S(2)}, u32[]{:S(2)}) collective-permute-start(bf16[128,2048]{1,0:T(8,128)(2,1)S(1)} %add_convert_fusion.11), channel_id=1, source_target_pairs={{0,8},{1,9},{2,10},{3,11},{4,0},{5,1},{6,2},{7,3},{8,12},{9,13},{1... | collective-permute-start | bytes 1572872 | tf_op jit(solution)/shard_map/ppermute | solution.py:601
  259.9 13.6 %collective-permute-start.46 = (bf16[128,2048]{1,0:T(8,128)(2,1)S(1)}, bf16[128,2048]{1,0:T(8,128)(2,1)S(1)}, u32[]{:S(2)}, u32[]{:S(2)}) collective-permute-start(bf16[128,2048]{1,0:T(8,128)(2,1)S(1)} %get-tuple-element.301.refs_0_), channel_id=1, source_target_pairs={{0,8},{1,9},{2,10},{3,11},{4,0},{5,1},{6,2},{7,3},{8,12},{9,13},{1... | collective-permute-start | bytes 1572872 | tf_op jit(solution)/shard_map/ppermute | solution.py:601
  273.4 15.2 %collective-permute-start.49 = (bf16[128,2048]{1,0:T(8,128)(2,1)S(1)}, bf16[128,2048]{1,0:T(8,128)(2,1)S(1)}, u32[]{:S(2)}, u32[]{:S(2)}) collective-permute-start(bf16[128,2048]{1,0:T(8,128)(2,1)S(1)} %collective-permute-done.46.refs_0_), channel_id=1, source_target_pairs={{0,8},{1,9},{2,10},{3,11},{4,0},{5,1},{6,2},{7,3},{8,12},{9,13},{1... | collective-permute-start | bytes 1572872 | tf_op jit(solution)/shard_map/ppermute | solution.py:601
  288.7 15.4 %collective-permute-start.50 = (bf16[128,2048]{1,0:T(8,128)(2,1)S(1)}, bf16[128,2048]{1,0:T(8,128)(2,1)S(1)}, u32[]{:S(2)}, u32[]{:S(2)}) collective-permute-start(bf16[128,2048]{1,0:T(8,128)(2,1)S(1)} %collective-permute-done.49.refs_0_), channel_id=1, source_target_pairs={{0,8},{1,9},{2,10},{3,11},{4,0},{5,1},{6,2},{7,3},{8,12},{9,13},{1... | collective-permute-start | bytes 1572872 | tf_op jit(solution)/shard_map/ppermute | solution.py:601
  291.2 24.0 %collective-permute-start.52 = (bf16[128,2048]{1,0:T(8,128)(2,1)S(1)}, bf16[128,2048]{1,0:T(8,128)(2,1)S(1)}, u32[]{:S(2)}, u32[]{:S(2)}) collective-permute-start(bf16[128,2048]{1,0:T(8,128)(2,1)S(1)} %add_convert_fusion.10), channel_id=1, source_target_pairs={{0,8},{1,9},{2,10},{3,11},{4,0},{5,1},{6,2},{7,3},{8,12},{9,13},{1... | collective-permute-start | bytes 1572872 | tf_op jit(solution)/shard_map/ppermute | solution.py:601
  302.2 13.5 %collective-permute-start.56 = (bf16[128,2048]{1,0:T(8,128)(2,1)S(1)}, bf16[128,2048]{1,0:T(8,128)(2,1)S(1)}, u32[]{:S(2)}, u32[]{:S(2)}) collective-permute-start(bf16[128,2048]{1,0:T(8,128)(2,1)S(1)} %get-tuple-element.339), channel_id=1, source_target_pairs={{0,1},{1,0},{2,3},{3,2},{4,5},{5,4},{6,7},{7,6},{8,9},{9,8},{10,11... | collective-permute-start | bytes 1572872 | tf_op jit(solution)/shard_map/ppermute | solution.py:601
  315.2 32.9 %collective-permute-start.48 = (bf16[128,2048]{1,0:T(8,128)(2,1)S(1)}, bf16[128,2048]{1,0:T(8,128)(2,1)S(1)}, u32[]{:S(2)}, u32[]{:S(2)}) collective-permute-start(bf16[128,2048]{1,0:T(8,128)(2,1)S(1)} %get-tuple-element.315), channel_id=1, source_target_pairs={{0,1},{1,0},{2,3},{3,2},{4,5},{5,4},{6,7},{7,6},{8,9},{9,8},{10,11... | collective-permute-start | bytes 1572872 | tf_op jit(solution)/shard_map/ppermute | solution.py:601
  315.9 16.7 %collective-permute-start.57 = (bf16[128,2048]{1,0:T(8,128)(2,1)S(1)}, bf16[128,2048]{1,0:T(8,128)(2,1)S(1)}, u32[]{:S(2)}, u32[]{:S(2)}) collective-permute-start(bf16[128,2048]{1,0:T(8,128)(2,1)S(1)} %add_convert_fusion.9), channel_id=1, source_target_pairs={{0,8},{1,9},{2,10},{3,11},{4,0},{5,1},{6,2},{7,3},{8,12},{9,13},{1... | collective-permute-start | bytes 1572872 | tf_op jit(solution)/shard_map/ppermute | solution.py:601
  328.1 14.4 %collective-permute-start.59 = (bf16[512,512]{1,0:T(8,128)(2,1)S(1)}, bf16[512,512]{1,0:T(8,128)(2,1)S(1)}, u32[]{:S(2)}, u32[]{:S(2)}) collective-permute-start(bf16[512,512]{1,0:T(8,128)(2,1)S(1)} %convolution_convert_fusion.12), channel_id=1, source_target_pairs={{0,16},{1,17},{2,18},{3,19},{4,20},{5,21},{6,22},{7,23},{8,24},{9,... | collective-permute-start | bytes 1572872 | tf_op jit(solution)/shard_map/ppermute | solution.py:601
  329.8 14.0 %collective-permute-start.60 = (bf16[512,512]{1,0:T(8,128)(2,1)S(1)}, bf16[512,512]{1,0:T(8,128)(2,1)S(1)}, u32[]{:S(2)}, u32[]{:S(2)}) collective-permute-start(bf16[512,512]{1,0:T(8,128)(2,1)S(1)} %convolution_convert_fusion.8), channel_id=1, source_target_pairs={{0,2},{1,3},{2,0},{3,1},{4,6},{5,7},{6,4},{7,5},{8,10},{9,11},{10,... | collective-permute-start | bytes 1572872 | tf_op jit(solution)/shard_map/ppermute | solution.py:601
  332.8 15.3 %collective-permute-start.58 = (bf16[128,2048]{1,0:T(8,128)(2,1)S(1)}, bf16[128,2048]{1,0:T(8,128)(2,1)S(1)}, u32[]{:S(2)}, u32[]{:S(2)}) collective-permute-start(bf16[128,2048]{1,0:T(8,128)(2,1)S(1)} %add_convert_fusion.8), channel_id=1, source_target_pairs={{0,8},{1,9},{2,10},{3,11},{4,0},{5,1},{6,2},{7,3},{8,12},{9,13},{1... | collective-permute-start | bytes 1572872 | tf_op jit(solution)/shard_map/ppermute | solution.py:601
  343.9 13.2 %collective-permute-start.61 = (bf16[512,512]{1,0:T(8,128)(2,1)S(1)}, bf16[512,512]{1,0:T(8,128)(2,1)S(1)}, u32[]{:S(2)}, u32[]{:S(2)}) collective-permute-start(bf16[512,512]{1,0:T(8,128)(2,1)S(1)} %convolution_convert_fusion.13), channel_id=1, source_target_pairs={{0,16},{1,17},{2,18},{3,19},{4,20},{5,21},{6,22},{7,23},{8,24},{9,... | collective-permute-start | bytes 1572872 | tf_op jit(solution)/shard_map/ppermute | solution.py:601
  344.3 13.2 %collective-permute-start.62 = (bf16[512,512]{1,0:T(8,128)(2,1)S(1)}, bf16[512,512]{1,0:T(8,128)(2,1)S(1)}, u32[]{:S(2)}, u32[]{:S(2)}) collective-permute-start(bf16[512,512]{1,0:T(8,128)(2,1)S(1)} %convolution_convert_fusion.10), channel_id=1, source_target_pairs={{0,2},{1,3},{2,0},{3,1},{4,6},{5,7},{6,4},{7,5},{8,10},{9,11},{10,... | collective-permute-start | bytes 1572872 | tf_op jit(solution)/shard_map/ppermute | solution.py:601
  357.4 14.0 %collective-permute-start.63 = (bf16[128,2048]{1,0:T(8,128)(2,1)S(1)}, bf16[128,2048]{1,0:T(8,128)(2,1)S(1)}, u32[]{:S(2)}, u32[]{:S(2)}) collective-permute-start(bf16[128,2048]{1,0:T(8,128)(2,1)S(1)} %get-tuple-element.366.refs_6_), channel_id=1, source_target_pairs={{0,2},{1,3},{2,0},{3,1},{4,6},{5,7},{6,4},{7,5},{8,10},{9,11},{10,... | collective-permute-start | bytes 1572872 | tf_op jit(solution)/shard_map/ppermute | solution.py:601
  358.7 14.9 %collective-permute-start.64 = (bf16[128,2048]{1,0:T(8,128)(2,1)S(1)}, bf16[128,2048]{1,0:T(8,128)(2,1)S(1)}, u32[]{:S(2)}, u32[]{:S(2)}) collective-permute-start(bf16[128,2048]{1,0:T(8,128)(2,1)S(1)} %get-tuple-element.366.refs_6_), channel_id=1, source_target_pairs={{0,16},{1,17},{2,18},{3,19},{4,20},{5,21},{6,22},{7,23},{8,24},{9,... | collective-permute-start | bytes 1572872 | tf_op jit(solution)/shard_map/ppermute | solution.py:601
  360.1 22.0 %collective-permute-start.65 = (bf16[128,2048]{1,0:T(8,128)(2,1)S(1)}, bf16[128,2048]{1,0:T(8,128)(2,1)S(1)}, u32[]{:S(2)}, u32[]{:S(2)}) collective-permute-start(bf16[128,2048]{1,0:T(8,128)(2,1)S(1)} %get-tuple-element.366.refs_6_), channel_id=1, source_target_pairs={{0,18},{1,19},{2,16},{3,17},{4,22},{5,23},{6,20},{7,21},{8,26},{9,... | collective-permute-start | bytes 1572872 | tf_op jit(solution)/shard_map/ppermute | solution.py:601
  382.1 26.5 %collective-permute-start.68 = (bf16[1024,512]{1,0:T(8,128)(2,1)S(1)}, bf16[1024,512]{1,0:T(8,128)(2,1)S(1)}, u32[]{:S(2)}, u32[]{:S(2)}) collective-permute-start(bf16[1024,512]{1,0:T(8,128)(2,1)S(1)} %convolution_convert_fusion.4), channel_id=1, source_target_pairs={{0,16},{1,17},{2,18},{3,19},{4,20},{5,21},{6,22},{7,23},{8,24},{9,... | collective-permute-start | bytes 3145736 | tf_op jit(solution)/shard_map/ppermute | solution.py:601
  383.3 25.3 %collective-permute-start.69 = (bf16[1024,512]{1,0:T(8,128)(2,1)S(1)}, bf16[1024,512]{1,0:T(8,128)(2,1)S(1)}, u32[]{:S(2)}, u32[]{:S(2)}) collective-permute-start(bf16[1024,512]{1,0:T(8,128)(2,1)S(1)} %convolution_convert_fusion), channel_id=1, source_target_pairs={{0,2},{1,3},{2,0},{3,1},{4,6},{5,7},{6,4},{7,5},{8,10},{9,11},{10,... | collective-permute-start | bytes 3145736 | tf_op jit(solution)/shard_map/ppermute | solution.py:601
  419.7 26.6 %collective-permute-start.71 = (bf16[3120,512]{1,0:T(8,128)(2,1)S(1)}, bf16[3120,512]{1,0:T(8,128)(2,1)S(1)}, u32[]{:S(2)}, u32[]{:S(2)}) collective-permute-start(bf16[3120,512]{1,0:T(8,128)(2,1)S(1)} %get-tuple-element.392), channel_id=1, source_target_pairs={{0,1},{1,0},{2,3},{3,2},{4,5},{5,4},{6,7},{7,6},{8,9},{9,8},{10,11... | collective-permute-start | bytes 9584648 | tf_op jit(solution)/shard_map/ppermute | solution.py:601
  420.2 26.1 %collective-permute-start.72 = (bf16[1040,512]{1,0:T(8,128)(2,1)S(1)}, bf16[1040,512]{1,0:T(8,128)(2,1)S(1)}, u32[]{:S(2)}, u32[]{:S(2)}) collective-permute-start(bf16[1040,512]{1,0:T(8,128)(2,1)S(1)} %add_convert_fusion.2), channel_id=1, source_target_pairs={{0,8},{1,9},{2,10},{3,11},{4,0},{5,1},{6,2},{7,3},{8,12},{9,13},{1... | collective-permute-start | bytes 3194888 | tf_op jit(solution)/shard_map/ppermute | solution.py:601
  421.3 25.5 %collective-permute-start.73 = (bf16[1024,512]{1,0:T(8,128)(2,1)S(1)}, bf16[1024,512]{1,0:T(8,128)(2,1)S(1)}, u32[]{:S(2)}, u32[]{:S(2)}) collective-permute-start(bf16[1024,512]{1,0:T(8,128)(2,1)S(1)} %convolution_convert_fusion.5), channel_id=1, source_target_pairs={{0,16},{1,17},{2,18},{3,19},{4,20},{5,21},{6,22},{7,23},{8,24},{9,... | collective-permute-start | bytes 3145736 | tf_op jit(solution)/shard_map/ppermute | solution.py:601
  422.4 24.9 %collective-permute-start.74 = (bf16[1024,512]{1,0:T(8,128)(2,1)S(1)}, bf16[1024,512]{1,0:T(8,128)(2,1)S(1)}, u32[]{:S(2)}, u32[]{:S(2)}) collective-permute-start(bf16[1024,512]{1,0:T(8,128)(2,1)S(1)} %convolution_convert_fusion.2), channel_id=1, source_target_pairs={{0,2},{1,3},{2,0},{3,1},{4,6},{5,7},{6,4},{7,5},{8,10},{9,11},{10,... | collective-permute-start | bytes 3145736 | tf_op jit(solution)/shard_map/ppermute | solution.py:601
  447.6 24.2 %collective-permute-start.83 = (bf16[1024,512]{1,0:T(8,128)(2,1)S(1)}, bf16[1024,512]{1,0:T(8,128)(2,1)S(1)}, u32[]{:S(2)}, u32[]{:S(2)}) collective-permute-start(bf16[1024,512]{1,0:T(8,128)(2,1)S(1)} %add_convert_fusion.4), channel_id=1, source_target_pairs={{0,2},{1,3},{2,0},{3,1},{4,6},{5,7},{6,4},{7,5},{8,10},{9,11},{10,... | collective-permute-start | bytes 3145736 | tf_op jit(solution)/shard_map/ppermute | solution.py:601
  448.7 24.8 %collective-permute-start.75 = (bf16[1040,512]{1,0:T(8,128)(2,1)S(1)}, bf16[1040,512]{1,0:T(8,128)(2,1)S(1)}, u32[]{:S(2)}, u32[]{:S(2)}) collective-permute-start(bf16[1040,512]{1,0:T(8,128)(2,1)S(1)} %add_convert_fusion.1), channel_id=1, source_target_pairs={{0,8},{1,9},{2,10},{3,11},{4,0},{5,1},{6,2},{7,3},{8,12},{9,13},{1... | collective-permute-start | bytes 3194888 | tf_op jit(solution)/shard_map/ppermute | solution.py:601
  451.4 25.1 %collective-permute-start.84 = (bf16[1024,512]{1,0:T(8,128)(2,1)S(1)}, bf16[1024,512]{1,0:T(8,128)(2,1)S(1)}, u32[]{:S(2)}, u32[]{:S(2)}) collective-permute-start(bf16[1024,512]{1,0:T(8,128)(2,1)S(1)} %add_convert_fusion.3), channel_id=1, source_target_pairs={{0,16},{1,17},{2,18},{3,19},{4,20},{5,21},{6,22},{7,23},{8,24},{9,... | collective-permute-start | bytes 3145736 | tf_op jit(solution)/shard_map/ppermute | solution.py:601
  473.9 23.6 %collective-permute-start.76 = (bf16[1040,512]{1,0:T(8,128)(2,1)S(1)}, bf16[1040,512]{1,0:T(8,128)(2,1)S(1)}, u32[]{:S(2)}, u32[]{:S(2)}) collective-permute-start(bf16[1040,512]{1,0:T(8,128)(2,1)S(1)} %add_convert_fusion), channel_id=1, source_target_pairs={{0,8},{1,9},{2,10},{3,11},{4,0},{5,1},{6,2},{7,3},{8,12},{9,13},{1... | collective-permute-start | bytes 3194888 | tf_op jit(solution)/shard_map/ppermute | solution.py:601
  478.4 21.9 %collective-permute-start.86 = (bf16[512,512]{1,0:T(8,128)(2,1)S(1)}, bf16[512,512]{1,0:T(8,128)(2,1)S(1)}, u32[]{:S(2)}, u32[]{:S(2)}) collective-permute-start(bf16[512,512]{1,0:T(8,128)(2,1)S(1)} %add_convert_fusion.5), channel_id=1, source_target_pairs={{0,16},{1,17},{2,18},{3,19},{4,20},{5,21},{6,22},{7,23},{8,24},{9,... | collective-permute-start | bytes 1572872 | tf_op jit(solution)/shard_map/ppermute | solution.py:601
  479.3 25.2 %collective-permute-start.85 = (bf16[512,512]{1,0:T(8,128)(2,1)S(1)}, bf16[512,512]{1,0:T(8,128)(2,1)S(1)}, u32[]{:S(2)}, u32[]{:S(2)}) collective-permute-start(bf16[512,512]{1,0:T(8,128)(2,1)S(1)} %add_convert_fusion.6), channel_id=1, source_target_pairs={{0,2},{1,3},{2,0},{3,1},{4,6},{5,7},{6,4},{7,5},{8,10},{9,11},{10,... | collective-permute-start | bytes 1572872 | tf_op jit(solution)/shard_map/ppermute | solution.py:601
  498.7 21.8 %collective-permute-start.80 = (bf16[80,1536]{1,0:T(8,128)(2,1)S(1)}, bf16[80,1536]{1,0:T(8,128)(2,1)S(1)}, u32[]{:S(2)}, u32[]{:S(2)}) collective-permute-start(bf16[80,1536]{1,0:T(8,128)(2,1)S(1)} %get-tuple-element.407), channel_id=1, source_target_pairs={{0,2},{1,3},{2,0},{3,1},{4,6},{5,7},{6,4},{7,5},{8,10},{9,11},{10,... | collective-permute-start | bytes 737288 | tf_op jit(solution)/shard_map/ppermute | solution.py:601
  500.5 23.2 %collective-permute-start.81 = (bf16[80,1536]{1,0:T(8,128)(2,1)S(1)}, bf16[80,1536]{1,0:T(8,128)(2,1)S(1)}, u32[]{:S(2)}, u32[]{:S(2)}) collective-permute-start(bf16[80,1536]{1,0:T(8,128)(2,1)S(1)} %get-tuple-element.408), channel_id=1, source_target_pairs={{0,16},{1,17},{2,18},{3,19},{4,20},{5,21},{6,22},{7,23},{8,24},{9,... | collective-permute-start | bytes 737288 | tf_op jit(solution)/shard_map/ppermute | solution.py:601
  501.5 22.2 %collective-permute-start.82 = (bf16[80,1536]{1,0:T(8,128)(2,1)S(1)}, bf16[80,1536]{1,0:T(8,128)(2,1)S(1)}, u32[]{:S(2)}, u32[]{:S(2)}) collective-permute-start(bf16[80,1536]{1,0:T(8,128)(2,1)S(1)} %get-tuple-element.409), channel_id=1, source_target_pairs={{0,18},{1,19},{2,16},{3,17},{4,22},{5,23},{6,20},{7,21},{8,26},{9,... | collective-permute-start | bytes 737288 | tf_op jit(solution)/shard_map/ppermute | solution.py:601
  502.4 23.6 %collective-permute-start.79 = (bf16[128,2048]{1,0:T(8,128)(2,1)S(1)}, bf16[128,2048]{1,0:T(8,128)(2,1)S(1)}, u32[]{:S(2)}, u32[]{:S(2)}) collective-permute-start(bf16[128,2048]{1,0:T(8,128)(2,1)S(1)} %get-tuple-element.413), channel_id=1, source_target_pairs={{0,18},{1,19},{2,16},{3,17},{4,22},{5,23},{6,20},{7,21},{8,26},{9,... | collective-permute-start | bytes 1572872 | tf_op jit(solution)/shard_map/ppermute | solution.py:601
  504.5 29.1 %collective-permute-start.78 = (bf16[128,2048]{1,0:T(8,128)(2,1)S(1)}, bf16[128,2048]{1,0:T(8,128)(2,1)S(1)}, u32[]{:S(2)}, u32[]{:S(2)}) collective-permute-start(bf16[128,2048]{1,0:T(8,128)(2,1)S(1)} %get-tuple-element.412), channel_id=1, source_target_pairs={{0,16},{1,17},{2,18},{3,19},{4,20},{5,21},{6,22},{7,23},{8,24},{9,... | collective-permute-start | bytes 1572872 | tf_op jit(solution)/shard_map/ppermute | solution.py:601
  520.5 13.1 %collective-permute-start.77 = (bf16[128,2048]{1,0:T(8,128)(2,1)S(1)}, bf16[128,2048]{1,0:T(8,128)(2,1)S(1)}, u32[]{:S(2)}, u32[]{:S(2)}) collective-permute-start(bf16[128,2048]{1,0:T(8,128)(2,1)S(1)} %get-tuple-element.411), channel_id=1, source_target_pairs={{0,2},{1,3},{2,0},{3,1},{4,6},{5,7},{6,4},{7,5},{8,10},{9,11},{10,... | collective-permute-start | bytes 1572872 | tf_op jit(solution)/shard_map/ppermute | solution.py:601
  (48 other events, 599.3 us)

commit v5 on v4

--- a/solution.py
+++ b/solution.py
@@ -22,6 +22,7 @@
 VMEM = pl.BlockSpec(memory_space=pltpu.VMEM)
 HBM = pl.BlockSpec(memory_space=pltpu.HBM)
 EXTRA = 16
+PLAN = {'far_down': 'join', 'turns': 'w2', 'far': 'w3', 'tokens': 'w2', 'tokens_xy': 'w2', 'near': 'c3', 'own_gate_c': 'w3', 'own_down_c': 'c3', 'far_c': 'c3', 'far_down_c': 'stats', 'total': 'c3', 'near_down': 'k4', 'near_c': 'rs', 'last_from': 'stats', 'last': 'rs', 'last_c': 'f1', 'near_down_c': 'rs', 'f_lead': 0, 'f_out': 0, 'f_hold': 0, 'b_lead': 0, 'b_out': 0, 'b_hold': 0, 'products_from': 1, 'products': 'b1', 'products_xy': 'b2', 'near_grads': 'b3', 'near_grads_xy': 'b4', 'dots_from': 'block', 'dots': 'blocks', 'far_grads_from': 'sent', 'far_grads': 'ag', 'far_grads_xy': 'g1', 'sums_late': 1, 'sums': 'g1', 'w_far_late': 1, 'w_far': 't2', 'w_near': 't3', 'w_last': 'collect', 'w_last_late': 1, 'factors': 'collect', 'grad_wd': 'collect', 'x_parts': 't3', 'x_from': 'near', 'x_sums': 'spread', 'tokens_first': 1, 'far_from': 'xy', 'second_after': 'first', 'x_last_from': 'messages'}
 SQUARE = [(dx, dy) for dx in range(NX) for dy in range(NY)]
 TOKEN_BLOCKS = [(dx, dy) for dy in range(NY) for dx in range(NX)]
 
@@ -516,73 +517,94 @@
     gains[...] = total[:8]
 
 
-def mlp_forward_kernel(nc, *refs):
-    blocks, refs = refs[:nc], refs[nc:]
-    gates, ups, downs, refs = refs[:4], refs[4:8], refs[8:16], refs[16:]
-    outs = refs[-(8 + nc + 1) :]
-    products, by_gate, by_up, kept = outs[0:2], outs[2:4], outs[4:6], outs[6:8]
-    sums, total = outs[8 : 8 + nc], outs[8 + nc]
-    tok = blocks[0].shape[0]
-    half = kept[0].shape[1]
-    quarter = half // 2
-    for k, block in enumerate(blocks):
-        for dx in range(NX):
-            kept[dx][k * tok : (k + 1) * tok] = block[:, dx * half : (dx + 1) * half]
-    for dy in range(NY):
-
-        def through(weights):
-            return nn(kept[0][...], weights[dy][...]) + nn(kept[1][...], weights[NY + dy][...])
-
-        gate, up = through(gates), through(ups)
-        chance = 1.0 / (1.0 + jnp.exp(-gate))
-        silu = gate * chance
-        product = (silu * up).astype(BF16)
-        products[dy][...] = product
-        by_up[dy][...] = silu.astype(BF16)
-        by_gate[dy][...] = (up * (chance + silu * (1.0 - chance))).astype(BF16)
-        for i in range(4):
-            lanes = slice(i * quarter, (i + 1) * quarter)
-            part = nt(product, downs[i * NY + dy][...])
-            if dy == 0:
-                total[:, lanes] = part
-            else:
-                part = total[:, lanes] + part
-                for k, out in enumerate(sums):
-                    out[:, lanes] = part[k * tok : (k + 1) * tok].astype(out.dtype)
-
-
-def mlp_back_kernel(nc, *refs):
-    blocks, refs = refs[:nc], refs[nc:]
-    gates, ups, downs, refs = refs[:4], refs[4:8], refs[8:16], refs[16:]
-    by_gate, by_up = refs[0:2], refs[2:4]
-    outs = refs[-(8 + nc + 1) :]
-    grad_gates, grad_ups, kept = outs[0:2], outs[2:4], outs[4:8]
-    sums, total = outs[8 : 8 + nc], outs[8 + nc]
-    tok = blocks[0].shape[0]
-    quarter = kept[0].shape[1]
-    for k, block in enumerate(blocks):
-        for i in range(4):
-            kept[i][k * tok : (k + 1) * tok] = block[:, i * quarter : (i + 1) * quarter]
-    for dy in range(NY):
-        grad = nn(kept[0][...], downs[dy][...])
-        for i in range(1, 4):
-            grad = grad + nn(kept[i][...], downs[i * NY + dy][...])
-        grad_gate = (grad * by_gate[dy][...].astype(F32)).astype(BF16)
-        grad_up = (grad * by_up[dy][...].astype(F32)).astype(BF16)
-        grad_gates[dy][...] = grad_gate
-        grad_ups[dy][...] = grad_up
-        for i in range(4):
-            lanes = slice(i * quarter, (i + 1) * quarter)
-            dx, rows = i // 2, slice((i % 2) * quarter, (i % 2 + 1) * quarter)
-            part = nt(grad_gate, gates[dx * NY + dy][rows, :]) + nt(
-                grad_up, ups[dx * NY + dy][rows, :]
-            )
-            if dy == 0:
-                total[:, lanes] = part
-            else:
-                part = total[:, lanes] + part
-                for k, out in enumerate(sums):
-                    out[:, lanes] = part[k * tok : (k + 1) * tok].astype(out.dtype)
+def take(refs, *counts):
+    groups = []
+    for count in counts:
+        groups.append(refs[:count])
+        refs = refs[count:]
+    return *groups, refs
+
+
+def put_columns(block, kept):
+    width = kept[0].shape[1]
+    for i, out in enumerate(kept):
+        out[...] = block[:, i * width : (i + 1) * width]
+
+
+def mlp_forward_kernel(nc, block, *refs):
+    count = NY * nc
+    gates, ups, downs, refs = take(refs, NX * count, NX * count, 4 * count)
+    refs = refs[-(2 * nc + NY + NX + 2) :]
+    products, by_gate, by_up, kept, (out, total) = take(refs, NY, nc, nc, NX)
+    put_columns(block, kept)
+    hidden = gates[0].shape[1]
+    quarter = kept[0].shape[1] // 2
+    for k in range(nc):
+        for dy in range(NY):
+            at = dy * nc + k
+            lanes = slice(dy * hidden, (dy + 1) * hidden)
+
+            def through(weights):
+                return nn(kept[0][...], weights[at][...]) + nn(
+                    kept[1][...], weights[count + at][...]
+                )
+
+            gate, up = through(gates), through(ups)
+            chance = 1.0 / (1.0 + jnp.exp(-gate))
+            silu = gate * chance
+            product = (silu * up).astype(BF16)
+            products[dy][:, k * hidden : (k + 1) * hidden] = product
+            by_up[k][:, lanes] = silu.astype(BF16)
+            by_gate[k][:, lanes] = (up * (chance + silu * (1.0 - chance))).astype(BF16)
+            for i in range(4):
+                columns = slice(i * quarter, (i + 1) * quarter)
+                part = nt(product, downs[i * count + at][...])
+                total[:, columns] = part if k + dy == 0 else total[:, columns] + part
+    out[...] = total[...]
+
+
+def mlp_back_kernel(nc, block, *refs):
+    count = NY * nc
+    gates, ups, downs, by_gate, by_up, refs = take(
+        refs, NX * count, NX * count, 4 * count, nc, nc
+    )
+    refs = refs[-(2 * nc + NX + 2) :]
+    grad_gates, grad_ups, kept, (out, total) = take(refs, nc, nc, NX)
+    put_columns(block, kept)
+    hidden = gates[0].shape[1]
+    quarter = kept[0].shape[1] // 2
+    for k in range(nc):
+        for dy in range(NY):
+            at = dy * nc + k
+            lanes = slice(dy * hidden, (dy + 1) * hidden)
+            grad = 0.0
+            for i in range(4):
+                columns = slice((i % 2) * quarter, (i % 2 + 1) * quarter)
+                grad = grad + nn(kept[i // 2][:, columns], downs[i * count + at][...])
+            grad_gate = (grad * by_gate[k][:, lanes].astype(F32)).astype(BF16)
+            grad_up = (grad * by_up[k][:, lanes].astype(F32)).astype(BF16)
+            grad_gates[k][:, lanes] = grad_gate
+            grad_ups[k][:, lanes] = grad_up
+            for i in range(4):
+                columns = slice(i * quarter, (i + 1) * quarter)
+                rows = slice((i % 2) * quarter, (i % 2 + 1) * quarter)
+                weight = (i // 2) * count + at
+                part = nt(grad_gate, gates[weight][rows, :]) + nt(grad_up, ups[weight][rows, :])
+                total[:, columns] = part if k + dy == 0 else total[:, columns] + part
+    out[...] = total[...]
+
+
+def down_back_kernel(*refs):
+    *parts, out = refs
+    count = len(parts) // 3
+    near, far, products, _ = take(parts, count, count, count)
+    tok = near[0].shape[0]
+    step = out.shape[0] // 2
+    for i in range(2):
+        rows = slice(i * step, (i + 1) * step)
+        for j, product in enumerate(products):
+            part = tn(near[j][:, rows], product[:tok]) + tn(far[j][:, rows], product[tok:])
+            out[rows, :] = part if j == 0 else out[rows, :] + part
 
 
 def make_body(wide):
@@ -621,16 +643,30 @@
     def scatter_near(first, second):
         return send(first[2], x=1), send(second[1], y=1)
 
-    def scatter_rest(first, second, far, near):
-        first_c = send((first[1].astype(F32) + far[0].astype(F32)).astype(BF16), y=1)
-        second_c = send((second[2].astype(F32) + far[1].astype(F32)).astype(BF16), x=1)
+    def scatter_last(first, second, far, near):
         return (
-            first[0].astype(F32) + near[0].astype(F32) + first_c.astype(F32),
-            second[0].astype(F32) + near[1].astype(F32) + second_c.astype(F32),
+            send((first[1].astype(F32) + far[0].astype(F32)).astype(BF16), y=1),
+            send((second[2].astype(F32) + far[1].astype(F32)).astype(BF16), x=1),
+        )
+
+    def scatter_sum(first, second, near, last):
+        return (
+            first[0].astype(F32) + near[0].astype(F32) + last[0].astype(F32),
+            second[0].astype(F32) + near[1].astype(F32) + last[1].astype(F32),
         )
 
     def core_gather(block):
         return [block] + [send(block, c=k) for k in range(1, nc)]
+
+    def core_sums(blocks, hidden):
+        sums = []
+        for row in blocks:
+            total = row[0].astype(F32)
+            for k in range(1, nc):
+                total = total + send(row[k], c=k).astype(F32)
+            total = total.astype(BF16)
+            sums += [total[:, dy * hidden : (dy + 1) * hidden] for dy in range(NY)]
+        return sums
 
     def core_parts(parts):
         return [parts[0]] + [send(parts[k], c=k) for k in range(1, nc)]
@@ -651,6 +687,16 @@
         w_down,
         grad_output,
     ):
+        due = {}
+
+        def mark(name, value):
+            due.setdefault(PLAN[name], []).append(value)
+            return value
+
+        def at(point, value):
+            ready = due.pop(point, [])
+            return after(value, ready) if ready else value
+
         x = lax.axis_index("blk")
         spot = lax.axis_index("wide")
         z, y, c = spot // (NY * nc), (spot // nc) % NY, spot % nc
@@ -695,7 +741,8 @@
         down_rows = w_down.shape[0] // 2
         down_halves = w_down[:down_rows], w_down[down_rows:]
         far_down = send(down_halves[0], x=1), send(down_halves[1], y=1)
-        received = after(square(pieces), far_down)
+        mark("far_down", far_down)
+        received = at("join", square(pieces))
         own_rows, lengths_row = run(
             join_kernel,
             [(message, VMEM), (shaped((8, HEAD_DIM), F32), VMEM)],
@@ -708,25 +755,48 @@
         frequency = jnp.exp((lane % half).astype(F32) * (-2.0 * math.log(500000.0) / HEAD_DIM))
         cosine = jnp.cos(row * frequency)
         sine = jnp.sin(row * jnp.where(lane < half, -frequency, frequency))
+        mark("turns", (cosine, sine))
         w_ring = [own_rows, send(own_rows, r=-1)]
-        far_gate = send(after(w_gate, own_rows), x=1)
-        far_up = send(after(w_up, own_rows), y=1)
-        from_x = send(after(inputs, far_gate), x=1)
-        from_y = send(after(inputs, far_up), y=1)
         half_tok = tok // 2
-        from_xy = send(from_x[:half_tok], y=1), send(from_y[half_tok:], x=1)
-        near_gate = send(after(w_gate, from_xy[0]), y=1)
-        near_up = send(after(w_up, from_xy[1]), x=1)
-        w_ring.append(send(after(w_ring[1], cosine, sine, far_gate, far_up), r=-1))
-        w_ring.append(send(after(w_ring[2], from_xy), r=-1))
+        if PLAN["tokens_first"]:
+            from_x = send(after(inputs, own_rows), x=1)
+            from_y = send(after(inputs, own_rows), y=1)
+            from_xy = send(from_x[:half_tok], y=1), send(from_y[half_tok:], x=1)
+            early = {"xy": from_xy, "x": (from_x, from_y)}[PLAN["far_from"]]
+            far_gate = send(after(w_gate, early), x=1)
+            far_up = send(after(w_up, early), y=1)
+            near_gate = send(after(w_gate, far_up), y=1)
+            near_up = send(after(w_up, far_gate), x=1)
+        else:
+            far_gate = send(after(w_gate, own_rows), x=1)
+            far_up = send(after(w_up, own_rows), y=1)
+            from_x = send(after(inputs, far_gate), x=1)
+            from_y = send(after(inputs, far_up), y=1)
+            from_xy = send(from_x[:half_tok], y=1), send(from_y[half_tok:], x=1)
+            near_gate = send(after(w_gate, from_xy[0]), y=1)
+            near_up = send(after(w_up, from_xy[1]), x=1)
+        mark("far", (far_gate, far_up))
+        mark("tokens", (from_x, from_y))
+        mark("tokens_xy", from_xy)
+        mark("near", (near_gate, near_up))
+        own_gate, own_up = core_gather(w_gate), core_gather(w_up)
+        own_down = core_gather(w_down)
+        far_gate, far_up = core_gather(far_gate), core_gather(far_up)
+        far_down = core_gather(far_down[0]), core_gather(far_down[1])
+        mark("own_gate_c", (own_gate, own_up))
+        mark("own_down_c", own_down)
+        mark("far_c", (far_gate, far_up))
+        mark("far_down_c", far_down)
+        first_blocks = core_gather(own_rows)
+        w_ring.append(send(at("w2", w_ring[1]), r=-1))
+        second_blocks = core_gather(w_ring[1])
+        w_ring.append(send(at("w3", w_ring[2]), r=-1))
         x_all, x_kept = run(
             gather_kernel,
             [(shaped((group_tok, width)), VMEM), (shaped((group_tok, width)), HBM)],
             each([inputs, from_x, from_y, *from_xy], VMEM),
             scratch_shapes=[pltpu.SemaphoreType.DMA],
         )
-        w_ring[3] = after(w_ring[3], near_gate, near_up)
-        w_blocks = [core_gather(block) for block in w_ring]
         w_shape = shaped((GROUP * HEAD_DIM, 3 * HEADS))
         by_three = shaped((group_tok, 3 * HEADS), F32)
         out_shape = shaped((HEADS, width))
@@ -747,22 +817,38 @@
                 ],
             )
 
-        blocks = w_blocks[0] + w_blocks[1] + w_blocks[2]
+        blocks = first_blocks + second_blocks + core_gather(w_ring[2])
         gains, out_w, *w_parts, total = project((0, 1, 2), blocks, (), [(by_three, VMEM)])
+        mark("total", total)
+        last_block = core_gather(at("c3", w_ring[3]))
+        near_down = (
+            send(after(down_halves[0], near_gate), y=1),
+            send(after(down_halves[1], near_up), x=1),
+        )
+        mark("near_down", near_down)
+        near_gate, near_up = core_gather(near_gate), core_gather(near_up)
+        mark("near_c", (near_gate, near_up))
         gains, out_w, w_part, query, key, value, query_h, key_h, value_h, out_kept, stats = project(
             (3,),
-            w_blocks[3],
+            last_block,
             (total, gains, out_w),
             [(by_head_wide, VMEM), (by_head_wide, VMEM), (by_head, VMEM)]
             + [(by_head_wide, HBM), (by_head_wide, HBM), (by_head, HBM)]
             + [(out_shape, HBM), (by_token, VMEM)],
         )
         w_parts.append(w_part)
-        group_stats = group_sum(stats, near_gate, near_up)
-        last_gate = send(after(far_gate, group_stats, near_gate), y=1)
-        last_up = send(after(far_up, group_stats, near_up), x=1)
-        gate_w = [w_gate, near_gate, far_gate, last_gate]
-        up_w = [w_up, far_up, near_up, last_up]
+        early = {"near": near_gate[0]}
+        group_stats = at("stats2", group_sum(at("stats", stats)))
+        early["stats"] = group_stats
+        last_gate = send(after(far_gate[0], early[PLAN["last_from"]], near_gate[0]), y=1)
+        last_up = send(after(far_up[0], early[PLAN["last_from"]], near_up[0]), x=1)
+        mark("last", (last_gate, last_up))
+        last_gate, last_up = core_gather(last_gate), core_gather(last_up)
+        mark("last_c", (last_gate, last_up))
+        gate_w = [*own_gate, *near_gate, *far_gate, *last_gate]
+        up_w = [*own_up, *far_up, *near_up, *last_up]
+        near_down = core_gather(near_down[0]), core_gather(near_down[1])
+        mark("near_down_c", near_down)
 
         query_r, key_r, attended, scales, *parts = run(
             attend_kernel,
@@ -775,49 +861,53 @@
             ],
             scratch_shapes=[held(by_head), held(by_head), held(by_head), dma(3)],
         )
-        parts = square(after(parts, gate_w, up_w))
-        first, second = after(down_halves, parts)
-        first_x, second_y = after(far_down, parts)
-        down_first = first, send(first, y=1), first_x, send(first_x, y=1)
-        down_second = second, second_y, send(second, x=1), send(second_y, x=1)
+        parts = square(at("rs", parts))
+        first_x, second_y = far_down
+        last_down = (
+            core_gather(send(after(first_x[0], parts), y=1)),
+            core_gather(send(after(second_y[0], parts), x=1)),
+        )
+        own_first = [part[:down_rows] for part in own_down]
+        own_second = [part[down_rows:] for part in own_down]
+        down_first = own_first, near_down[0], first_x, last_down[0]
+        down_second = own_second, second_y, near_down[1], last_down[1]
         down_w = [
-            half[dx * NY + dy]
+            piece
             for dx in range(NX)
             for half in (down_first, down_second)
             for dy in range(NY)
+            for piece in half[dx * NY + dy]
         ]
         branch, hidden_state, mlp_in = run(
             branch_kernel,
             [(tokens_wide, auto), (tokens_wide, auto), (tokens_shape, VMEM)],
-            [(pos, SMEM), *each(parts, auto), (inputs, auto), (gains, VMEM)],
+            [(pos, SMEM), *each(at("k4", parts), auto), (inputs, auto), (gains, VMEM)],
         )
 
         half_width = width // NX
         quarter = half_width // 2
-        m = nc * tok
-
-        def mlp_call(kernel, s, block, extra, kept_columns, before):
+
+        def mlp_call(kernel, s, block, extra, narrow, before):
             def rows_of(array):
-                return pl.BlockSpec((m, array.shape[1]), lambda i: (s, 0))
-
-            ins = each(core_gather(block), auto)
-            ins += each((*gate_w, *up_w, *down_w), VMEM) + each(extra, rows_of)
-            columns = [hidden] * (8 - len(kept_columns)) + list(kept_columns)
-            outs = each([shaped((NZ * m, count)) for count in columns], rows_of)
-            outs += [(tokens_wide, VMEM)] + [(tokens_shape, VMEM)] * (nc - 1)
+                count = array.shape[0] // tok
+                return pl.BlockSpec((tok, array.shape[1]), lambda i: (s % count, 0))
+
+            ins = each((block, *gate_w, *up_w, *down_w), VMEM) + each(extra, rows_of)
+            columns, height = narrow
+            outs = [shaped((NZ * tok, count)) for count in columns]
+            outs = each(outs + [shaped((height, half_width))] * NX, rows_of)
             aliases = {}
             if before is not None:
-                aliases = {len(ins) + i: i for i in range(8)}
+                aliases = {len(ins) + i: i for i in range(len(before))}
                 ins += each(before, HBM)
-            results = run(
+            *kept, total = run(
                 functools.partial(kernel, nc),
-                outs,
+                [*outs, (tokens_wide, VMEM)],
                 ins,
-                limit=20 if nc == 2 else 56,
                 input_output_aliases=aliases,
-                scratch_shapes=[pltpu.VMEM((m, width), F32)],
+                scratch_shapes=[held(tokens_wide)],
             )
-            return results[:8], core_parts(results[8:])
+            return kept, total
 
         def summed(parts):
             total = parts[0].astype(F32)
@@ -825,29 +915,49 @@
                 total = total + part.astype(F32)
             return total
 
-        def mlp_pass(kernel, block, extra, kept_columns):
+        def mlp_pass(name, kernel, block, extra, columns, height):
+            narrow = columns, height
             near = send(block, r=-1)
-            kept, first = mlp_call(kernel, 1, near, extra, kept_columns, None)
             middle = send(near, r=-1)
-            moving = send(summed(first).astype(BF16), r=-1)
-            kept, own = mlp_call(kernel, 0, block, extra, kept_columns, kept)
-            far = send(after(middle, first[0]), r=-1)
-            kept, second = mlp_call(kernel, 2, middle, extra, kept_columns, kept)
-            far = after(far, moving)
-            kept, third = mlp_call(kernel, 3, far, extra, kept_columns, kept)
-            sent = [summed(second + [moving]).astype(BF16)]
-            sent.append(summed(third + [send(sent[0], r=-1)]).astype(BF16))
-            return kept, own + [send(sent[1], r=-1)], sent
-
-        kept, parts, _ = mlp_pass(mlp_forward_kernel, mlp_in, (), (half_width, half_width))
-
-        products, by_gate, by_up, mlp_all = kept[0:2], kept[2:4], kept[4:6], kept[6:8]
+            kept, first = mlp_call(kernel, 1, at(name + "1", near), extra, narrow, None)
+            far = send(after(middle, first) if PLAN[name + "_lead"] else middle, r=-1)
+            sent = [first.astype(BF16)]
+            moving = send(sent[0], r=-1)
+            kept, own = mlp_call(kernel, 0, block, extra, narrow, kept)
+            early = []
+            if height < NZ * tok:
+                early, kept = kept[-NX:], kept[:-NX]
+                early = square([early[dx] for dx, dy in SQUARE])
+                mark("near_grads", early[1:3])
+                mark("near_grads_xy", early[3])
+            middle = at(name + "2", middle)
+            if PLAN[name + "_out"]:
+                middle = after(middle, sent[0])
+            kept, second = mlp_call(kernel, 2, middle, extra, narrow, kept)
+            far = at(name + "3", far)
+            if PLAN[name + "_hold"]:
+                far = after(far, moving)
+            kept, third = mlp_call(kernel, 3, far, extra, narrow, kept)
+            sent.append(summed([second, moving]).astype(BF16))
+            sent.append(summed([third, send(sent[1], r=-1)]).astype(BF16))
+            parts = [own, send(at(name + "4", sent[2]), r=-1)]
+            return kept, parts, sent, early
+
+        columns = [nc * hidden] * NY + [NY * hidden] * 2 * nc
+        kept, parts, sent, _ = mlp_pass(
+            "f", mlp_forward_kernel, mlp_in, (), columns, NZ * tok
+        )
+        products, by_gate, by_up, mlp_all = take(kept, NY, nc, nc)
+
+        got_products = square([after(products, sent[PLAN["products_from"]])[dy] for dx, dy in SQUARE])
+        mark("products", got_products[1:3])
+        mark("products_xy", got_products[3])
         output, grad_mlp, grad_gain_mlp = run(
             functools.partial(mlp_kernel, len(parts)),
             [(tokens_shape, auto), (tokens_shape, VMEM), (wide_small, VMEM)],
             [
                 (pos, SMEM),
-                *each(parts, auto),
+                *each(at("m1", parts), auto),
                 (hidden_state, auto),
                 (gains, VMEM),
                 (grad_out, auto),
@@ -855,14 +965,17 @@
             scratch_shapes=[held(tokens_wide)] * 2,
         )
         extra = *by_gate, *by_up
-        kept, parts, sent = mlp_pass(mlp_back_kernel, grad_mlp, extra, (quarter,) * 4)
-        grad_gates, grad_ups, grad_all = kept[0:2], kept[2:4], kept[4:8]
+        columns = [NY * hidden] * 2 * nc
+        kept, parts, sent, near_grads = mlp_pass(
+            "b", mlp_back_kernel, grad_mlp, extra, columns, 2 * tok
+        )
+        grad_gates, grad_ups, grad_all = take(kept, nc, nc)
         grad_hidden, grad_branch, grad_gain_attn = run(
             functools.partial(branch_back_kernel, len(parts)),
             [(tokens_wide, auto), (tokens_shape, VMEM), (wide_small, VMEM)],
             [
                 (pos, SMEM),
-                *each(parts, auto),
+                *each(at("k9", parts), auto),
                 (branch, auto),
                 (gains, VMEM),
                 (grad_out, auto),
@@ -871,21 +984,30 @@
         )
 
         def products_of(left, right):
-            return [tn(left[dx], right[dy]).astype(BF16) for dx, dy in SQUARE]
-
-        grad_all = after(grad_all, sent[0])
-        wd_pair = products_of(grad_all[0::2], products), products_of(grad_all[1::2], products)
-        wd_far = scatter_far(*wd_pair)
-        wd_near = scatter_near(*after(wd_pair, wd_far))
-        grad_branch = after(grad_branch, wd_near)
-        mlp_all = after(mlp_all, sent[1])
-        grad_wg = products_of(mlp_all, grad_gates)
-        grad_wu = products_of(mlp_all, grad_ups)
-
-        blocks = square([grad_branch] * GROUP)
-        w_pair = grad_wg, grad_wu
-        blocks = after(blocks, w_pair)
-        w_far = scatter_far(*after(w_pair, blocks))
+            return [[tn(block, grad).astype(BF16) for grad in right] for block in left]
+
+        early = {"branch": grad_branch, "sent": sent[2]}
+        if PLAN["far_grads_from"] in early:
+            far_grads = after(grad_all, early[PLAN["far_grads_from"]])
+            far_grads = square([far_grads[dx] for dx, dy in SQUARE])
+            mark("far_grads", far_grads[1:3])
+            mark("far_grads_xy", far_grads[3])
+        blocks = square([at("ag", grad_branch)] * GROUP)
+        early.update({"block": blocks[1], "all": blocks})
+        mlp_all = after(mlp_all, early[PLAN["dots_from"]])
+        wg_blocks = products_of(mlp_all, grad_gates)
+        wu_blocks = products_of(mlp_all, grad_ups)
+        mark("dots", (wg_blocks, wu_blocks))
+        if PLAN["far_grads_from"] in ("block", "all"):
+            far_grads = after(grad_all, early[PLAN["far_grads_from"]])
+            far_grads = square([far_grads[dx] for dx, dy in SQUARE])
+            mark("far_grads", far_grads[1:3])
+            mark("far_grads_xy", far_grads[3])
+        blocks = at("blocks", blocks)
+        if PLAN["sums_late"]:
+            wg_blocks, wu_blocks = after((wg_blocks, wu_blocks), blocks)
+        w_pair = core_sums(wg_blocks, hidden), core_sums(wu_blocks, hidden)
+        mark("sums", w_pair)
         grad_query, grad_key, grad_value, stats, head_gains, branch_all = run(
             attend_back_kernel,
             [
@@ -918,12 +1040,17 @@
             project_back_kernel,
             [(shaped((group_tok, 3 * HEADS)), VMEM)],
             [
-                (after(group_sum(stats), w_far), VMEM),
+                (at("g2", group_sum(at("g1", stats))), VMEM),
                 (scales, VMEM),
                 *each((grad_query, grad_key, grad_value, query_h, key_h), VMEM),
             ],
         )
-        w_near = scatter_near(*after(w_pair, grads))
+        w_far = scatter_far(*(after(w_pair, grads) if PLAN["w_far_late"] else w_pair))
+        w_near = scatter_near(*after(w_pair, w_far))
+        w_last = scatter_last(*w_pair, after(w_far, w_near) if PLAN["w_last_late"] else w_far, w_near)
+        mark("w_far", w_far)
+        mark("w_near", w_near)
+        mark("w_last", w_last)
 
         def weight_parts(places):
             height = message.shape[0]
@@ -948,17 +1075,39 @@
             ]
 
         (first,) = weight_parts((1,))
-        w_moving = send(after(summed(first).astype(BF16), w_far), r=-1)
-        grads = after(grads, first)
+        factors = []
+        for *grads_of, product in zip(near_grads, far_grads, got_products):
+            for k in range(nc):
+                pieces = *grads_of, product[:, k * hidden : (k + 1) * hidden]
+                factors.append([send(piece, c=k) if k else piece for piece in pieces])
+        mark("factors", factors)
+        (grad_wd,) = run(
+            down_back_kernel,
+            [(shaped(w_down.shape, F32), VMEM)],
+            each([entry[i] for i in range(3) for entry in factors], VMEM),
+        )
+
+        mark("grad_wd", grad_wd)
+        w_moving = send(at("w1", summed(first).astype(BF16)), r=-1)
+        early = {"first": first, "far": w_far, "none": (), "both": (first, w_far)}
+        grads = after(grads, early[PLAN["second_after"]])
         second, third, own = weight_parts((2, 3, 0))
+        x_parts = run(
+            input_back_kernel,
+            [(tokens_shape, VMEM)] * GROUP,
+            [(pos, SMEM), (after(grads, own), VMEM), *each(w_parts, VMEM)],
+            scratch_shapes=[pltpu.VMEM((group_tok, GROUP * HEAD_DIM), BF16)],
+        )
+        mark("x_parts", x_parts)
+        early = {"parts": x_parts, "near": w_near, "last": w_last}
+        from_x = [x_parts[0]] + square([x_parts[0], *after(x_parts[1:3], early[PLAN["x_from"]]), x_parts[3]])[1:3]
+        mark("x_sums", from_x)
         sent = summed(second + [w_moving]).astype(BF16)
-        w_moving = send(after(sent, own, w_near), r=-1)
-        grad_wg, grad_wu = scatter_rest(*w_pair, *after((w_far, w_near), sent))
-        wd_far, wd_near = after((wd_far, wd_near), grad_wg, grad_wu)
-        grad_wd = jnp.concatenate(scatter_rest(*wd_pair, wd_far, wd_near), axis=0)
+        w_moving = send(after(at("t2", sent), own), r=-1)
         sent = summed(third + [w_moving]).astype(BF16)
-        w_moving = send(sent, r=-1)
-        parts = own + [w_moving]
+        w_moving = send(at("t3", sent), r=-1)
+        grad_wg, grad_wu = scatter_sum(*w_pair, w_near, w_last)
+        parts = at("collect", own + [w_moving])
         grad_wo, *messages = run(
             functools.partial(collect_kernel, len(parts)),
             [(shaped((rows, width), F32), auto)] + [(piece, VMEM)] * GROUP,
@@ -967,15 +1116,11 @@
         grad_wq, grad_wk, grad_wv, total_gains = run(
             spread_kernel,
             [(shaped((rows, width), F32), auto)] * 3 + [(shaped((8, HEAD_DIM), F32), VMEM)],
-            [(pos, SMEM), *each(square(messages), auto)],
-        )
-        parts = run(
-            input_back_kernel,
-            [(tokens_shape, VMEM)] * GROUP,
-            [(pos, SMEM), (after(grads, sent), VMEM), *each(w_parts, VMEM)],
-            scratch_shapes=[pltpu.VMEM((group_tok, GROUP * HEAD_DIM), BF16)],
-        )
-        grad_x = summed([grad_hidden, *square(after(parts, messages))])
+            [(pos, SMEM), *each(at("spread", square(messages)), auto)],
+        )
+        early = {"messages": messages, "parts": x_parts, "sent": from_x[1:]}
+        last_x = send(after(x_parts[3], early[PLAN["x_last_from"]]), x=1, y=1)
+        grad_x = summed([grad_hidden, *from_x, last_x])
 
         return (
             output[None],

time: 538 us -> 517 us (0.961)
  waiting for transfers between devices: 321 us -> 258 us
  Pallas kernels: 87.9 us -> 113 us
  starting transfers between devices: 89.5 us -> 104 us
    ppermute x87 -> x105, waiting for transfers between devices: 321 us -> 258 us  [send(): return lax.ppermute(value, AXES, pairs)]
    pallas_call x24 -> x25, Pallas kernels: 87.9 us -> 113 us  [run(): pl.pallas_call(body, grid=(1,), out_shape=[pltpu.HBM(out.shape, out.dtype...]
    ppermute x87 -> x105, starting transfers between devices: 89.5 us -> 104 us  [send(): return lax.ppermute(value, AXES, pairs)]
    dot_general x16 -> x8, matrix products: 16.1 us -> 13 us  [tn(): lax.dot_general(left, right, (((0,), (0,)), ((), ())), preferred_element_...]
  transfers between devices with their start and end apart: 87 -> 105, of which waited for: 45 -> 49; matrix products, arithmetic and copies ran while one was open for 5% -> 5% of each run, Pallas kernels for 14% -> 20%
where the time goes in v5:
time: 517 us; the launch traced here: 514 us
  waiting for transfers between devices  258 us (50%)
  Pallas kernels  113 us (22%)
  starting transfers between devices  104 us (20%)
  matrix products  13 us (3%)
  other arithmetic  12.1 us (2%)
  local copies, waits for them, and re-layouts  11.6 us (2%)
    ppermute x105, waiting for transfers between devices, send(): return lax.ppermute(value, AXES, pairs)  258 us
    pallas_call x25, Pallas kernels, run(): pl.pallas_call(body, grid=(1,), out_shape=[pltpu.HBM(out.shape, out.dtype...  113 us
    ppermute x105, starting transfers between devices, send(): return lax.ppermute(value, AXES, pairs)  104 us
    dot_general x8, matrix products, tn(): lax.dot_general(left, right, (((0,), (0,)), ((), ())), preferred_element_...  13 us
  transfers between devices with their start and end apart: 105, of which 49 were waited for; matrix products, arithmetic and copies ran while one was open for 5% of the time, Pallas kernels for 20%

profile of v5, /device:TPU:0, one launch (start us, length us, event | category | flops | bytes accessed | tf_op | source)
XLA Modules:
  0.0 514.3 jit_solution(15946993872014650552)
XLA Ops:
  2.0 3.0 collective-permute-start.3
  11.6 2.9 collective-permute-start.2
  14.5 14.5 %collective-permute-done.refs_1_ = bf16[80,1536]{1,0:T(8,128)(2,1)S(1)} collective-permute-done((bf16[80,1536]{1,0:T(8,128)(2,1)S(1)}, bf16[80,1536]{1,0:T(8,128)(2,1)S(1)}, u32[]{:S(2)}, u32[]{:S(2)}) %collective-permute-start) | collective-permute-done | bytes 245792 | tf_op jit(solution)/shard_map/ppermute | solution.py:623
  30.0 2.6 collective-permute-start.9
  34.7 10.5 %collective-permute-done.5.refs_1_ = bf16[128,2048]{1,0:T(8,128)(2,1)} collective-permute-done((bf16[128,2048]{1,0:T(8,128)(2,1)}, bf16[128,2048]{1,0:T(8,128)(2,1)}, u32[]{:S(2)}, u32[]{:S(2)}) %collective-permute-start.5) | collective-permute-done | bytes 524320 | tf_op jit(solution)/shard_map/ppermute | solution.py:623
  50.2 2.4 collective-permute-done.7.refs_3_
  54.6 3.4 collective-permute-start.10
  62.3 16.8 %collective-permute-done.10.refs_4_ = bf16[1040,512]{1,0:T(8,128)(2,1)S(1)} collective-permute-done((bf16[1040,512]{1,0:T(8,128)(2,1)}, bf16[1040,512]{1,0:T(8,128)(2,1)S(1)}, u32[]{:S(2)}, u32[]{:S(2)}) %collective-permute-start.10) | collective-permute-done | bytes 1064992 | tf_op jit(solution)/shard_map/ppermute | solution.py:623
  79.1 4.6 collective-permute-done.11.refs_4_
  83.7 2.2 collective-permute-done.12.refs_10_
  90.4 2.7 shard_map.239
  93.0 5.8 %shard_map.240 = (f32[8,2048]{1,0:T(8,128)S(1)}, bf16[512,2048]{1,0:T(8,128)(2,1)S(1)}, bf16[512,1536]{1,0:T(8,128)(2,1)}, bf16[512,1536]{1,0:T(8,128)(2,1)}, bf...) custom-call(s32[5]{0:T(128)S(1)} %stack.34.pos, bf16[512,2048]{1,0:T(8,128)(2,1)S(1)} %get-tuple-element.225.x_all, ...), custom_call_target="tpu_custom_call" | custom-call | tf_op jit(solution)/shard_map/pallas_call | solution.py:51
  98.9 12.8 %collective-permute-done.16.refs_2_ = bf16[1024,512]{1,0:T(8,128)(2,1)S(1)} collective-permute-done((bf16[1024,512]{1,0:T(8,128)(2,1)S(1)}, bf16[1024,512]{1,0:T(8,128)(2,1)S(1)}, u32[]{:S(2)}, u32[]{:S(2)}) %collective-permute-start.16) | collective-permute-done | bytes 1048608 | tf_op jit(solution)/shard_map/ppermute | solution.py:623
  115.4 3.8 shard_map.241
  128.8 6.8 %collective-permute-done.35.refs_28_ = bf16[512,512]{1,0:T(8,128)(2,1)S(1)} collective-permute-done((bf16[512,512]{1,0:T(8,128)(2,1)S(1)}, bf16[512,512]{1,0:T(8,128)(2,1)S(1)}, u32[]{:S(2)}, u32[]{:S(2)}) %collective-permute-start.35) | collective-permute-done | bytes 524320 | tf_op jit(solution)/shard_map/ppermute | solution.py:623
  137.1 6.2 %shard_map.242 = (bf16[512,512]{1,0:T(8,128)(2,1)}, bf16[512,512]{1,0:T(8,128)(2,1)}, bf16[512,512]{1,0:T(8,128)(2,1)}, f32[8,512]{1,0:T(8,128)S(1)}, bf16[128,2...) custom-call(s32[5]{0:T(128)S(1)} %stack.34.pos, ...), custom_call_target="tpu_custom_call" | custom-call | tf_op jit(solution)/shard_map/pallas_call | solution.py:51
  143.4 13.6 %collective-permute-done.32.refs_14_ = bf16[1024,512]{1,0:T(8,128)(2,1)S(1)} collective-permute-done((bf16[1024,512]{1,0:T(8,128)(2,1)S(1)}, bf16[1024,512]{1,0:T(8,128)(2,1)S(1)}, u32[]{:S(2)}, u32[]{:S(2)}) %collective-permute-start.32) | collective-permute-done | bytes 1048608 | tf_op jit(solution)/shard_map/ppermute | solution.py:623
  162.5 10.0 %collective-permute-done.37.refs_1_ = bf16[128,2048]{1,0:T(8,128)(2,1)S(1)} collective-permute-done((bf16[128,2048]{1,0:T(8,128)(2,1)S(1)}, bf16[128,2048]{1,0:T(8,128)(2,1)S(1)}, u32[]{:S(2)}, u32[]{:S(2)}) %collective-permute-start.37) | collective-permute-done | bytes 524320 | tf_op jit(solution)/shard_map/ppermute | solution.py:623
  172.5 2.4 collective-permute-done.38.refs_2_
  174.9 7.3 %collective-permute-done.39.refs_3_ = bf16[128,2048]{1,0:T(8,128)(2,1)S(1)} collective-permute-done((bf16[128,2048]{1,0:T(8,128)(2,1)S(1)}, bf16[128,2048]{1,0:T(8,128)(2,1)S(1)}, u32[]{:S(2)}, u32[]{:S(2)}) %collective-permute-start.39) | collective-permute-done | bytes 524320 | tf_op jit(solution)/shard_map/ppermute | solution.py:623
  183.1 2.5 collective-permute-start.42
  187.3 6.2 %collective-permute-done.44.refs_30_ = bf16[512,512]{1,0:T(8,128)(2,1)S(1)} collective-permute-done((bf16[512,512]{1,0:T(8,128)(2,1)}, bf16[512,512]{1,0:T(8,128)(2,1)S(1)}, u32[]{:S(2)}, u32[]{:S(2)}) %collective-permute-start.44) | collective-permute-done | bytes 524320 | tf_op jit(solution)/shard_map/ppermute | solution.py:623
  194.0 2.0 collective-permute-done.46.block
  198.0 6.7 %shard_map.244 = (bf16[512,1024]{1,0:T(8,128)(2,1)S(1)}, bf16[512,1024]{1,0:T(8,128)(2,1)S(1)}, bf16[512,1024]{1,0:T(8,128)(2,1)S(1)}, bf16[512,1024]{1,0:T(8,12...) custom-call(bf16[128,2048]{1,0:T(8,128)(2,1)S(1)} %collective-permut, ...), custom_call_target="tpu_custom_call" | custom-call | tf_op jit(solution)/shard_map/pallas_call | solution.py:51
  205.3 5.8 %collective-permute-done.47.block = bf16[128,2048]{1,0:T(8,128)(2,1)S(1)} collective-permute-done((bf16[128,2048]{1,0:T(8,128)(2,1)S(1)}, bf16[128,2048]{1,0:T(8,128)(2,1)S(1)}, u32[]{:S(2)}, u32[]{:S(2)}) %collective-permute-start.47) | collective-permute-done | bytes 524320 | tf_op jit(solution)/shard_map/ppermute | solution.py:623
  212.7 6.6 %shard_map.245 = (bf16[512,1024]{1,0:T(8,128)(2,1)S(1)}, bf16[512,1024]{1,0:T(8,128)(2,1)S(1)}, bf16[512,1024]{1,0:T(8,128)(2,1)S(1)}, bf16[512,1024]{1,0:T(8,12...) custom-call(bf16[128,2048]{1,0:T(8,128)(2,1)S(1)} %get-tuple-element, ...), custom_call_target="tpu_custom_call", output_to_operand_aliasing={{0}: (33, {}), {1}: (34, {}), {2}: (35, {}), {3}: (36, {}),... | custom-call | tf_op jit(solution)/shard_map/pallas_call | solution.py:51
  219.3 6.7 %shard_map.246 = (bf16[512,1024]{1,0:T(8,128)(2,1)S(1)}, bf16[512,1024]{1,0:T(8,128)(2,1)S(1)}, bf16[512,1024]{1,0:T(8,128)(2,1)S(1)}, bf16[512,1024]{1,0:T(8,12...) custom-call(bf16[128,2048]{1,0:T(8,128)(2,1)S(1)} %collective-permut, ...), custom_call_target="tpu_custom_call", output_to_operand_aliasing={{0}: (33, {}), {1}: (34, {}), {2}: (35, {}), {3}: (36, {}),... | custom-call | tf_op jit(solution)/shard_map/pallas_call | solution.py:51
  226.6 7.0 %collective-permute-done.48.block = bf16[128,2048]{1,0:T(8,128)(2,1)S(1)} collective-permute-done((bf16[128,2048]{1,0:T(8,128)(2,1)S(1)}, bf16[128,2048]{1,0:T(8,128)(2,1)S(1)}, u32[]{:S(2)}, u32[]{:S(2)}) %collective-permute-start.48) | collective-permute-done | bytes 524320 | tf_op jit(solution)/shard_map/ppermute | solution.py:623
  233.6 6.6 %shard_map.247 = (bf16[512,1024]{1,0:T(8,128)(2,1)S(1)}, bf16[512,1024]{1,0:T(8,128)(2,1)S(1)}, bf16[512,1024]{1,0:T(8,128)(2,1)S(1)}, bf16[512,1024]{1,0:T(8,12...) custom-call(bf16[128,2048]{1,0:T(8,128)(2,1)S(1)} %collective-permut, ...), custom_call_target="tpu_custom_call", output_to_operand_aliasing={{0}: (33, {}), {1}: (34, {}), {2}: (35, {}), {3}: (36, {}),... | custom-call | tf_op jit(solution)/shard_map/pallas_call | solution.py:51
  246.4 7.0 %collective-permute-done.51.refs_1_ = bf16[128,2048]{1,0:T(8,128)(2,1)S(1)} collective-permute-done((bf16[128,2048]{1,0:T(8,128)(2,1)S(1)}, bf16[128,2048]{1,0:T(8,128)(2,1)S(1)}, u32[]{:S(2)}, u32[]{:S(2)}) %collective-permute-start.51) | collective-permute-done | bytes 524320 | tf_op jit(solution)/shard_map/ppermute | solution.py:623
  253.4 1.9 shard_map.248
  255.4 2.5 collective-permute-start.52
  257.8 2.5 collective-permute-start.59
  260.3 6.8 %collective-permute-done.52.block = bf16[128,2048]{1,0:T(8,128)(2,1)S(1)} collective-permute-done((bf16[128,2048]{1,0:T(8,128)(2,1)S(1)}, bf16[128,2048]{1,0:T(8,128)(2,1)S(1)}, u32[]{:S(2)}, u32[]{:S(2)}) %collective-permute-start.52) | collective-permute-done | bytes 524320 | tf_op jit(solution)/shard_map/ppermute | solution.py:623
  267.1 2.8 collective-permute-start.55
  272.6 8.2 %shard_map.249 = (bf16[512,1024]{1,0:T(8,128)(2,1)S(1)}, bf16[512,1024]{1,0:T(8,128)(2,1)S(1)}, bf16[512,1024]{1,0:T(8,128)(2,1)S(1)}, bf16[512,1024]{1,0:T(8,12...) custom-call(bf16[128,2048]{1,0:T(8,128)(2,1)S(1)} %collective-permute-done.52.blo, ...), custom_call_target="tpu_custom_call" | custom-call | tf_op jit(solution)/shard_map/pallas_call | solution.py:51
  281.4 8.1 %shard_map.250 = (bf16[512,1024]{1,0:T(8,128)(2,1)S(1)}, bf16[512,1024]{1,0:T(8,128)(2,1)S(1)}, bf16[512,1024]{1,0:T(8,128)(2,1)S(1)}, bf16[512,1024]{1,0:T(8,12...) custom-call(bf16[128,2048]{1,0:T(8,128)(2,1)S(1)} %get-tuple-element, ...), custom_call_target="tpu_custom_call", output_to_operand_aliasing={{0}: (37, {}), {1}: (38, {}), {2}: (39, {}), {3}: (40, {}),... | custom-call | tf_op jit(solution)/shard_map/pallas_call | solution.py:51
  291.3 2.5 collective-permute-start.56
  293.8 8.1 %shard_map.251 = (bf16[512,1024]{1,0:T(8,128)(2,1)S(1)}, bf16[512,1024]{1,0:T(8,128)(2,1)S(1)}, bf16[512,1024]{1,0:T(8,128)(2,1)S(1)}, bf16[512,1024]{1,0:T(8,12...) custom-call(bf16[128,2048]{1,0:T(8,128)(2,1)S(1)} %collective-permut, ...), custom_call_target="tpu_custom_call", output_to_operand_aliasing={{0}: (37, {}), {1}: (38, {}), {2}: (39, {}), {3}: (40, {})} | custom-call | tf_op jit(solution)/shard_map/pallas_call | solution.py:51
  302.7 2.3 collective-permute-start.62
  305.0 8.2 %shard_map.252 = (bf16[512,1024]{1,0:T(8,128)(2,1)S(1)}, bf16[512,1024]{1,0:T(8,128)(2,1)S(1)}, bf16[512,1024]{1,0:T(8,128)(2,1)S(1)}, bf16[512,1024]{1,0:T(8,12...) custom-call(bf16[128,2048]{1,0:T(8,128)(2,1)S(1)} %collective-permut, ...), custom_call_target="tpu_custom_call", output_to_operand_aliasing={{0}: (37, {}), {1}: (38, {}), {2}: (39, {}), {3}: (40, {}),... | custom-call | tf_op jit(solution)/shard_map/pallas_call | solution.py:51
  313.4 2.9 collective-permute-start.63
  318.6 6.2 %collective-permute-done.63.refs_1_ = bf16[128,2048]{1,0:T(8,128)(2,1)S(1)} collective-permute-done((bf16[128,2048]{1,0:T(8,128)(2,1)S(1)}, bf16[128,2048]{1,0:T(8,128)(2,1)S(1)}, u32[]{:S(2)}, u32[]{:S(2)}) %collective-permute-start.63) | collective-permute-done | bytes 524320 | tf_op jit(solution)/shard_map/ppermute | solution.py:623
  329.1 2.1 collective-permute-start.68
  331.2 10.5 %collective-permute-done.66.refs_7_ = bf16[128,2048]{1,0:T(8,128)(2,1)S(1)} collective-permute-done((bf16[128,2048]{1,0:T(8,128)(2,1)S(1)}, bf16[128,2048]{1,0:T(8,128)(2,1)S(1)}, u32[]{:S(2)}, u32[]{:S(2)}) %collective-permute-start.66) | collective-permute-done | bytes 524320 | tf_op jit(solution)/shard_map/ppermute | solution.py:623
  346.9 2.6 convolution_convert_fusion.4
  349.5 2.6 convolution_convert_fusion.6
  356.5 8.1 %shard_map.254 = (f32[512,512]{1,0:T(8,128)S(1)}, f32[512,512]{1,0:T(8,128)S(1)}, bf16[512,512]{1,0:T(8,128)(2,1)S(1)}, f32[8,512]{1,0:T(8,128)S(1)}, f32[8,512]...) custom-call(s32[5]{0:T(128)S(1)} %stack.34.pos, f32[8,128]{1,0:T(8,128)S(1)} %get-tuple-element.238.refs_1_.refs_0_, ...), custom_call_target="tpu_custom_call" | custom-call | tf_op jit(solution)/shard_map/pallas_call | solution.py:51
  371.7 2.7 collective-permute-done.74
  375.4 2.8 collective-permute-done.75
  379.9 2.3 shard_map.256
  382.3 2.7 collective-permute-done.76
  385.0 4.6 shard_map.257
  390.1 2.4 collective-permute-start.84
  394.5 23.1 %collective-permute-done.78 = bf16[1024,512]{1,0:T(8,128)(2,1)S(1)} collective-permute-done((bf16[1024,512]{1,0:T(8,128)(2,1)S(1)}, bf16[1024,512]{1,0:T(8,128)(2,1)S(1)}, u32[]{:S(2)}, u32[]{:S(2)}) %collective-permute-start.78) | collective-permute-done | bytes 1048608 | tf_op jit(solution)/shard_map/ppermute | solution.py:623
  420.5 3.9 collective-permute-start.85
  426.6 15.4 %collective-permute-done.80 = bf16[1024,512]{1,0:T(8,128)(2,1)S(1)} collective-permute-done((bf16[1024,512]{1,0:T(8,128)(2,1)S(1)}, bf16[1024,512]{1,0:T(8,128)(2,1)S(1)}, u32[]{:S(2)}, u32[]{:S(2)}) %collective-permute-start.80) | collective-permute-done | bytes 1048608 | tf_op jit(solution)/shard_map/ppermute | solution.py:623
  443.7 4.3 shard_map.258
  450.3 3.9 collective-permute-start.86
  458.6 5.8 %shard_map.259 = f32[1024,512]{1,0:T(8,128)} custom-call(bf16[256,1024]{1,0:T(8,128)(2,1)S(1)} %get-tuple-element.311.refs_0_, bf16[256,1024]{1,0:T(8,128)(2,1)S(1)} %collective-permute-done.89.refs_1_, bf16[256,1024]{1,0:T(8,128)(2,1)S(1)} %collective-permute-done.57.refs_2_, bf16[256,1024]{1,0:T(8,128)(2,1)S(1)} %collective-permute-done.92.refs_3_, ...), custom_call_target="tpu_custom_call" | custom-call | tf_op jit(solution)/shard_map/pallas_call | solution.py:51
  465.4 9.8 %collective-permute-done.88 = bf16[1024,512]{1,0:T(8,128)(2,1)S(1)} collective-permute-done((bf16[1024,512]{1,0:T(8,128)(2,1)S(1)}, bf16[1024,512]{1,0:T(8,128)(2,1)S(1)}, u32[]{:S(2)}, u32[]{:S(2)}) %collective-permute-start.88) | collective-permute-done | bytes 1048608 | tf_op jit(solution)/shard_map/ppermute | solution.py:623
  476.9 3.7 collective-permute-done.87
  485.3 17.5 %collective-permute-done.82 = bf16[128,2048]{1,0:T(8,128)(2,1)S(1)} collective-permute-done((bf16[128,2048]{1,0:T(8,128)(2,1)S(1)}, bf16[128,2048]{1,0:T(8,128)(2,1)S(1)}, u32[]{:S(2)}, u32[]{:S(2)}) %collective-permute-start.82) | collective-permute-done | bytes 524320 | tf_op jit(solution)/shard_map/ppermute | solution.py:623
  509.3 3.5 collective-permute-done.101
  (286 shorter events, 123.2 us)
Async XLA Ops:
  2.0 26.9 %collective-permute-start.3 = (bf16[512,512]{1,0:T(8,128)(2,1)S(1)}, bf16[512,512]{1,0:T(8,128)(2,1)}, u32[]{:S(2)}, u32[]{:S(2)}) collective-permute-start(bf16[512,512]{1,0:T(8,128)(2,1)S(1)} %get-tuple-element.250.refs_16_), channel_id=1, source_target_pairs={{0,16},{1,17},{2,18},{3,19},{4,20},{5,21},{6,22},{7,23},{8,24},{9,... | collective-permute-start | bytes 1572872 | tf_op jit(solution)/shard_map/ppermute | solution.py:623
  5.0 23.9 %collective-permute-start.4 = (bf16[512,512]{1,0:T(8,128)(2,1)S(1)}, bf16[512,512]{1,0:T(8,128)(2,1)}, u32[]{:S(2)}, u32[]{:S(2)}) collective-permute-start(bf16[512,512]{1,0:T(8,128)(2,1)S(1)} %get-tuple-element.251.refs_20_), channel_id=1, source_target_pairs={{0,2},{1,3},{2,0},{3,1},{4,6},{5,7},{6,4},{7,5},{8,10},{9,11},{10,... | collective-permute-start | bytes 1572872 | tf_op jit(solution)/shard_map/ppermute | solution.py:623
  11.0 18.0 %collective-permute-start = (bf16[80,1536]{1,0:T(8,128)(2,1)S(1)}, bf16[80,1536]{1,0:T(8,128)(2,1)S(1)}, u32[]{:S(2)}, u32[]{:S(2)}) collective-permute-start(bf16[80,1536]{1,0:T(8,128)(2,1)S(1)} %get-tuple-element.216), channel_id=1, source_target_pairs={{0,2},{1,3},{2,0},{3,1},{4,6},{5,7},{6,4},{7,5},{8,10},{9,11},{10,... | collective-permute-start | bytes 737288 | tf_op jit(solution)/shard_map/ppermute | solution.py:623
  11.5 17.4 %collective-permute-start.1 = (bf16[80,1536]{1,0:T(8,128)(2,1)S(1)}, bf16[80,1536]{1,0:T(8,128)(2,1)S(1)}, u32[]{:S(2)}, u32[]{:S(2)}) collective-permute-start(bf16[80,1536]{1,0:T(8,128)(2,1)S(1)} %get-tuple-element.217), channel_id=1, source_target_pairs={{0,16},{1,17},{2,18},{3,19},{4,20},{5,21},{6,22},{7,23},{8,24},{9,... | collective-permute-start | bytes 737288 | tf_op jit(solution)/shard_map/ppermute | solution.py:623
  11.6 17.3 %collective-permute-start.2 = (bf16[80,1536]{1,0:T(8,128)(2,1)S(1)}, bf16[80,1536]{1,0:T(8,128)(2,1)S(1)}, u32[]{:S(2)}, u32[]{:S(2)}) collective-permute-start(bf16[80,1536]{1,0:T(8,128)(2,1)S(1)} %get-tuple-element.218), channel_id=1, source_target_pairs={{0,18},{1,19},{2,16},{3,17},{4,22},{5,23},{6,20},{7,21},{8,26},{9,... | collective-permute-start | bytes 737288 | tf_op jit(solution)/shard_map/ppermute | solution.py:623
  30.0 24.6 %collective-permute-start.9 = (bf16[1040,512]{1,0:T(8,128)(2,1)}, bf16[1040,512]{1,0:T(8,128)(2,1)}, u32[]{:S(2)}, u32[]{:S(2)}) collective-permute-start(bf16[1040,512]{1,0:T(8,128)(2,1)} %get-tuple-element.223.refs_0_), channel_id=1, source_target_pairs={{0,8},{1,9},{2,10},{3,11},{4,0},{5,1},{6,2},{7,3},{8,12},{9,13},{1... | collective-permute-start | bytes 3194888 | tf_op jit(solution)/shard_map/ppermute | solution.py:623
  32.6 12.6 %collective-permute-start.5 = (bf16[128,2048]{1,0:T(8,128)(2,1)}, bf16[128,2048]{1,0:T(8,128)(2,1)}, u32[]{:S(2)}, u32[]{:S(2)}) collective-permute-start(bf16[128,2048]{1,0:T(8,128)(2,1)} %bitcast.37), channel_id=1, source_target_pairs={{0,16},{1,17},{2,18},{3,19},{4,20},{5,21},{6,22},{7,23},{8,24},{9,... | collective-permute-start | bytes 1572872 | tf_op jit(solution)/shard_map/ppermute | solution.py:623
  33.8 12.9 %collective-permute-start.6 = (bf16[128,2048]{1,0:T(8,128)(2,1)}, bf16[128,2048]{1,0:T(8,128)(2,1)}, u32[]{:S(2)}, u32[]{:S(2)}) collective-permute-start(bf16[128,2048]{1,0:T(8,128)(2,1)} %bitcast.38), channel_id=1, source_target_pairs={{0,2},{1,3},{2,0},{3,1},{4,6},{5,7},{6,4},{7,5},{8,10},{9,11},{10,... | collective-permute-start | bytes 1572872 | tf_op jit(solution)/shard_map/ppermute | solution.py:623
  54.6 24.4 %collective-permute-start.10 = (bf16[1040,512]{1,0:T(8,128)(2,1)}, bf16[1040,512]{1,0:T(8,128)(2,1)S(1)}, u32[]{:S(2)}, u32[]{:S(2)}) collective-permute-start(bf16[1040,512]{1,0:T(8,128)(2,1)} %collective-permute-done.9.refs_2_), channel_id=1, source_target_pairs={{0,8},{1,9},{2,10},{3,11},{4,0},{5,1},{6,2},{7,3},{8,12},{9,13},{1... | collective-permute-start | bytes 3194888 | tf_op jit(solution)/shard_map/ppermute | solution.py:623
  58.5 25.1 %collective-permute-start.11 = (bf16[1024,512]{1,0:T(8,128)(2,1)S(1)}, bf16[1024,512]{1,0:T(8,128)(2,1)S(1)}, u32[]{:S(2)}, u32[]{:S(2)}) collective-permute-start(bf16[1024,512]{1,0:T(8,128)(2,1)S(1)} %copy-done), channel_id=1, source_target_pairs={{0,16},{1,17},{2,18},{3,19},{4,20},{5,21},{6,22},{7,23},{8,24},{9,... | collective-permute-start | bytes 3145736 | tf_op jit(solution)/shard_map/ppermute | solution.py:623
  60.0 27.6 %collective-permute-start.21 = (bf16[1040,512]{1,0:T(8,128)(2,1)}, bf16[1040,512]{1,0:T(8,128)(2,1)S(1)}, u32[]{:S(2)}, u32[]{:S(2)}) collective-permute-start(bf16[1040,512]{1,0:T(8,128)(2,1)} %get-tuple-element.223.refs_0_), channel_id=1, source_target_pairs={{0,1},{1,0},{2,3},{3,2},{4,5},{5,4},{6,7},{7,6},{8,9},{9,8},{10,11... | collective-permute-start | bytes 3194888 | tf_op jit(solution)/shard_map/ppermute | solution.py:623
  60.7 25.2 %collective-permute-start.12 = (bf16[1024,512]{1,0:T(8,128)(2,1)S(1)}, bf16[1024,512]{1,0:T(8,128)(2,1)S(1)}, u32[]{:S(2)}, u32[]{:S(2)}) collective-permute-start(bf16[1024,512]{1,0:T(8,128)(2,1)S(1)} %copy-done.1), channel_id=1, source_target_pairs={{0,2},{1,3},{2,0},{3,1},{4,6},{5,7},{6,4},{7,5},{8,10},{9,11},{10,... | collective-permute-start | bytes 3145736 | tf_op jit(solution)/shard_map/ppermute | solution.py:623
  62.2 26.7 %collective-permute-start.22 = (bf16[1040,512]{1,0:T(8,128)(2,1)}, bf16[1040,512]{1,0:T(8,128)(2,1)S(1)}, u32[]{:S(2)}, u32[]{:S(2)}) collective-permute-start(bf16[1040,512]{1,0:T(8,128)(2,1)} %collective-permute-done.9.refs_2_), channel_id=1, source_target_pairs={{0,1},{1,0},{2,3},{3,2},{4,5},{5,4},{6,7},{7,6},{8,9},{9,8},{10,11... | collective-permute-start | bytes 3194888 | tf_op jit(solution)/shard_map/ppermute | solution.py:623
  85.9 26.1 %collective-permute-start.15 = (bf16[1040,512]{1,0:T(8,128)(2,1)S(1)}, bf16[1040,512]{1,0:T(8,128)(2,1)S(1)}, u32[]{:S(2)}, u32[]{:S(2)}) collective-permute-start(bf16[1040,512]{1,0:T(8,128)(2,1)S(1)} %collective-permute-done.10.refs_4_), channel_id=1, source_target_pairs={{0,8},{1,9},{2,10},{3,11},{4,0},{5,1},{6,2},{7,3},{8,12},{9,13},{1... | collective-permute-start | bytes 3194888 | tf_op jit(solution)/shard_map/ppermute | solution.py:623
  86.8 24.9 %collective-permute-start.16 = (bf16[1024,512]{1,0:T(8,128)(2,1)S(1)}, bf16[1024,512]{1,0:T(8,128)(2,1)S(1)}, u32[]{:S(2)}, u32[]{:S(2)}) collective-permute-start(bf16[1024,512]{1,0:T(8,128)(2,1)S(1)} %copy-done), channel_id=1, source_target_pairs={{0,2},{1,3},{2,0},{3,1},{4,6},{5,7},{6,4},{7,5},{8,10},{9,11},{10,... | collective-permute-start | bytes 3145736 | tf_op jit(solution)/shard_map/ppermute | solution.py:623
  87.5 24.4 %collective-permute-start.17 = (bf16[1024,512]{1,0:T(8,128)(2,1)S(1)}, bf16[1024,512]{1,0:T(8,128)(2,1)S(1)}, u32[]{:S(2)}, u32[]{:S(2)}) collective-permute-start(bf16[1024,512]{1,0:T(8,128)(2,1)S(1)} %copy-done.1), channel_id=1, source_target_pairs={{0,16},{1,17},{2,18},{3,19},{4,20},{5,21},{6,22},{7,23},{8,24},{9,... | collective-permute-start | bytes 3145736 | tf_op jit(solution)/shard_map/ppermute | solution.py:623
  88.8 23.1 %collective-permute-start.19 = (bf16[1024,512]{1,0:T(8,128)(2,1)S(1)}, bf16[1024,512]{1,0:T(8,128)(2,1)S(1)}, u32[]{:S(2)}, u32[]{:S(2)}) collective-permute-start(bf16[1024,512]{1,0:T(8,128)(2,1)S(1)} %collective-permute-done.11.refs_4_), channel_id=1, source_target_pairs={{0,1},{1,0},{2,3},{3,2},{4,5},{5,4},{6,7},{7,6},{8,9},{9,8},{10,11... | collective-permute-start | bytes 3145736 | tf_op jit(solution)/shard_map/ppermute | solution.py:623
  88.8 23.1 %collective-permute-start.20 = (bf16[1024,512]{1,0:T(8,128)(2,1)S(1)}, bf16[1024,512]{1,0:T(8,128)(2,1)S(1)}, u32[]{:S(2)}, u32[]{:S(2)}) collective-permute-start(bf16[1024,512]{1,0:T(8,128)(2,1)S(1)} %collective-permute-done.12.refs_10_), channel_id=1, source_target_pairs={{0,1},{1,0},{2,3},{3,2},{4,5},{5,4},{6,7},{7,6},{8,9},{9,8},{10,11... | collective-permute-start | bytes 3145736 | tf_op jit(solution)/shard_map/ppermute | solution.py:623
  112.6 14.4 %collective-permute-start.33 = (bf16[512,512]{1,0:T(8,128)(2,1)S(1)}, bf16[512,512]{1,0:T(8,128)(2,1)S(1)}, u32[]{:S(2)}, u32[]{:S(2)}) collective-permute-start(bf16[512,512]{1,0:T(8,128)(2,1)S(1)} %get-tuple-element.250.refs_16_), channel_id=1, source_target_pairs={{0,2},{1,3},{2,0},{3,1},{4,6},{5,7},{6,4},{7,5},{8,10},{9,11},{10,... | collective-permute-start | bytes 1572872 | tf_op jit(solution)/shard_map/ppermute | solution.py:623
  120.8 14.8 %collective-permute-start.35 = (bf16[512,512]{1,0:T(8,128)(2,1)S(1)}, bf16[512,512]{1,0:T(8,128)(2,1)S(1)}, u32[]{:S(2)}, u32[]{:S(2)}) collective-permute-start(bf16[512,512]{1,0:T(8,128)(2,1)S(1)} %get-tuple-element.251.refs_20_), channel_id=1, source_target_pairs={{0,16},{1,17},{2,18},{3,19},{4,20},{5,21},{6,22},{7,23},{8,24},{9,... | collective-permute-start | bytes 1572872 | tf_op jit(solution)/shard_map/ppermute | solution.py:623
  124.6 18.7 %collective-permute-start.29 = (bf16[1024,512]{1,0:T(8,128)(2,1)S(1)}, bf16[1024,512]{1,0:T(8,128)(2,1)S(1)}, u32[]{:S(2)}, u32[]{:S(2)}) collective-permute-start(bf16[1024,512]{1,0:T(8,128)(2,1)S(1)} %collective-permute-done.16.refs_2_), channel_id=1, source_target_pairs={{0,1},{1,0},{2,3},{3,2},{4,5},{5,4},{6,7},{7,6},{8,9},{9,8},{10,11... | collective-permute-start | bytes 3145736 | tf_op jit(solution)/shard_map/ppermute | solution.py:623
  124.6 18.7 %collective-permute-start.30 = (bf16[1024,512]{1,0:T(8,128)(2,1)S(1)}, bf16[1024,512]{1,0:T(8,128)(2,1)S(1)}, u32[]{:S(2)}, u32[]{:S(2)}) collective-permute-start(bf16[1024,512]{1,0:T(8,128)(2,1)S(1)} %collective-permute-done.17.refs_12_), channel_id=1, source_target_pairs={{0,1},{1,0},{2,3},{3,2},{4,5},{5,4},{6,7},{7,6},{8,9},{9,8},{10,11... | collective-permute-start | bytes 3145736 | tf_op jit(solution)/shard_map/ppermute | solution.py:623
  127.3 29.7 %collective-permute-start.32 = (bf16[1024,512]{1,0:T(8,128)(2,1)S(1)}, bf16[1024,512]{1,0:T(8,128)(2,1)S(1)}, u32[]{:S(2)}, u32[]{:S(2)}) collective-permute-start(bf16[1024,512]{1,0:T(8,128)(2,1)S(1)} %collective-permute-done.12.refs_10_), channel_id=1, source_target_pairs={{0,16},{1,17},{2,18},{3,19},{4,20},{5,21},{6,22},{7,23},{8,24},{9,... | collective-permute-start | bytes 3145736 | tf_op jit(solution)/shard_map/ppermute | solution.py:623
  135.6 22.9 %collective-permute-start.31 = (bf16[1024,512]{1,0:T(8,128)(2,1)S(1)}, bf16[1024,512]{1,0:T(8,128)(2,1)S(1)}, u32[]{:S(2)}, u32[]{:S(2)}) collective-permute-start(bf16[1024,512]{1,0:T(8,128)(2,1)S(1)} %collective-permute-done.11.refs_4_), channel_id=1, source_target_pairs={{0,2},{1,3},{2,0},{3,1},{4,6},{5,7},{6,4},{7,5},{8,10},{9,11},{10,... | collective-permute-start | bytes 3145736 | tf_op jit(solution)/shard_map/ppermute | solution.py:623
  158.5 14.0 %collective-permute-start.37 = (bf16[128,2048]{1,0:T(8,128)(2,1)S(1)}, bf16[128,2048]{1,0:T(8,128)(2,1)S(1)}, u32[]{:S(2)}, u32[]{:S(2)}) collective-permute-start(bf16[128,2048]{1,0:T(8,128)(2,1)S(1)} %get-tuple-element.253), channel_id=1, source_target_pairs={{0,2},{1,3},{2,0},{3,1},{4,6},{5,7},{6,4},{7,5},{8,10},{9,11},{10,... | collective-permute-start | bytes 1572872 | tf_op jit(solution)/shard_map/ppermute | solution.py:623
  160.0 14.9 %collective-permute-start.38 = (bf16[128,2048]{1,0:T(8,128)(2,1)S(1)}, bf16[128,2048]{1,0:T(8,128)(2,1)S(1)}, u32[]{:S(2)}, u32[]{:S(2)}) collective-permute-start(bf16[128,2048]{1,0:T(8,128)(2,1)S(1)} %get-tuple-element.254), channel_id=1, source_target_pairs={{0,16},{1,17},{2,18},{3,19},{4,20},{5,21},{6,22},{7,23},{8,24},{9,... | collective-permute-start | bytes 1572872 | tf_op jit(solution)/shard_map/ppermute | solution.py:623
  160.9 21.3 %collective-permute-start.39 = (bf16[128,2048]{1,0:T(8,128)(2,1)S(1)}, bf16[128,2048]{1,0:T(8,128)(2,1)S(1)}, u32[]{:S(2)}, u32[]{:S(2)}) collective-permute-start(bf16[128,2048]{1,0:T(8,128)(2,1)S(1)} %get-tuple-element.255), channel_id=1, source_target_pairs={{0,18},{1,19},{2,16},{3,17},{4,22},{5,23},{6,20},{7,21},{8,26},{9,... | collective-permute-start | bytes 1572872 | tf_op jit(solution)/shard_map/ppermute | solution.py:623
  162.0 35.9 %collective-permute-start.41 = (bf16[1024,512]{1,0:T(8,128)(2,1)S(1)}, bf16[1024,512]{1,0:T(8,128)(2,1)S(1)}, u32[]{:S(2)}, u32[]{:S(2)}) collective-permute-start(bf16[1024,512]{1,0:T(8,128)(2,1)S(1)} %collective-permute-done.32.refs_14_), channel_id=1, source_target_pairs={{0,1},{1,0},{2,3},{3,2},{4,5},{5,4},{6,7},{7,6},{8,9},{9,8},{10,11... | collective-permute-start | bytes 3145736 | tf_op jit(solution)/shard_map/ppermute | solution.py:623
  162.0 35.9 %collective-permute-start.40 = (bf16[1024,512]{1,0:T(8,128)(2,1)S(1)}, bf16[1024,512]{1,0:T(8,128)(2,1)S(1)}, u32[]{:S(2)}, u32[]{:S(2)}) collective-permute-start(bf16[1024,512]{1,0:T(8,128)(2,1)S(1)} %collective-permute-done.31.refs_6_), channel_id=1, source_target_pairs={{0,1},{1,0},{2,3},{3,2},{4,5},{5,4},{6,7},{7,6},{8,9},{9,8},{10,11... | collective-permute-start | bytes 3145736 | tf_op jit(solution)/shard_map/ppermute | solution.py:623
  196.0 15.1 %collective-permute-start.47 = (bf16[128,2048]{1,0:T(8,128)(2,1)S(1)}, bf16[128,2048]{1,0:T(8,128)(2,1)S(1)}, u32[]{:S(2)}, u32[]{:S(2)}) collective-permute-start(bf16[128,2048]{1,0:T(8,128)(2,1)S(1)} %collective-permute-done.46.block), channel_id=1, source_target_pairs={{0,8},{1,9},{2,10},{3,11},{4,0},{5,1},{6,2},{7,3},{8,12},{9,13},{1... | collective-permute-start | bytes 1572872 | tf_op jit(solution)/shard_map/ppermute | solution.py:623
  204.7 21.3 %collective-permute-start.49 = (bf16[128,2048]{1,0:T(8,128)(2,1)S(1)}, bf16[128,2048]{1,0:T(8,128)(2,1)S(1)}, u32[]{:S(2)}, u32[]{:S(2)}) collective-permute-start(bf16[128,2048]{1,0:T(8,128)(2,1)S(1)} %convert_element_type.197), channel_id=1, source_target_pairs={{0,8},{1,9},{2,10},{3,11},{4,0},{5,1},{6,2},{7,3},{8,12},{9,13},{1... | collective-permute-start | bytes 1572872 | tf_op jit(solution)/shard_map/ppermute | solution.py:623
  211.1 22.5 %collective-permute-start.48 = (bf16[128,2048]{1,0:T(8,128)(2,1)S(1)}, bf16[128,2048]{1,0:T(8,128)(2,1)S(1)}, u32[]{:S(2)}, u32[]{:S(2)}) collective-permute-start(bf16[128,2048]{1,0:T(8,128)(2,1)S(1)} %collective-permute-done.47.block), channel_id=1, source_target_pairs={{0,8},{1,9},{2,10},{3,11},{4,0},{5,1},{6,2},{7,3},{8,12},{9,13},{1... | collective-permute-start | bytes 1572872 | tf_op jit(solution)/shard_map/ppermute | solution.py:623
  226.1 16.0 %collective-permute-start.50 = (bf16[128,2048]{1,0:T(8,128)(2,1)S(1)}, bf16[128,2048]{1,0:T(8,128)(2,1)S(1)}, u32[]{:S(2)}, u32[]{:S(2)}) collective-permute-start(bf16[128,2048]{1,0:T(8,128)(2,1)S(1)} %add_convert_fusion.13), channel_id=1, source_target_pairs={{0,8},{1,9},{2,10},{3,11},{4,0},{5,1},{6,2},{7,3},{8,12},{9,13},{1... | collective-permute-start | bytes 1572872 | tf_op jit(solution)/shard_map/ppermute | solution.py:623
  243.8 26.1 %collective-permute-start.53 = (bf16[512,1024]{1,0:T(8,128)(2,1)S(1)}, bf16[512,1024]{1,0:T(8,128)(2,1)S(1)}, u32[]{:S(2)}, u32[]{:S(2)}) collective-permute-start(bf16[512,1024]{1,0:T(8,128)(2,1)S(1)} %get-tuple-element.301), channel_id=1, source_target_pairs={{0,2},{1,3},{2,0},{3,1},{4,6},{5,7},{6,4},{7,5},{8,10},{9,11},{10,... | collective-permute-start | bytes 3145736 | tf_op jit(solution)/shard_map/ppermute | solution.py:623
  245.5 26.1 %collective-permute-start.54 = (bf16[512,1024]{1,0:T(8,128)(2,1)S(1)}, bf16[512,1024]{1,0:T(8,128)(2,1)S(1)}, u32[]{:S(2)}, u32[]{:S(2)}) collective-permute-start(bf16[512,1024]{1,0:T(8,128)(2,1)S(1)} %get-tuple-element.302), channel_id=1, source_target_pairs={{0,16},{1,17},{2,18},{3,19},{4,20},{5,21},{6,22},{7,23},{8,24},{9,... | collective-permute-start | bytes 3145736 | tf_op jit(solution)/shard_map/ppermute | solution.py:623
  257.8 33.4 %collective-permute-start.59 = (bf16[512,1024]{1,0:T(8,128)(2,1)S(1)}, bf16[512,1024]{1,0:T(8,128)(2,1)S(1)}, u32[]{:S(2)}, u32[]{:S(2)}) collective-permute-start(bf16[512,1024]{1,0:T(8,128)(2,1)S(1)} %get-tuple-element.301), channel_id=1, source_target_pairs={{0,18},{1,19},{2,16},{3,17},{4,22},{5,23},{6,20},{7,21},{8,26},{9,... | collective-permute-start | bytes 3145736 | tf_op jit(solution)/shard_map/ppermute | solution.py:623
  267.1 24.1 %collective-permute-start.55 = (bf16[128,2048]{1,0:T(8,128)(2,1)S(1)}, bf16[128,2048]{1,0:T(8,128)(2,1)S(1)}, u32[]{:S(2)}, u32[]{:S(2)}) collective-permute-start(bf16[128,2048]{1,0:T(8,128)(2,1)S(1)} %collective-permute-done.52.block), channel_id=1, source_target_pairs={{0,8},{1,9},{2,10},{3,11},{4,0},{5,1},{6,2},{7,3},{8,12},{9,13},{1... | collective-permute-start | bytes 1572872 | tf_op jit(solution)/shard_map/ppermute | solution.py:623
  280.8 21.2 %collective-permute-start.60 = (bf16[128,2048]{1,0:T(8,128)(2,1)S(1)}, bf16[128,2048]{1,0:T(8,128)(2,1)S(1)}, u32[]{:S(2)}, u32[]{:S(2)}) collective-permute-start(bf16[128,2048]{1,0:T(8,128)(2,1)S(1)} %convert_element_type.202), channel_id=1, source_target_pairs={{0,8},{1,9},{2,10},{3,11},{4,0},{5,1},{6,2},{7,3},{8,12},{9,13},{1... | collective-permute-start | bytes 1572872 | tf_op jit(solution)/shard_map/ppermute | solution.py:623
  289.6 15.4 %collective-permute-start.57 = (bf16[256,1024]{1,0:T(8,128)(2,1)S(1)}, bf16[256,1024]{1,0:T(8,128)(2,1)S(1)}, u32[]{:S(2)}, u32[]{:S(2)}) collective-permute-start(bf16[256,1024]{1,0:T(8,128)(2,1)S(1)} %get-tuple-element.311.refs_0_), channel_id=1, source_target_pairs={{0,2},{1,3},{2,0},{3,1},{4,6},{5,7},{6,4},{7,5},{8,10},{9,11},{10,... | collective-permute-start | bytes 1572872 | tf_op jit(solution)/shard_map/ppermute | solution.py:623
  290.3 14.7 %collective-permute-start.58 = (bf16[256,1024]{1,0:T(8,128)(2,1)S(1)}, bf16[256,1024]{1,0:T(8,128)(2,1)S(1)}, u32[]{:S(2)}, u32[]{:S(2)}) collective-permute-start(bf16[256,1024]{1,0:T(8,128)(2,1)S(1)} %get-tuple-element.312), channel_id=1, source_target_pairs={{0,16},{1,17},{2,18},{3,19},{4,20},{5,21},{6,22},{7,23},{8,24},{9,... | collective-permute-start | bytes 1572872 | tf_op jit(solution)/shard_map/ppermute | solution.py:623
  291.3 13.8 %collective-permute-start.56 = (bf16[128,2048]{1,0:T(8,128)(2,1)S(1)}, bf16[128,2048]{1,0:T(8,128)(2,1)S(1)}, u32[]{:S(2)}, u32[]{:S(2)}) collective-permute-start(bf16[128,2048]{1,0:T(8,128)(2,1)S(1)} %collective-permute-done.55.block), channel_id=1, source_target_pairs={{0,8},{1,9},{2,10},{3,11},{4,0},{5,1},{6,2},{7,3},{8,12},{9,13},{1... | collective-permute-start | bytes 1572872 | tf_op jit(solution)/shard_map/ppermute | solution.py:623
  327.7 14.0 %collective-permute-start.66 = (bf16[128,2048]{1,0:T(8,128)(2,1)S(1)}, bf16[128,2048]{1,0:T(8,128)(2,1)S(1)}, u32[]{:S(2)}, u32[]{:S(2)}) collective-permute-start(bf16[128,2048]{1,0:T(8,128)(2,1)S(1)} %get-tuple-element.347.refs_6_), channel_id=1, source_target_pairs={{0,2},{1,3},{2,0},{3,1},{4,6},{5,7},{6,4},{7,5},{8,10},{9,11},{10,... | collective-permute-start | bytes 1572872 | tf_op jit(solution)/shard_map/ppermute | solution.py:623
  328.6 26.1 %collective-permute-start.67 = (bf16[128,2048]{1,0:T(8,128)(2,1)S(1)}, bf16[128,2048]{1,0:T(8,128)(2,1)S(1)}, u32[]{:S(2)}, u32[]{:S(2)}) collective-permute-start(bf16[128,2048]{1,0:T(8,128)(2,1)S(1)} %get-tuple-element.347.refs_6_), channel_id=1, source_target_pairs={{0,16},{1,17},{2,18},{3,19},{4,20},{5,21},{6,22},{7,23},{8,24},{9,... | collective-permute-start | bytes 1572872 | tf_op jit(solution)/shard_map/ppermute | solution.py:623
  329.1 25.6 %collective-permute-start.68 = (bf16[128,2048]{1,0:T(8,128)(2,1)S(1)}, bf16[128,2048]{1,0:T(8,128)(2,1)S(1)}, u32[]{:S(2)}, u32[]{:S(2)}) collective-permute-start(bf16[128,2048]{1,0:T(8,128)(2,1)S(1)} %get-tuple-element.347.refs_6_), channel_id=1, source_target_pairs={{0,18},{1,19},{2,16},{3,17},{4,22},{5,23},{6,20},{7,21},{8,26},{9,... | collective-permute-start | bytes 1572872 | tf_op jit(solution)/shard_map/ppermute | solution.py:623
  355.4 13.3 %collective-permute-start.70 = (bf16[1024,1024]{1,0:T(8,128)(2,1)}, bf16[1024,1024]{1,0:T(8,128)(2,1)S(1)}, u32[]{:S(2)}, u32[]{:S(2)}) collective-permute-start(bf16[1024,1024]{1,0:T(8,128)(2,1)} %convolution_convert_fusion.6), channel_id=1, source_target_pairs={{0,1},{1,0},{2,3},{3,2},{4,5},{5,4},{6,7},{7,6},{8,9},{9,8},{10,11... | collective-permute-start | bytes 6291464 | tf_op jit(solution)/shard_map/ppermute | solution.py:623
  355.9 14.8 %collective-permute-start.69 = (bf16[256,1024]{1,0:T(8,128)(2,1)S(1)}, bf16[256,1024]{1,0:T(8,128)(2,1)S(1)}, u32[]{:S(2)}, u32[]{:S(2)}) collective-permute-start(bf16[256,1024]{1,0:T(8,128)(2,1)S(1)} %get-tuple-element.337), channel_id=1, source_target_pairs={{0,18},{1,19},{2,16},{3,17},{4,22},{5,23},{6,20},{7,21},{8,26},{9,... | collective-permute-start | bytes 1572872 | tf_op jit(solution)/shard_map/ppermute | solution.py:623
  389.5 30.4 %collective-permute-start.77 = (bf16[3120,512]{1,0:T(8,128)(2,1)S(1)}, bf16[3120,512]{1,0:T(8,128)(2,1)S(1)}, u32[]{:S(2)}, u32[]{:S(2)}) collective-permute-start(bf16[3120,512]{1,0:T(8,128)(2,1)S(1)} %get-tuple-element.379), channel_id=1, source_target_pairs={{0,1},{1,0},{2,3},{3,2},{4,5},{5,4},{6,7},{7,6},{8,9},{9,8},{10,11... | collective-permute-start | bytes 9584648 | tf_op jit(solution)/shard_map/ppermute | solution.py:623
  390.1 29.9 %collective-permute-start.84 = (bf16[1040,512]{1,0:T(8,128)(2,1)S(1)}, bf16[1040,512]{1,0:T(8,128)(2,1)S(1)}, u32[]{:S(2)}, u32[]{:S(2)}) collective-permute-start(bf16[1040,512]{1,0:T(8,128)(2,1)S(1)} %add_convert_fusion.6), channel_id=1, source_target_pairs={{0,8},{1,9},{2,10},{3,11},{4,0},{5,1},{6,2},{7,3},{8,12},{9,13},{1... | collective-permute-start | bytes 3194888 | tf_op jit(solution)/shard_map/ppermute | solution.py:623
  392.5 25.1 %collective-permute-start.78 = (bf16[1024,512]{1,0:T(8,128)(2,1)S(1)}, bf16[1024,512]{1,0:T(8,128)(2,1)S(1)}, u32[]{:S(2)}, u32[]{:S(2)}) collective-permute-start(bf16[1024,512]{1,0:T(8,128)(2,1)S(1)} %get-tuple-element.388), channel_id=1, source_target_pairs={{0,16},{1,17},{2,18},{3,19},{4,20},{5,21},{6,22},{7,23},{8,24},{9,... | collective-permute-start | bytes 3145736 | tf_op jit(solution)/shard_map/ppermute | solution.py:623
  393.1 24.9 %collective-permute-start.79 = (bf16[1024,512]{1,0:T(8,128)(2,1)S(1)}, bf16[1024,512]{1,0:T(8,128)(2,1)S(1)}, u32[]{:S(2)}, u32[]{:S(2)}) collective-permute-start(bf16[1024,512]{1,0:T(8,128)(2,1)S(1)} %fusion.5), channel_id=1, source_target_pairs={{0,2},{1,3},{2,0},{3,1},{4,6},{5,7},{6,4},{7,5},{8,10},{9,11},{10,... | collective-permute-start | bytes 3145736 | tf_op jit(solution)/shard_map/ppermute | solution.py:623
  394.5 30.3 %collective-permute-start.91 = (bf16[512,512]{1,0:T(8,128)(2,1)S(1)}, bf16[512,512]{1,0:T(8,128)(2,1)S(1)}, u32[]{:S(2)}, u32[]{:S(2)}) collective-permute-start(bf16[512,512]{1,0:T(8,128)(2,1)S(1)} %get-tuple-element.431), channel_id=1, source_target_pairs={{0,1},{1,0},{2,3},{3,2},{4,5},{5,4},{6,7},{7,6},{8,9},{9,8},{10,11... | collective-permute-start | bytes 1572872 | tf_op jit(solution)/shard_map/ppermute | solution.py:623
  418.0 24.0 %collective-permute-start.80 = (bf16[1024,512]{1,0:T(8,128)(2,1)S(1)}, bf16[1024,512]{1,0:T(8,128)(2,1)S(1)}, u32[]{:S(2)}, u32[]{:S(2)}) collective-permute-start(bf16[1024,512]{1,0:T(8,128)(2,1)S(1)} %get-tuple-element.390), channel_id=1, source_target_pairs={{0,16},{1,17},{2,18},{3,19},{4,20},{5,21},{6,22},{7,23},{8,24},{9,... | collective-permute-start | bytes 3145736 | tf_op jit(solution)/shard_map/ppermute | solution.py:623
  419.3 23.9 %collective-permute-start.81 = (bf16[1024,512]{1,0:T(8,128)(2,1)}, bf16[1024,512]{1,0:T(8,128)(2,1)S(1)}, u32[]{:S(2)}, u32[]{:S(2)}) collective-permute-start(bf16[1024,512]{1,0:T(8,128)(2,1)} %fusion.6), channel_id=1, source_target_pairs={{0,2},{1,3},{2,0},{3,1},{4,6},{5,7},{6,4},{7,5},{8,10},{9,11},{10,... | collective-permute-start | bytes 3145736 | tf_op jit(solution)/shard_map/ppermute | solution.py:623
  420.5 28.6 %collective-permute-start.85 = (bf16[1040,512]{1,0:T(8,128)(2,1)S(1)}, bf16[1040,512]{1,0:T(8,128)(2,1)S(1)}, u32[]{:S(2)}, u32[]{:S(2)}) collective-permute-start(bf16[1040,512]{1,0:T(8,128)(2,1)S(1)} %add_convert_fusion.5), channel_id=1, source_target_pairs={{0,8},{1,9},{2,10},{3,11},{4,0},{5,1},{6,2},{7,3},{8,12},{9,13},{1... | collective-permute-start | bytes 3194888 | tf_op jit(solution)/shard_map/ppermute | solution.py:623
  424.8 23.2 %collective-permute-start.94 = (bf16[512,512]{1,0:T(8,128)(2,1)S(1)}, bf16[512,512]{1,0:T(8,128)(2,1)S(1)}, u32[]{:S(2)}, u32[]{:S(2)}) collective-permute-start(bf16[512,512]{1,0:T(8,128)(2,1)S(1)} %get-tuple-element.429), channel_id=1, source_target_pairs={{0,1},{1,0},{2,3},{3,2},{4,5},{5,4},{6,7},{7,6},{8,9},{9,8},{10,11... | collective-permute-start | bytes 1572872 | tf_op jit(solution)/shard_map/ppermute | solution.py:623
  426.5 22.1 %collective-permute-start.97 = (bf16[512,512]{1,0:T(8,128)(2,1)S(1)}, bf16[512,512]{1,0:T(8,128)(2,1)S(1)}, u32[]{:S(2)}, u32[]{:S(2)}) collective-permute-start(bf16[512,512]{1,0:T(8,128)(2,1)S(1)} %get-tuple-element.427), channel_id=1, source_target_pairs={{0,1},{1,0},{2,3},{3,2},{4,5},{5,4},{6,7},{7,6},{8,9},{9,8},{10,11... | collective-permute-start | bytes 1572872 | tf_op jit(solution)/shard_map/ppermute | solution.py:623
  449.2 26.0 %collective-permute-start.88 = (bf16[1024,512]{1,0:T(8,128)(2,1)S(1)}, bf16[1024,512]{1,0:T(8,128)(2,1)S(1)}, u32[]{:S(2)}, u32[]{:S(2)}) collective-permute-start(bf16[1024,512]{1,0:T(8,128)(2,1)S(1)} %add_convert_fusion.7), channel_id=1, source_target_pairs={{0,16},{1,17},{2,18},{3,19},{4,20},{5,21},{6,22},{7,23},{8,24},{9,... | collective-permute-start | bytes 3145736 | tf_op jit(solution)/shard_map/ppermute | solution.py:623
  450.3 30.4 %collective-permute-start.86 = (bf16[1040,512]{1,0:T(8,128)(2,1)S(1)}, bf16[1040,512]{1,0:T(8,128)(2,1)S(1)}, u32[]{:S(2)}, u32[]{:S(2)}) collective-permute-start(bf16[1040,512]{1,0:T(8,128)(2,1)S(1)} %add_convert_fusion.4), channel_id=1, source_target_pairs={{0,8},{1,9},{2,10},{3,11},{4,0},{5,1},{6,2},{7,3},{8,12},{9,13},{1... | collective-permute-start | bytes 3194888 | tf_op jit(solution)/shard_map/ppermute | solution.py:623
  454.6 26.1 %collective-permute-start.87 = (bf16[1024,512]{1,0:T(8,128)(2,1)S(1)}, bf16[1024,512]{1,0:T(8,128)(2,1)S(1)}, u32[]{:S(2)}, u32[]{:S(2)}) collective-permute-start(bf16[1024,512]{1,0:T(8,128)(2,1)S(1)} %add_convert_fusion.8), channel_id=1, source_target_pairs={{0,2},{1,3},{2,0},{3,1},{4,6},{5,7},{6,4},{7,5},{8,10},{9,11},{10,... | collective-permute-start | bytes 3145736 | tf_op jit(solution)/shard_map/ppermute | solution.py:623
  457.6 45.2 %collective-permute-start.82 = (bf16[128,2048]{1,0:T(8,128)(2,1)S(1)}, bf16[128,2048]{1,0:T(8,128)(2,1)S(1)}, u32[]{:S(2)}, u32[]{:S(2)}) collective-permute-start(bf16[128,2048]{1,0:T(8,128)(2,1)S(1)} %get-tuple-element.392), channel_id=1, source_target_pairs={{0,2},{1,3},{2,0},{3,1},{4,6},{5,7},{6,4},{7,5},{8,10},{9,11},{10,... | collective-permute-start | bytes 1572872 | tf_op jit(solution)/shard_map/ppermute | solution.py:623
  464.4 41.7 %collective-permute-start.83 = (bf16[128,2048]{1,0:T(8,128)(2,1)S(1)}, bf16[128,2048]{1,0:T(8,128)(2,1)S(1)}, u32[]{:S(2)}, u32[]{:S(2)}) collective-permute-start(bf16[128,2048]{1,0:T(8,128)(2,1)S(1)} %get-tuple-element.393), channel_id=1, source_target_pairs={{0,16},{1,17},{2,18},{3,19},{4,20},{5,21},{6,22},{7,23},{8,24},{9,... | collective-permute-start | bytes 1572872 | tf_op jit(solution)/shard_map/ppermute | solution.py:623
  481.8 25.2 %collective-permute-start.102 = (bf16[80,1536]{1,0:T(8,128)(2,1)S(1)}, bf16[80,1536]{1,0:T(8,128)(2,1)S(1)}, u32[]{:S(2)}, u32[]{:S(2)}) collective-permute-start(bf16[80,1536]{1,0:T(8,128)(2,1)S(1)} %get-tuple-element.404), channel_id=1, source_target_pairs={{0,2},{1,3},{2,0},{3,1},{4,6},{5,7},{6,4},{7,5},{8,10},{9,11},{10,... | collective-permute-start | bytes 737288 | tf_op jit(solution)/shard_map/ppermute | solution.py:623
  482.8 24.1 %collective-permute-start.103 = (bf16[80,1536]{1,0:T(8,128)(2,1)S(1)}, bf16[80,1536]{1,0:T(8,128)(2,1)S(1)}, u32[]{:S(2)}, u32[]{:S(2)}) collective-permute-start(bf16[80,1536]{1,0:T(8,128)(2,1)S(1)} %get-tuple-element.405), channel_id=1, source_target_pairs={{0,16},{1,17},{2,18},{3,19},{4,20},{5,21},{6,22},{7,23},{8,24},{9,... | collective-permute-start | bytes 737288 | tf_op jit(solution)/shard_map/ppermute | solution.py:623
  483.9 23.1 %collective-permute-start.104 = (bf16[80,1536]{1,0:T(8,128)(2,1)S(1)}, bf16[80,1536]{1,0:T(8,128)(2,1)S(1)}, u32[]{:S(2)}, u32[]{:S(2)}) collective-permute-start(bf16[80,1536]{1,0:T(8,128)(2,1)S(1)} %get-tuple-element.406), channel_id=1, source_target_pairs={{0,18},{1,19},{2,16},{3,17},{4,22},{5,23},{6,20},{7,21},{8,26},{9,... | collective-permute-start | bytes 737288 | tf_op jit(solution)/shard_map/ppermute | solution.py:623
  (72 other events, 651.0 us)

commit v6 on v5

--- a/solution.py
+++ b/solution.py
@@ -1,3 +1,4 @@
+import enum
 import functools
 import math
 
@@ -22,7 +23,70 @@
 VMEM = pl.BlockSpec(memory_space=pltpu.VMEM)
 HBM = pl.BlockSpec(memory_space=pltpu.HBM)
 EXTRA = 16
-PLAN = {'far_down': 'join', 'turns': 'w2', 'far': 'w3', 'tokens': 'w2', 'tokens_xy': 'w2', 'near': 'c3', 'own_gate_c': 'w3', 'own_down_c': 'c3', 'far_c': 'c3', 'far_down_c': 'stats', 'total': 'c3', 'near_down': 'k4', 'near_c': 'rs', 'last_from': 'stats', 'last': 'rs', 'last_c': 'f1', 'near_down_c': 'rs', 'f_lead': 0, 'f_out': 0, 'f_hold': 0, 'b_lead': 0, 'b_out': 0, 'b_hold': 0, 'products_from': 1, 'products': 'b1', 'products_xy': 'b2', 'near_grads': 'b3', 'near_grads_xy': 'b4', 'dots_from': 'block', 'dots': 'blocks', 'far_grads_from': 'sent', 'far_grads': 'ag', 'far_grads_xy': 'g1', 'sums_late': 1, 'sums': 'g1', 'w_far_late': 1, 'w_far': 't2', 'w_near': 't3', 'w_last': 'collect', 'w_last_late': 1, 'factors': 'collect', 'grad_wd': 'collect', 'x_parts': 't3', 'x_from': 'near', 'x_sums': 'spread', 'tokens_first': 1, 'far_from': 'xy', 'second_after': 'first', 'x_last_from': 'messages'}
+class Point(enum.IntEnum):
+    JOIN = 0
+    RING_2 = 1
+    RING_3 = 2
+    LAST_ROWS = 3
+    STATS = 4
+    SCALES = 5
+    BRANCH_SEND = 6
+    BRANCH = 7
+    F1 = 8
+    F2 = 9
+    F3 = 10
+    F4 = 11
+    MLP_OUT = 12
+    B1 = 13
+    B2 = 14
+    B3 = 15
+    B4 = 16
+    MIDDLE = 17
+    BRANCH_BACK = 18
+    ATTEND_BACK = 19
+    STATS_BACK = 20
+    PROJECT_BACK = 21
+    SUM_1 = 22
+    SUM_2 = 23
+    SUM_3 = 24
+    COLLECT = 25
+    SPREAD = 26
+    NEVER = 27
+
+
+class Due:
+    far_down = Point.JOIN
+    turns = Point.RING_2
+    far = Point.RING_3
+    tokens = Point.RING_2
+    tokens_xy = Point.RING_2
+    near = Point.LAST_ROWS
+    own_gate_c = Point.RING_3
+    own_down_c = Point.LAST_ROWS
+    far_c = Point.LAST_ROWS
+    far_down_c = Point.STATS
+    total = Point.LAST_ROWS
+    near_down = Point.BRANCH
+    near_c = Point.BRANCH_SEND
+    last = Point.BRANCH_SEND
+    last_c = Point.F1
+    near_down_c = Point.BRANCH_SEND
+    near_grads = Point.B3
+    near_grads_xy = Point.B4
+    products = Point.B1
+    products_xy = Point.B2
+    far_grads = Point.BRANCH_BACK
+    far_grads_xy = Point.STATS_BACK
+    dots = Point.ATTEND_BACK
+    sums = Point.STATS_BACK
+    w_far = Point.SUM_2
+    w_near = Point.COLLECT
+    w_last = Point.COLLECT
+    factors = Point.COLLECT
+    grad_wd = Point.COLLECT
+    x_parts = Point.SUM_3
+    x_sums = Point.SPREAD
+
 SQUARE = [(dx, dy) for dx in range(NX) for dy in range(NY)]
 TOKEN_BLOCKS = [(dx, dy) for dy in range(NY) for dx in range(NX)]
 
@@ -57,6 +121,7 @@
         out_specs=[spec if isinstance(spec, pl.BlockSpec) else spec(out) for out, spec in outs],
         in_specs=[spec if isinstance(spec, pl.BlockSpec) else spec(array) for array, spec in ins],
         compiler_params=pltpu.CompilerParams(vmem_limit_bytes=limit * MIB),
+        cost_estimate=pl.CostEstimate(flops=0, bytes_accessed=0, transcendentals=0),
         **options,
     )(*[array for array, _ in ins])
 
@@ -689,9 +754,8 @@
     ):
         due = {}
 
-        def mark(name, value):
-            due.setdefault(PLAN[name], []).append(value)
-            return value
+        def mark(point, value):
+            due.setdefault(point, []).append(value)
 
         def at(point, value):
             ready = due.pop(point, [])
@@ -741,8 +805,8 @@
         down_rows = w_down.shape[0] // 2
         down_halves = w_down[:down_rows], w_down[down_rows:]
         far_down = send(down_halves[0], x=1), send(down_halves[1], y=1)
-        mark("far_down", far_down)
-        received = at("join", square(pieces))
+        mark(Due.far_down, far_down)
+        received = at(Point.JOIN, square(pieces))
         own_rows, lengths_row = run(
             join_kernel,
             [(message, VMEM), (shaped((8, HEAD_DIM), F32), VMEM)],
@@ -755,42 +819,32 @@
         frequency = jnp.exp((lane % half).astype(F32) * (-2.0 * math.log(500000.0) / HEAD_DIM))
         cosine = jnp.cos(row * frequency)
         sine = jnp.sin(row * jnp.where(lane < half, -frequency, frequency))
-        mark("turns", (cosine, sine))
+        mark(Due.turns, (cosine, sine))
         w_ring = [own_rows, send(own_rows, r=-1)]
         half_tok = tok // 2
-        if PLAN["tokens_first"]:
-            from_x = send(after(inputs, own_rows), x=1)
-            from_y = send(after(inputs, own_rows), y=1)
-            from_xy = send(from_x[:half_tok], y=1), send(from_y[half_tok:], x=1)
-            early = {"xy": from_xy, "x": (from_x, from_y)}[PLAN["far_from"]]
-            far_gate = send(after(w_gate, early), x=1)
-            far_up = send(after(w_up, early), y=1)
-            near_gate = send(after(w_gate, far_up), y=1)
-            near_up = send(after(w_up, far_gate), x=1)
-        else:
-            far_gate = send(after(w_gate, own_rows), x=1)
-            far_up = send(after(w_up, own_rows), y=1)
-            from_x = send(after(inputs, far_gate), x=1)
-            from_y = send(after(inputs, far_up), y=1)
-            from_xy = send(from_x[:half_tok], y=1), send(from_y[half_tok:], x=1)
-            near_gate = send(after(w_gate, from_xy[0]), y=1)
-            near_up = send(after(w_up, from_xy[1]), x=1)
-        mark("far", (far_gate, far_up))
-        mark("tokens", (from_x, from_y))
-        mark("tokens_xy", from_xy)
-        mark("near", (near_gate, near_up))
+        from_x = send(after(inputs, own_rows), x=1)
+        from_y = send(after(inputs, own_rows), y=1)
+        from_xy = send(from_x[:half_tok], y=1), send(from_y[half_tok:], x=1)
+        far_gate = send(after(w_gate, from_xy), x=1)
+        far_up = send(after(w_up, from_xy), y=1)
+        near_gate = send(after(w_gate, far_up), y=1)
+        near_up = send(after(w_up, far_gate), x=1)
+        mark(Due.far, (far_gate, far_up))
+        mark(Due.tokens, (from_x, from_y))
+        mark(Due.tokens_xy, from_xy)
+        mark(Due.near, (near_gate, near_up))
         own_gate, own_up = core_gather(w_gate), core_gather(w_up)
         own_down = core_gather(w_down)
         far_gate, far_up = core_gather(far_gate), core_gather(far_up)
         far_down = core_gather(far_down[0]), core_gather(far_down[1])
-        mark("own_gate_c", (own_gate, own_up))
-        mark("own_down_c", own_down)
-        mark("far_c", (far_gate, far_up))
-        mark("far_down_c", far_down)
+        mark(Due.own_gate_c, (own_gate, own_up))
+        mark(Due.own_down_c, own_down)
+        mark(Due.far_c, (far_gate, far_up))
+        mark(Due.far_down_c, far_down)
         first_blocks = core_gather(own_rows)
-        w_ring.append(send(at("w2", w_ring[1]), r=-1))
+        w_ring.append(send(at(Point.RING_2, w_ring[1]), r=-1))
         second_blocks = core_gather(w_ring[1])
-        w_ring.append(send(at("w3", w_ring[2]), r=-1))
+        w_ring.append(send(at(Point.RING_3, w_ring[2]), r=-1))
         x_all, x_kept = run(
             gather_kernel,
             [(shaped((group_tok, width)), VMEM), (shaped((group_tok, width)), HBM)],
@@ -819,15 +873,15 @@
 
         blocks = first_blocks + second_blocks + core_gather(w_ring[2])
         gains, out_w, *w_parts, total = project((0, 1, 2), blocks, (), [(by_three, VMEM)])
-        mark("total", total)
-        last_block = core_gather(at("c3", w_ring[3]))
+        mark(Due.total, total)
+        last_block = core_gather(at(Point.LAST_ROWS, w_ring[3]))
         near_down = (
             send(after(down_halves[0], near_gate), y=1),
             send(after(down_halves[1], near_up), x=1),
         )
-        mark("near_down", near_down)
+        mark(Due.near_down, near_down)
         near_gate, near_up = core_gather(near_gate), core_gather(near_up)
-        mark("near_c", (near_gate, near_up))
+        mark(Due.near_c, (near_gate, near_up))
         gains, out_w, w_part, query, key, value, query_h, key_h, value_h, out_kept, stats = project(
             (3,),
             last_block,
@@ -837,18 +891,16 @@
             + [(out_shape, HBM), (by_token, VMEM)],
         )
         w_parts.append(w_part)
-        early = {"near": near_gate[0]}
-        group_stats = at("stats2", group_sum(at("stats", stats)))
-        early["stats"] = group_stats
-        last_gate = send(after(far_gate[0], early[PLAN["last_from"]], near_gate[0]), y=1)
-        last_up = send(after(far_up[0], early[PLAN["last_from"]], near_up[0]), x=1)
-        mark("last", (last_gate, last_up))
+        group_stats = at(Point.SCALES, group_sum(at(Point.STATS, stats)))
+        last_gate = send(after(far_gate[0], group_stats, near_gate[0]), y=1)
+        last_up = send(after(far_up[0], group_stats, near_up[0]), x=1)
+        mark(Due.last, (last_gate, last_up))
         last_gate, last_up = core_gather(last_gate), core_gather(last_up)
-        mark("last_c", (last_gate, last_up))
+        mark(Due.last_c, (last_gate, last_up))
         gate_w = [*own_gate, *near_gate, *far_gate, *last_gate]
         up_w = [*own_up, *far_up, *near_up, *last_up]
         near_down = core_gather(near_down[0]), core_gather(near_down[1])
-        mark("near_down_c", near_down)
+        mark(Due.near_down_c, near_down)
 
         query_r, key_r, attended, scales, *parts = run(
             attend_kernel,
@@ -861,7 +913,7 @@
             ],
             scratch_shapes=[held(by_head), held(by_head), held(by_head), dma(3)],
         )
-        parts = square(at("rs", parts))
+        parts = square(at(Point.BRANCH_SEND, parts))
         first_x, second_y = far_down
         last_down = (
             core_gather(send(after(first_x[0], parts), y=1)),
@@ -881,7 +933,7 @@
         branch, hidden_state, mlp_in = run(
             branch_kernel,
             [(tokens_wide, auto), (tokens_wide, auto), (tokens_shape, VMEM)],
-            [(pos, SMEM), *each(at("k4", parts), auto), (inputs, auto), (gains, VMEM)],
+            [(pos, SMEM), *each(at(Point.BRANCH, parts), auto), (inputs, auto), (gains, VMEM)],
         )
 
         half_width = width // NX
@@ -915,12 +967,12 @@
                 total = total + part.astype(F32)
             return total
 
-        def mlp_pass(name, kernel, block, extra, columns, height):
+        def mlp_pass(points, kernel, block, extra, columns, height):
             narrow = columns, height
             near = send(block, r=-1)
             middle = send(near, r=-1)
-            kept, first = mlp_call(kernel, 1, at(name + "1", near), extra, narrow, None)
-            far = send(after(middle, first) if PLAN[name + "_lead"] else middle, r=-1)
+            kept, first = mlp_call(kernel, 1, at(points, near), extra, narrow, None)
+            far = send(middle, r=-1)
             sent = [first.astype(BF16)]
             moving = send(sent[0], r=-1)
             kept, own = mlp_call(kernel, 0, block, extra, narrow, kept)
@@ -928,36 +980,33 @@
             if height < NZ * tok:
                 early, kept = kept[-NX:], kept[:-NX]
                 early = square([early[dx] for dx, dy in SQUARE])
-                mark("near_grads", early[1:3])
-                mark("near_grads_xy", early[3])
-            middle = at(name + "2", middle)
-            if PLAN[name + "_out"]:
-                middle = after(middle, sent[0])
+                mark(Due.near_grads, early[1:3])
+                mark(Due.near_grads_xy, early[3])
+            middle = at(points + 1, middle)
             kept, second = mlp_call(kernel, 2, middle, extra, narrow, kept)
-            far = at(name + "3", far)
-            if PLAN[name + "_hold"]:
-                far = after(far, moving)
+            far = at(points + 2, far)
             kept, third = mlp_call(kernel, 3, far, extra, narrow, kept)
             sent.append(summed([second, moving]).astype(BF16))
             sent.append(summed([third, send(sent[1], r=-1)]).astype(BF16))
-            parts = [own, send(at(name + "4", sent[2]), r=-1)]
+            parts = [own, send(at(points + 3, sent[2]), r=-1)]
             return kept, parts, sent, early
 
         columns = [nc * hidden] * NY + [NY * hidden] * 2 * nc
         kept, parts, sent, _ = mlp_pass(
-            "f", mlp_forward_kernel, mlp_in, (), columns, NZ * tok
+            Point.F1, mlp_forward_kernel, mlp_in, (), columns, NZ * tok
         )
         products, by_gate, by_up, mlp_all = take(kept, NY, nc, nc)
 
-        got_products = square([after(products, sent[PLAN["products_from"]])[dy] for dx, dy in SQUARE])
-        mark("products", got_products[1:3])
-        mark("products_xy", got_products[3])
+        late = after(products, sent[1])
+        got_products = square([late[dy] for dx, dy in SQUARE])
+        mark(Due.products, got_products[1:3])
+        mark(Due.products_xy, got_products[3])
         output, grad_mlp, grad_gain_mlp = run(
             functools.partial(mlp_kernel, len(parts)),
             [(tokens_shape, auto), (tokens_shape, VMEM), (wide_small, VMEM)],
             [
                 (pos, SMEM),
-                *each(at("m1", parts), auto),
+                *each(at(Point.MLP_OUT, parts), auto),
                 (hidden_state, auto),
                 (gains, VMEM),
                 (grad_out, auto),
@@ -967,7 +1016,7 @@
         extra = *by_gate, *by_up
         columns = [NY * hidden] * 2 * nc
         kept, parts, sent, near_grads = mlp_pass(
-            "b", mlp_back_kernel, grad_mlp, extra, columns, 2 * tok
+            Point.B1, mlp_back_kernel, grad_mlp, extra, columns, 2 * tok
         )
         grad_gates, grad_ups, grad_all = take(kept, nc, nc)
         grad_hidden, grad_branch, grad_gain_attn = run(
@@ -975,7 +1024,7 @@
             [(tokens_wide, auto), (tokens_shape, VMEM), (wide_small, VMEM)],
             [
                 (pos, SMEM),
-                *each(at("k9", parts), auto),
+                *each(at(Point.MIDDLE, parts), auto),
                 (branch, auto),
                 (gains, VMEM),
                 (grad_out, auto),
@@ -986,28 +1035,19 @@
         def products_of(left, right):
             return [[tn(block, grad).astype(BF16) for grad in right] for block in left]
 
-        early = {"branch": grad_branch, "sent": sent[2]}
-        if PLAN["far_grads_from"] in early:
-            far_grads = after(grad_all, early[PLAN["far_grads_from"]])
-            far_grads = square([far_grads[dx] for dx, dy in SQUARE])
-            mark("far_grads", far_grads[1:3])
-            mark("far_grads_xy", far_grads[3])
-        blocks = square([at("ag", grad_branch)] * GROUP)
-        early.update({"block": blocks[1], "all": blocks})
-        mlp_all = after(mlp_all, early[PLAN["dots_from"]])
+        late = after(grad_all, sent[2])
+        far_grads = square([late[dx] for dx, dy in SQUARE])
+        mark(Due.far_grads, far_grads[1:3])
+        mark(Due.far_grads_xy, far_grads[3])
+        blocks = square([at(Point.BRANCH_BACK, grad_branch)] * GROUP)
+        mlp_all = after(mlp_all, blocks[1])
         wg_blocks = products_of(mlp_all, grad_gates)
         wu_blocks = products_of(mlp_all, grad_ups)
-        mark("dots", (wg_blocks, wu_blocks))
-        if PLAN["far_grads_from"] in ("block", "all"):
-            far_grads = after(grad_all, early[PLAN["far_grads_from"]])
-            far_grads = square([far_grads[dx] for dx, dy in SQUARE])
-            mark("far_grads", far_grads[1:3])
-            mark("far_grads_xy", far_grads[3])
-        blocks = at("blocks", blocks)
-        if PLAN["sums_late"]:
-            wg_blocks, wu_blocks = after((wg_blocks, wu_blocks), blocks)
+        mark(Due.dots, (wg_blocks, wu_blocks))
+        blocks = at(Point.ATTEND_BACK, blocks)
+        wg_blocks, wu_blocks = after((wg_blocks, wu_blocks), blocks)
         w_pair = core_sums(wg_blocks, hidden), core_sums(wu_blocks, hidden)
-        mark("sums", w_pair)
+        mark(Due.sums, w_pair)
         grad_query, grad_key, grad_value, stats, head_gains, branch_all = run(
             attend_back_kernel,
             [
@@ -1040,17 +1080,17 @@
             project_back_kernel,
             [(shaped((group_tok, 3 * HEADS)), VMEM)],
             [
-                (at("g2", group_sum(at("g1", stats))), VMEM),
+                (at(Point.PROJECT_BACK, group_sum(at(Point.STATS_BACK, stats))), VMEM),
                 (scales, VMEM),
                 *each((grad_query, grad_key, grad_value, query_h, key_h), VMEM),
             ],
         )
-        w_far = scatter_far(*(after(w_pair, grads) if PLAN["w_far_late"] else w_pair))
+        w_far = scatter_far(*after(w_pair, grads))
         w_near = scatter_near(*after(w_pair, w_far))
-        w_last = scatter_last(*w_pair, after(w_far, w_near) if PLAN["w_last_late"] else w_far, w_near)
-        mark("w_far", w_far)
-        mark("w_near", w_near)
-        mark("w_last", w_last)
+        w_last = scatter_last(*w_pair, w_far, w_near)
+        mark(Due.w_far, w_far)
+        mark(Due.w_near, w_near)
+        mark(Due.w_last, w_last)
 
         def weight_parts(places):
             height = message.shape[0]
@@ -1080,34 +1120,34 @@
             for k in range(nc):
                 pieces = *grads_of, product[:, k * hidden : (k + 1) * hidden]
                 factors.append([send(piece, c=k) if k else piece for piece in pieces])
-        mark("factors", factors)
+        mark(Due.factors, factors)
         (grad_wd,) = run(
             down_back_kernel,
             [(shaped(w_down.shape, F32), VMEM)],
             each([entry[i] for i in range(3) for entry in factors], VMEM),
         )
 
-        mark("grad_wd", grad_wd)
-        w_moving = send(at("w1", summed(first).astype(BF16)), r=-1)
-        early = {"first": first, "far": w_far, "none": (), "both": (first, w_far)}
-        grads = after(grads, early[PLAN["second_after"]])
-        second, third, own = weight_parts((2, 3, 0))
+        mark(Due.grad_wd, grad_wd)
+        w_moving = send(at(Point.SUM_1, summed(first).astype(BF16)), r=-1)
+        (second,) = weight_parts((2,))
+        (third,) = weight_parts((3,))
+        (own,) = weight_parts((0,))
         x_parts = run(
             input_back_kernel,
             [(tokens_shape, VMEM)] * GROUP,
-            [(pos, SMEM), (after(grads, own), VMEM), *each(w_parts, VMEM)],
+            [(pos, SMEM), (after(grads, second), VMEM), *each(w_parts, VMEM)],
             scratch_shapes=[pltpu.VMEM((group_tok, GROUP * HEAD_DIM), BF16)],
         )
-        mark("x_parts", x_parts)
-        early = {"parts": x_parts, "near": w_near, "last": w_last}
-        from_x = [x_parts[0]] + square([x_parts[0], *after(x_parts[1:3], early[PLAN["x_from"]]), x_parts[3]])[1:3]
-        mark("x_sums", from_x)
+        mark(Due.x_parts, x_parts)
+        late = after(x_parts[1:3], w_last)
+        from_x = [x_parts[0], send(late[0], y=1), send(late[1], x=1)]
+        mark(Due.x_sums, from_x)
         sent = summed(second + [w_moving]).astype(BF16)
-        w_moving = send(after(at("t2", sent), own), r=-1)
+        w_moving = send(at(Point.SUM_2, sent), r=-1)
         sent = summed(third + [w_moving]).astype(BF16)
-        w_moving = send(at("t3", sent), r=-1)
+        w_moving = send(at(Point.SUM_3, sent), r=-1)
         grad_wg, grad_wu = scatter_sum(*w_pair, w_near, w_last)
-        parts = at("collect", own + [w_moving])
+        parts = at(Point.COLLECT, own + [w_moving])
         grad_wo, *messages = run(
             functools.partial(collect_kernel, len(parts)),
             [(shaped((rows, width), F32), auto)] + [(piece, VMEM)] * GROUP,
@@ -1116,10 +1156,9 @@
         grad_wq, grad_wk, grad_wv, total_gains = run(
             spread_kernel,
             [(shaped((rows, width), F32), auto)] * 3 + [(shaped((8, HEAD_DIM), F32), VMEM)],
-            [(pos, SMEM), *each(at("spread", square(messages)), auto)],
-        )
-        early = {"messages": messages, "parts": x_parts, "sent": from_x[1:]}
-        last_x = send(after(x_parts[3], early[PLAN["x_last_from"]]), x=1, y=1)
+            [(pos, SMEM), *each(at(Point.SPREAD, square(messages)), auto)],
+        )
+        last_x = send(after(x_parts[3], messages), x=1, y=1)
         grad_x = summed([grad_hidden, *from_x, last_x])
 
         return (

time: 517 us -> 510 us (0.986)
  waiting for transfers between devices: 258 us -> 250 us
    ppermute x105 -> x107, waiting for transfers between devices: 258 us -> 250 us  [send(): return lax.ppermute(value, AXES, pairs)]
    pallas_call x25 -> x27, Pallas kernels: 113 us -> 114 us  [run(): pl.pallas_call(body, grid=(1,), out_shape=[pltpu.HBM(out.shape, out.dtype...]
    ppermute x105 -> x107, starting transfers between devices: 104 us -> 105 us  [send(): return lax.ppermute(value, AXES, pairs)]
  transfers between devices with their start and end apart: 105 -> 107, of which waited for: 49 -> 50; matrix products, arithmetic and copies ran while one was open for 5% -> 5% of each run, Pallas kernels for 20% -> 22%
where the time goes in v6:
time: 510 us; the launch traced here: 507 us
  waiting for transfers between devices  250 us (49%)
  Pallas kernels  114 us (22%)
  starting transfers between devices  105 us (21%)
  matrix products  13 us (3%)
  other arithmetic  12.1 us (2%)
  local copies, waits for them, and re-layouts  10.5 us (2%)
    ppermute x107, waiting for transfers between devices, send(): return lax.ppermute(value, AXES, pairs)  250 us
    pallas_call x27, Pallas kernels, run(): pl.pallas_call(body, grid=(1,), out_shape=[pltpu.HBM(out.shape, out.dtype...  114 us
    ppermute x107, starting transfers between devices, send(): return lax.ppermute(value, AXES, pairs)  105 us
    dot_general x8, matrix products, tn(): lax.dot_general(left, right, (((0,), (0,)), ((), ())), preferred_element_...  13 us
  transfers between devices with their start and end apart: 107, of which 50 were waited for; matrix products, arithmetic and copies ran while one was open for 5% of the time, Pallas kernels for 22%

profile of v6, /device:TPU:0, one launch (start us, length us, event | category | flops | bytes accessed | tf_op | source)
XLA Modules:
  0.0 506.9 jit_solution(8419028121226623890)
XLA Ops:
  2.0 3.0 collective-permute-start.3
  11.6 2.9 collective-permute-start.2
  14.5 14.5 %collective-permute-done.refs_1_ = bf16[80,1536]{1,0:T(8,128)(2,1)S(1)} collective-permute-done((bf16[80,1536]{1,0:T(8,128)(2,1)S(1)}, bf16[80,1536]{1,0:T(8,128)(2,1)S(1)}, u32[]{:S(2)}, u32[]{:S(2)}) %collective-permute-start) | collective-permute-done | bytes 245792 | tf_op jit(solution)/shard_map/ppermute | solution.py:688
  30.0 2.6 collective-permute-start.9
  34.7 10.5 %collective-permute-done.5.refs_1_ = bf16[128,2048]{1,0:T(8,128)(2,1)} collective-permute-done((bf16[128,2048]{1,0:T(8,128)(2,1)}, bf16[128,2048]{1,0:T(8,128)(2,1)}, u32[]{:S(2)}, u32[]{:S(2)}) %collective-permute-start.5) | collective-permute-done | bytes 524320 | tf_op jit(solution)/shard_map/ppermute | solution.py:688
  50.2 2.4 collective-permute-done.7.refs_3_
  54.6 3.4 collective-permute-start.10
  62.3 16.8 %collective-permute-done.10.refs_4_ = bf16[1040,512]{1,0:T(8,128)(2,1)S(1)} collective-permute-done((bf16[1040,512]{1,0:T(8,128)(2,1)}, bf16[1040,512]{1,0:T(8,128)(2,1)S(1)}, u32[]{:S(2)}, u32[]{:S(2)}) %collective-permute-start.10) | collective-permute-done | bytes 1064992 | tf_op jit(solution)/shard_map/ppermute | solution.py:688
  79.1 4.6 collective-permute-done.11.refs_4_
  83.7 2.2 collective-permute-done.12.refs_10_
  90.4 2.7 shard_map.239
  93.0 5.8 %shard_map.240 = (f32[8,2048]{1,0:T(8,128)S(1)}, bf16[512,2048]{1,0:T(8,128)(2,1)S(1)}, bf16[512,1536]{1,0:T(8,128)(2,1)}, bf16[512,1536]{1,0:T(8,128)(2,1)}, bf...) custom-call(s32[5]{0:T(128)S(1)} %stack.34.pos, bf16[512,2048]{1,0:T(8,128)(2,1)S(1)} %get-tuple-element.225.x_all, ...), custom_call_target="tpu_custom_call" | custom-call | tf_op jit(solution)/shard_map/pallas_call | solution.py:115
  98.9 12.8 %collective-permute-done.16.refs_2_ = bf16[1024,512]{1,0:T(8,128)(2,1)S(1)} collective-permute-done((bf16[1024,512]{1,0:T(8,128)(2,1)S(1)}, bf16[1024,512]{1,0:T(8,128)(2,1)S(1)}, u32[]{:S(2)}, u32[]{:S(2)}) %collective-permute-start.16) | collective-permute-done | bytes 1048608 | tf_op jit(solution)/shard_map/ppermute | solution.py:688
  115.4 3.8 shard_map.241
  128.8 6.8 %collective-permute-done.35.refs_28_ = bf16[512,512]{1,0:T(8,128)(2,1)S(1)} collective-permute-done((bf16[512,512]{1,0:T(8,128)(2,1)S(1)}, bf16[512,512]{1,0:T(8,128)(2,1)S(1)}, u32[]{:S(2)}, u32[]{:S(2)}) %collective-permute-start.35) | collective-permute-done | bytes 524320 | tf_op jit(solution)/shard_map/ppermute | solution.py:688
  137.1 6.2 %shard_map.242 = (bf16[512,512]{1,0:T(8,128)(2,1)}, bf16[512,512]{1,0:T(8,128)(2,1)}, bf16[512,512]{1,0:T(8,128)(2,1)}, f32[8,512]{1,0:T(8,128)S(1)}, bf16[128,2...) custom-call(s32[5]{0:T(128)S(1)} %stack.34.pos, ...), custom_call_target="tpu_custom_call" | custom-call | tf_op jit(solution)/shard_map/pallas_call | solution.py:115
  143.4 13.6 %collective-permute-done.32.refs_14_ = bf16[1024,512]{1,0:T(8,128)(2,1)S(1)} collective-permute-done((bf16[1024,512]{1,0:T(8,128)(2,1)S(1)}, bf16[1024,512]{1,0:T(8,128)(2,1)S(1)}, u32[]{:S(2)}, u32[]{:S(2)}) %collective-permute-start.32) | collective-permute-done | bytes 1048608 | tf_op jit(solution)/shard_map/ppermute | solution.py:688
  162.5 10.0 %collective-permute-done.37.refs_1_ = bf16[128,2048]{1,0:T(8,128)(2,1)S(1)} collective-permute-done((bf16[128,2048]{1,0:T(8,128)(2,1)S(1)}, bf16[128,2048]{1,0:T(8,128)(2,1)S(1)}, u32[]{:S(2)}, u32[]{:S(2)}) %collective-permute-start.37) | collective-permute-done | bytes 524320 | tf_op jit(solution)/shard_map/ppermute | solution.py:688
  172.5 2.4 collective-permute-done.38.refs_2_
  174.9 7.3 %collective-permute-done.39.refs_3_ = bf16[128,2048]{1,0:T(8,128)(2,1)S(1)} collective-permute-done((bf16[128,2048]{1,0:T(8,128)(2,1)S(1)}, bf16[128,2048]{1,0:T(8,128)(2,1)S(1)}, u32[]{:S(2)}, u32[]{:S(2)}) %collective-permute-start.39) | collective-permute-done | bytes 524320 | tf_op jit(solution)/shard_map/ppermute | solution.py:688
  183.1 2.5 collective-permute-start.42
  187.3 6.2 %collective-permute-done.44.refs_30_ = bf16[512,512]{1,0:T(8,128)(2,1)S(1)} collective-permute-done((bf16[512,512]{1,0:T(8,128)(2,1)}, bf16[512,512]{1,0:T(8,128)(2,1)S(1)}, u32[]{:S(2)}, u32[]{:S(2)}) %collective-permute-start.44) | collective-permute-done | bytes 524320 | tf_op jit(solution)/shard_map/ppermute | solution.py:688
  194.0 2.0 collective-permute-done.46.block
  198.0 6.7 %shard_map.244 = (bf16[512,1024]{1,0:T(8,128)(2,1)S(1)}, bf16[512,1024]{1,0:T(8,128)(2,1)S(1)}, bf16[512,1024]{1,0:T(8,128)(2,1)S(1)}, bf16[512,1024]{1,0:T(8,12...) custom-call(bf16[128,2048]{1,0:T(8,128)(2,1)S(1)} %collective-permut, ...), custom_call_target="tpu_custom_call" | custom-call | tf_op jit(solution)/shard_map/pallas_call | solution.py:115
  205.3 5.8 %collective-permute-done.47.block = bf16[128,2048]{1,0:T(8,128)(2,1)S(1)} collective-permute-done((bf16[128,2048]{1,0:T(8,128)(2,1)S(1)}, bf16[128,2048]{1,0:T(8,128)(2,1)S(1)}, u32[]{:S(2)}, u32[]{:S(2)}) %collective-permute-start.47) | collective-permute-done | bytes 524320 | tf_op jit(solution)/shard_map/ppermute | solution.py:688
  212.7 6.6 %shard_map.245 = (bf16[512,1024]{1,0:T(8,128)(2,1)S(1)}, bf16[512,1024]{1,0:T(8,128)(2,1)S(1)}, bf16[512,1024]{1,0:T(8,128)(2,1)S(1)}, bf16[512,1024]{1,0:T(8,12...) custom-call(bf16[128,2048]{1,0:T(8,128)(2,1)S(1)} %get-tuple-element, ...), custom_call_target="tpu_custom_call", output_to_operand_aliasing={{0}: (33, {}), {1}: (34, {}), {2}: (35, {}), {3}: (36, {}),... | custom-call | tf_op jit(solution)/shard_map/pallas_call | solution.py:115
  219.3 6.7 %shard_map.246 = (bf16[512,1024]{1,0:T(8,128)(2,1)S(1)}, bf16[512,1024]{1,0:T(8,128)(2,1)S(1)}, bf16[512,1024]{1,0:T(8,128)(2,1)S(1)}, bf16[512,1024]{1,0:T(8,12...) custom-call(bf16[128,2048]{1,0:T(8,128)(2,1)S(1)} %collective-permut, ...), custom_call_target="tpu_custom_call", output_to_operand_aliasing={{0}: (33, {}), {1}: (34, {}), {2}: (35, {}), {3}: (36, {}),... | custom-call | tf_op jit(solution)/shard_map/pallas_call | solution.py:115
  226.6 7.0 %collective-permute-done.48.block = bf16[128,2048]{1,0:T(8,128)(2,1)S(1)} collective-permute-done((bf16[128,2048]{1,0:T(8,128)(2,1)S(1)}, bf16[128,2048]{1,0:T(8,128)(2,1)S(1)}, u32[]{:S(2)}, u32[]{:S(2)}) %collective-permute-start.48) | collective-permute-done | bytes 524320 | tf_op jit(solution)/shard_map/ppermute | solution.py:688
  233.6 6.6 %shard_map.247 = (bf16[512,1024]{1,0:T(8,128)(2,1)S(1)}, bf16[512,1024]{1,0:T(8,128)(2,1)S(1)}, bf16[512,1024]{1,0:T(8,128)(2,1)S(1)}, bf16[512,1024]{1,0:T(8,12...) custom-call(bf16[128,2048]{1,0:T(8,128)(2,1)S(1)} %collective-permut, ...), custom_call_target="tpu_custom_call", output_to_operand_aliasing={{0}: (33, {}), {1}: (34, {}), {2}: (35, {}), {3}: (36, {}),... | custom-call | tf_op jit(solution)/shard_map/pallas_call | solution.py:115
  246.4 7.0 %collective-permute-done.51.refs_1_ = bf16[128,2048]{1,0:T(8,128)(2,1)S(1)} collective-permute-done((bf16[128,2048]{1,0:T(8,128)(2,1)S(1)}, bf16[128,2048]{1,0:T(8,128)(2,1)S(1)}, u32[]{:S(2)}, u32[]{:S(2)}) %collective-permute-start.51) | collective-permute-done | bytes 524320 | tf_op jit(solution)/shard_map/ppermute | solution.py:688
  255.4 2.5 collective-permute-start.52
  257.8 2.5 collective-permute-start.59
  260.3 6.8 %collective-permute-done.52.block = bf16[128,2048]{1,0:T(8,128)(2,1)S(1)} collective-permute-done((bf16[128,2048]{1,0:T(8,128)(2,1)S(1)}, bf16[128,2048]{1,0:T(8,128)(2,1)S(1)}, u32[]{:S(2)}, u32[]{:S(2)}) %collective-permute-start.52) | collective-permute-done | bytes 524320 | tf_op jit(solution)/shard_map/ppermute | solution.py:688
  267.1 2.8 collective-permute-start.55
  272.6 8.1 %shard_map.249 = (bf16[512,1024]{1,0:T(8,128)(2,1)S(1)}, bf16[512,1024]{1,0:T(8,128)(2,1)S(1)}, bf16[512,1024]{1,0:T(8,128)(2,1)S(1)}, bf16[512,1024]{1,0:T(8,12...) custom-call(bf16[128,2048]{1,0:T(8,128)(2,1)S(1)} %collective-permute-done.52.blo, ...), custom_call_target="tpu_custom_call" | custom-call | tf_op jit(solution)/shard_map/pallas_call | solution.py:115
  281.5 8.1 %shard_map.250 = (bf16[512,1024]{1,0:T(8,128)(2,1)S(1)}, bf16[512,1024]{1,0:T(8,128)(2,1)S(1)}, bf16[512,1024]{1,0:T(8,128)(2,1)S(1)}, bf16[512,1024]{1,0:T(8,12...) custom-call(bf16[128,2048]{1,0:T(8,128)(2,1)S(1)} %get-tuple-element, ...), custom_call_target="tpu_custom_call", output_to_operand_aliasing={{0}: (37, {}), {1}: (38, {}), {2}: (39, {}), {3}: (40, {}),... | custom-call | tf_op jit(solution)/shard_map/pallas_call | solution.py:115
  291.2 2.6 collective-permute-start.56
  293.8 8.1 %shard_map.251 = (bf16[512,1024]{1,0:T(8,128)(2,1)S(1)}, bf16[512,1024]{1,0:T(8,128)(2,1)S(1)}, bf16[512,1024]{1,0:T(8,128)(2,1)S(1)}, bf16[512,1024]{1,0:T(8,12...) custom-call(bf16[128,2048]{1,0:T(8,128)(2,1)S(1)} %collective-permut, ...), custom_call_target="tpu_custom_call", output_to_operand_aliasing={{0}: (37, {}), {1}: (38, {}), {2}: (39, {}), {3}: (40, {})} | custom-call | tf_op jit(solution)/shard_map/pallas_call | solution.py:115
  302.7 2.3 collective-permute-start.62
  305.0 8.2 %shard_map.252 = (bf16[512,1024]{1,0:T(8,128)(2,1)S(1)}, bf16[512,1024]{1,0:T(8,128)(2,1)S(1)}, bf16[512,1024]{1,0:T(8,128)(2,1)S(1)}, bf16[512,1024]{1,0:T(8,12...) custom-call(bf16[128,2048]{1,0:T(8,128)(2,1)S(1)} %collective-permut, ...), custom_call_target="tpu_custom_call", output_to_operand_aliasing={{0}: (37, {}), {1}: (38, {}), {2}: (39, {}), {3}: (40, {}),... | custom-call | tf_op jit(solution)/shard_map/pallas_call | solution.py:115
  313.4 2.9 collective-permute-start.63
  318.6 6.2 %collective-permute-done.63.refs_1_ = bf16[128,2048]{1,0:T(8,128)(2,1)S(1)} collective-permute-done((bf16[128,2048]{1,0:T(8,128)(2,1)S(1)}, bf16[128,2048]{1,0:T(8,128)(2,1)S(1)}, u32[]{:S(2)}, u32[]{:S(2)}) %collective-permute-start.63) | collective-permute-done | bytes 524320 | tf_op jit(solution)/shard_map/ppermute | solution.py:688
  329.1 2.1 collective-permute-start.68
  331.3 10.5 %collective-permute-done.66.refs_7_ = bf16[128,2048]{1,0:T(8,128)(2,1)S(1)} collective-permute-done((bf16[128,2048]{1,0:T(8,128)(2,1)S(1)}, bf16[128,2048]{1,0:T(8,128)(2,1)S(1)}, u32[]{:S(2)}, u32[]{:S(2)}) %collective-permute-start.66) | collective-permute-done | bytes 524320 | tf_op jit(solution)/shard_map/ppermute | solution.py:688
  344.3 2.6 convolution_convert_fusion.2
  348.3 2.6 convolution_convert_fusion.4
  356.6 8.1 %shard_map.254 = (f32[512,512]{1,0:T(8,128)S(1)}, f32[512,512]{1,0:T(8,128)S(1)}, bf16[512,512]{1,0:T(8,128)(2,1)S(1)}, f32[8,512]{1,0:T(8,128)S(1)}, f32[8,512]...) custom-call(s32[5]{0:T(128)S(1)} %stack.34.pos, f32[8,128]{1,0:T(8,128)S(1)} %get-tuple-element.238.refs_1_.refs_0_, ...), custom_call_target="tpu_custom_call" | custom-call | tf_op jit(solution)/shard_map/pallas_call | solution.py:115
  370.8 3.7 collective-permute-done.74
  375.4 2.9 collective-permute-done.75
  380.0 2.3 shard_map.260
  382.4 2.1 shard_map.256
  390.2 2.1 shard_map.259
  392.9 19.6 %collective-permute-done.79 = bf16[1024,512]{1,0:T(8,128)(2,1)S(1)} collective-permute-done((bf16[1024,512]{1,0:T(8,128)(2,1)S(1)}, bf16[1024,512]{1,0:T(8,128)(2,1)S(1)}, u32[]{:S(2)}, u32[]{:S(2)}) %collective-permute-start.79) | collective-permute-done | bytes 1048608 | tf_op jit(solution)/shard_map/ppermute | solution.py:688
  415.1 3.4 collective-permute-start.87
  422.4 2.1 shard_map.258
  424.6 4.3 shard_map.257
  429.4 12.1 %collective-permute-done.87 = bf16[1040,512]{1,0:T(8,128)(2,1)S(1)} collective-permute-done((bf16[1040,512]{1,0:T(8,128)(2,1)S(1)}, bf16[1040,512]{1,0:T(8,128)(2,1)S(1)}, u32[]{:S(2)}, u32[]{:S(2)}) %collective-permute-start.87) | collective-permute-done | bytes 1064992 | tf_op jit(solution)/shard_map/ppermute | solution.py:688
  443.4 3.7 collective-permute-start.88
  450.8 5.8 %shard_map.261 = f32[1024,512]{1,0:T(8,128)} custom-call(bf16[256,1024]{1,0:T(8,128)(2,1)S(1)} %get-tuple-element.311.refs_0_, bf16[256,1024]{1,0:T(8,128)(2,1)S(1)} %collective-permute-done.91.refs_1_, bf16[256,1024]{1,0:T(8,128)(2,1)S(1)} %collective-permute-done.57.refs_2_, bf16[256,1024]{1,0:T(8,128)(2,1)S(1)} %collective-permute-done.94.refs_3_, ...), custom_call_target="tpu_custom_call" | custom-call | tf_op jit(solution)/shard_map/pallas_call | solution.py:115
  456.7 12.9 %collective-permute-done.90 = bf16[1024,512]{1,0:T(8,128)(2,1)S(1)} collective-permute-done((bf16[1024,512]{1,0:T(8,128)(2,1)S(1)}, bf16[1024,512]{1,0:T(8,128)(2,1)S(1)}, u32[]{:S(2)}, u32[]{:S(2)}) %collective-permute-start.90) | collective-permute-done | bytes 1048608 | tf_op jit(solution)/shard_map/ppermute | solution.py:688
  477.7 3.1 collective-permute-done.81
  484.9 4.8 collective-permute-done.105.refs_2_
  489.7 6.1 %collective-permute-done.106.refs_3_ = bf16[80,1536]{1,0:T(8,128)(2,1)S(1)} collective-permute-done((bf16[80,1536]{1,0:T(8,128)(2,1)S(1)}, bf16[80,1536]{1,0:T(8,128)(2,1)S(1)}, u32[]{:S(2)}, u32[]{:S(2)}) %collective-permute-start.106) | collective-permute-done | bytes 245792 | tf_op jit(solution)/shard_map/ppermute | solution.py:688
  498.2 7.3 %collective-permute-done.103 = bf16[128,2048]{1,0:T(8,128)(2,1)S(1)} collective-permute-done((bf16[128,2048]{1,0:T(8,128)(2,1)S(1)}, bf16[128,2048]{1,0:T(8,128)(2,1)S(1)}, u32[]{:S(2)}, u32[]{:S(2)}) %collective-permute-start.103) | collective-permute-done | bytes 524320 | tf_op jit(solution)/shard_map/ppermute | solution.py:688
  (290 shorter events, 127.7 us)
Async XLA Ops:
  2.0 26.9 %collective-permute-start.3 = (bf16[512,512]{1,0:T(8,128)(2,1)S(1)}, bf16[512,512]{1,0:T(8,128)(2,1)}, u32[]{:S(2)}, u32[]{:S(2)}) collective-permute-start(bf16[512,512]{1,0:T(8,128)(2,1)S(1)} %get-tuple-element.250.refs_16_), channel_id=1, source_target_pairs={{0,16},{1,17},{2,18},{3,19},{4,20},{5,21},{6,22},{7,23},{8,24},{9,... | collective-permute-start | bytes 1572872 | tf_op jit(solution)/shard_map/ppermute | solution.py:688
  5.0 23.9 %collective-permute-start.4 = (bf16[512,512]{1,0:T(8,128)(2,1)S(1)}, bf16[512,512]{1,0:T(8,128)(2,1)}, u32[]{:S(2)}, u32[]{:S(2)}) collective-permute-start(bf16[512,512]{1,0:T(8,128)(2,1)S(1)} %get-tuple-element.251.refs_20_), channel_id=1, source_target_pairs={{0,2},{1,3},{2,0},{3,1},{4,6},{5,7},{6,4},{7,5},{8,10},{9,11},{10,... | collective-permute-start | bytes 1572872 | tf_op jit(solution)/shard_map/ppermute | solution.py:688
  11.0 18.0 %collective-permute-start = (bf16[80,1536]{1,0:T(8,128)(2,1)S(1)}, bf16[80,1536]{1,0:T(8,128)(2,1)S(1)}, u32[]{:S(2)}, u32[]{:S(2)}) collective-permute-start(bf16[80,1536]{1,0:T(8,128)(2,1)S(1)} %get-tuple-element.216), channel_id=1, source_target_pairs={{0,2},{1,3},{2,0},{3,1},{4,6},{5,7},{6,4},{7,5},{8,10},{9,11},{10,... | collective-permute-start | bytes 737288 | tf_op jit(solution)/shard_map/ppermute | solution.py:688
  11.5 17.4 %collective-permute-start.1 = (bf16[80,1536]{1,0:T(8,128)(2,1)S(1)}, bf16[80,1536]{1,0:T(8,128)(2,1)S(1)}, u32[]{:S(2)}, u32[]{:S(2)}) collective-permute-start(bf16[80,1536]{1,0:T(8,128)(2,1)S(1)} %get-tuple-element.217), channel_id=1, source_target_pairs={{0,16},{1,17},{2,18},{3,19},{4,20},{5,21},{6,22},{7,23},{8,24},{9,... | collective-permute-start | bytes 737288 | tf_op jit(solution)/shard_map/ppermute | solution.py:688
  11.6 17.3 %collective-permute-start.2 = (bf16[80,1536]{1,0:T(8,128)(2,1)S(1)}, bf16[80,1536]{1,0:T(8,128)(2,1)S(1)}, u32[]{:S(2)}, u32[]{:S(2)}) collective-permute-start(bf16[80,1536]{1,0:T(8,128)(2,1)S(1)} %get-tuple-element.218), channel_id=1, source_target_pairs={{0,18},{1,19},{2,16},{3,17},{4,22},{5,23},{6,20},{7,21},{8,26},{9,... | collective-permute-start | bytes 737288 | tf_op jit(solution)/shard_map/ppermute | solution.py:688
  30.0 24.6 %collective-permute-start.9 = (bf16[1040,512]{1,0:T(8,128)(2,1)}, bf16[1040,512]{1,0:T(8,128)(2,1)}, u32[]{:S(2)}, u32[]{:S(2)}) collective-permute-start(bf16[1040,512]{1,0:T(8,128)(2,1)} %get-tuple-element.223.refs_0_), channel_id=1, source_target_pairs={{0,8},{1,9},{2,10},{3,11},{4,0},{5,1},{6,2},{7,3},{8,12},{9,13},{1... | collective-permute-start | bytes 3194888 | tf_op jit(solution)/shard_map/ppermute | solution.py:688
  54.6 24.4 %collective-permute-start.10 = (bf16[1040,512]{1,0:T(8,128)(2,1)}, bf16[1040,512]{1,0:T(8,128)(2,1)S(1)}, u32[]{:S(2)}, u32[]{:S(2)}) collective-permute-start(bf16[1040,512]{1,0:T(8,128)(2,1)} %collective-permute-done.9.refs_2_), channel_id=1, source_target_pairs={{0,8},{1,9},{2,10},{3,11},{4,0},{5,1},{6,2},{7,3},{8,12},{9,13},{1... | collective-permute-start | bytes 3194888 | tf_op jit(solution)/shard_map/ppermute | solution.py:688
  58.5 25.1 %collective-permute-start.11 = (bf16[1024,512]{1,0:T(8,128)(2,1)S(1)}, bf16[1024,512]{1,0:T(8,128)(2,1)S(1)}, u32[]{:S(2)}, u32[]{:S(2)}) collective-permute-start(bf16[1024,512]{1,0:T(8,128)(2,1)S(1)} %copy-done), channel_id=1, source_target_pairs={{0,16},{1,17},{2,18},{3,19},{4,20},{5,21},{6,22},{7,23},{8,24},{9,... | collective-permute-start | bytes 3145736 | tf_op jit(solution)/shard_map/ppermute | solution.py:688
  60.0 27.6 %collective-permute-start.21 = (bf16[1040,512]{1,0:T(8,128)(2,1)}, bf16[1040,512]{1,0:T(8,128)(2,1)S(1)}, u32[]{:S(2)}, u32[]{:S(2)}) collective-permute-start(bf16[1040,512]{1,0:T(8,128)(2,1)} %get-tuple-element.223.refs_0_), channel_id=1, source_target_pairs={{0,1},{1,0},{2,3},{3,2},{4,5},{5,4},{6,7},{7,6},{8,9},{9,8},{10,11... | collective-permute-start | bytes 3194888 | tf_op jit(solution)/shard_map/ppermute | solution.py:688
  60.7 25.2 %collective-permute-start.12 = (bf16[1024,512]{1,0:T(8,128)(2,1)S(1)}, bf16[1024,512]{1,0:T(8,128)(2,1)S(1)}, u32[]{:S(2)}, u32[]{:S(2)}) collective-permute-start(bf16[1024,512]{1,0:T(8,128)(2,1)S(1)} %copy-done.1), channel_id=1, source_target_pairs={{0,2},{1,3},{2,0},{3,1},{4,6},{5,7},{6,4},{7,5},{8,10},{9,11},{10,... | collective-permute-start | bytes 3145736 | tf_op jit(solution)/shard_map/ppermute | solution.py:688
  62.2 26.7 %collective-permute-start.22 = (bf16[1040,512]{1,0:T(8,128)(2,1)}, bf16[1040,512]{1,0:T(8,128)(2,1)S(1)}, u32[]{:S(2)}, u32[]{:S(2)}) collective-permute-start(bf16[1040,512]{1,0:T(8,128)(2,1)} %collective-permute-done.9.refs_2_), channel_id=1, source_target_pairs={{0,1},{1,0},{2,3},{3,2},{4,5},{5,4},{6,7},{7,6},{8,9},{9,8},{10,11... | collective-permute-start | bytes 3194888 | tf_op jit(solution)/shard_map/ppermute | solution.py:688
  85.9 26.1 %collective-permute-start.15 = (bf16[1040,512]{1,0:T(8,128)(2,1)S(1)}, bf16[1040,512]{1,0:T(8,128)(2,1)S(1)}, u32[]{:S(2)}, u32[]{:S(2)}) collective-permute-start(bf16[1040,512]{1,0:T(8,128)(2,1)S(1)} %collective-permute-done.10.refs_4_), channel_id=1, source_target_pairs={{0,8},{1,9},{2,10},{3,11},{4,0},{5,1},{6,2},{7,3},{8,12},{9,13},{1... | collective-permute-start | bytes 3194888 | tf_op jit(solution)/shard_map/ppermute | solution.py:688
  86.8 24.9 %collective-permute-start.16 = (bf16[1024,512]{1,0:T(8,128)(2,1)S(1)}, bf16[1024,512]{1,0:T(8,128)(2,1)S(1)}, u32[]{:S(2)}, u32[]{:S(2)}) collective-permute-start(bf16[1024,512]{1,0:T(8,128)(2,1)S(1)} %copy-done), channel_id=1, source_target_pairs={{0,2},{1,3},{2,0},{3,1},{4,6},{5,7},{6,4},{7,5},{8,10},{9,11},{10,... | collective-permute-start | bytes 3145736 | tf_op jit(solution)/shard_map/ppermute | solution.py:688
  87.5 24.4 %collective-permute-start.17 = (bf16[1024,512]{1,0:T(8,128)(2,1)S(1)}, bf16[1024,512]{1,0:T(8,128)(2,1)S(1)}, u32[]{:S(2)}, u32[]{:S(2)}) collective-permute-start(bf16[1024,512]{1,0:T(8,128)(2,1)S(1)} %copy-done.1), channel_id=1, source_target_pairs={{0,16},{1,17},{2,18},{3,19},{4,20},{5,21},{6,22},{7,23},{8,24},{9,... | collective-permute-start | bytes 3145736 | tf_op jit(solution)/shard_map/ppermute | solution.py:688
  88.8 23.1 %collective-permute-start.19 = (bf16[1024,512]{1,0:T(8,128)(2,1)S(1)}, bf16[1024,512]{1,0:T(8,128)(2,1)S(1)}, u32[]{:S(2)}, u32[]{:S(2)}) collective-permute-start(bf16[1024,512]{1,0:T(8,128)(2,1)S(1)} %collective-permute-done.11.refs_4_), channel_id=1, source_target_pairs={{0,1},{1,0},{2,3},{3,2},{4,5},{5,4},{6,7},{7,6},{8,9},{9,8},{10,11... | collective-permute-start | bytes 3145736 | tf_op jit(solution)/shard_map/ppermute | solution.py:688
  88.8 23.1 %collective-permute-start.20 = (bf16[1024,512]{1,0:T(8,128)(2,1)S(1)}, bf16[1024,512]{1,0:T(8,128)(2,1)S(1)}, u32[]{:S(2)}, u32[]{:S(2)}) collective-permute-start(bf16[1024,512]{1,0:T(8,128)(2,1)S(1)} %collective-permute-done.12.refs_10_), channel_id=1, source_target_pairs={{0,1},{1,0},{2,3},{3,2},{4,5},{5,4},{6,7},{7,6},{8,9},{9,8},{10,11... | collective-permute-start | bytes 3145736 | tf_op jit(solution)/shard_map/ppermute | solution.py:688
  112.6 14.4 %collective-permute-start.33 = (bf16[512,512]{1,0:T(8,128)(2,1)S(1)}, bf16[512,512]{1,0:T(8,128)(2,1)S(1)}, u32[]{:S(2)}, u32[]{:S(2)}) collective-permute-start(bf16[512,512]{1,0:T(8,128)(2,1)S(1)} %get-tuple-element.250.refs_16_), channel_id=1, source_target_pairs={{0,2},{1,3},{2,0},{3,1},{4,6},{5,7},{6,4},{7,5},{8,10},{9,11},{10,... | collective-permute-start | bytes 1572872 | tf_op jit(solution)/shard_map/ppermute | solution.py:688
  120.8 14.8 %collective-permute-start.35 = (bf16[512,512]{1,0:T(8,128)(2,1)S(1)}, bf16[512,512]{1,0:T(8,128)(2,1)S(1)}, u32[]{:S(2)}, u32[]{:S(2)}) collective-permute-start(bf16[512,512]{1,0:T(8,128)(2,1)S(1)} %get-tuple-element.251.refs_20_), channel_id=1, source_target_pairs={{0,16},{1,17},{2,18},{3,19},{4,20},{5,21},{6,22},{7,23},{8,24},{9,... | collective-permute-start | bytes 1572872 | tf_op jit(solution)/shard_map/ppermute | solution.py:688
  124.6 18.7 %collective-permute-start.29 = (bf16[1024,512]{1,0:T(8,128)(2,1)S(1)}, bf16[1024,512]{1,0:T(8,128)(2,1)S(1)}, u32[]{:S(2)}, u32[]{:S(2)}) collective-permute-start(bf16[1024,512]{1,0:T(8,128)(2,1)S(1)} %collective-permute-done.16.refs_2_), channel_id=1, source_target_pairs={{0,1},{1,0},{2,3},{3,2},{4,5},{5,4},{6,7},{7,6},{8,9},{9,8},{10,11... | collective-permute-start | bytes 3145736 | tf_op jit(solution)/shard_map/ppermute | solution.py:688
  124.6 18.7 %collective-permute-start.30 = (bf16[1024,512]{1,0:T(8,128)(2,1)S(1)}, bf16[1024,512]{1,0:T(8,128)(2,1)S(1)}, u32[]{:S(2)}, u32[]{:S(2)}) collective-permute-start(bf16[1024,512]{1,0:T(8,128)(2,1)S(1)} %collective-permute-done.17.refs_12_), channel_id=1, source_target_pairs={{0,1},{1,0},{2,3},{3,2},{4,5},{5,4},{6,7},{7,6},{8,9},{9,8},{10,11... | collective-permute-start | bytes 3145736 | tf_op jit(solution)/shard_map/ppermute | solution.py:688
  127.3 29.7 %collective-permute-start.32 = (bf16[1024,512]{1,0:T(8,128)(2,1)S(1)}, bf16[1024,512]{1,0:T(8,128)(2,1)S(1)}, u32[]{:S(2)}, u32[]{:S(2)}) collective-permute-start(bf16[1024,512]{1,0:T(8,128)(2,1)S(1)} %collective-permute-done.12.refs_10_), channel_id=1, source_target_pairs={{0,16},{1,17},{2,18},{3,19},{4,20},{5,21},{6,22},{7,23},{8,24},{9,... | collective-permute-start | bytes 3145736 | tf_op jit(solution)/shard_map/ppermute | solution.py:688
  135.6 22.9 %collective-permute-start.31 = (bf16[1024,512]{1,0:T(8,128)(2,1)S(1)}, bf16[1024,512]{1,0:T(8,128)(2,1)S(1)}, u32[]{:S(2)}, u32[]{:S(2)}) collective-permute-start(bf16[1024,512]{1,0:T(8,128)(2,1)S(1)} %collective-permute-done.11.refs_4_), channel_id=1, source_target_pairs={{0,2},{1,3},{2,0},{3,1},{4,6},{5,7},{6,4},{7,5},{8,10},{9,11},{10,... | collective-permute-start | bytes 3145736 | tf_op jit(solution)/shard_map/ppermute | solution.py:688
  158.5 14.0 %collective-permute-start.37 = (bf16[128,2048]{1,0:T(8,128)(2,1)S(1)}, bf16[128,2048]{1,0:T(8,128)(2,1)S(1)}, u32[]{:S(2)}, u32[]{:S(2)}) collective-permute-start(bf16[128,2048]{1,0:T(8,128)(2,1)S(1)} %get-tuple-element.253), channel_id=1, source_target_pairs={{0,2},{1,3},{2,0},{3,1},{4,6},{5,7},{6,4},{7,5},{8,10},{9,11},{10,... | collective-permute-start | bytes 1572872 | tf_op jit(solution)/shard_map/ppermute | solution.py:688
  160.0 14.9 %collective-permute-start.38 = (bf16[128,2048]{1,0:T(8,128)(2,1)S(1)}, bf16[128,2048]{1,0:T(8,128)(2,1)S(1)}, u32[]{:S(2)}, u32[]{:S(2)}) collective-permute-start(bf16[128,2048]{1,0:T(8,128)(2,1)S(1)} %get-tuple-element.254), channel_id=1, source_target_pairs={{0,16},{1,17},{2,18},{3,19},{4,20},{5,21},{6,22},{7,23},{8,24},{9,... | collective-permute-start | bytes 1572872 | tf_op jit(solution)/shard_map/ppermute | solution.py:688
  160.9 21.3 %collective-permute-start.39 = (bf16[128,2048]{1,0:T(8,128)(2,1)S(1)}, bf16[128,2048]{1,0:T(8,128)(2,1)S(1)}, u32[]{:S(2)}, u32[]{:S(2)}) collective-permute-start(bf16[128,2048]{1,0:T(8,128)(2,1)S(1)} %get-tuple-element.255), channel_id=1, source_target_pairs={{0,18},{1,19},{2,16},{3,17},{4,22},{5,23},{6,20},{7,21},{8,26},{9,... | collective-permute-start | bytes 1572872 | tf_op jit(solution)/shard_map/ppermute | solution.py:688
  162.0 35.9 %collective-permute-start.41 = (bf16[1024,512]{1,0:T(8,128)(2,1)S(1)}, bf16[1024,512]{1,0:T(8,128)(2,1)S(1)}, u32[]{:S(2)}, u32[]{:S(2)}) collective-permute-start(bf16[1024,512]{1,0:T(8,128)(2,1)S(1)} %collective-permute-done.32.refs_14_), channel_id=1, source_target_pairs={{0,1},{1,0},{2,3},{3,2},{4,5},{5,4},{6,7},{7,6},{8,9},{9,8},{10,11... | collective-permute-start | bytes 3145736 | tf_op jit(solution)/shard_map/ppermute | solution.py:688
  162.0 35.9 %collective-permute-start.40 = (bf16[1024,512]{1,0:T(8,128)(2,1)S(1)}, bf16[1024,512]{1,0:T(8,128)(2,1)S(1)}, u32[]{:S(2)}, u32[]{:S(2)}) collective-permute-start(bf16[1024,512]{1,0:T(8,128)(2,1)S(1)} %collective-permute-done.31.refs_6_), channel_id=1, source_target_pairs={{0,1},{1,0},{2,3},{3,2},{4,5},{5,4},{6,7},{7,6},{8,9},{9,8},{10,11... | collective-permute-start | bytes 3145736 | tf_op jit(solution)/shard_map/ppermute | solution.py:688
  196.0 15.1 %collective-permute-start.47 = (bf16[128,2048]{1,0:T(8,128)(2,1)S(1)}, bf16[128,2048]{1,0:T(8,128)(2,1)S(1)}, u32[]{:S(2)}, u32[]{:S(2)}) collective-permute-start(bf16[128,2048]{1,0:T(8,128)(2,1)S(1)} %collective-permute-done.46.block), channel_id=1, source_target_pairs={{0,8},{1,9},{2,10},{3,11},{4,0},{5,1},{6,2},{7,3},{8,12},{9,13},{1... | collective-permute-start | bytes 1572872 | tf_op jit(solution)/shard_map/ppermute | solution.py:688
  204.7 21.3 %collective-permute-start.49 = (bf16[128,2048]{1,0:T(8,128)(2,1)S(1)}, bf16[128,2048]{1,0:T(8,128)(2,1)S(1)}, u32[]{:S(2)}, u32[]{:S(2)}) collective-permute-start(bf16[128,2048]{1,0:T(8,128)(2,1)S(1)} %convert_element_type.197), channel_id=1, source_target_pairs={{0,8},{1,9},{2,10},{3,11},{4,0},{5,1},{6,2},{7,3},{8,12},{9,13},{1... | collective-permute-start | bytes 1572872 | tf_op jit(solution)/shard_map/ppermute | solution.py:688
  211.1 22.5 %collective-permute-start.48 = (bf16[128,2048]{1,0:T(8,128)(2,1)S(1)}, bf16[128,2048]{1,0:T(8,128)(2,1)S(1)}, u32[]{:S(2)}, u32[]{:S(2)}) collective-permute-start(bf16[128,2048]{1,0:T(8,128)(2,1)S(1)} %collective-permute-done.47.block), channel_id=1, source_target_pairs={{0,8},{1,9},{2,10},{3,11},{4,0},{5,1},{6,2},{7,3},{8,12},{9,13},{1... | collective-permute-start | bytes 1572872 | tf_op jit(solution)/shard_map/ppermute | solution.py:688
  226.1 16.0 %collective-permute-start.50 = (bf16[128,2048]{1,0:T(8,128)(2,1)S(1)}, bf16[128,2048]{1,0:T(8,128)(2,1)S(1)}, u32[]{:S(2)}, u32[]{:S(2)}) collective-permute-start(bf16[128,2048]{1,0:T(8,128)(2,1)S(1)} %add_convert_fusion.13), channel_id=1, source_target_pairs={{0,8},{1,9},{2,10},{3,11},{4,0},{5,1},{6,2},{7,3},{8,12},{9,13},{1... | collective-permute-start | bytes 1572872 | tf_op jit(solution)/shard_map/ppermute | solution.py:688
  243.8 26.1 %collective-permute-start.53 = (bf16[512,1024]{1,0:T(8,128)(2,1)S(1)}, bf16[512,1024]{1,0:T(8,128)(2,1)S(1)}, u32[]{:S(2)}, u32[]{:S(2)}) collective-permute-start(bf16[512,1024]{1,0:T(8,128)(2,1)S(1)} %get-tuple-element.301), channel_id=1, source_target_pairs={{0,2},{1,3},{2,0},{3,1},{4,6},{5,7},{6,4},{7,5},{8,10},{9,11},{10,... | collective-permute-start | bytes 3145736 | tf_op jit(solution)/shard_map/ppermute | solution.py:688
  245.5 26.1 %collective-permute-start.54 = (bf16[512,1024]{1,0:T(8,128)(2,1)S(1)}, bf16[512,1024]{1,0:T(8,128)(2,1)S(1)}, u32[]{:S(2)}, u32[]{:S(2)}) collective-permute-start(bf16[512,1024]{1,0:T(8,128)(2,1)S(1)} %get-tuple-element.302), channel_id=1, source_target_pairs={{0,16},{1,17},{2,18},{3,19},{4,20},{5,21},{6,22},{7,23},{8,24},{9,... | collective-permute-start | bytes 3145736 | tf_op jit(solution)/shard_map/ppermute | solution.py:688
  257.8 33.4 %collective-permute-start.59 = (bf16[512,1024]{1,0:T(8,128)(2,1)S(1)}, bf16[512,1024]{1,0:T(8,128)(2,1)S(1)}, u32[]{:S(2)}, u32[]{:S(2)}) collective-permute-start(bf16[512,1024]{1,0:T(8,128)(2,1)S(1)} %get-tuple-element.301), channel_id=1, source_target_pairs={{0,18},{1,19},{2,16},{3,17},{4,22},{5,23},{6,20},{7,21},{8,26},{9,... | collective-permute-start | bytes 3145736 | tf_op jit(solution)/shard_map/ppermute | solution.py:688
  267.1 24.1 %collective-permute-start.55 = (bf16[128,2048]{1,0:T(8,128)(2,1)S(1)}, bf16[128,2048]{1,0:T(8,128)(2,1)S(1)}, u32[]{:S(2)}, u32[]{:S(2)}) collective-permute-start(bf16[128,2048]{1,0:T(8,128)(2,1)S(1)} %collective-permute-done.52.block), channel_id=1, source_target_pairs={{0,8},{1,9},{2,10},{3,11},{4,0},{5,1},{6,2},{7,3},{8,12},{9,13},{1... | collective-permute-start | bytes 1572872 | tf_op jit(solution)/shard_map/ppermute | solution.py:688
  280.8 21.2 %collective-permute-start.60 = (bf16[128,2048]{1,0:T(8,128)(2,1)S(1)}, bf16[128,2048]{1,0:T(8,128)(2,1)S(1)}, u32[]{:S(2)}, u32[]{:S(2)}) collective-permute-start(bf16[128,2048]{1,0:T(8,128)(2,1)S(1)} %convert_element_type.202), channel_id=1, source_target_pairs={{0,8},{1,9},{2,10},{3,11},{4,0},{5,1},{6,2},{7,3},{8,12},{9,13},{1... | collective-permute-start | bytes 1572872 | tf_op jit(solution)/shard_map/ppermute | solution.py:688
  289.6 15.4 %collective-permute-start.57 = (bf16[256,1024]{1,0:T(8,128)(2,1)S(1)}, bf16[256,1024]{1,0:T(8,128)(2,1)S(1)}, u32[]{:S(2)}, u32[]{:S(2)}) collective-permute-start(bf16[256,1024]{1,0:T(8,128)(2,1)S(1)} %get-tuple-element.311.refs_0_), channel_id=1, source_target_pairs={{0,2},{1,3},{2,0},{3,1},{4,6},{5,7},{6,4},{7,5},{8,10},{9,11},{10,... | collective-permute-start | bytes 1572872 | tf_op jit(solution)/shard_map/ppermute | solution.py:688
  290.4 14.7 %collective-permute-start.58 = (bf16[256,1024]{1,0:T(8,128)(2,1)S(1)}, bf16[256,1024]{1,0:T(8,128)(2,1)S(1)}, u32[]{:S(2)}, u32[]{:S(2)}) collective-permute-start(bf16[256,1024]{1,0:T(8,128)(2,1)S(1)} %get-tuple-element.312), channel_id=1, source_target_pairs={{0,16},{1,17},{2,18},{3,19},{4,20},{5,21},{6,22},{7,23},{8,24},{9,... | collective-permute-start | bytes 1572872 | tf_op jit(solution)/shard_map/ppermute | solution.py:688
  291.2 13.8 %collective-permute-start.56 = (bf16[128,2048]{1,0:T(8,128)(2,1)S(1)}, bf16[128,2048]{1,0:T(8,128)(2,1)S(1)}, u32[]{:S(2)}, u32[]{:S(2)}) collective-permute-start(bf16[128,2048]{1,0:T(8,128)(2,1)S(1)} %collective-permute-done.55.block), channel_id=1, source_target_pairs={{0,8},{1,9},{2,10},{3,11},{4,0},{5,1},{6,2},{7,3},{8,12},{9,13},{1... | collective-permute-start | bytes 1572872 | tf_op jit(solution)/shard_map/ppermute | solution.py:688
  327.8 14.0 %collective-permute-start.66 = (bf16[128,2048]{1,0:T(8,128)(2,1)S(1)}, bf16[128,2048]{1,0:T(8,128)(2,1)S(1)}, u32[]{:S(2)}, u32[]{:S(2)}) collective-permute-start(bf16[128,2048]{1,0:T(8,128)(2,1)S(1)} %get-tuple-element.347.refs_6_), channel_id=1, source_target_pairs={{0,2},{1,3},{2,0},{3,1},{4,6},{5,7},{6,4},{7,5},{8,10},{9,11},{10,... | collective-permute-start | bytes 1572872 | tf_op jit(solution)/shard_map/ppermute | solution.py:688
  328.6 26.2 %collective-permute-start.67 = (bf16[128,2048]{1,0:T(8,128)(2,1)S(1)}, bf16[128,2048]{1,0:T(8,128)(2,1)S(1)}, u32[]{:S(2)}, u32[]{:S(2)}) collective-permute-start(bf16[128,2048]{1,0:T(8,128)(2,1)S(1)} %get-tuple-element.347.refs_6_), channel_id=1, source_target_pairs={{0,16},{1,17},{2,18},{3,19},{4,20},{5,21},{6,22},{7,23},{8,24},{9,... | collective-permute-start | bytes 1572872 | tf_op jit(solution)/shard_map/ppermute | solution.py:688
  329.1 25.7 %collective-permute-start.68 = (bf16[128,2048]{1,0:T(8,128)(2,1)S(1)}, bf16[128,2048]{1,0:T(8,128)(2,1)S(1)}, u32[]{:S(2)}, u32[]{:S(2)}) collective-permute-start(bf16[128,2048]{1,0:T(8,128)(2,1)S(1)} %get-tuple-element.347.refs_6_), channel_id=1, source_target_pairs={{0,18},{1,19},{2,16},{3,17},{4,22},{5,23},{6,20},{7,21},{8,26},{9,... | collective-permute-start | bytes 1572872 | tf_op jit(solution)/shard_map/ppermute | solution.py:688
  355.5 13.8 %collective-permute-start.70 = (bf16[1024,1024]{1,0:T(8,128)(2,1)S(1)}, bf16[1024,1024]{1,0:T(8,128)(2,1)S(1)}, u32[]{:S(2)}, u32[]{:S(2)}) collective-permute-start(bf16[1024,1024]{1,0:T(8,128)(2,1)S(1)} %convolution_convert_fusion.6), channel_id=1, source_target_pairs={{0,1},{1,0},{2,3},{3,2},{4,5},{5,4},{6,7},{7,6},{8,9},{9,8},{10,11... | collective-permute-start | bytes 6291464 | tf_op jit(solution)/shard_map/ppermute | solution.py:688
  355.9 14.8 %collective-permute-start.69 = (bf16[256,1024]{1,0:T(8,128)(2,1)S(1)}, bf16[256,1024]{1,0:T(8,128)(2,1)S(1)}, u32[]{:S(2)}, u32[]{:S(2)}) collective-permute-start(bf16[256,1024]{1,0:T(8,128)(2,1)S(1)} %get-tuple-element.337), channel_id=1, source_target_pairs={{0,18},{1,19},{2,16},{3,17},{4,22},{5,23},{6,20},{7,21},{8,26},{9,... | collective-permute-start | bytes 1572872 | tf_op jit(solution)/shard_map/ppermute | solution.py:688
  384.5 29.1 %collective-permute-start.76 = (bf16[1040,512]{1,0:T(8,128)(2,1)S(1)}, bf16[1040,512]{1,0:T(8,128)(2,1)S(1)}, u32[]{:S(2)}, u32[]{:S(2)}) collective-permute-start(bf16[1040,512]{1,0:T(8,128)(2,1)S(1)} %get-tuple-element.376), channel_id=1, source_target_pairs={{0,1},{1,0},{2,3},{3,2},{4,5},{5,4},{6,7},{7,6},{8,9},{9,8},{10,11... | collective-permute-start | bytes 3194888 | tf_op jit(solution)/shard_map/ppermute | solution.py:688
  385.4 28.7 %collective-permute-start.86 = (bf16[1040,512]{1,0:T(8,128)(2,1)S(1)}, bf16[1040,512]{1,0:T(8,128)(2,1)S(1)}, u32[]{:S(2)}, u32[]{:S(2)}) collective-permute-start(bf16[1040,512]{1,0:T(8,128)(2,1)S(1)} %add_convert_fusion.6), channel_id=1, source_target_pairs={{0,8},{1,9},{2,10},{3,11},{4,0},{5,1},{6,2},{7,3},{8,12},{9,13},{1... | collective-permute-start | bytes 3194888 | tf_op jit(solution)/shard_map/ppermute | solution.py:688
  386.9 25.6 %collective-permute-start.79 = (bf16[1024,512]{1,0:T(8,128)(2,1)S(1)}, bf16[1024,512]{1,0:T(8,128)(2,1)S(1)}, u32[]{:S(2)}, u32[]{:S(2)}) collective-permute-start(bf16[1024,512]{1,0:T(8,128)(2,1)S(1)} %fusion.5), channel_id=1, source_target_pairs={{0,2},{1,3},{2,0},{3,1},{4,6},{5,7},{6,4},{7,5},{8,10},{9,11},{10,... | collective-permute-start | bytes 3145736 | tf_op jit(solution)/shard_map/ppermute | solution.py:688
  388.3 25.2 %collective-permute-start.77 = (bf16[1024,512]{1,0:T(8,128)(2,1)S(1)}, bf16[1024,512]{1,0:T(8,128)(2,1)S(1)}, u32[]{:S(2)}, u32[]{:S(2)}) collective-permute-start(bf16[1024,512]{1,0:T(8,128)(2,1)S(1)} %get-tuple-element.385), channel_id=1, source_target_pairs={{0,16},{1,17},{2,18},{3,19},{4,20},{5,21},{6,22},{7,23},{8,24},{9,... | collective-permute-start | bytes 3145736 | tf_op jit(solution)/shard_map/ppermute | solution.py:688
  392.3 22.3 %collective-permute-start.96 = (bf16[512,512]{1,0:T(8,128)(2,1)S(1)}, bf16[512,512]{1,0:T(8,128)(2,1)S(1)}, u32[]{:S(2)}, u32[]{:S(2)}) collective-permute-start(bf16[512,512]{1,0:T(8,128)(2,1)S(1)} %get-tuple-element.429), channel_id=1, source_target_pairs={{0,1},{1,0},{2,3},{3,2},{4,5},{5,4},{6,7},{7,6},{8,9},{9,8},{10,11... | collective-permute-start | bytes 1572872 | tf_op jit(solution)/shard_map/ppermute | solution.py:688
  414.6 14.3 %collective-permute-start.84 = (bf16[1040,512]{1,0:T(8,128)(2,1)S(1)}, bf16[1040,512]{1,0:T(8,128)(2,1)S(1)}, u32[]{:S(2)}, u32[]{:S(2)}) collective-permute-start(bf16[1040,512]{1,0:T(8,128)(2,1)S(1)} %get-tuple-element.393), channel_id=1, source_target_pairs={{0,1},{1,0},{2,3},{3,2},{4,5},{5,4},{6,7},{7,6},{8,9},{9,8},{10,11... | collective-permute-start | bytes 3194888 | tf_op jit(solution)/shard_map/ppermute | solution.py:688
  415.1 26.5 %collective-permute-start.87 = (bf16[1040,512]{1,0:T(8,128)(2,1)S(1)}, bf16[1040,512]{1,0:T(8,128)(2,1)S(1)}, u32[]{:S(2)}, u32[]{:S(2)}) collective-permute-start(bf16[1040,512]{1,0:T(8,128)(2,1)S(1)} %add_convert_fusion.5), channel_id=1, source_target_pairs={{0,8},{1,9},{2,10},{3,11},{4,0},{5,1},{6,2},{7,3},{8,12},{9,13},{1... | collective-permute-start | bytes 3194888 | tf_op jit(solution)/shard_map/ppermute | solution.py:688
  419.5 27.6 %collective-permute-start.80 = (bf16[1024,512]{1,0:T(8,128)(2,1)S(1)}, bf16[1024,512]{1,0:T(8,128)(2,1)S(1)}, u32[]{:S(2)}, u32[]{:S(2)}) collective-permute-start(bf16[1024,512]{1,0:T(8,128)(2,1)S(1)} %add_convert_fusion.7), channel_id=1, source_target_pairs={{0,16},{1,17},{2,18},{3,19},{4,20},{5,21},{6,22},{7,23},{8,24},{9,... | collective-permute-start | bytes 3145736 | tf_op jit(solution)/shard_map/ppermute | solution.py:688
  421.0 27.2 %collective-permute-start.78 = (bf16[1024,512]{1,0:T(8,128)(2,1)S(1)}, bf16[1024,512]{1,0:T(8,128)(2,1)S(1)}, u32[]{:S(2)}, u32[]{:S(2)}) collective-permute-start(bf16[1024,512]{1,0:T(8,128)(2,1)S(1)} %add_convert_fusion.8), channel_id=1, source_target_pairs={{0,2},{1,3},{2,0},{3,1},{4,6},{5,7},{6,4},{7,5},{8,10},{9,11},{10,... | collective-permute-start | bytes 3145736 | tf_op jit(solution)/shard_map/ppermute | solution.py:688
  428.9 14.4 %collective-permute-start.101 = (bf16[256,1024]{1,0:T(8,128)(2,1)S(1)}, bf16[256,1024]{1,0:T(8,128)(2,1)S(1)}, u32[]{:S(2)}, u32[]{:S(2)}) collective-permute-start(bf16[256,1024]{1,0:T(8,128)(2,1)S(1)} %collective-permute-done.69.refs_14_), channel_id=1, source_target_pairs={{0,1},{1,0},{2,3},{3,2},{4,5},{5,4},{6,7},{7,6},{8,9},{9,8},{10,11... | collective-permute-start | bytes 1572872 | tf_op jit(solution)/shard_map/ppermute | solution.py:688
  428.9 14.4 %collective-permute-start.95 = (bf16[256,1024]{1,0:T(8,128)(2,1)S(1)}, bf16[256,1024]{1,0:T(8,128)(2,1)S(1)}, u32[]{:S(2)}, u32[]{:S(2)}) collective-permute-start(bf16[256,1024]{1,0:T(8,128)(2,1)S(1)} %collective-permute-done.64.refs_10_), channel_id=1, source_target_pairs={{0,1},{1,0},{2,3},{3,2},{4,5},{5,4},{6,7},{7,6},{8,9},{9,8},{10,11... | collective-permute-start | bytes 1572872 | tf_op jit(solution)/shard_map/ppermute | solution.py:688
  441.6 28.0 %collective-permute-start.90 = (bf16[1024,512]{1,0:T(8,128)(2,1)S(1)}, bf16[1024,512]{1,0:T(8,128)(2,1)S(1)}, u32[]{:S(2)}, u32[]{:S(2)}) collective-permute-start(bf16[1024,512]{1,0:T(8,128)(2,1)S(1)} %fusion.6), channel_id=1, source_target_pairs={{0,2},{1,3},{2,0},{3,1},{4,6},{5,7},{6,4},{7,5},{8,10},{9,11},{10,... | collective-permute-start | bytes 3145736 | tf_op jit(solution)/shard_map/ppermute | solution.py:688
  443.3 29.0 %collective-permute-start.83 = (bf16[1040,512]{1,0:T(8,128)(2,1)S(1)}, bf16[1040,512]{1,0:T(8,128)(2,1)S(1)}, u32[]{:S(2)}, u32[]{:S(2)}) collective-permute-start(bf16[1040,512]{1,0:T(8,128)(2,1)S(1)} %get-tuple-element.391), channel_id=1, source_target_pairs={{0,1},{1,0},{2,3},{3,2},{4,5},{5,4},{6,7},{7,6},{8,9},{9,8},{10,11... | collective-permute-start | bytes 3194888 | tf_op jit(solution)/shard_map/ppermute | solution.py:688
  443.4 29.7 %collective-permute-start.88 = (bf16[1040,512]{1,0:T(8,128)(2,1)S(1)}, bf16[1040,512]{1,0:T(8,128)(2,1)S(1)}, u32[]{:S(2)}, u32[]{:S(2)}) collective-permute-start(bf16[1040,512]{1,0:T(8,128)(2,1)S(1)} %add_convert_fusion.4), channel_id=1, source_target_pairs={{0,8},{1,9},{2,10},{3,11},{4,0},{5,1},{6,2},{7,3},{8,12},{9,13},{1... | collective-permute-start | bytes 3194888 | tf_op jit(solution)/shard_map/ppermute | solution.py:688
  447.1 26.0 %collective-permute-start.89 = (bf16[1024,512]{1,0:T(8,128)(2,1)S(1)}, bf16[1024,512]{1,0:T(8,128)(2,1)S(1)}, u32[]{:S(2)}, u32[]{:S(2)}) collective-permute-start(bf16[1024,512]{1,0:T(8,128)(2,1)S(1)} %get-tuple-element.398), channel_id=1, source_target_pairs={{0,16},{1,17},{2,18},{3,19},{4,20},{5,21},{6,22},{7,23},{8,24},{9,... | collective-permute-start | bytes 3145736 | tf_op jit(solution)/shard_map/ppermute | solution.py:688
  450.1 30.7 %collective-permute-start.81 = (bf16[128,2048]{1,0:T(8,128)(2,1)S(1)}, bf16[128,2048]{1,0:T(8,128)(2,1)S(1)}, u32[]{:S(2)}, u32[]{:S(2)}) collective-permute-start(bf16[128,2048]{1,0:T(8,128)(2,1)S(1)} %get-tuple-element.387), channel_id=1, source_target_pairs={{0,2},{1,3},{2,0},{3,1},{4,6},{5,7},{6,4},{7,5},{8,10},{9,11},{10,... | collective-permute-start | bytes 1572872 | tf_op jit(solution)/shard_map/ppermute | solution.py:688
  469.6 14.9 %collective-permute-start.82 = (bf16[128,2048]{1,0:T(8,128)(2,1)S(1)}, bf16[128,2048]{1,0:T(8,128)(2,1)S(1)}, u32[]{:S(2)}, u32[]{:S(2)}) collective-permute-start(bf16[128,2048]{1,0:T(8,128)(2,1)S(1)} %get-tuple-element.388), channel_id=1, source_target_pairs={{0,16},{1,17},{2,18},{3,19},{4,20},{5,21},{6,22},{7,23},{8,24},{9,... | collective-permute-start | bytes 1572872 | tf_op jit(solution)/shard_map/ppermute | solution.py:688
  474.9 14.8 %collective-permute-start.105 = (bf16[80,1536]{1,0:T(8,128)(2,1)S(1)}, bf16[80,1536]{1,0:T(8,128)(2,1)S(1)}, u32[]{:S(2)}, u32[]{:S(2)}) collective-permute-start(bf16[80,1536]{1,0:T(8,128)(2,1)S(1)} %get-tuple-element.405), channel_id=1, source_target_pairs={{0,16},{1,17},{2,18},{3,19},{4,20},{5,21},{6,22},{7,23},{8,24},{9,... | collective-permute-start | bytes 737288 | tf_op jit(solution)/shard_map/ppermute | solution.py:688
  476.0 19.8 %collective-permute-start.106 = (bf16[80,1536]{1,0:T(8,128)(2,1)S(1)}, bf16[80,1536]{1,0:T(8,128)(2,1)S(1)}, u32[]{:S(2)}, u32[]{:S(2)}) collective-permute-start(bf16[80,1536]{1,0:T(8,128)(2,1)S(1)} %get-tuple-element.406), channel_id=1, source_target_pairs={{0,18},{1,19},{2,16},{3,17},{4,22},{5,23},{6,20},{7,21},{8,26},{9,... | collective-permute-start | bytes 737288 | tf_op jit(solution)/shard_map/ppermute | solution.py:688
  480.8 24.6 %collective-permute-start.103 = (bf16[128,2048]{1,0:T(8,128)(2,1)S(1)}, bf16[128,2048]{1,0:T(8,128)(2,1)S(1)}, u32[]{:S(2)}, u32[]{:S(2)}) collective-permute-start(bf16[128,2048]{1,0:T(8,128)(2,1)S(1)} %get-tuple-element.407), channel_id=1, source_target_pairs={{0,18},{1,19},{2,16},{3,17},{4,22},{5,23},{6,20},{7,21},{8,26},{9,... | collective-permute-start | bytes 1572872 | tf_op jit(solution)/shard_map/ppermute | solution.py:688
  (74 other events, 613.3 us)

commit v7 on v6

--- a/solution.py
+++ b/solution.py
@@ -650,13 +650,17 @@
             grad_up = (grad * by_up[k][:, lanes].astype(F32)).astype(BF16)
             grad_gates[k][:, lanes] = grad_gate
             grad_ups[k][:, lanes] = grad_up
-            for i in range(4):
-                columns = slice(i * quarter, (i + 1) * quarter)
-                rows = slice((i % 2) * quarter, (i % 2 + 1) * quarter)
-                weight = (i // 2) * count + at
-                part = nt(grad_gate, gates[weight][rows, :]) + nt(grad_up, ups[weight][rows, :])
-                total[:, columns] = part if k + dy == 0 else total[:, columns] + part
-    out[...] = total[...]
+    for i in range(4):
+        columns = slice(i * quarter, (i + 1) * quarter)
+        rows = slice((i % 2) * quarter, (i % 2 + 1) * quarter)
+        result = 0.0
+        for k in range(nc):
+            for dy in range(NY):
+                lanes = slice(dy * hidden, (dy + 1) * hidden)
+                weight = (i // 2) * count + dy * nc + k
+                result = result + nt(grad_gates[k][:, lanes], gates[weight][rows, :])
+                result = result + nt(grad_ups[k][:, lanes], ups[weight][rows, :])
+        out[:, columns] = result
 
 
 def down_back_kernel(*refs):

time: 510 us -> 510 us (level)
  transfers between devices with their start and end apart: 107 -> 107, of which waited for: 50 -> 49; matrix products, arithmetic and copies ran while one was open for 5% -> 5% of each run, Pallas kernels for 22% -> 22%
where the time goes in v7:
time: 510 us; the launch traced here: 507 us
  waiting for transfers between devices  246 us (48%)
  Pallas kernels  114 us (22%)
  starting transfers between devices  109 us (21%)
  matrix products  13 us (3%)
  other arithmetic  12.1 us (2%)
  local copies, waits for them, and re-layouts  10.5 us (2%)
    ppermute x107, waiting for transfers between devices, send(): return lax.ppermute(value, AXES, pairs)  246 us
    pallas_call x27, Pallas kernels, run(): pl.pallas_call(body, grid=(1,), out_shape=[pltpu.HBM(out.shape, out.dtype...  114 us
    ppermute x107, starting transfers between devices, send(): return lax.ppermute(value, AXES, pairs)  109 us
    dot_general x8, matrix products, tn(): lax.dot_general(left, right, (((0,), (0,)), ((), ())), preferred_element_...  13 us
  transfers between devices with their start and end apart: 107, of which 49 were waited for; matrix products, arithmetic and copies ran while one was open for 5% of the time, Pallas kernels for 22%

profile of v7, /device:TPU:0, one launch (start us, length us, event | category | flops | bytes accessed | tf_op | source)
XLA Modules:
  0.0 507.2 jit_solution(1316844628243788659)
XLA Ops:
  2.0 3.0 collective-permute-start.3
  11.6 2.9 collective-permute-start.2
  14.5 14.5 %collective-permute-done.refs_1_ = bf16[80,1536]{1,0:T(8,128)(2,1)S(1)} collective-permute-done((bf16[80,1536]{1,0:T(8,128)(2,1)S(1)}, bf16[80,1536]{1,0:T(8,128)(2,1)S(1)}, u32[]{:S(2)}, u32[]{:S(2)}) %collective-permute-start) | collective-permute-done | bytes 245792 | tf_op jit(solution)/shard_map/ppermute | solution.py:692
  30.0 2.6 collective-permute-start.9
  34.7 10.5 %collective-permute-done.5.refs_1_ = bf16[128,2048]{1,0:T(8,128)(2,1)} collective-permute-done((bf16[128,2048]{1,0:T(8,128)(2,1)}, bf16[128,2048]{1,0:T(8,128)(2,1)}, u32[]{:S(2)}, u32[]{:S(2)}) %collective-permute-start.5) | collective-permute-done | bytes 524320 | tf_op jit(solution)/shard_map/ppermute | solution.py:692
  50.2 2.4 collective-permute-done.7.refs_3_
  54.6 3.4 collective-permute-start.10
  62.3 16.8 %collective-permute-done.10.refs_4_ = bf16[1040,512]{1,0:T(8,128)(2,1)S(1)} collective-permute-done((bf16[1040,512]{1,0:T(8,128)(2,1)}, bf16[1040,512]{1,0:T(8,128)(2,1)S(1)}, u32[]{:S(2)}, u32[]{:S(2)}) %collective-permute-start.10) | collective-permute-done | bytes 1064992 | tf_op jit(solution)/shard_map/ppermute | solution.py:692
  79.1 4.6 collective-permute-done.11.refs_4_
  83.7 2.2 collective-permute-done.12.refs_10_
  90.4 2.7 shard_map.239
  93.0 5.8 %shard_map.240 = (f32[8,2048]{1,0:T(8,128)S(1)}, bf16[512,2048]{1,0:T(8,128)(2,1)S(1)}, bf16[512,1536]{1,0:T(8,128)(2,1)}, bf16[512,1536]{1,0:T(8,128)(2,1)}, bf...) custom-call(s32[5]{0:T(128)S(1)} %stack.34.pos, bf16[512,2048]{1,0:T(8,128)(2,1)S(1)} %get-tuple-element.225.x_all, ...), custom_call_target="tpu_custom_call" | custom-call | tf_op jit(solution)/shard_map/pallas_call | solution.py:115
  98.9 12.8 %collective-permute-done.16.refs_2_ = bf16[1024,512]{1,0:T(8,128)(2,1)S(1)} collective-permute-done((bf16[1024,512]{1,0:T(8,128)(2,1)S(1)}, bf16[1024,512]{1,0:T(8,128)(2,1)S(1)}, u32[]{:S(2)}, u32[]{:S(2)}) %collective-permute-start.16) | collective-permute-done | bytes 1048608 | tf_op jit(solution)/shard_map/ppermute | solution.py:692
  115.4 3.8 shard_map.241
  128.8 6.8 %collective-permute-done.35.refs_28_ = bf16[512,512]{1,0:T(8,128)(2,1)S(1)} collective-permute-done((bf16[512,512]{1,0:T(8,128)(2,1)S(1)}, bf16[512,512]{1,0:T(8,128)(2,1)S(1)}, u32[]{:S(2)}, u32[]{:S(2)}) %collective-permute-start.35) | collective-permute-done | bytes 524320 | tf_op jit(solution)/shard_map/ppermute | solution.py:692
  137.1 6.2 %shard_map.242 = (bf16[512,512]{1,0:T(8,128)(2,1)}, bf16[512,512]{1,0:T(8,128)(2,1)}, bf16[512,512]{1,0:T(8,128)(2,1)}, f32[8,512]{1,0:T(8,128)S(1)}, bf16[128,2...) custom-call(s32[5]{0:T(128)S(1)} %stack.34.pos, ...), custom_call_target="tpu_custom_call" | custom-call | tf_op jit(solution)/shard_map/pallas_call | solution.py:115
  143.4 13.6 %collective-permute-done.32.refs_14_ = bf16[1024,512]{1,0:T(8,128)(2,1)S(1)} collective-permute-done((bf16[1024,512]{1,0:T(8,128)(2,1)S(1)}, bf16[1024,512]{1,0:T(8,128)(2,1)S(1)}, u32[]{:S(2)}, u32[]{:S(2)}) %collective-permute-start.32) | collective-permute-done | bytes 1048608 | tf_op jit(solution)/shard_map/ppermute | solution.py:692
  162.5 10.0 %collective-permute-done.37.refs_1_ = bf16[128,2048]{1,0:T(8,128)(2,1)S(1)} collective-permute-done((bf16[128,2048]{1,0:T(8,128)(2,1)S(1)}, bf16[128,2048]{1,0:T(8,128)(2,1)S(1)}, u32[]{:S(2)}, u32[]{:S(2)}) %collective-permute-start.37) | collective-permute-done | bytes 524320 | tf_op jit(solution)/shard_map/ppermute | solution.py:692
  172.5 2.4 collective-permute-done.38.refs_2_
  174.9 7.3 %collective-permute-done.39.refs_3_ = bf16[128,2048]{1,0:T(8,128)(2,1)S(1)} collective-permute-done((bf16[128,2048]{1,0:T(8,128)(2,1)S(1)}, bf16[128,2048]{1,0:T(8,128)(2,1)S(1)}, u32[]{:S(2)}, u32[]{:S(2)}) %collective-permute-start.39) | collective-permute-done | bytes 524320 | tf_op jit(solution)/shard_map/ppermute | solution.py:692
  183.1 2.5 collective-permute-start.42
  187.3 6.2 %collective-permute-done.44.refs_30_ = bf16[512,512]{1,0:T(8,128)(2,1)S(1)} collective-permute-done((bf16[512,512]{1,0:T(8,128)(2,1)}, bf16[512,512]{1,0:T(8,128)(2,1)S(1)}, u32[]{:S(2)}, u32[]{:S(2)}) %collective-permute-start.44) | collective-permute-done | bytes 524320 | tf_op jit(solution)/shard_map/ppermute | solution.py:692
  194.0 2.0 collective-permute-done.46.block
  198.0 6.7 %shard_map.244 = (bf16[512,1024]{1,0:T(8,128)(2,1)S(1)}, bf16[512,1024]{1,0:T(8,128)(2,1)S(1)}, bf16[512,1024]{1,0:T(8,128)(2,1)S(1)}, bf16[512,1024]{1,0:T(8,12...) custom-call(bf16[128,2048]{1,0:T(8,128)(2,1)S(1)} %collective-permut, ...), custom_call_target="tpu_custom_call" | custom-call | tf_op jit(solution)/shard_map/pallas_call | solution.py:115
  205.3 5.8 %collective-permute-done.47.block = bf16[128,2048]{1,0:T(8,128)(2,1)S(1)} collective-permute-done((bf16[128,2048]{1,0:T(8,128)(2,1)S(1)}, bf16[128,2048]{1,0:T(8,128)(2,1)S(1)}, u32[]{:S(2)}, u32[]{:S(2)}) %collective-permute-start.47) | collective-permute-done | bytes 524320 | tf_op jit(solution)/shard_map/ppermute | solution.py:692
  212.7 6.6 %shard_map.245 = (bf16[512,1024]{1,0:T(8,128)(2,1)S(1)}, bf16[512,1024]{1,0:T(8,128)(2,1)S(1)}, bf16[512,1024]{1,0:T(8,128)(2,1)S(1)}, bf16[512,1024]{1,0:T(8,12...) custom-call(bf16[128,2048]{1,0:T(8,128)(2,1)S(1)} %get-tuple-element, ...), custom_call_target="tpu_custom_call", output_to_operand_aliasing={{0}: (33, {}), {1}: (34, {}), {2}: (35, {}), {3}: (36, {}),... | custom-call | tf_op jit(solution)/shard_map/pallas_call | solution.py:115
  219.3 6.7 %shard_map.246 = (bf16[512,1024]{1,0:T(8,128)(2,1)S(1)}, bf16[512,1024]{1,0:T(8,128)(2,1)S(1)}, bf16[512,1024]{1,0:T(8,128)(2,1)S(1)}, bf16[512,1024]{1,0:T(8,12...) custom-call(bf16[128,2048]{1,0:T(8,128)(2,1)S(1)} %collective-permut, ...), custom_call_target="tpu_custom_call", output_to_operand_aliasing={{0}: (33, {}), {1}: (34, {}), {2}: (35, {}), {3}: (36, {}),... | custom-call | tf_op jit(solution)/shard_map/pallas_call | solution.py:115
  226.6 7.0 %collective-permute-done.48.block = bf16[128,2048]{1,0:T(8,128)(2,1)S(1)} collective-permute-done((bf16[128,2048]{1,0:T(8,128)(2,1)S(1)}, bf16[128,2048]{1,0:T(8,128)(2,1)S(1)}, u32[]{:S(2)}, u32[]{:S(2)}) %collective-permute-start.48) | collective-permute-done | bytes 524320 | tf_op jit(solution)/shard_map/ppermute | solution.py:692
  233.6 6.6 %shard_map.247 = (bf16[512,1024]{1,0:T(8,128)(2,1)S(1)}, bf16[512,1024]{1,0:T(8,128)(2,1)S(1)}, bf16[512,1024]{1,0:T(8,128)(2,1)S(1)}, bf16[512,1024]{1,0:T(8,12...) custom-call(bf16[128,2048]{1,0:T(8,128)(2,1)S(1)} %collective-permut, ...), custom_call_target="tpu_custom_call", output_to_operand_aliasing={{0}: (33, {}), {1}: (34, {}), {2}: (35, {}), {3}: (36, {}),... | custom-call | tf_op jit(solution)/shard_map/pallas_call | solution.py:115
  246.4 7.0 %collective-permute-done.51.refs_1_ = bf16[128,2048]{1,0:T(8,128)(2,1)S(1)} collective-permute-done((bf16[128,2048]{1,0:T(8,128)(2,1)S(1)}, bf16[128,2048]{1,0:T(8,128)(2,1)S(1)}, u32[]{:S(2)}, u32[]{:S(2)}) %collective-permute-start.51) | collective-permute-done | bytes 524320 | tf_op jit(solution)/shard_map/ppermute | solution.py:692
  255.4 2.5 collective-permute-start.52
  257.8 2.5 collective-permute-start.59
  260.3 6.8 %collective-permute-done.52.block = bf16[128,2048]{1,0:T(8,128)(2,1)S(1)} collective-permute-done((bf16[128,2048]{1,0:T(8,128)(2,1)S(1)}, bf16[128,2048]{1,0:T(8,128)(2,1)S(1)}, u32[]{:S(2)}, u32[]{:S(2)}) %collective-permute-start.52) | collective-permute-done | bytes 524320 | tf_op jit(solution)/shard_map/ppermute | solution.py:692
  267.1 2.8 collective-permute-start.55
  272.6 7.9 %shard_map.249 = (bf16[512,1024]{1,0:T(8,128)(2,1)S(1)}, bf16[512,1024]{1,0:T(8,128)(2,1)S(1)}, bf16[512,1024]{1,0:T(8,128)(2,1)S(1)}, bf16[512,1024]{1,0:T(8,12...) custom-call(bf16[128,2048]{1,0:T(8,128)(2,1)S(1)} %collective-permute-done.52.blo, ...), custom_call_target="tpu_custom_call" | custom-call | tf_op jit(solution)/shard_map/pallas_call | solution.py:115
  281.3 8.0 %shard_map.250 = (bf16[512,1024]{1,0:T(8,128)(2,1)S(1)}, bf16[512,1024]{1,0:T(8,128)(2,1)S(1)}, bf16[512,1024]{1,0:T(8,128)(2,1)S(1)}, bf16[512,1024]{1,0:T(8,12...) custom-call(bf16[128,2048]{1,0:T(8,128)(2,1)S(1)} %get-tuple-element, ...), custom_call_target="tpu_custom_call", output_to_operand_aliasing={{0}: (37, {}), {1}: (38, {}), {2}: (39, {}), {3}: (40, {}),... | custom-call | tf_op jit(solution)/shard_map/pallas_call | solution.py:115
  293.4 7.9 %shard_map.251 = (bf16[512,1024]{1,0:T(8,128)(2,1)S(1)}, bf16[512,1024]{1,0:T(8,128)(2,1)S(1)}, bf16[512,1024]{1,0:T(8,128)(2,1)S(1)}, bf16[512,1024]{1,0:T(8,12...) custom-call(bf16[128,2048]{1,0:T(8,128)(2,1)S(1)} %collective-permut, ...), custom_call_target="tpu_custom_call", output_to_operand_aliasing={{0}: (37, {}), {1}: (38, {}), {2}: (39, {}), {3}: (40, {})} | custom-call | tf_op jit(solution)/shard_map/pallas_call | solution.py:115
  302.6 2.6 collective-permute-start.62
  305.2 8.0 %shard_map.252 = (bf16[512,1024]{1,0:T(8,128)(2,1)S(1)}, bf16[512,1024]{1,0:T(8,128)(2,1)S(1)}, bf16[512,1024]{1,0:T(8,128)(2,1)S(1)}, bf16[512,1024]{1,0:T(8,12...) custom-call(bf16[128,2048]{1,0:T(8,128)(2,1)S(1)} %collective-permut, ...), custom_call_target="tpu_custom_call", output_to_operand_aliasing={{0}: (37, {}), {1}: (38, {}), {2}: (39, {}), {3}: (40, {}),... | custom-call | tf_op jit(solution)/shard_map/pallas_call | solution.py:115
  313.4 2.7 collective-permute-start.63
  318.6 6.3 %collective-permute-done.63.refs_1_ = bf16[128,2048]{1,0:T(8,128)(2,1)S(1)} collective-permute-done((bf16[128,2048]{1,0:T(8,128)(2,1)S(1)}, bf16[128,2048]{1,0:T(8,128)(2,1)S(1)}, u32[]{:S(2)}, u32[]{:S(2)}) %collective-permute-start.63) | collective-permute-done | bytes 524320 | tf_op jit(solution)/shard_map/ppermute | solution.py:692
  330.4 10.1 %collective-permute-done.66.refs_7_ = bf16[128,2048]{1,0:T(8,128)(2,1)S(1)} collective-permute-done((bf16[128,2048]{1,0:T(8,128)(2,1)S(1)}, bf16[128,2048]{1,0:T(8,128)(2,1)S(1)}, u32[]{:S(2)}, u32[]{:S(2)}) %collective-permute-start.66) | collective-permute-done | bytes 524320 | tf_op jit(solution)/shard_map/ppermute | solution.py:692
  343.1 2.6 convolution_convert_fusion.2
  347.0 2.6 convolution_convert_fusion.4
  356.3 8.1 %shard_map.254 = (f32[512,512]{1,0:T(8,128)S(1)}, f32[512,512]{1,0:T(8,128)S(1)}, bf16[512,512]{1,0:T(8,128)(2,1)S(1)}, f32[8,512]{1,0:T(8,128)S(1)}, f32[8,512]...) custom-call(s32[5]{0:T(128)S(1)} %stack.34.pos, f32[8,128]{1,0:T(8,128)S(1)} %get-tuple-element.238.refs_1_.refs_0_, ...), custom_call_target="tpu_custom_call" | custom-call | tf_op jit(solution)/shard_map/pallas_call | solution.py:115
  371.2 2.0 collective-permute-done.74
  375.1 2.0 collective-permute-done.75
  378.7 2.3 shard_map.260
  381.1 2.1 shard_map.256
  384.1 2.9 collective-permute-start.86
  390.5 2.1 shard_map.259
  393.2 19.6 %collective-permute-done.79 = bf16[1024,512]{1,0:T(8,128)(2,1)S(1)} collective-permute-done((bf16[1024,512]{1,0:T(8,128)(2,1)S(1)}, bf16[1024,512]{1,0:T(8,128)(2,1)S(1)}, u32[]{:S(2)}, u32[]{:S(2)}) %collective-permute-start.79) | collective-permute-done | bytes 1048608 | tf_op jit(solution)/shard_map/ppermute | solution.py:692
  415.7 3.1 collective-permute-start.87
  422.5 2.1 shard_map.258
  424.6 4.3 shard_map.257
  429.5 12.4 %collective-permute-done.87 = bf16[1040,512]{1,0:T(8,128)(2,1)S(1)} collective-permute-done((bf16[1040,512]{1,0:T(8,128)(2,1)S(1)}, bf16[1040,512]{1,0:T(8,128)(2,1)S(1)}, u32[]{:S(2)}, u32[]{:S(2)}) %collective-permute-start.87) | collective-permute-done | bytes 1064992 | tf_op jit(solution)/shard_map/ppermute | solution.py:692
  443.7 3.7 collective-permute-start.88
  450.9 5.8 %shard_map.261 = f32[1024,512]{1,0:T(8,128)} custom-call(bf16[256,1024]{1,0:T(8,128)(2,1)S(1)} %get-tuple-element.311.refs_0_, bf16[256,1024]{1,0:T(8,128)(2,1)S(1)} %collective-permute-done.91.refs_1_, bf16[256,1024]{1,0:T(8,128)(2,1)S(1)} %collective-permute-done.57.refs_2_, bf16[256,1024]{1,0:T(8,128)(2,1)S(1)} %collective-permute-done.94.refs_3_, ...), custom_call_target="tpu_custom_call" | custom-call | tf_op jit(solution)/shard_map/pallas_call | solution.py:115
  456.7 12.9 %collective-permute-done.90 = bf16[1024,512]{1,0:T(8,128)(2,1)S(1)} collective-permute-done((bf16[1024,512]{1,0:T(8,128)(2,1)S(1)}, bf16[1024,512]{1,0:T(8,128)(2,1)S(1)}, u32[]{:S(2)}, u32[]{:S(2)}) %collective-permute-start.90) | collective-permute-done | bytes 1048608 | tf_op jit(solution)/shard_map/ppermute | solution.py:692
  477.9 2.9 collective-permute-done.81
  480.9 2.0 collective-permute-start.103
  484.9 4.9 collective-permute-done.105.refs_2_
  489.8 6.0 %collective-permute-done.106.refs_3_ = bf16[80,1536]{1,0:T(8,128)(2,1)S(1)} collective-permute-done((bf16[80,1536]{1,0:T(8,128)(2,1)S(1)}, bf16[80,1536]{1,0:T(8,128)(2,1)S(1)}, u32[]{:S(2)}, u32[]{:S(2)}) %collective-permute-start.106) | collective-permute-done | bytes 245792 | tf_op jit(solution)/shard_map/ppermute | solution.py:692
  498.2 7.5 %collective-permute-done.103 = bf16[128,2048]{1,0:T(8,128)(2,1)S(1)} collective-permute-done((bf16[128,2048]{1,0:T(8,128)(2,1)S(1)}, bf16[128,2048]{1,0:T(8,128)(2,1)S(1)}, u32[]{:S(2)}, u32[]{:S(2)}) %collective-permute-start.103) | collective-permute-done | bytes 524320 | tf_op jit(solution)/shard_map/ppermute | solution.py:692
  (290 shorter events, 131.3 us)
Async XLA Ops:
  2.0 26.9 %collective-permute-start.3 = (bf16[512,512]{1,0:T(8,128)(2,1)S(1)}, bf16[512,512]{1,0:T(8,128)(2,1)}, u32[]{:S(2)}, u32[]{:S(2)}) collective-permute-start(bf16[512,512]{1,0:T(8,128)(2,1)S(1)} %get-tuple-element.250.refs_16_), channel_id=1, source_target_pairs={{0,16},{1,17},{2,18},{3,19},{4,20},{5,21},{6,22},{7,23},{8,24},{9,... | collective-permute-start | bytes 1572872 | tf_op jit(solution)/shard_map/ppermute | solution.py:692
  5.0 23.9 %collective-permute-start.4 = (bf16[512,512]{1,0:T(8,128)(2,1)S(1)}, bf16[512,512]{1,0:T(8,128)(2,1)}, u32[]{:S(2)}, u32[]{:S(2)}) collective-permute-start(bf16[512,512]{1,0:T(8,128)(2,1)S(1)} %get-tuple-element.251.refs_20_), channel_id=1, source_target_pairs={{0,2},{1,3},{2,0},{3,1},{4,6},{5,7},{6,4},{7,5},{8,10},{9,11},{10,... | collective-permute-start | bytes 1572872 | tf_op jit(solution)/shard_map/ppermute | solution.py:692
  11.0 18.0 %collective-permute-start = (bf16[80,1536]{1,0:T(8,128)(2,1)S(1)}, bf16[80,1536]{1,0:T(8,128)(2,1)S(1)}, u32[]{:S(2)}, u32[]{:S(2)}) collective-permute-start(bf16[80,1536]{1,0:T(8,128)(2,1)S(1)} %get-tuple-element.216), channel_id=1, source_target_pairs={{0,2},{1,3},{2,0},{3,1},{4,6},{5,7},{6,4},{7,5},{8,10},{9,11},{10,... | collective-permute-start | bytes 737288 | tf_op jit(solution)/shard_map/ppermute | solution.py:692
  11.5 17.4 %collective-permute-start.1 = (bf16[80,1536]{1,0:T(8,128)(2,1)S(1)}, bf16[80,1536]{1,0:T(8,128)(2,1)S(1)}, u32[]{:S(2)}, u32[]{:S(2)}) collective-permute-start(bf16[80,1536]{1,0:T(8,128)(2,1)S(1)} %get-tuple-element.217), channel_id=1, source_target_pairs={{0,16},{1,17},{2,18},{3,19},{4,20},{5,21},{6,22},{7,23},{8,24},{9,... | collective-permute-start | bytes 737288 | tf_op jit(solution)/shard_map/ppermute | solution.py:692
  11.6 17.3 %collective-permute-start.2 = (bf16[80,1536]{1,0:T(8,128)(2,1)S(1)}, bf16[80,1536]{1,0:T(8,128)(2,1)S(1)}, u32[]{:S(2)}, u32[]{:S(2)}) collective-permute-start(bf16[80,1536]{1,0:T(8,128)(2,1)S(1)} %get-tuple-element.218), channel_id=1, source_target_pairs={{0,18},{1,19},{2,16},{3,17},{4,22},{5,23},{6,20},{7,21},{8,26},{9,... | collective-permute-start | bytes 737288 | tf_op jit(solution)/shard_map/ppermute | solution.py:692
  30.0 24.6 %collective-permute-start.9 = (bf16[1040,512]{1,0:T(8,128)(2,1)}, bf16[1040,512]{1,0:T(8,128)(2,1)}, u32[]{:S(2)}, u32[]{:S(2)}) collective-permute-start(bf16[1040,512]{1,0:T(8,128)(2,1)} %get-tuple-element.223.refs_0_), channel_id=1, source_target_pairs={{0,8},{1,9},{2,10},{3,11},{4,0},{5,1},{6,2},{7,3},{8,12},{9,13},{1... | collective-permute-start | bytes 3194888 | tf_op jit(solution)/shard_map/ppermute | solution.py:692
  54.6 24.4 %collective-permute-start.10 = (bf16[1040,512]{1,0:T(8,128)(2,1)}, bf16[1040,512]{1,0:T(8,128)(2,1)S(1)}, u32[]{:S(2)}, u32[]{:S(2)}) collective-permute-start(bf16[1040,512]{1,0:T(8,128)(2,1)} %collective-permute-done.9.refs_2_), channel_id=1, source_target_pairs={{0,8},{1,9},{2,10},{3,11},{4,0},{5,1},{6,2},{7,3},{8,12},{9,13},{1... | collective-permute-start | bytes 3194888 | tf_op jit(solution)/shard_map/ppermute | solution.py:692
  58.5 25.1 %collective-permute-start.11 = (bf16[1024,512]{1,0:T(8,128)(2,1)S(1)}, bf16[1024,512]{1,0:T(8,128)(2,1)S(1)}, u32[]{:S(2)}, u32[]{:S(2)}) collective-permute-start(bf16[1024,512]{1,0:T(8,128)(2,1)S(1)} %copy-done), channel_id=1, source_target_pairs={{0,16},{1,17},{2,18},{3,19},{4,20},{5,21},{6,22},{7,23},{8,24},{9,... | collective-permute-start | bytes 3145736 | tf_op jit(solution)/shard_map/ppermute | solution.py:692
  60.0 27.6 %collective-permute-start.21 = (bf16[1040,512]{1,0:T(8,128)(2,1)}, bf16[1040,512]{1,0:T(8,128)(2,1)S(1)}, u32[]{:S(2)}, u32[]{:S(2)}) collective-permute-start(bf16[1040,512]{1,0:T(8,128)(2,1)} %get-tuple-element.223.refs_0_), channel_id=1, source_target_pairs={{0,1},{1,0},{2,3},{3,2},{4,5},{5,4},{6,7},{7,6},{8,9},{9,8},{10,11... | collective-permute-start | bytes 3194888 | tf_op jit(solution)/shard_map/ppermute | solution.py:692
  60.7 25.2 %collective-permute-start.12 = (bf16[1024,512]{1,0:T(8,128)(2,1)S(1)}, bf16[1024,512]{1,0:T(8,128)(2,1)S(1)}, u32[]{:S(2)}, u32[]{:S(2)}) collective-permute-start(bf16[1024,512]{1,0:T(8,128)(2,1)S(1)} %copy-done.1), channel_id=1, source_target_pairs={{0,2},{1,3},{2,0},{3,1},{4,6},{5,7},{6,4},{7,5},{8,10},{9,11},{10,... | collective-permute-start | bytes 3145736 | tf_op jit(solution)/shard_map/ppermute | solution.py:692
  62.2 26.7 %collective-permute-start.22 = (bf16[1040,512]{1,0:T(8,128)(2,1)}, bf16[1040,512]{1,0:T(8,128)(2,1)S(1)}, u32[]{:S(2)}, u32[]{:S(2)}) collective-permute-start(bf16[1040,512]{1,0:T(8,128)(2,1)} %collective-permute-done.9.refs_2_), channel_id=1, source_target_pairs={{0,1},{1,0},{2,3},{3,2},{4,5},{5,4},{6,7},{7,6},{8,9},{9,8},{10,11... | collective-permute-start | bytes 3194888 | tf_op jit(solution)/shard_map/ppermute | solution.py:692
  85.9 26.1 %collective-permute-start.15 = (bf16[1040,512]{1,0:T(8,128)(2,1)S(1)}, bf16[1040,512]{1,0:T(8,128)(2,1)S(1)}, u32[]{:S(2)}, u32[]{:S(2)}) collective-permute-start(bf16[1040,512]{1,0:T(8,128)(2,1)S(1)} %collective-permute-done.10.refs_4_), channel_id=1, source_target_pairs={{0,8},{1,9},{2,10},{3,11},{4,0},{5,1},{6,2},{7,3},{8,12},{9,13},{1... | collective-permute-start | bytes 3194888 | tf_op jit(solution)/shard_map/ppermute | solution.py:692
  86.8 24.9 %collective-permute-start.16 = (bf16[1024,512]{1,0:T(8,128)(2,1)S(1)}, bf16[1024,512]{1,0:T(8,128)(2,1)S(1)}, u32[]{:S(2)}, u32[]{:S(2)}) collective-permute-start(bf16[1024,512]{1,0:T(8,128)(2,1)S(1)} %copy-done), channel_id=1, source_target_pairs={{0,2},{1,3},{2,0},{3,1},{4,6},{5,7},{6,4},{7,5},{8,10},{9,11},{10,... | collective-permute-start | bytes 3145736 | tf_op jit(solution)/shard_map/ppermute | solution.py:692
  87.5 24.4 %collective-permute-start.17 = (bf16[1024,512]{1,0:T(8,128)(2,1)S(1)}, bf16[1024,512]{1,0:T(8,128)(2,1)S(1)}, u32[]{:S(2)}, u32[]{:S(2)}) collective-permute-start(bf16[1024,512]{1,0:T(8,128)(2,1)S(1)} %copy-done.1), channel_id=1, source_target_pairs={{0,16},{1,17},{2,18},{3,19},{4,20},{5,21},{6,22},{7,23},{8,24},{9,... | collective-permute-start | bytes 3145736 | tf_op jit(solution)/shard_map/ppermute | solution.py:692
  88.8 23.1 %collective-permute-start.19 = (bf16[1024,512]{1,0:T(8,128)(2,1)S(1)}, bf16[1024,512]{1,0:T(8,128)(2,1)S(1)}, u32[]{:S(2)}, u32[]{:S(2)}) collective-permute-start(bf16[1024,512]{1,0:T(8,128)(2,1)S(1)} %collective-permute-done.11.refs_4_), channel_id=1, source_target_pairs={{0,1},{1,0},{2,3},{3,2},{4,5},{5,4},{6,7},{7,6},{8,9},{9,8},{10,11... | collective-permute-start | bytes 3145736 | tf_op jit(solution)/shard_map/ppermute | solution.py:692
  88.8 23.1 %collective-permute-start.20 = (bf16[1024,512]{1,0:T(8,128)(2,1)S(1)}, bf16[1024,512]{1,0:T(8,128)(2,1)S(1)}, u32[]{:S(2)}, u32[]{:S(2)}) collective-permute-start(bf16[1024,512]{1,0:T(8,128)(2,1)S(1)} %collective-permute-done.12.refs_10_), channel_id=1, source_target_pairs={{0,1},{1,0},{2,3},{3,2},{4,5},{5,4},{6,7},{7,6},{8,9},{9,8},{10,11... | collective-permute-start | bytes 3145736 | tf_op jit(solution)/shard_map/ppermute | solution.py:692
  112.6 14.4 %collective-permute-start.33 = (bf16[512,512]{1,0:T(8,128)(2,1)S(1)}, bf16[512,512]{1,0:T(8,128)(2,1)S(1)}, u32[]{:S(2)}, u32[]{:S(2)}) collective-permute-start(bf16[512,512]{1,0:T(8,128)(2,1)S(1)} %get-tuple-element.250.refs_16_), channel_id=1, source_target_pairs={{0,2},{1,3},{2,0},{3,1},{4,6},{5,7},{6,4},{7,5},{8,10},{9,11},{10,... | collective-permute-start | bytes 1572872 | tf_op jit(solution)/shard_map/ppermute | solution.py:692
  120.8 14.8 %collective-permute-start.35 = (bf16[512,512]{1,0:T(8,128)(2,1)S(1)}, bf16[512,512]{1,0:T(8,128)(2,1)S(1)}, u32[]{:S(2)}, u32[]{:S(2)}) collective-permute-start(bf16[512,512]{1,0:T(8,128)(2,1)S(1)} %get-tuple-element.251.refs_20_), channel_id=1, source_target_pairs={{0,16},{1,17},{2,18},{3,19},{4,20},{5,21},{6,22},{7,23},{8,24},{9,... | collective-permute-start | bytes 1572872 | tf_op jit(solution)/shard_map/ppermute | solution.py:692
  124.6 18.7 %collective-permute-start.29 = (bf16[1024,512]{1,0:T(8,128)(2,1)S(1)}, bf16[1024,512]{1,0:T(8,128)(2,1)S(1)}, u32[]{:S(2)}, u32[]{:S(2)}) collective-permute-start(bf16[1024,512]{1,0:T(8,128)(2,1)S(1)} %collective-permute-done.16.refs_2_), channel_id=1, source_target_pairs={{0,1},{1,0},{2,3},{3,2},{4,5},{5,4},{6,7},{7,6},{8,9},{9,8},{10,11... | collective-permute-start | bytes 3145736 | tf_op jit(solution)/shard_map/ppermute | solution.py:692
  124.6 18.7 %collective-permute-start.30 = (bf16[1024,512]{1,0:T(8,128)(2,1)S(1)}, bf16[1024,512]{1,0:T(8,128)(2,1)S(1)}, u32[]{:S(2)}, u32[]{:S(2)}) collective-permute-start(bf16[1024,512]{1,0:T(8,128)(2,1)S(1)} %collective-permute-done.17.refs_12_), channel_id=1, source_target_pairs={{0,1},{1,0},{2,3},{3,2},{4,5},{5,4},{6,7},{7,6},{8,9},{9,8},{10,11... | collective-permute-start | bytes 3145736 | tf_op jit(solution)/shard_map/ppermute | solution.py:692
  127.3 29.7 %collective-permute-start.32 = (bf16[1024,512]{1,0:T(8,128)(2,1)S(1)}, bf16[1024,512]{1,0:T(8,128)(2,1)S(1)}, u32[]{:S(2)}, u32[]{:S(2)}) collective-permute-start(bf16[1024,512]{1,0:T(8,128)(2,1)S(1)} %collective-permute-done.12.refs_10_), channel_id=1, source_target_pairs={{0,16},{1,17},{2,18},{3,19},{4,20},{5,21},{6,22},{7,23},{8,24},{9,... | collective-permute-start | bytes 3145736 | tf_op jit(solution)/shard_map/ppermute | solution.py:692
  135.6 22.9 %collective-permute-start.31 = (bf16[1024,512]{1,0:T(8,128)(2,1)S(1)}, bf16[1024,512]{1,0:T(8,128)(2,1)S(1)}, u32[]{:S(2)}, u32[]{:S(2)}) collective-permute-start(bf16[1024,512]{1,0:T(8,128)(2,1)S(1)} %collective-permute-done.11.refs_4_), channel_id=1, source_target_pairs={{0,2},{1,3},{2,0},{3,1},{4,6},{5,7},{6,4},{7,5},{8,10},{9,11},{10,... | collective-permute-start | bytes 3145736 | tf_op jit(solution)/shard_map/ppermute | solution.py:692
  158.5 14.0 %collective-permute-start.37 = (bf16[128,2048]{1,0:T(8,128)(2,1)S(1)}, bf16[128,2048]{1,0:T(8,128)(2,1)S(1)}, u32[]{:S(2)}, u32[]{:S(2)}) collective-permute-start(bf16[128,2048]{1,0:T(8,128)(2,1)S(1)} %get-tuple-element.253), channel_id=1, source_target_pairs={{0,2},{1,3},{2,0},{3,1},{4,6},{5,7},{6,4},{7,5},{8,10},{9,11},{10,... | collective-permute-start | bytes 1572872 | tf_op jit(solution)/shard_map/ppermute | solution.py:692
  160.0 14.9 %collective-permute-start.38 = (bf16[128,2048]{1,0:T(8,128)(2,1)S(1)}, bf16[128,2048]{1,0:T(8,128)(2,1)S(1)}, u32[]{:S(2)}, u32[]{:S(2)}) collective-permute-start(bf16[128,2048]{1,0:T(8,128)(2,1)S(1)} %get-tuple-element.254), channel_id=1, source_target_pairs={{0,16},{1,17},{2,18},{3,19},{4,20},{5,21},{6,22},{7,23},{8,24},{9,... | collective-permute-start | bytes 1572872 | tf_op jit(solution)/shard_map/ppermute | solution.py:692
  160.9 21.3 %collective-permute-start.39 = (bf16[128,2048]{1,0:T(8,128)(2,1)S(1)}, bf16[128,2048]{1,0:T(8,128)(2,1)S(1)}, u32[]{:S(2)}, u32[]{:S(2)}) collective-permute-start(bf16[128,2048]{1,0:T(8,128)(2,1)S(1)} %get-tuple-element.255), channel_id=1, source_target_pairs={{0,18},{1,19},{2,16},{3,17},{4,22},{5,23},{6,20},{7,21},{8,26},{9,... | collective-permute-start | bytes 1572872 | tf_op jit(solution)/shard_map/ppermute | solution.py:692
  162.0 35.9 %collective-permute-start.41 = (bf16[1024,512]{1,0:T(8,128)(2,1)S(1)}, bf16[1024,512]{1,0:T(8,128)(2,1)S(1)}, u32[]{:S(2)}, u32[]{:S(2)}) collective-permute-start(bf16[1024,512]{1,0:T(8,128)(2,1)S(1)} %collective-permute-done.32.refs_14_), channel_id=1, source_target_pairs={{0,1},{1,0},{2,3},{3,2},{4,5},{5,4},{6,7},{7,6},{8,9},{9,8},{10,11... | collective-permute-start | bytes 3145736 | tf_op jit(solution)/shard_map/ppermute | solution.py:692
  162.0 35.9 %collective-permute-start.40 = (bf16[1024,512]{1,0:T(8,128)(2,1)S(1)}, bf16[1024,512]{1,0:T(8,128)(2,1)S(1)}, u32[]{:S(2)}, u32[]{:S(2)}) collective-permute-start(bf16[1024,512]{1,0:T(8,128)(2,1)S(1)} %collective-permute-done.31.refs_6_), channel_id=1, source_target_pairs={{0,1},{1,0},{2,3},{3,2},{4,5},{5,4},{6,7},{7,6},{8,9},{9,8},{10,11... | collective-permute-start | bytes 3145736 | tf_op jit(solution)/shard_map/ppermute | solution.py:692
  196.0 15.1 %collective-permute-start.47 = (bf16[128,2048]{1,0:T(8,128)(2,1)S(1)}, bf16[128,2048]{1,0:T(8,128)(2,1)S(1)}, u32[]{:S(2)}, u32[]{:S(2)}) collective-permute-start(bf16[128,2048]{1,0:T(8,128)(2,1)S(1)} %collective-permute-done.46.block), channel_id=1, source_target_pairs={{0,8},{1,9},{2,10},{3,11},{4,0},{5,1},{6,2},{7,3},{8,12},{9,13},{1... | collective-permute-start | bytes 1572872 | tf_op jit(solution)/shard_map/ppermute | solution.py:692
  204.7 21.3 %collective-permute-start.49 = (bf16[128,2048]{1,0:T(8,128)(2,1)S(1)}, bf16[128,2048]{1,0:T(8,128)(2,1)S(1)}, u32[]{:S(2)}, u32[]{:S(2)}) collective-permute-start(bf16[128,2048]{1,0:T(8,128)(2,1)S(1)} %convert_element_type.197), channel_id=1, source_target_pairs={{0,8},{1,9},{2,10},{3,11},{4,0},{5,1},{6,2},{7,3},{8,12},{9,13},{1... | collective-permute-start | bytes 1572872 | tf_op jit(solution)/shard_map/ppermute | solution.py:692
  211.1 22.5 %collective-permute-start.48 = (bf16[128,2048]{1,0:T(8,128)(2,1)S(1)}, bf16[128,2048]{1,0:T(8,128)(2,1)S(1)}, u32[]{:S(2)}, u32[]{:S(2)}) collective-permute-start(bf16[128,2048]{1,0:T(8,128)(2,1)S(1)} %collective-permute-done.47.block), channel_id=1, source_target_pairs={{0,8},{1,9},{2,10},{3,11},{4,0},{5,1},{6,2},{7,3},{8,12},{9,13},{1... | collective-permute-start | bytes 1572872 | tf_op jit(solution)/shard_map/ppermute | solution.py:692
  226.1 16.0 %collective-permute-start.50 = (bf16[128,2048]{1,0:T(8,128)(2,1)S(1)}, bf16[128,2048]{1,0:T(8,128)(2,1)S(1)}, u32[]{:S(2)}, u32[]{:S(2)}) collective-permute-start(bf16[128,2048]{1,0:T(8,128)(2,1)S(1)} %add_convert_fusion.13), channel_id=1, source_target_pairs={{0,8},{1,9},{2,10},{3,11},{4,0},{5,1},{6,2},{7,3},{8,12},{9,13},{1... | collective-permute-start | bytes 1572872 | tf_op jit(solution)/shard_map/ppermute | solution.py:692
  243.8 26.1 %collective-permute-start.53 = (bf16[512,1024]{1,0:T(8,128)(2,1)S(1)}, bf16[512,1024]{1,0:T(8,128)(2,1)S(1)}, u32[]{:S(2)}, u32[]{:S(2)}) collective-permute-start(bf16[512,1024]{1,0:T(8,128)(2,1)S(1)} %get-tuple-element.301), channel_id=1, source_target_pairs={{0,2},{1,3},{2,0},{3,1},{4,6},{5,7},{6,4},{7,5},{8,10},{9,11},{10,... | collective-permute-start | bytes 3145736 | tf_op jit(solution)/shard_map/ppermute | solution.py:692
  245.5 26.1 %collective-permute-start.54 = (bf16[512,1024]{1,0:T(8,128)(2,1)S(1)}, bf16[512,1024]{1,0:T(8,128)(2,1)S(1)}, u32[]{:S(2)}, u32[]{:S(2)}) collective-permute-start(bf16[512,1024]{1,0:T(8,128)(2,1)S(1)} %get-tuple-element.302), channel_id=1, source_target_pairs={{0,16},{1,17},{2,18},{3,19},{4,20},{5,21},{6,22},{7,23},{8,24},{9,... | collective-permute-start | bytes 3145736 | tf_op jit(solution)/shard_map/ppermute | solution.py:692
  257.8 33.8 %collective-permute-start.59 = (bf16[512,1024]{1,0:T(8,128)(2,1)S(1)}, bf16[512,1024]{1,0:T(8,128)(2,1)S(1)}, u32[]{:S(2)}, u32[]{:S(2)}) collective-permute-start(bf16[512,1024]{1,0:T(8,128)(2,1)S(1)} %get-tuple-element.301), channel_id=1, source_target_pairs={{0,18},{1,19},{2,16},{3,17},{4,22},{5,23},{6,20},{7,21},{8,26},{9,... | collective-permute-start | bytes 3145736 | tf_op jit(solution)/shard_map/ppermute | solution.py:692
  267.1 24.5 %collective-permute-start.55 = (bf16[128,2048]{1,0:T(8,128)(2,1)S(1)}, bf16[128,2048]{1,0:T(8,128)(2,1)S(1)}, u32[]{:S(2)}, u32[]{:S(2)}) collective-permute-start(bf16[128,2048]{1,0:T(8,128)(2,1)S(1)} %collective-permute-done.52.block), channel_id=1, source_target_pairs={{0,8},{1,9},{2,10},{3,11},{4,0},{5,1},{6,2},{7,3},{8,12},{9,13},{1... | collective-permute-start | bytes 1572872 | tf_op jit(solution)/shard_map/ppermute | solution.py:692
  280.6 20.8 %collective-permute-start.60 = (bf16[128,2048]{1,0:T(8,128)(2,1)S(1)}, bf16[128,2048]{1,0:T(8,128)(2,1)S(1)}, u32[]{:S(2)}, u32[]{:S(2)}) collective-permute-start(bf16[128,2048]{1,0:T(8,128)(2,1)S(1)} %convert_element_type.202), channel_id=1, source_target_pairs={{0,8},{1,9},{2,10},{3,11},{4,0},{5,1},{6,2},{7,3},{8,12},{9,13},{1... | collective-permute-start | bytes 1572872 | tf_op jit(solution)/shard_map/ppermute | solution.py:692
  289.2 16.0 %collective-permute-start.57 = (bf16[256,1024]{1,0:T(8,128)(2,1)S(1)}, bf16[256,1024]{1,0:T(8,128)(2,1)S(1)}, u32[]{:S(2)}, u32[]{:S(2)}) collective-permute-start(bf16[256,1024]{1,0:T(8,128)(2,1)S(1)} %get-tuple-element.311.refs_0_), channel_id=1, source_target_pairs={{0,2},{1,3},{2,0},{3,1},{4,6},{5,7},{6,4},{7,5},{8,10},{9,11},{10,... | collective-permute-start | bytes 1572872 | tf_op jit(solution)/shard_map/ppermute | solution.py:692
  290.0 15.2 %collective-permute-start.58 = (bf16[256,1024]{1,0:T(8,128)(2,1)S(1)}, bf16[256,1024]{1,0:T(8,128)(2,1)S(1)}, u32[]{:S(2)}, u32[]{:S(2)}) collective-permute-start(bf16[256,1024]{1,0:T(8,128)(2,1)S(1)} %get-tuple-element.312), channel_id=1, source_target_pairs={{0,16},{1,17},{2,18},{3,19},{4,20},{5,21},{6,22},{7,23},{8,24},{9,... | collective-permute-start | bytes 1572872 | tf_op jit(solution)/shard_map/ppermute | solution.py:692
  291.6 13.6 %collective-permute-start.56 = (bf16[128,2048]{1,0:T(8,128)(2,1)S(1)}, bf16[128,2048]{1,0:T(8,128)(2,1)S(1)}, u32[]{:S(2)}, u32[]{:S(2)}) collective-permute-start(bf16[128,2048]{1,0:T(8,128)(2,1)S(1)} %collective-permute-done.55.block), channel_id=1, source_target_pairs={{0,8},{1,9},{2,10},{3,11},{4,0},{5,1},{6,2},{7,3},{8,12},{9,13},{1... | collective-permute-start | bytes 1572872 | tf_op jit(solution)/shard_map/ppermute | solution.py:692
  326.9 13.6 %collective-permute-start.66 = (bf16[128,2048]{1,0:T(8,128)(2,1)S(1)}, bf16[128,2048]{1,0:T(8,128)(2,1)S(1)}, u32[]{:S(2)}, u32[]{:S(2)}) collective-permute-start(bf16[128,2048]{1,0:T(8,128)(2,1)S(1)} %get-tuple-element.347.refs_6_), channel_id=1, source_target_pairs={{0,2},{1,3},{2,0},{3,1},{4,6},{5,7},{6,4},{7,5},{8,10},{9,11},{10,... | collective-permute-start | bytes 1572872 | tf_op jit(solution)/shard_map/ppermute | solution.py:692
  328.3 25.3 %collective-permute-start.67 = (bf16[128,2048]{1,0:T(8,128)(2,1)S(1)}, bf16[128,2048]{1,0:T(8,128)(2,1)S(1)}, u32[]{:S(2)}, u32[]{:S(2)}) collective-permute-start(bf16[128,2048]{1,0:T(8,128)(2,1)S(1)} %get-tuple-element.347.refs_6_), channel_id=1, source_target_pairs={{0,16},{1,17},{2,18},{3,19},{4,20},{5,21},{6,22},{7,23},{8,24},{9,... | collective-permute-start | bytes 1572872 | tf_op jit(solution)/shard_map/ppermute | solution.py:692
  329.2 24.4 %collective-permute-start.68 = (bf16[128,2048]{1,0:T(8,128)(2,1)S(1)}, bf16[128,2048]{1,0:T(8,128)(2,1)S(1)}, u32[]{:S(2)}, u32[]{:S(2)}) collective-permute-start(bf16[128,2048]{1,0:T(8,128)(2,1)S(1)} %get-tuple-element.347.refs_6_), channel_id=1, source_target_pairs={{0,18},{1,19},{2,16},{3,17},{4,22},{5,23},{6,20},{7,21},{8,26},{9,... | collective-permute-start | bytes 1572872 | tf_op jit(solution)/shard_map/ppermute | solution.py:692
  354.3 13.8 %collective-permute-start.70 = (bf16[1024,1024]{1,0:T(8,128)(2,1)S(1)}, bf16[1024,1024]{1,0:T(8,128)(2,1)S(1)}, u32[]{:S(2)}, u32[]{:S(2)}) collective-permute-start(bf16[1024,1024]{1,0:T(8,128)(2,1)S(1)} %convolution_convert_fusion.6), channel_id=1, source_target_pairs={{0,1},{1,0},{2,3},{3,2},{4,5},{5,4},{6,7},{7,6},{8,9},{9,8},{10,11... | collective-permute-start | bytes 6291464 | tf_op jit(solution)/shard_map/ppermute | solution.py:692
  354.7 14.8 %collective-permute-start.69 = (bf16[256,1024]{1,0:T(8,128)(2,1)S(1)}, bf16[256,1024]{1,0:T(8,128)(2,1)S(1)}, u32[]{:S(2)}, u32[]{:S(2)}) collective-permute-start(bf16[256,1024]{1,0:T(8,128)(2,1)S(1)} %get-tuple-element.337), channel_id=1, source_target_pairs={{0,18},{1,19},{2,16},{3,17},{4,22},{5,23},{6,20},{7,21},{8,26},{9,... | collective-permute-start | bytes 1572872 | tf_op jit(solution)/shard_map/ppermute | solution.py:692
  383.2 30.9 %collective-permute-start.76 = (bf16[1040,512]{1,0:T(8,128)(2,1)S(1)}, bf16[1040,512]{1,0:T(8,128)(2,1)S(1)}, u32[]{:S(2)}, u32[]{:S(2)}) collective-permute-start(bf16[1040,512]{1,0:T(8,128)(2,1)S(1)} %get-tuple-element.376), channel_id=1, source_target_pairs={{0,1},{1,0},{2,3},{3,2},{4,5},{5,4},{6,7},{7,6},{8,9},{9,8},{10,11... | collective-permute-start | bytes 3194888 | tf_op jit(solution)/shard_map/ppermute | solution.py:692
  384.1 30.6 %collective-permute-start.86 = (bf16[1040,512]{1,0:T(8,128)(2,1)S(1)}, bf16[1040,512]{1,0:T(8,128)(2,1)S(1)}, u32[]{:S(2)}, u32[]{:S(2)}) collective-permute-start(bf16[1040,512]{1,0:T(8,128)(2,1)S(1)} %add_convert_fusion.6), channel_id=1, source_target_pairs={{0,8},{1,9},{2,10},{3,11},{4,0},{5,1},{6,2},{7,3},{8,12},{9,13},{1... | collective-permute-start | bytes 3194888 | tf_op jit(solution)/shard_map/ppermute | solution.py:692
  387.2 25.6 %collective-permute-start.79 = (bf16[1024,512]{1,0:T(8,128)(2,1)S(1)}, bf16[1024,512]{1,0:T(8,128)(2,1)S(1)}, u32[]{:S(2)}, u32[]{:S(2)}) collective-permute-start(bf16[1024,512]{1,0:T(8,128)(2,1)S(1)} %fusion.5), channel_id=1, source_target_pairs={{0,2},{1,3},{2,0},{3,1},{4,6},{5,7},{6,4},{7,5},{8,10},{9,11},{10,... | collective-permute-start | bytes 3145736 | tf_op jit(solution)/shard_map/ppermute | solution.py:692
  388.9 25.2 %collective-permute-start.77 = (bf16[1024,512]{1,0:T(8,128)(2,1)S(1)}, bf16[1024,512]{1,0:T(8,128)(2,1)S(1)}, u32[]{:S(2)}, u32[]{:S(2)}) collective-permute-start(bf16[1024,512]{1,0:T(8,128)(2,1)S(1)} %get-tuple-element.385), channel_id=1, source_target_pairs={{0,16},{1,17},{2,18},{3,19},{4,20},{5,21},{6,22},{7,23},{8,24},{9,... | collective-permute-start | bytes 3145736 | tf_op jit(solution)/shard_map/ppermute | solution.py:692
  392.6 22.6 %collective-permute-start.96 = (bf16[512,512]{1,0:T(8,128)(2,1)S(1)}, bf16[512,512]{1,0:T(8,128)(2,1)S(1)}, u32[]{:S(2)}, u32[]{:S(2)}) collective-permute-start(bf16[512,512]{1,0:T(8,128)(2,1)S(1)} %get-tuple-element.429), channel_id=1, source_target_pairs={{0,1},{1,0},{2,3},{3,2},{4,5},{5,4},{6,7},{7,6},{8,9},{9,8},{10,11... | collective-permute-start | bytes 1572872 | tf_op jit(solution)/shard_map/ppermute | solution.py:692
  415.2 13.8 %collective-permute-start.84 = (bf16[1040,512]{1,0:T(8,128)(2,1)S(1)}, bf16[1040,512]{1,0:T(8,128)(2,1)S(1)}, u32[]{:S(2)}, u32[]{:S(2)}) collective-permute-start(bf16[1040,512]{1,0:T(8,128)(2,1)S(1)} %get-tuple-element.393), channel_id=1, source_target_pairs={{0,1},{1,0},{2,3},{3,2},{4,5},{5,4},{6,7},{7,6},{8,9},{9,8},{10,11... | collective-permute-start | bytes 3194888 | tf_op jit(solution)/shard_map/ppermute | solution.py:692
  415.7 26.1 %collective-permute-start.87 = (bf16[1040,512]{1,0:T(8,128)(2,1)S(1)}, bf16[1040,512]{1,0:T(8,128)(2,1)S(1)}, u32[]{:S(2)}, u32[]{:S(2)}) collective-permute-start(bf16[1040,512]{1,0:T(8,128)(2,1)S(1)} %add_convert_fusion.5), channel_id=1, source_target_pairs={{0,8},{1,9},{2,10},{3,11},{4,0},{5,1},{6,2},{7,3},{8,12},{9,13},{1... | collective-permute-start | bytes 3194888 | tf_op jit(solution)/shard_map/ppermute | solution.py:692
  419.7 27.6 %collective-permute-start.80 = (bf16[1024,512]{1,0:T(8,128)(2,1)S(1)}, bf16[1024,512]{1,0:T(8,128)(2,1)S(1)}, u32[]{:S(2)}, u32[]{:S(2)}) collective-permute-start(bf16[1024,512]{1,0:T(8,128)(2,1)S(1)} %add_convert_fusion.7), channel_id=1, source_target_pairs={{0,16},{1,17},{2,18},{3,19},{4,20},{5,21},{6,22},{7,23},{8,24},{9,... | collective-permute-start | bytes 3145736 | tf_op jit(solution)/shard_map/ppermute | solution.py:692
  421.0 27.2 %collective-permute-start.78 = (bf16[1024,512]{1,0:T(8,128)(2,1)S(1)}, bf16[1024,512]{1,0:T(8,128)(2,1)S(1)}, u32[]{:S(2)}, u32[]{:S(2)}) collective-permute-start(bf16[1024,512]{1,0:T(8,128)(2,1)S(1)} %add_convert_fusion.8), channel_id=1, source_target_pairs={{0,2},{1,3},{2,0},{3,1},{4,6},{5,7},{6,4},{7,5},{8,10},{9,11},{10,... | collective-permute-start | bytes 3145736 | tf_op jit(solution)/shard_map/ppermute | solution.py:692
  428.9 14.7 %collective-permute-start.101 = (bf16[256,1024]{1,0:T(8,128)(2,1)S(1)}, bf16[256,1024]{1,0:T(8,128)(2,1)S(1)}, u32[]{:S(2)}, u32[]{:S(2)}) collective-permute-start(bf16[256,1024]{1,0:T(8,128)(2,1)S(1)} %collective-permute-done.69.refs_14_), channel_id=1, source_target_pairs={{0,1},{1,0},{2,3},{3,2},{4,5},{5,4},{6,7},{7,6},{8,9},{9,8},{10,11... | collective-permute-start | bytes 1572872 | tf_op jit(solution)/shard_map/ppermute | solution.py:692
  429.0 14.7 %collective-permute-start.95 = (bf16[256,1024]{1,0:T(8,128)(2,1)S(1)}, bf16[256,1024]{1,0:T(8,128)(2,1)S(1)}, u32[]{:S(2)}, u32[]{:S(2)}) collective-permute-start(bf16[256,1024]{1,0:T(8,128)(2,1)S(1)} %collective-permute-done.64.refs_10_), channel_id=1, source_target_pairs={{0,1},{1,0},{2,3},{3,2},{4,5},{5,4},{6,7},{7,6},{8,9},{9,8},{10,11... | collective-permute-start | bytes 1572872 | tf_op jit(solution)/shard_map/ppermute | solution.py:692
  441.8 27.8 %collective-permute-start.90 = (bf16[1024,512]{1,0:T(8,128)(2,1)S(1)}, bf16[1024,512]{1,0:T(8,128)(2,1)S(1)}, u32[]{:S(2)}, u32[]{:S(2)}) collective-permute-start(bf16[1024,512]{1,0:T(8,128)(2,1)S(1)} %fusion.6), channel_id=1, source_target_pairs={{0,2},{1,3},{2,0},{3,1},{4,6},{5,7},{6,4},{7,5},{8,10},{9,11},{10,... | collective-permute-start | bytes 3145736 | tf_op jit(solution)/shard_map/ppermute | solution.py:692
  443.6 29.0 %collective-permute-start.83 = (bf16[1040,512]{1,0:T(8,128)(2,1)S(1)}, bf16[1040,512]{1,0:T(8,128)(2,1)S(1)}, u32[]{:S(2)}, u32[]{:S(2)}) collective-permute-start(bf16[1040,512]{1,0:T(8,128)(2,1)S(1)} %get-tuple-element.391), channel_id=1, source_target_pairs={{0,1},{1,0},{2,3},{3,2},{4,5},{5,4},{6,7},{7,6},{8,9},{9,8},{10,11... | collective-permute-start | bytes 3194888 | tf_op jit(solution)/shard_map/ppermute | solution.py:692
  443.7 29.7 %collective-permute-start.88 = (bf16[1040,512]{1,0:T(8,128)(2,1)S(1)}, bf16[1040,512]{1,0:T(8,128)(2,1)S(1)}, u32[]{:S(2)}, u32[]{:S(2)}) collective-permute-start(bf16[1040,512]{1,0:T(8,128)(2,1)S(1)} %add_convert_fusion.4), channel_id=1, source_target_pairs={{0,8},{1,9},{2,10},{3,11},{4,0},{5,1},{6,2},{7,3},{8,12},{9,13},{1... | collective-permute-start | bytes 3194888 | tf_op jit(solution)/shard_map/ppermute | solution.py:692
  447.3 26.0 %collective-permute-start.89 = (bf16[1024,512]{1,0:T(8,128)(2,1)S(1)}, bf16[1024,512]{1,0:T(8,128)(2,1)S(1)}, u32[]{:S(2)}, u32[]{:S(2)}) collective-permute-start(bf16[1024,512]{1,0:T(8,128)(2,1)S(1)} %get-tuple-element.398), channel_id=1, source_target_pairs={{0,16},{1,17},{2,18},{3,19},{4,20},{5,21},{6,22},{7,23},{8,24},{9,... | collective-permute-start | bytes 3145736 | tf_op jit(solution)/shard_map/ppermute | solution.py:692
  450.1 30.7 %collective-permute-start.81 = (bf16[128,2048]{1,0:T(8,128)(2,1)S(1)}, bf16[128,2048]{1,0:T(8,128)(2,1)S(1)}, u32[]{:S(2)}, u32[]{:S(2)}) collective-permute-start(bf16[128,2048]{1,0:T(8,128)(2,1)S(1)} %get-tuple-element.387), channel_id=1, source_target_pairs={{0,2},{1,3},{2,0},{3,1},{4,6},{5,7},{6,4},{7,5},{8,10},{9,11},{10,... | collective-permute-start | bytes 1572872 | tf_op jit(solution)/shard_map/ppermute | solution.py:692
  469.6 15.0 %collective-permute-start.82 = (bf16[128,2048]{1,0:T(8,128)(2,1)S(1)}, bf16[128,2048]{1,0:T(8,128)(2,1)S(1)}, u32[]{:S(2)}, u32[]{:S(2)}) collective-permute-start(bf16[128,2048]{1,0:T(8,128)(2,1)S(1)} %get-tuple-element.388), channel_id=1, source_target_pairs={{0,16},{1,17},{2,18},{3,19},{4,20},{5,21},{6,22},{7,23},{8,24},{9,... | collective-permute-start | bytes 1572872 | tf_op jit(solution)/shard_map/ppermute | solution.py:692
  475.2 14.7 %collective-permute-start.105 = (bf16[80,1536]{1,0:T(8,128)(2,1)S(1)}, bf16[80,1536]{1,0:T(8,128)(2,1)S(1)}, u32[]{:S(2)}, u32[]{:S(2)}) collective-permute-start(bf16[80,1536]{1,0:T(8,128)(2,1)S(1)} %get-tuple-element.405), channel_id=1, source_target_pairs={{0,16},{1,17},{2,18},{3,19},{4,20},{5,21},{6,22},{7,23},{8,24},{9,... | collective-permute-start | bytes 737288 | tf_op jit(solution)/shard_map/ppermute | solution.py:692
  476.0 19.8 %collective-permute-start.106 = (bf16[80,1536]{1,0:T(8,128)(2,1)S(1)}, bf16[80,1536]{1,0:T(8,128)(2,1)S(1)}, u32[]{:S(2)}, u32[]{:S(2)}) collective-permute-start(bf16[80,1536]{1,0:T(8,128)(2,1)S(1)} %get-tuple-element.406), channel_id=1, source_target_pairs={{0,18},{1,19},{2,16},{3,17},{4,22},{5,23},{6,20},{7,21},{8,26},{9,... | collective-permute-start | bytes 737288 | tf_op jit(solution)/shard_map/ppermute | solution.py:692
  480.9 24.9 %collective-permute-start.103 = (bf16[128,2048]{1,0:T(8,128)(2,1)S(1)}, bf16[128,2048]{1,0:T(8,128)(2,1)S(1)}, u32[]{:S(2)}, u32[]{:S(2)}) collective-permute-start(bf16[128,2048]{1,0:T(8,128)(2,1)S(1)} %get-tuple-element.407), channel_id=1, source_target_pairs={{0,18},{1,19},{2,16},{3,17},{4,22},{5,23},{6,20},{7,21},{8,26},{9,... | collective-permute-start | bytes 1572872 | tf_op jit(solution)/shard_map/ppermute | solution.py:692
  (74 other events, 620.5 us)
